TPU v7x, 32 devices: a whole 2x2x4 slice. The times are simulated.
32 devices in a mesh: dp: 16 (over z, x, core), map: 2 (over y).
Axes of the slice: x: 2, y: 2, z: 4, core: 2. Of those that a mesh axis runs over, the one named last changes fastest.
Arguments:
- patches: bfloat16 [32, 576, 1024], P(('dp', 'map')), may hold values from -6 to 6
- keep_mask: int32 [32, 576], P(('dp', 'map')), may hold values from 0 to 1, as said below
- block_cotangent: bfloat16 [32, 576, 1024], P(('dp', 'map')), may hold values from -6 to 6
- token_cotangent: bfloat16 [32, 8, 1024], P('dp', 'map'), may hold values from -6 to 6
- first_gain: float32 [1024], P(('dp', 'map')), may hold values from 0.1 to 1.9
- first_shift: float32 [1024], P(('dp', 'map')), may hold values from -3 to 3
- qkv_weight: float32 [1024, 3072], P(('dp', 'map')), may hold values from -0.1875 to 0.1875
- query_bias: float32 [1024], P(('dp', 'map')), may hold values from -3 to 3
- value_bias: float32 [1024], P(('dp', 'map')), may hold values from -3 to 3
- out_weight: float32 [1024, 1024], P(('dp', 'map')), may hold values from -1.5 to 1.5
- out_bias: float32 [1024], P(('dp', 'map')), may hold values from -3 to 3
- second_gain: float32 [1024], P(('dp', 'map')), may hold values from 0.1 to 1.9
- second_shift: float32 [1024], P(('dp', 'map')), may hold values from -3 to 3
- up_weight: float32 [1024, 4096], P(('dp', 'map')), may hold values from -0.1875 to 0.1875
- up_bias: float32 [4096], P(('dp', 'map')), may hold values from -3 to 3
- down_weight: float32 [4096, 1024], P(('dp', 'map')), may hold values from -0.09375 to 0.09375
- down_bias: float32 [1024], P(('dp', 'map')), may hold values from -3 to 3
- learn_gain: float32 [1024], P(('dp', 'map')), may hold values from 0.1 to 1.9
- learn_shift: float32 [1024], P(('dp', 'map')), may hold values from -3 to 3
- map_weight: float32 [1024, 8], P(('dp', 'map')), may hold values from -0.1875 to 0.1875
Outputs:
- block_out: bfloat16 [32, 576, 1024], P(('dp', 'map'))
- tokens: bfloat16 [32, 8, 1024], P('dp', 'map')
- grad_patches: bfloat16 [32, 576, 1024], P(('dp', 'map'))
- grad_first_gain: float32 [1024], P(('dp', 'map'))
- grad_first_shift: float32 [1024], P(('dp', 'map'))
- grad_qkv_weight: float32 [1024, 3072], P(('dp', 'map'))
- grad_query_bias: float32 [1024], P(('dp', 'map'))
- grad_value_bias: float32 [1024], P(('dp', 'map'))
- grad_out_weight: float32 [1024, 1024], P(('dp', 'map'))
- grad_out_bias: float32 [1024], P(('dp', 'map'))
- grad_second_gain: float32 [1024], P(('dp', 'map'))
- grad_second_shift: float32 [1024], P(('dp', 'map'))
- grad_up_weight: float32 [1024, 4096], P(('dp', 'map'))
- grad_up_bias: float32 [4096], P(('dp', 'map'))
- grad_down_weight: float32 [4096, 1024], P(('dp', 'map'))
- grad_down_bias: float32 [1024], P(('dp', 'map'))
- grad_learn_gain: float32 [1024], P(('dp', 'map'))
- grad_learn_shift: float32 [1024], P(('dp', 'map'))
- grad_map_weight: float32 [1024, 8], P(('dp', 'map'))
Inputs may be any that keep to these rules, and one draw needn't show every extreme that they name: `keep_mask`: each image keeps exactly 512 of its 576 patches.
All inputs are finite; a program needn't handle non-finite values.
Results may differ from a plain program's by a relative error of at most 0.012.
The roundings to bfloat16 on the way count: a program that leaves them out, or rounds other values in their place, can miss the bound.
Values may be sent and summed in bfloat16 or wider, within the bound.
No kernel may reach another device: no remote copies, remote signals or barrier semaphores. Data moves between devices by JAX's collectives and lax.ppermute only.
A program may use at most 192 MiB of HBM per device.

v0:
```python
from functools import partial

import jax
import jax.numpy as jnp
from jax import lax
from jax.sharding import PartitionSpec as P

HD = 64
KEEP = 512


HIGHEST = lax.Precision.HIGHEST
EPSILON = 1e-06
MASKED_SCORE = -1e30


def normalize(values):
    center = values - jnp.mean(values, axis=-1, keepdims=True)
    spread = lax.rsqrt(jnp.mean(center * center, axis=-1, keepdims=True) + EPSILON)
    return (center * spread, spread)


def norm_back(grad_hat, normed, spread):
    return spread * (
        grad_hat
        - jnp.mean(grad_hat, axis=-1, keepdims=True)
        - normed * jnp.mean(grad_hat * normed, axis=-1, keepdims=True)
    )


def matmul(left, right):
    return jnp.dot(left, right, preferred_element_type=jnp.float32)


def sum_rows(left, right):
    return lax.dot_general(
        left, right, (((0,), (0,)), ((), ())), preferred_element_type=jnp.float32
    )


def sum_cols(left, right):
    return lax.dot_general(
        left, right, (((1,), (1,)), ((), ())), preferred_element_type=jnp.float32
    )


def column_sum(values):
    return jnp.sum(values.astype(jnp.float32), axis=0)


def widen(values):
    return values.astype(jnp.float32)


def per_device(
    patches,
    keep_mask,
    block_cotangent,
    token_cotangent,
    first_gain,
    first_shift,
    qkv_weight,
    query_bias,
    value_bias,
    out_weight,
    out_bias,
    second_gain,
    second_shift,
    up_weight,
    up_bias,
    down_weight,
    down_bias,
    learn_gain,
    learn_shift,
    map_weight,
):
    masters = (
        first_gain,
        first_shift,
        qkv_weight,
        query_bias,
        value_bias,
        out_weight,
        out_bias,
        second_gain,
        second_shift,
        up_weight,
        up_bias,
        down_weight,
        down_bias,
        learn_gain,
        learn_shift,
        map_weight,
    )
    wire_weights = tuple((entry.astype(jnp.bfloat16) for entry in masters))
    gathered = (
        lax.all_gather(wire_weights[0], ("dp", "map"), axis=0, tiled=True),
        lax.all_gather(wire_weights[1], ("dp", "map"), axis=0, tiled=True),
        lax.all_gather(wire_weights[2], ("dp", "map"), axis=0, tiled=True),
        lax.all_gather(wire_weights[3], ("dp", "map"), axis=0, tiled=True),
        lax.all_gather(wire_weights[4], ("dp", "map"), axis=0, tiled=True),
        lax.all_gather(wire_weights[5], ("dp", "map"), axis=0, tiled=True),
        lax.all_gather(wire_weights[6], ("dp", "map"), axis=0, tiled=True),
        lax.all_gather(wire_weights[7], ("dp", "map"), axis=0, tiled=True),
        lax.all_gather(wire_weights[8], ("dp", "map"), axis=0, tiled=True),
        lax.all_gather(wire_weights[9], ("dp", "map"), axis=0, tiled=True),
        lax.all_gather(wire_weights[10], ("dp", "map"), axis=0, tiled=True),
        lax.all_gather(wire_weights[11], ("dp", "map"), axis=0, tiled=True),
        lax.all_gather(wire_weights[12], ("dp", "map"), axis=0, tiled=True),
        lax.all_gather(wire_weights[13], ("dp", "map"), axis=0, tiled=True),
        lax.all_gather(wire_weights[14], ("dp", "map"), axis=0, tiled=True),
        lax.all_gather(wire_weights[15], ("dp", "map"), axis=0, tiled=True),
    )
    (
        gain_one,
        shift_one,
        qkv_full,
        query_shift,
        value_shift,
        out_full,
        out_shift,
        gain_two,
        shift_two,
        up_full,
        up_shift,
        down_full,
        down_shift,
        learn_scale,
        learn_offset,
        map_full,
    ) = gathered
    images, patch_count, model_width = patches.shape
    row_count = images * patch_count
    head_count = model_width // HD
    scaling = HD ** (-0.5)

    def as_heads(tensor):
        return tensor.reshape(images, patch_count, head_count, HD)

    key_live = (keep_mask > 0)[:, None, None, :]
    inputs = patches.reshape(row_count, model_width).astype(jnp.float32)
    normed_one, spread_one = normalize(inputs)
    hidden_one = (normed_one * widen(gain_one) + widen(shift_one)).astype(jnp.bfloat16)
    qkv_proj = matmul(hidden_one, qkv_full)
    queries = ((qkv_proj[:, :model_width] + widen(query_shift)) * scaling).astype(jnp.bfloat16)
    keys_all = qkv_proj[:, model_width : 2 * model_width].astype(jnp.bfloat16)
    values_all = (qkv_proj[:, 2 * model_width :] + widen(value_shift)).astype(jnp.bfloat16)

    def raw_scores():
        scores = jnp.einsum(
            "bphd,bkhd->bhpk",
            as_heads(queries),
            as_heads(keys_all),
            preferred_element_type=jnp.float32,
        )
        return jnp.where(key_live, scores, MASKED_SCORE)

    scores = raw_scores()
    row_max = jnp.max(scores, axis=-1, keepdims=True)
    expons = jnp.exp(scores - row_max)
    denominator = jnp.sum(expons, axis=-1, keepdims=True)
    log_total = row_max + jnp.log(denominator)
    attention = (expons / denominator).astype(jnp.bfloat16)
    mixed = jnp.einsum(
        "bhpk,bkhd->bphd", attention, as_heads(values_all), preferred_element_type=jnp.float32
    )
    mixed_low = mixed.reshape(row_count, model_width).astype(jnp.bfloat16)
    residual_one = inputs + matmul(mixed_low, out_full) + widen(out_shift)
    normed_two, spread_two = normalize(residual_one)
    hidden_two = (normed_two * widen(gain_two) + widen(shift_two)).astype(jnp.bfloat16)
    pre_act = matmul(hidden_two, up_full) + widen(up_shift)
    activation = jax.nn.gelu(pre_act, approximate=False).astype(jnp.bfloat16)
    block = residual_one + matmul(activation, down_full) + widen(down_shift)
    normed_three, spread_three = normalize(block)
    learned_in = normed_three * widen(learn_scale) + widen(learn_offset)
    sigma = jax.nn.sigmoid(jnp.dot(learned_in, widen(map_full), precision=HIGHEST))
    live_rows = keep_mask.reshape(row_count, 1).astype(jnp.float32) * KEEP ** (-0.5)
    token_weights = sigma * live_rows
    block_images = block.reshape(images, patch_count, model_width)
    token_local = jnp.einsum(
        "bps,bpd->bsd",
        token_weights.reshape(images, patch_count, -1),
        block_images,
        precision=HIGHEST,
    )
    tokens_out = lax.all_to_all(
        token_local.astype(jnp.bfloat16), "map", split_axis=1, concat_axis=0, tiled=True
    )
    block_out = block.reshape(images, patch_count, model_width).astype(jnp.bfloat16)
    regathered = (
        lax.all_gather(wire_weights[0], ("dp", "map"), axis=0, tiled=True),
        lax.all_gather(wire_weights[1], ("dp", "map"), axis=0, tiled=True),
        lax.all_gather(wire_weights[2], ("dp", "map"), axis=0, tiled=True),
        lax.all_gather(wire_weights[3], ("dp", "map"), axis=0, tiled=True),
        lax.all_gather(wire_weights[4], ("dp", "map"), axis=0, tiled=True),
        lax.all_gather(wire_weights[5], ("dp", "map"), axis=0, tiled=True),
        lax.all_gather(wire_weights[6], ("dp", "map"), axis=0, tiled=True),
        lax.all_gather(wire_weights[7], ("dp", "map"), axis=0, tiled=True),
        lax.all_gather(wire_weights[8], ("dp", "map"), axis=0, tiled=True),
        lax.all_gather(wire_weights[9], ("dp", "map"), axis=0, tiled=True),
        lax.all_gather(wire_weights[10], ("dp", "map"), axis=0, tiled=True),
        lax.all_gather(wire_weights[11], ("dp", "map"), axis=0, tiled=True),
        lax.all_gather(wire_weights[12], ("dp", "map"), axis=0, tiled=True),
        lax.all_gather(wire_weights[13], ("dp", "map"), axis=0, tiled=True),
        lax.all_gather(wire_weights[14], ("dp", "map"), axis=0, tiled=True),
        lax.all_gather(wire_weights[15], ("dp", "map"), axis=0, tiled=True),
    )
    (
        gain_one,
        shift_one,
        qkv_full,
        query_shift,
        value_shift,
        out_full,
        out_shift,
        gain_two,
        shift_two,
        up_full,
        up_shift,
        down_full,
        down_shift,
        learn_scale,
        learn_offset,
        map_full,
    ) = regathered
    token_grad = lax.all_to_all(
        token_cotangent, "map", split_axis=0, concat_axis=1, tiled=True
    ).astype(jnp.float32)
    grad_block = block_cotangent.reshape(row_count, model_width).astype(jnp.float32)
    grad_block = grad_block + jnp.einsum(
        "bps,bsd->bpd",
        token_weights.reshape(images, patch_count, -1),
        token_grad,
        precision=HIGHEST,
    ).reshape(row_count, model_width)
    grad_token_weights = jnp.einsum(
        "bpd,bsd->bps", block_images, token_grad, precision=HIGHEST
    ).reshape(row_count, -1)
    grad_logits = grad_token_weights * live_rows * sigma * (1.0 - sigma)
    grad_map = lax.dot_general(learned_in, grad_logits, (((0,), (0,)), ((), ())), precision=HIGHEST)
    grad_learned = lax.dot_general(
        grad_logits, widen(map_full), (((1,), (1,)), ((), ())), precision=HIGHEST
    )
    grad_learn_scale = jnp.sum(grad_learned * normed_three, axis=0)
    grad_learn_offset = jnp.sum(grad_learned, axis=0)
    grad_block = grad_block + norm_back(
        grad_learned * widen(learn_scale), normed_three, spread_three
    )
    grad_down_low = grad_block.astype(jnp.bfloat16)
    grad_down = sum_rows(activation, grad_down_low)
    grad_down_shift = column_sum(grad_down_low)
    grad_act = sum_cols(grad_down_low, down_full)
    gelu_pull = jax.vjp(partial(jax.nn.gelu, approximate=False), pre_act)[1]
    grad_pre = gelu_pull(grad_act)[0].astype(jnp.bfloat16)
    grad_up = sum_rows(hidden_two, grad_pre)
    grad_up_shift = column_sum(grad_pre)
    grad_hidden_two = sum_cols(grad_pre, up_full)
    grad_gain_two = jnp.sum(grad_hidden_two * normed_two, axis=0)
    grad_shift_two = jnp.sum(grad_hidden_two, axis=0)
    grad_residual = grad_block + norm_back(
        grad_hidden_two * widen(gain_two), normed_two, spread_two
    )
    grad_attn = grad_residual.astype(jnp.bfloat16)
    grad_out = sum_rows(mixed_low, grad_attn)
    grad_out_shift = column_sum(grad_attn)
    grad_mixed = as_heads(sum_cols(grad_attn, out_full).astype(jnp.bfloat16))
    probs = jnp.exp(raw_scores() - log_total)
    grad_probs = jnp.einsum(
        "bphd,bkhd->bhpk", grad_mixed, as_heads(values_all), preferred_element_type=jnp.float32
    )
    grad_values = jnp.einsum(
        "bhpk,bphd->bkhd",
        probs.astype(jnp.bfloat16),
        grad_mixed,
        preferred_element_type=jnp.float32,
    ).astype(jnp.bfloat16)
    along = jnp.sum(probs * grad_probs, axis=-1, keepdims=True)
    grad_scores = (probs * (grad_probs - along)).astype(jnp.bfloat16)
    grad_queries = jnp.einsum(
        "bhpk,bkhd->bphd", grad_scores, as_heads(keys_all), preferred_element_type=jnp.float32
    ).astype(jnp.bfloat16)
    grad_keys = jnp.einsum(
        "bhpk,bphd->bkhd", grad_scores, as_heads(queries), preferred_element_type=jnp.float32
    ).astype(jnp.bfloat16)
    grad_query_part = (widen(grad_queries.reshape(row_count, model_width)) * scaling).astype(
        jnp.bfloat16
    )
    grad_value_part = grad_values.reshape(row_count, model_width)
    grad_qkv = jnp.concatenate(
        [grad_query_part, grad_keys.reshape(row_count, model_width), grad_value_part], axis=1
    )
    grad_qkv_full = sum_rows(hidden_one, grad_qkv)
    grad_query_shift = column_sum(grad_query_part)
    grad_value_shift = column_sum(grad_value_part)
    grad_hidden_one = sum_cols(grad_qkv, qkv_full)
    grad_gain_one = jnp.sum(grad_hidden_one * normed_one, axis=0)
    grad_shift_one = jnp.sum(grad_hidden_one, axis=0)
    grad_inputs = grad_residual + norm_back(
        grad_hidden_one * widen(gain_one), normed_one, spread_one
    )
    grad_patches = grad_inputs.reshape(images, patch_count, model_width).astype(jnp.bfloat16)
    summed = (
        lax.psum_scatter(grad_gain_one, ("dp", "map"), scatter_dimension=0, tiled=True),
        lax.psum_scatter(grad_shift_one, ("dp", "map"), scatter_dimension=0, tiled=True),
        lax.psum_scatter(grad_qkv_full, ("dp", "map"), scatter_dimension=0, tiled=True),
        lax.psum_scatter(grad_query_shift, ("dp", "map"), scatter_dimension=0, tiled=True),
        lax.psum_scatter(grad_value_shift, ("dp", "map"), scatter_dimension=0, tiled=True),
        lax.psum_scatter(grad_out, ("dp", "map"), scatter_dimension=0, tiled=True),
        lax.psum_scatter(grad_out_shift, ("dp", "map"), scatter_dimension=0, tiled=True),
        lax.psum_scatter(grad_gain_two, ("dp", "map"), scatter_dimension=0, tiled=True),
        lax.psum_scatter(grad_shift_two, ("dp", "map"), scatter_dimension=0, tiled=True),
        lax.psum_scatter(grad_up, ("dp", "map"), scatter_dimension=0, tiled=True),
        lax.psum_scatter(grad_up_shift, ("dp", "map"), scatter_dimension=0, tiled=True),
        lax.psum_scatter(grad_down, ("dp", "map"), scatter_dimension=0, tiled=True),
        lax.psum_scatter(grad_down_shift, ("dp", "map"), scatter_dimension=0, tiled=True),
        lax.psum_scatter(grad_learn_scale, ("dp", "map"), scatter_dimension=0, tiled=True),
        lax.psum_scatter(grad_learn_offset, ("dp", "map"), scatter_dimension=0, tiled=True),
        lax.psum_scatter(grad_map, ("dp", "map"), scatter_dimension=0, tiled=True),
    )
    return (
        block_out,
        tokens_out,
        grad_patches,
        summed[0],
        summed[1],
        summed[2],
        summed[3],
        summed[4],
        summed[5],
        summed[6],
        summed[7],
        summed[8],
        summed[9],
        summed[10],
        summed[11],
        summed[12],
        summed[13],
        summed[14],
        summed[15],
    )


def solution(mesh):
    in_specs = (
        P(("dp", "map"), None, None),
        P(("dp", "map"), None),
        P(("dp", "map"), None, None),
        P("dp", "map", None),
        P(("dp", "map")),
        P(("dp", "map")),
        P(("dp", "map"), None),
        P(("dp", "map")),
        P(("dp", "map")),
        P(("dp", "map"), None),
        P(("dp", "map")),
        P(("dp", "map")),
        P(("dp", "map")),
        P(("dp", "map"), None),
        P(("dp", "map")),
        P(("dp", "map"), None),
        P(("dp", "map")),
        P(("dp", "map")),
        P(("dp", "map")),
        P(("dp", "map"), None),
    )
    out_specs = (
        P(("dp", "map"), None, None),
        P("dp", "map", None),
        P(("dp", "map"), None, None),
        P(("dp", "map")),
        P(("dp", "map")),
        P(("dp", "map"), None),
        P(("dp", "map")),
        P(("dp", "map")),
        P(("dp", "map"), None),
        P(("dp", "map")),
        P(("dp", "map")),
        P(("dp", "map")),
        P(("dp", "map"), None),
        P(("dp", "map")),
        P(("dp", "map"), None),
        P(("dp", "map")),
        P(("dp", "map")),
        P(("dp", "map")),
        P(("dp", "map"), None),
    )
    return jax.shard_map(
        per_device, mesh=mesh, in_specs=in_specs, out_specs=out_specs, check_vma=False
    )
```

profile of v0, /device:TPU:0, one launch (start us, length us, event | category | flops | bytes accessed | tf_op | source)
XLA Modules:
  0.0 1484.8 jit_solution(8600641471852131652)
XLA Ops:
  7.4 1.9 convert_element_type.243
  9.3 1.5 convert_element_type.255
  11.0 1.8 convert_element_type.263
  12.8 4.2 all-to-all-start.1
  20.8 42.1 %all-reduce.22 = (bf16[1024]{0:T(1024)(128)(2,1)S(1)}, bf16[1024]{0:T(1024)(128)(2,1)S(1)}, bf16[1024]{0:T(1024)(128)(2,1)S(1)}, bf16[1024]{0:T(1024)(128)(2,1)S...) all-reduce(bf16[1024]{0:T(1024)(128)(2,1)S(1)} %dynamic-update-slic, ...), channel_id=1, replica_groups=mesh['dp'=16,'map'=2] {'dp','map'}, use_global_device_ids=true, to_apply=%add.1 | all-reduce | flops 10240 | bytes 40960
  65.5 65.5 %all-gather = bf16[32,1,128]{2,1,0:T(2,128)(2,1)S(1)} all-gather(bf16[1,1,128]{2,1,0:T(2,128)(2,1)S(1)} %convert_bitcast_fusion.3), channel_id=1, replica_groups=mesh['dp'=16,'map'=2] {'dp','map'}, dimensions={0}, use_global_device_ids=true | all-gather | bytes 8448 | tf_op jit(solution)/shard_map/all_gather | solution.py:107
  132.2 64.5 %all-gather.1 = bf16[32,32,8]{1,2,0:T(8,128)(2,1)S(1)} all-gather(bf16[1,32,8]{1,2,0:T(8,128)(2,1)S(1)} %convert_bitcast_fusion.2), channel_id=1, replica_groups=mesh['dp'=16,'map'=2] {'dp','map'}, dimensions={0}, use_global_device_ids=true | all-gather | bytes 16896 | tf_op jit(solution)/shard_map/all_gather | solution.py:112
  198.1 6.2 fusion.78
  205.5 1.7 fusion.33
  207.9 2.1 copy.72
  210.1 2.9 copy.70
  213.0 10.4 select_reduce_fusion
  223.4 10.5 fusion
  234.5 11.5 fusion.40
  246.0 3.6 fusion.83
  250.3 30.9 %multiply_convert_fusion.1 = (bf16[576,4096]{1,0:T(8,128)(2,1)}, f32[576,4096]{1,0:T(8,128)}, f32[576,4096]{1,0:T(8,128)}) fusion(f32[4096]{0:T(1024)S(1)} %bitcast.136, bf16[1024,4096]{1,0:T(8,128)(2,1)} %all-gather.11.cloned.1.call-done, f32[576,1024]{1,0:T(8,128)S(1)} %get-tuple-element.63, f32[1024]{0:T(1024)S(1)} %convert_element_type.261, ...), kind=kOutput, calls=%fused_computation.17 | convolution fusion | flops 4990500864 | bytes 34370048 | tf_op jit(solution)/shard_map/dot_general | solution.py:32
  281.2 21.6 %all-gather.13.cloned.1.call-done = bf16[4096,1024]{1,0:T(8,128)(2,1)} async-done(((bf16[128,1024]{1,0:T(8,128)(2,1)}), bf16[4096,1024]{1,0:T(8,128)(2,1)}) %all-gather.13.cloned.1.call-update) | async-done | bytes 8388624 | tf_op jit(solution)/shard_map/all_gather | solution.py:108
  302.7 9.8 fusion.84
  313.3 1.6 fusion.56
  316.1 5.4 fusion.36
  321.5 2.6 fusion.85
  324.2 4.5 multiply_reduce_fusion.1
  328.8 1.9 fusion.35
  330.7 18.0 %convert_reduce_fusion = (f32[4096]{0:T(1024)}, bf16[576,4096]{1,0:T(8,128)(2,1)}) fusion(f32[576,4096]{1,0:T(8,128)} %get-tuple-element.55, bf16[4096,1024]{1,0:T(8,128)(2,1)} %all-gather.13.cloned.1.call-done, f32[576,1024]{1,0:T(8,128)S(1)} %fusion.35, f32[576,4096]{1,0:T(8,128)} %get-tuple-element.64, f32[4096]{0:T(1024)} %bitcast.135), kind=kOutput, calls=%fused_computation.15 | convolution fusion | flops 4872531968 | bytes 34373632 | tf_op jit(solution)/shard_map/dot_general | solution.py:42
  348.8 10.4 multiply_reduce_fusion.2
  359.2 1.7 convert_reduce_fusion.5
  360.9 1.4 copy-done.10
  362.3 3.8 fusion.66
  367.5 3.7 convolution_convert_fusion.2
  371.2 1.5 copy.76
  372.7 19.4 %multiply_reduce_fusion = (f32[16,576]{1,0:T(8,128)S(1)}, f32[16,576,576]{1,2,0:T(8,128)}) fusion(f32[16,576,576]{1,2,0:T(8,128)} %get-tuple-element.61, f32[16,576]{1,0:T(8,128)} %log_add_fusion, pred[576]{0:T(1024)(128)(4,1)} %copy-done.39, bf16[576,16,64]{0,2,1:T(8,128)(2,1)} %bitcast.128, bf16[576,16,64]{0,2,1:T(8,128)(2,1)} %bitcast.126), kind=kOutput, calls=%fused_computation.1 | convolution fusion | flops 700701696 | bytes 44900928 | tf_op jit(solution)/shard_map/bphd,bkhd->bhpk/dot_general | solution.py:268
  392.1 20.5 %multiply_convert_fusion = bf16[16,576,576]{1,2,0:T(8,128)(2,1)} fusion(f32[16,576,576]{1,2,0:T(8,128)} %get-tuple-element.69, f32[16,576,576]{1,2,0:T(8,128)} %get-tuple-element.61, f32[16,576]{1,0:T(8,128)S(1)} %get-tuple-element.68, f32[16,576]{1,0:T(8,128)S(1)} %copy-done.17, pred[576]{0:T(1024)(128)(4,1)S(1)} %copy-done.40), kind=kLoop, calls=%fused_computation | loop fusion | flops 26542080 | bytes 53158464 | tf_op jit(solution)/shard_map/convert_element_type | solution.py:278
  412.6 9.1 convolution_convert_fusion
  421.7 8.3 convert_reduce_fusion.3
  430.0 14.7 convert_reduce_fusion.2
  444.7 12.2 fusion.38
  457.0 13.2 fusion.80
  470.3 13.0 fusion.69
  484.0 1.9 fusion.59
  487.8 3.4 all-to-all-start
  491.3 9.1 fusion.29
  500.5 1.9 fusion.44
  502.6 42.5 %all-reduce.21 = (f32[1024]{0:T(1024)S(1)}, f32[1024]{0:T(1024)S(1)}, f32[1024]{0:T(1024)S(1)}, f32[1024]{0:T(1024)S(1)}, f32[1024]{0:T(1024)S(1)}, /*index=5*/f...) all-reduce(f32[1024]{0:T(1024)S(1)} %get-tuple-element.23, ...), channel_id=2, replica_groups=mesh['dp'=16,'map'=2] {'dp','map'}, use_global_device_ids=true, to_apply=%region_16.17.clone | all-reduce | flops 14336 | bytes 114688
  552.3 1.4 copy.85
  553.7 43.7 %reduce-scatter.10.cloned.1.call-done = f32[32,1024]{1,0:T(8,128)} async-done(((f32[1024,1024]{1,0:T(8,128)}), f32[32,1024]{1,0:T(8,128)}) %reduce-scatter.10.cloned.1.call-update) | async-done | bytes 131088 | tf_op jit(solution)/shard_map/reduce_scatter | solution.py:308
  597.3 160.1 %reduce-scatter.8.cloned.1.call-done = f32[32,3072]{1,0:T(8,128)} async-done(((f32[1024,3072]{1,0:T(8,128)}), f32[32,3072]{1,0:T(8,128)}) %reduce-scatter.8.cloned.1.call-update) | async-done | bytes 393232 | tf_op jit(solution)/shard_map/reduce_scatter | solution.py:305
  757.4 359.3 %reduce-scatter.12.cloned.1.call-done = f32[32,4096]{1,0:T(8,128)} async-done(((f32[1024,4096]{1,0:T(8,128)}), f32[32,4096]{1,0:T(8,128)}) %reduce-scatter.12.cloned.1.call-update) | async-done | bytes 524304 | tf_op jit(solution)/shard_map/reduce_scatter | solution.py:312
  1116.7 361.4 %reduce-scatter.14.cloned.1.call-done = f32[128,1024]{1,0:T(8,128)} async-done(((f32[4096,1024]{1,0:T(8,128)}), f32[128,1024]{1,0:T(8,128)}) %reduce-scatter.14.cloned.1.call-update) | async-done | bytes 524304 | tf_op jit(solution)/shard_map/reduce_scatter | solution.py:314
  (255 shorter events, 25.5 us)
Async XLA Ops:
  7.2 9.8 copy-start.16
  7.2 10.6 copy-start.52
  7.2 11.3 copy-start.60
  7.2 11.3 copy-start.61
  7.2 11.3 copy-start.62
  7.2 11.3 copy-start.63
  7.3 11.3 copy-start.64
  7.3 11.3 copy-start.65
  7.3 11.3 copy-start.66
  7.3 11.3 copy-start.67
  7.3 11.3 copy-start.68
  7.3 11.3 copy-start.69
  7.3 11.3 copy-start.70
  7.3 11.4 copy-start.56
  7.3 57.4 %copy-start.7 = (bf16[1,576,1024]{2,1,0:T(8,128)(2,1)S(1)}, bf16[1,576,1024]{2,1,0:T(8,128)(2,1)}, u32[]{:S(2)}) copy-start(bf16[1,576,1024]{2,1,0:T(8,128)(2,1)} %param.20) | copy-start | bytes 3538948
  7.3 190.7 %all-gather.7.cloned.1.call-start = ((), (), s32[]{:S(2)}) async-start(), calls=%async_computation.7 | async-start | bytes 6488064 | tf_op jit(solution)/shard_map/all_gather | solution.py:99
  9.3 236.7 %all-gather.9.cloned.1.call-start = ((), (), s32[]{:S(2)}) async-start(), calls=%async_computation.8 | async-start | bytes 2162688 | tf_op jit(solution)/shard_map/all_gather | solution.py:102
  10.9 239.1 %all-gather.11.cloned.1.call-start = ((), (), s32[]{:S(2)}) async-start(), calls=%async_computation.9 | async-start | bytes 8650752 | tf_op jit(solution)/shard_map/all_gather | solution.py:106
  12.8 184.7 %all-to-all-start.1 = ((bf16[2,4,1024]{2,1,0:T(4,128)(2,1)}), bf16[2,4,1024]{2,1,0:T(4,128)(2,1)S(1)}, u32[]{:S(2)}, u32[]{:S(2)}) async-start(bf16[2,4,1024]{2,1,0:T(4,128)(2,1)} %param.23), calls=%async_computation.1 | async-start | bytes 32768 | tf_op jit(solution)/shard_map/all_to_all | solution.py:226
  17.0 285.7 %all-gather.13.cloned.1.call-start = ((), (), s32[]{:S(2)}) async-start(), calls=%async_computation.10 | async-start | bytes 8650752 | tf_op jit(solution)/shard_map/all_gather | solution.py:108
  17.8 534.5 %reduce-scatter.16.cloned.1.call-start = ((), (), s32[]{:S(2)}) async-start(), calls=%async_computation.15 | async-start | bytes 540672
  17.9 216.1 %copy-start.39 = (pred[576]{0:T(1024)(128)(4,1)}, pred[576]{0:T(1024)(128)(4,1)S(1)}, u32[]{:S(2)}) copy-start(pred[576]{0:T(1024)(128)(4,1)S(1)} %compare_reduce_fusion) | copy-start | bytes 1732
  62.9 141.3 %copy-start.57 = (f32[1024]{0:T(1024)}, f32[1024]{0:T(1024)S(1)}, u32[]{:S(2)}) copy-start(f32[1024]{0:T(1024)S(1)} %convert_element_type.241) | copy-start | bytes 12292
  62.9 141.3 %copy-start.45 = (f32[1024]{0:T(1024)}, f32[1024]{0:T(1024)S(1)}, u32[]{:S(2)}) copy-start(f32[1024]{0:T(1024)S(1)} %convert_element_type.239) | copy-start | bytes 12292
  65.0 139.3 %copy-start.36 = (f32[576]{0:T(1024)}, f32[576]{0:T(1024)S(1)}, u32[]{:S(2)}) copy-start(f32[576]{0:T(1024)S(1)} %broadcast_multiply_fusion.8) | copy-start | bytes 6916
  65.5 138.8 %copy-start.47 = (f32[576]{0:T(1024)}, f32[576]{0:T(1024)S(1)}, u32[]{:S(2)}) copy-start(f32[576]{0:T(1024)S(1)} %add_rsqrt_fusion.2) | copy-start | bytes 6916
  210.1 13.3 copy-start.3
  223.3 10.6 copy-start.18
  223.4 11.2 copy-start.14
  234.5 11.5 copy-start.8
  234.5 11.5 copy-start.59
  249.6 31.6 %copy-start = (f32[576,1024]{1,0:T(8,128)}, f32[576,1024]{1,0:T(8,128)S(1)}, u32[]{:S(2)}) copy-start(f32[576,1024]{1,0:T(8,128)S(1)} %get-tuple-element.63) | copy-start | bytes 7077892
  250.3 52.4 %copy-start.58 = (f32[1024]{0:T(1024)S(1)}, f32[1024]{0:T(1024)}, u32[]{:S(2)}) copy-start(f32[1024]{0:T(1024)} %convert_element_type.269) | copy-start | bytes 12292
  324.1 273.2 %reduce-scatter.10.cloned.1.call-start = ((), (), s32[]{:S(2)}) async-start(), calls=%async_computation.12 | async-start | bytes 4325376 | tf_op jit(solution)/shard_map/reduce_scatter | solution.py:308
  330.7 18.1 %copy-start.12 = (f32[576,1024]{1,0:T(8,128)}, f32[576,1024]{1,0:T(8,128)S(1)}, u32[]{:S(2)}) copy-start(f32[576,1024]{1,0:T(8,128)S(1)} %fusion.35) | copy-start | bytes 7077892
  330.7 18.0 %copy-start.1 = (f32[576,1024]{1,0:T(8,128)S(1)}, f32[576,1024]{1,0:T(8,128)}, u32[]{:S(2)}) copy-start(f32[576,1024]{1,0:T(8,128)} %copy-done) | copy-start | bytes 7077892
  348.8 10.4 copy-start.13
  366.1 391.3 %reduce-scatter.8.cloned.1.call-start = ((), (), s32[]{:S(2)}) async-start(), calls=%async_computation.11 | async-start | bytes 12976128 | tf_op jit(solution)/shard_map/reduce_scatter | solution.py:305
  372.7 19.4 %copy-start.17 = (f32[16,576]{1,0:T(8,128)S(1)}, f32[16,576]{1,0:T(8,128)}, u32[]{:S(2)}) copy-start(f32[16,576]{1,0:T(8,128)} %log_add_fusion) | copy-start | bytes 110596
  372.7 19.4 %copy-start.40 = (pred[576]{0:T(1024)(128)(4,1)S(1)}, pred[576]{0:T(1024)(128)(4,1)}, u32[]{:S(2)}) copy-start(pred[576]{0:T(1024)(128)(4,1)} %copy-done.39) | copy-start | bytes 1732
  392.1 20.5 %copy-start.6 = (bf16[576,1024]{0,1:T(8,128)(2,1)S(1)}, bf16[576,1024]{0,1:T(8,128)(2,1)}, u32[]{:S(2)}) copy-start(bf16[576,1024]{0,1:T(8,128)(2,1)} %copy-done.5) | copy-start | bytes 3538948
  412.6 9.1 copy-start.4
  430.0 14.7 copy-start.9
  457.0 659.7 %reduce-scatter.12.cloned.1.call-start = ((), (), s32[]{:S(2)}) async-start(), calls=%async_computation.13 | async-start | bytes 17301504 | tf_op jit(solution)/shard_map/reduce_scatter | solution.py:312
  470.2 1007.8 %reduce-scatter.14.cloned.1.call-start = ((), (), s32[]{:S(2)}) async-start(), calls=%async_computation.14 | async-start | bytes 17301504 | tf_op jit(solution)/shard_map/reduce_scatter | solution.py:314
  483.3 8.0 copy-start.37
  487.8 63.7 %all-to-all-start = ((bf16[2,2,2048]{2,1,0:T(2,128)(2,1)}), bf16[2,2,2048]{2,1,0:T(2,128)(2,1)S(1)}, u32[]{:S(2)}, u32[]{:S(2)}) async-start(bf16[2,2,2048]{2,1,0:T(2,128)(2,1)} %reshape.318), calls=%async_computation | async-start | bytes 32768 | tf_op jit(solution)/shard_map/all_to_all | solution.py:186
  491.3 9.1 copy-start.11
  (35 other events, 103.6 us)
Sparse Core Ops, SparseCore 0:
  11.6 72.5 all-gather.6
  87.9 55.2 all-gather.8
  146.8 76.2 all-gather.10
  226.7 76.0 all-gather.12
  324.2 132.5 reduce-scatter.15
  459.7 137.6 reduce-scatter.9
  605.0 152.3 reduce-scatter.7
  760.2 356.4 reduce-scatter.11
  1119.6 358.4 reduce-scatter.13
where the time goes:
time: 1490 us; the launch traced here: 1480 us
  waiting for transfers between devices  946 us (63%)
  matrix products  222 us (15%)
  blocking collectives  215 us (14%)
  other arithmetic  53.2 us (4%)
  local copies, waits for them, and re-layouts  25.9 us (2%)
  between operations  15.2 us (1%)
    reduce_scatter x1, waiting for transfers between devices, per_device(): lax.psum_scatter(grad_down, ('dp', 'map'), scatter_dimension=0, tiled=True)  361 us
    reduce_scatter x1, waiting for transfers between devices, per_device(): lax.psum_scatter(grad_up, ('dp', 'map'), scatter_dimension=0, tiled=True)  359 us
    reduce_scatter x1, waiting for transfers between devices, per_device(): lax.psum_scatter(grad_qkv_full, ('dp', 'map'), scatter_dimension=0, tiled...  160 us
    unnamed x2, blocking collectives  84.7 us
    all_gather x1, blocking collectives, per_device(): lax.all_gather(wire_weights[10], ('dp', 'map'), axis=0, tiled=True)  65.5 us
    all_gather x1, blocking collectives, per_device(): lax.all_gather(wire_weights[15], ('dp', 'map'), axis=0, tiled=True)  64.5 us
    dot_general x4, matrix products, matmul(): return jnp.dot(left, right, preferred_element_type=jnp.float32)  50.4 us
    reduce_scatter x1, waiting for transfers between devices, per_device(): lax.psum_scatter(grad_out, ('dp', 'map'), scatter_dimension=0, tiled=True)  43.7 us
  transfers between devices with their start and end apart: 11, of which 5 were waited for; matrix products, arithmetic and copies ran while one was open for 18% of the time, Pallas kernels for 0%

commit v1 on v0

v1 whole, which is shorter than its diff:
```python
import jax
import jax.numpy as jnp
from jax import lax
from jax.experimental import pallas as pl
from jax.experimental.pallas import tpu as pltpu
from jax.sharding import PartitionSpec as P

HD = 64
KEEP = 512
AXES = ("dp", "map")
BLOCKS = 32
CHUNKS = 4
HIGHEST = lax.Precision.HIGHEST
EPSILON = 1e-06
MASKED_SCORE = -1e30
BF = jnp.bfloat16
F32 = jnp.float32


def params(*semantics, vmem=56):
    return pltpu.CompilerParams(
        dimension_semantics=semantics or None, vmem_limit_bytes=vmem * 2**20
    )


def cost(flops, moved, trans=0):
    return pl.CostEstimate(
        flops=int(flops), bytes_accessed=int(moved), transcendentals=int(trans)
    )


def shape(dims, dtype):
    return jax.ShapeDtypeStruct(tuple(dims), dtype)


def normalize(values):
    center = values - jnp.mean(values, axis=-1, keepdims=True)
    spread = lax.rsqrt(jnp.mean(center * center, axis=-1, keepdims=True) + EPSILON)
    return (center * spread, spread)


def norm_back(grad_hat, normed, spread):
    return spread * (
        grad_hat
        - jnp.mean(grad_hat, axis=-1, keepdims=True)
        - normed * jnp.mean(grad_hat * normed, axis=-1, keepdims=True)
    )


def dot(left, right, dims, precision=None):
    return lax.dot_general(
        left, right, (dims, ((), ())), preferred_element_type=F32, precision=precision
    )


NN = ((1,), (0,))
NT = ((1,), (1,))
TN = ((0,), (0,))


def column_sum(values):
    return jnp.sum(values.astype(F32), axis=0)


def permute(values, masks):
    pairs = [(i, i ^ masks[(i >> 1) & 1]) for i in range(BLOCKS)]
    return lax.ppermute(values, AXES, pairs)


CORE, MAP, XDIM, Z_NEAR, Z_FAR = 2, 1, 4, 8, 16
BOTH = lambda mask: (mask, mask)
FIRST = (XDIM, MAP)
LAST = (MAP, XDIM)


def slot_table(layered):
    slots = jnp.arange(BLOCKS, dtype=jnp.int32)
    if not layered:
        return slots
    me = (lax.axis_index("dp") * lax.axis_size("map") + lax.axis_index("map")).astype(jnp.int32)
    other, last, first, near, far = ((slots >> bit) & 1 for bit in (4, 3, 2, 1, 0))
    owner = ((me >> 1) & 1) ^ other
    plane = jnp.where(owner == 0, last * MAP + first * XDIM, last * XDIM + first * MAP)
    return me ^ (other * CORE + near * Z_NEAR + far * Z_FAR + plane)


def gather_layered(wire):
    stack = jnp.concatenate([wire, permute(wire, BOTH(Z_FAR))], axis=0)
    stack = jnp.concatenate([stack, permute(stack, BOTH(Z_NEAR))], axis=0)
    stack = jnp.concatenate([stack, permute(stack, FIRST)], axis=0)
    rest = permute(stack, LAST)
    return stack, rest, permute(stack, BOTH(CORE)), permute(rest, BOTH(CORE))


def assemble(table, pieces):
    rows, cols = pieces[0].shape
    step = rows * 4 // BLOCKS

    def kernel(table_ref, *refs):
        sources, out, sems = refs[:4], refs[4], refs[5]
        copies = []
        for slot in range(BLOCKS):
            piece, place = divmod(slot, BLOCKS // 4)
            start = pl.multiple_of(table_ref[slot] * step, step)
            copies.append(
                pltpu.make_async_copy(
                    sources[piece].at[pl.ds(place * step, step)],
                    out.at[pl.ds(start, step)],
                    sems.at[slot],
                )
            )
        for copy in copies:
            copy.start()
        for copy in copies:
            copy.wait()

    return pl.pallas_call(
        kernel,
        out_shape=shape((rows * 4, cols), pieces[0].dtype),
        in_specs=[pl.BlockSpec(memory_space=pltpu.SMEM)]
        + [pl.BlockSpec(memory_space=pl.ANY)] * 4,
        out_specs=pl.BlockSpec(memory_space=pl.ANY),
        scratch_shapes=[pltpu.SemaphoreType.DMA((BLOCKS,))],
        compiler_params=params(vmem=8),
        cost_estimate=cost(0, 16 * rows * cols),
        name="assemble",
    )(table, *pieces)


def scatter_sum(keep, send, layered):
    rows, cols = keep.shape
    if not layered:
        whole = jnp.concatenate([keep, send], axis=0)
        return lax.psum_scatter(whole.astype(F32), AXES, scatter_dimension=0, tiled=True)
    stages = (BOTH(CORE), LAST, FIRST, BOTH(Z_NEAR), BOTH(Z_FAR))
    for at, masks in enumerate(stages):
        got = permute(send, masks)
        if at == len(stages) - 1:
            return keep.astype(F32) + got.astype(F32)
        half = rows // 2
        low = (keep[:half].astype(F32) + got[:half].astype(F32)).astype(BF)
        send = (keep[half:].astype(F32) + got[half:].astype(F32)).astype(BF)
        keep, rows = low, half


def attend(qkv, live):
    rows, width = qkv.shape[0], qkv.shape[1] // 3
    pairs = width // (2 * HD)

    def kernel(q_ref, k_ref, v_ref, live_ref, mixed_ref, total_ref):
        alive = live_ref[...] > 0
        q, k = q_ref[...], k_ref[...]
        value_t = v_ref[...].T
        parts = []
        for h in range(2):
            cut = slice(h * HD, (h + 1) * HD)
            scores = jnp.where(alive, dot(k[:, cut], q[:, cut], NT), MASKED_SCORE)
            peak = jnp.max(scores, axis=0, keepdims=True)
            expons = jnp.exp(scores - peak)
            total = jnp.sum(expons, axis=0, keepdims=True)
            attention = (expons * (1.0 / total)).astype(BF)
            parts.append(dot(value_t[cut], attention, NN))
            total_ref[0, h : h + 1, :] = peak + jnp.log(total)
        mixed_ref[...] = jnp.concatenate(parts, axis=0).T.astype(BF)

    pair = 2 * HD
    return pl.pallas_call(
        kernel,
        grid=(pairs,),
        in_specs=[
            pl.BlockSpec((rows, pair), lambda i: (0, i)),
            pl.BlockSpec((rows, pair), lambda i: (0, pairs + i)),
            pl.BlockSpec((rows, pair), lambda i: (0, 2 * pairs + i)),
            pl.BlockSpec((rows, 1), lambda i: (0, 0)),
        ],
        out_specs=[
            pl.BlockSpec((rows, pair), lambda i: (0, i)),
            pl.BlockSpec((1, 2, rows), lambda i: (i, 0, 0)),
        ],
        out_shape=[shape((rows, width), BF), shape((pairs, 2, rows), F32)],
        compiler_params=params("arbitrary"),
        cost_estimate=cost(16 * rows * rows * width, 8 * rows * width, rows * rows * pairs * 2),
        name="attend",
    )(qkv, qkv, qkv, live)


def attend_back(qkv, live, totals, grad_mixed):
    rows, width = grad_mixed.shape
    pairs = width // (2 * HD)
    scaling = HD ** (-0.5)

    def kernel(q_ref, k_ref, v_ref, live_ref, total_ref, gm_ref, out_ref, sum_ref):
        alive = live_ref[...] > 0
        q, k, v, gm = q_ref[...], k_ref[...], v_ref[...], gm_ref[...]
        key_t = k.T
        queries, keys, values = [], [], []
        for h in range(2):
            cut = slice(h * HD, (h + 1) * HD)
            scores = jnp.where(alive, dot(k[:, cut], q[:, cut], NT), MASKED_SCORE)
            probs = jnp.exp(scores - total_ref[0, h : h + 1, :])
            grad_probs = dot(v[:, cut], gm[:, cut], NT)
            along = jnp.sum(probs * grad_probs, axis=0, keepdims=True)
            grad_scores = (probs * (grad_probs - along)).astype(BF)
            values.append(dot(probs.astype(BF), gm[:, cut], NN))
            keys.append(dot(grad_scores, q[:, cut], NN))
            queries.append(dot(key_t[cut], grad_scores, NN))
        grad_q = jnp.concatenate(queries, axis=0).T.astype(BF).astype(F32) * scaling
        grad_v = jnp.concatenate(values, axis=1).astype(BF)
        out_ref[0] = grad_q.astype(BF)
        out_ref[1] = jnp.concatenate(keys, axis=1).astype(BF)
        out_ref[2] = grad_v
        sum_ref[0:1, :] = jnp.sum(grad_q, axis=0, keepdims=True)
        sum_ref[1:2, :] = jnp.sum(grad_v.astype(F32), axis=0, keepdims=True)

    pair = 2 * HD
    return pl.pallas_call(
        kernel,
        grid=(pairs,),
        in_specs=[
            pl.BlockSpec((rows, pair), lambda i: (0, i)),
            pl.BlockSpec((rows, pair), lambda i: (0, pairs + i)),
            pl.BlockSpec((rows, pair), lambda i: (0, 2 * pairs + i)),
            pl.BlockSpec((rows, 1), lambda i: (0, 0)),
            pl.BlockSpec((1, 2, rows), lambda i: (i, 0, 0)),
            pl.BlockSpec((rows, pair), lambda i: (0, i)),
        ],
        out_specs=[
            pl.BlockSpec((3, rows, pair), lambda i: (0, 0, i)),
            pl.BlockSpec((2, pair), lambda i: (0, i)),
        ],
        out_shape=[shape((3, rows, width), BF), shape((2, width), F32)],
        compiler_params=params("arbitrary"),
        cost_estimate=cost(40 * rows * rows * width, 14 * rows * width, rows * rows * pairs * 2),
        name="attend_back",
    )(qkv, qkv, qkv, live, totals, grad_mixed)


def feed_forward(hidden, residual, up, up_at, up_bias, down, down_bias):
    rows, width = hidden.shape
    span = up_bias.shape[1]

    def kernel(h_ref, r_ref, up_ref, ub_ref, down_ref, db_ref, block_ref, act_ref, slope_ref):
        step = pl.program_id(0)

        @pl.when(step == 0)
        def _():
            block_ref[...] = r_ref[...] + db_ref[...]

        weight = up_ref[...].reshape(width, span)
        x = dot(h_ref[...], weight, NN) + ub_ref[pl.ds(step, 1), :]
        half = 0.5 + 0.5 * lax.erf(x * (0.5**0.5))
        act = (x * half).astype(BF)
        act_ref[...] = act
        slope_ref[...] = (half + x * jnp.exp(-0.5 * x * x) * 0.3989422804014327).astype(BF)
        block_ref[...] += dot(act, down_ref[...], NN)

    return pl.pallas_call(
        kernel,
        grid=(CHUNKS,),
        in_specs=[
            pl.BlockSpec((rows, width), lambda j: (0, 0)),
            pl.BlockSpec((rows, width), lambda j: (0, 0)),
            pl.BlockSpec((BLOCKS, None, width // BLOCKS, span), lambda j: (0, j, 0, up_at)),
            pl.BlockSpec((CHUNKS, span), lambda j: (0, 0)),
            pl.BlockSpec((span, width), lambda j: (j, 0)),
            pl.BlockSpec((1, width), lambda j: (0, 0)),
        ],
        out_specs=[
            pl.BlockSpec((rows, width), lambda j: (0, 0)),
            pl.BlockSpec((rows, span), lambda j: (0, j)),
            pl.BlockSpec((rows, span), lambda j: (0, j)),
        ],
        out_shape=[
            shape((rows, width), F32),
            shape((rows, span * CHUNKS), BF),
            shape((rows, span * CHUNKS), BF),
        ],
        compiler_params=params("arbitrary"),
        cost_estimate=cost(4 * rows * width * span * CHUNKS, 30 * 2**20),
        name="feed_forward",
    )(hidden, residual, up, up_bias, down, down_bias)


def feed_forward_back(grad_down, slope, up, up_at, down):
    rows, width = grad_down.shape
    span = slope.shape[1] // CHUNKS

    def kernel(g_ref, slope_ref, up_ref, down_ref, pre_ref, sum_ref, out_ref):
        step = pl.program_id(0)
        grad_act = dot(g_ref[...], down_ref[...], NT)
        grad_pre = (grad_act * slope_ref[...].astype(F32)).astype(BF)
        pre_ref[...] = grad_pre
        sum_ref[pl.ds(step, 1), :] = jnp.sum(grad_pre.astype(F32), axis=0, keepdims=True)
        part = dot(grad_pre, up_ref[...].reshape(width, span), NT)

        @pl.when(step == 0)
        def _():
            out_ref[...] = part

        @pl.when(step > 0)
        def _():
            out_ref[...] += part

    return pl.pallas_call(
        kernel,
        grid=(CHUNKS,),
        in_specs=[
            pl.BlockSpec((rows, width), lambda j: (0, 0)),
            pl.BlockSpec((rows, span), lambda j: (0, j)),
            pl.BlockSpec((BLOCKS, None, width // BLOCKS, span), lambda j: (0, j, 0, up_at)),
            pl.BlockSpec((span, width), lambda j: (j, 0)),
        ],
        out_specs=[
            pl.BlockSpec((rows, span), lambda j: (0, j)),
            pl.BlockSpec((CHUNKS, span), lambda j: (0, 0)),
            pl.BlockSpec((rows, width), lambda j: (0, 0)),
        ],
        out_shape=[
            shape((rows, span * CHUNKS), BF),
            shape((CHUNKS, span), F32),
            shape((rows, width), F32),
        ],
        compiler_params=params("arbitrary"),
        cost_estimate=cost(4 * rows * width * span * CHUNKS, 28 * 2**20),
        name="feed_forward_back",
    )(grad_down, slope, up, down)


def token_learner(block, cotangent, live, token_grad, map_t, scale, offset):
    rows, width = block.shape
    count = map_t.shape[0]
    band = rows // 4

    def kernel(b_ref, c_ref, live_ref, tg_ref, map_ref, s_ref, o_ref, *outs):
        out_ref, tok_ref, grad_ref, low_ref, gmap_ref, sums_ref = outs
        values, alive = b_ref[...], live_ref[...]
        grads, weights, scale_row = tg_ref[...], map_ref[...], s_ref[...]
        normed, spread = normalize(values)
        learned = normed * scale_row + o_ref[...]
        sigma = jax.nn.sigmoid(dot(learned, weights, NT, HIGHEST))
        token_weights = sigma * alive
        tokens = dot(token_weights, values, TN, HIGHEST)
        logits = dot(values, grads, NT, HIGHEST) * alive * sigma * (1.0 - sigma)
        grad_map = dot(logits, learned, TN, HIGHEST)
        grad_learned = dot(logits, weights, NN, HIGHEST)
        grad = c_ref[...].astype(F32) + dot(token_weights, grads, NN, HIGHEST)
        grad = grad + norm_back(grad_learned * scale_row, normed, spread)
        low = grad.astype(BF)
        out_ref[...] = values.astype(BF)
        grad_ref[...] = grad
        low_ref[...] = low
        sums = jnp.concatenate(
            [
                jnp.sum(grad_learned * normed, axis=0, keepdims=True),
                jnp.sum(grad_learned, axis=0, keepdims=True),
                jnp.sum(low.astype(F32), axis=0, keepdims=True),
            ],
            axis=0,
        )

        @pl.when(pl.program_id(0) == 0)
        def _():
            tok_ref[...] = tokens
            gmap_ref[...] = grad_map
            sums_ref[...] = sums

        @pl.when(pl.program_id(0) > 0)
        def _():
            tok_ref[...] += tokens
            gmap_ref[...] += grad_map
            sums_ref[...] += sums

    banded = pl.BlockSpec((band, width), lambda i: (i, 0))
    fixed = lambda n: pl.BlockSpec((n, width), lambda i: (0, 0))
    return pl.pallas_call(
        kernel,
        grid=(4,),
        in_specs=[banded, banded, pl.BlockSpec((band, 1), lambda i: (i, 0))]
        + [fixed(count), fixed(count), fixed(1), fixed(1)],
        out_specs=[banded, fixed(count), banded, banded, fixed(count), fixed(3)],
        out_shape=[
            shape((rows, width), BF),
            shape((count, width), F32),
            shape((rows, width), F32),
            shape((rows, width), BF),
            shape((count, width), F32),
            shape((3, width), F32),
        ],
        compiler_params=params("arbitrary"),
        cost_estimate=cost(80 * rows * width * count * 4, 14 * rows * width),
        name="token_learner",
    )(block, cotangent, live, token_grad, map_t, scale, offset)


def weight_grad(table, left, right, tile):
    rows, height = left.shape
    step = height // BLOCKS
    parts = right.shape[0] if right.ndim == 3 else 1
    per_part = right.shape[-1] // tile
    cols = parts * right.shape[-1]

    def kernel(table_ref, l_ref, r_ref, keep_ref, send_ref, turned, *spare):
        @pl.when(pl.program_id(0) == 0)
        def _():
            if step % 128 == 0:
                for slot in range(BLOCKS):
                    at = pl.multiple_of(table_ref[slot] * step, step)
                    turned[slot * step : (slot + 1) * step, :] = l_ref[:, pl.ds(at, step)].T
            else:
                spare[0][...] = l_ref[...].T
                for slot in range(BLOCKS):
                    at = pl.multiple_of(table_ref[slot] * step, step)
                    turned[slot * step : (slot + 1) * step, :] = spare[0][pl.ds(at, step), :]

        value = r_ref[...]
        half = height // 2
        send_ref[...] = dot(turned[half:, :], value, NN).astype(BF)
        keep_ref[...] = dot(turned[:half, :], value, NN).astype(BF)

    if right.ndim == 3:
        right_spec = pl.BlockSpec((None, rows, tile), lambda n: (n // per_part, 0, n % per_part))
    else:
        right_spec = pl.BlockSpec((rows, tile), lambda n: (0, n))
    scratch = [pltpu.VMEM((height, rows), BF)]
    if step % 128:
        scratch.append(pltpu.VMEM((height, rows), BF))
    half_spec = pl.BlockSpec((height // 2, tile), lambda n: (0, n))
    return pl.pallas_call(
        kernel,
        grid=(cols // tile,),
        in_specs=[
            pl.BlockSpec(memory_space=pltpu.SMEM),
            pl.BlockSpec((rows, height), lambda n: (0, 0)),
            right_spec,
        ],
        out_specs=[half_spec, half_spec],
        out_shape=[shape((height // 2, cols), BF)] * 2,
        scratch_shapes=scratch,
        compiler_params=params("arbitrary"),
        cost_estimate=cost(
            2 * rows * height * cols, 2 * (rows * height + rows * cols + height * cols)
        ),
        name="weight_grad",
    )(table, left, right)


def gather_weights(layered, table, qkv_wire, out_wire, up_wire, down_wire):
    span = up_wire.shape[1] // CHUNKS
    if layered:
        chunks = [up_wire[:, j * span : (j + 1) * span] for j in range(CHUNKS)]
        both = jnp.concatenate([down_wire, jnp.concatenate(chunks, axis=0)], axis=1)
        both = lax.all_gather(both, AXES, axis=0, tiled=True)
        qkv = assemble(table, gather_layered(qkv_wire))
        out = assemble(table, gather_layered(out_wire))
        up = both.reshape(BLOCKS, CHUNKS, -1, both.shape[1])
        return qkv, out, up, 1, both
    whole = lambda wire: lax.all_gather(wire, AXES, axis=0, tiled=True)
    up = whole(up_wire)
    up = up.reshape(BLOCKS, -1, CHUNKS, span).transpose(0, 2, 1, 3)
    return whole(qkv_wire), whole(out_wire), up, 0, whole(down_wire)


def per_device(
    patches,
    keep_mask,
    block_cotangent,
    token_cotangent,
    first_gain,
    first_shift,
    qkv_weight,
    query_bias,
    value_bias,
    out_weight,
    out_bias,
    second_gain,
    second_shift,
    up_weight,
    up_bias,
    down_weight,
    down_bias,
    learn_gain,
    learn_shift,
    map_weight,
):
    devices = lax.axis_size("dp") * lax.axis_size("map")
    layered = devices == BLOCKS and lax.axis_size("map") == 2
    images, patch_count, width = patches.shape
    rows = images * patch_count
    own = first_gain.shape[0]
    scaling = HD ** (-0.5)
    table = slot_table(layered)

    vectors = (
        first_gain,
        first_shift,
        query_bias,
        value_bias,
        out_bias,
        second_gain,
        second_shift,
        down_bias,
        learn_gain,
        learn_shift,
    )
    fan = up_bias.shape[0] // own
    count = map_weight.shape[1]
    small = jnp.concatenate(
        [jnp.stack(vectors, axis=1), up_bias.reshape(own, fan), map_weight], axis=1
    )
    small = jnp.pad(small, ((0, 0), (0, 128 - small.shape[1]))).astype(BF)
    qkv_wire = jnp.concatenate([qkv_weight.astype(BF), small], axis=1)
    qkv_full, out_full, up_full, up_at, down_full = gather_weights(
        layered,
        table,
        qkv_wire,
        out_weight.astype(BF),
        up_weight.astype(BF),
        down_weight.astype(BF),
    )
    small = qkv_full[:, 3 * width :].astype(F32)
    qkv_full = qkv_full[:, : 3 * width]
    small_t = small.T
    (
        gain_one,
        shift_one,
        query_shift,
        value_shift,
        out_shift,
        gain_two,
        shift_two,
        down_shift,
        learn_scale,
        learn_offset,
    ) = (small_t[i] for i in range(len(vectors)))
    at = len(vectors)
    up_shift = small[:, at : at + fan].reshape(CHUNKS, -1)
    map_t = small_t[at + fan : at + fan + count]

    token_grad = lax.all_to_all(
        token_cotangent, "map", split_axis=0, concat_axis=1, tiled=True
    ).astype(F32)
    live = keep_mask.reshape(rows, 1).astype(F32)

    inputs = patches.reshape(rows, width).astype(F32)
    normed_one, spread_one = normalize(inputs)
    hidden_one = (normed_one * gain_one + shift_one).astype(BF)
    qkv = dot(hidden_one, qkv_full, NN)
    added = jnp.concatenate([query_shift, jnp.zeros_like(query_shift), value_shift])
    factor = jnp.concatenate([jnp.full((width,), scaling, F32), jnp.ones((2 * width,), F32)])
    qkv = ((qkv + added) * factor).astype(BF)
    mixed, totals = attend(qkv, live)
    residual_one = inputs + dot(mixed, out_full, NN) + out_shift
    normed_two, spread_two = normalize(residual_one)
    hidden_two = (normed_two * gain_two + shift_two).astype(BF)
    block, activation, slope = feed_forward(
        hidden_two, residual_one, up_full, up_at, up_shift, down_full, down_shift[None]
    )
    block_out, token_local, grad_block, grad_down_low, grad_map, sums = token_learner(
        block,
        block_cotangent.reshape(rows, width),
        live * KEEP ** (-0.5),
        token_grad.reshape(count, width),
        map_t,
        learn_scale[None],
        learn_offset[None],
    )
    tokens_out = lax.all_to_all(
        token_local.reshape(images, count, width).astype(BF),
        "map",
        split_axis=1,
        concat_axis=0,
        tiled=True,
    )
    grad_down = scatter_sum(*weight_grad(table, activation, grad_down_low, 256), layered)
    grad_pre, grad_up_shift, grad_hidden_two = feed_forward_back(
        grad_down_low, slope, up_full, up_at, down_full
    )
    grad_up = scatter_sum(*weight_grad(table, hidden_two, grad_pre, 512), layered)
    grad_gain_two = jnp.sum(grad_hidden_two * normed_two, axis=0)
    grad_shift_two = jnp.sum(grad_hidden_two, axis=0)
    grad_residual = grad_block + norm_back(grad_hidden_two * gain_two, normed_two, spread_two)
    grad_attn = grad_residual.astype(BF)
    grad_out = scatter_sum(*weight_grad(table, mixed, grad_attn, 512), layered)
    grad_out_shift = column_sum(grad_attn)
    grad_mixed = dot(grad_attn, out_full, NT).astype(BF)
    grad_qkv, qv_sums = attend_back(qkv, live, totals, grad_mixed)
    grad_qkv_full = scatter_sum(*weight_grad(table, hidden_one, grad_qkv, 512), layered)
    grad_hidden_one = sum(
        dot(grad_qkv[i], qkv_full[:, i * width : (i + 1) * width], NT) for i in range(3)
    )
    grad_gain_one = jnp.sum(grad_hidden_one * normed_one, axis=0)
    grad_shift_one = jnp.sum(grad_hidden_one, axis=0)
    grad_inputs = grad_residual + norm_back(grad_hidden_one * gain_one, normed_one, spread_one)
    grad_patches = grad_inputs.reshape(images, patch_count, width).astype(BF)

    terms = (
        grad_gain_one,
        grad_shift_one,
        qv_sums[0],
        qv_sums[1],
        grad_out_shift,
        grad_gain_two,
        grad_shift_two,
        sums[2],
        sums[0],
        sums[1],
        grad_up_shift.reshape(-1),
    )
    packed = [term.reshape(devices, -1) for term in terms]
    packed.append(grad_map.reshape(count, devices, own).transpose(1, 2, 0).reshape(devices, -1))
    packed = jnp.concatenate(packed, axis=1)
    summed = jnp.sum(lax.all_to_all(packed, AXES, 0, 0, tiled=True), axis=0)
    pieces = [summed[i * own : (i + 1) * own] for i in range(10)]
    at = 10 * own
    up_piece = summed[at : at + fan * own]
    map_piece = summed[at + fan * own :].reshape(own, count)
    return (
        block_out.reshape(images, patch_count, width),
        tokens_out,
        grad_patches,
        pieces[0],
        pieces[1],
        grad_qkv_full,
        pieces[2],
        pieces[3],
        grad_out,
        pieces[4],
        pieces[5],
        pieces[6],
        grad_up,
        up_piece,
        grad_down,
        pieces[7],
        pieces[8],
        pieces[9],
        map_piece,
    )


def solution(mesh):
    rows = P(("dp", "map"))
    wide = P(("dp", "map"), None)
    images = P(("dp", "map"), None, None)
    tokens = P("dp", "map", None)
    weights = (
        rows, rows, wide, rows, rows, wide, rows, rows,
        rows, wide, rows, wide, rows, rows, rows, wide,
    )
    return jax.shard_map(
        per_device,
        mesh=mesh,
        in_specs=(images, wide, images, tokens) + weights,
        out_specs=(images, tokens, images) + weights,
        check_vma=False,
    )
```

time: 1490 us -> 518 us (0.35)
  waiting for transfers between devices: 946 us -> 208 us
  blocking collectives: 215 us -> 0 us
  matrix products: 222 us -> 22.3 us
  Pallas kernels: 0 us -> 140 us
  starting transfers between devices: 8.03 us -> 47 us
    reduce_scatter x4 -> x0, waiting for transfers between devices: 924 us -> none  [the longest x1 361 us: per_device(): lax.psum_scatter(grad_down, ('dp', 'map'), scatter_dimension=0, tiled=True)]
    dot_general x23 -> x6, matrix products: 216 us -> 22.3 us  [dot(): lax.dot_general(left, right, (dims, ((), ())), preferred_element_type=F32...]
    ppermute x0 -> x32, waiting for transfers between devices: none -> 181 us  [permute(): return lax.ppermute(values, AXES, pairs)]
    pallas_call x0 -> x11, Pallas kernels: none -> 140 us  [the longest x4 39.4 us: weight_grad(): pl.pallas_call(kernel, grid=(cols // tile,), in_specs=[pl.BlockSpec(memor...]
    all_gather x2 -> x0, blocking collectives: 130 us -> none  [the longest x1 65.5 us: per_device(): lax.all_gather(wire_weights[10], ('dp', 'map'), axis=0, tiled=True)]
    unnamed x2 -> x0, blocking collectives: 84.7 us -> none
    ppermute x0 -> x32, starting transfers between devices: none -> 34.7 us  [permute(): return lax.ppermute(values, AXES, pairs)]
    all_to_all x1 -> x2, waiting for transfers between devices: 0.01 us -> 27.3 us  [the longest x1 27.3 us: per_device(): summed = jnp.sum(lax.all_to_all(packed, AXES, 0, 0, tiled=True), axis=0)]
  transfers between devices with their start and end apart: 11 -> 36, of which waited for: 5 -> 17; matrix products, arithmetic and copies ran while one was open for 18% -> 15% of each run, Pallas kernels for 0% -> 9%
where the time goes in v1:
time: 518 us; the launch traced here: 508 us
  waiting for transfers between devices  208 us (40%)
  Pallas kernels  140 us (27%)
  other arithmetic  52.5 us (10%)
  starting transfers between devices  47 us (9%)
  local copies, waits for them, and re-layouts  22.9 us (4%)
  matrix products  22.3 us (4%)
  between operations  15.1 us (3%)
    ppermute x32, waiting for transfers between devices, permute(): return lax.ppermute(values, AXES, pairs)  181 us
    pallas_call x4, Pallas kernels, weight_grad(): pl.pallas_call(kernel, grid=(cols // tile,), in_specs=[pl.BlockSpec(memor...  39.4 us
    ppermute x32, starting transfers between devices, permute(): return lax.ppermute(values, AXES, pairs)  34.7 us
    all_to_all x1, waiting for transfers between devices, per_device(): summed = jnp.sum(lax.all_to_all(packed, AXES, 0, 0, tiled=True), axis=0)  27.3 us
    convert_element_type x12, other arithmetic, scatter_sum(): low = (keep[:half].astype(F32) + got[:half].astype(F32)).astype(BF)  25.1 us
    dot_general x6, matrix products, dot(): lax.dot_general(left, right, (dims, ((), ())), preferred_element_type=F32...  22.3 us
    pallas_call x1, Pallas kernels, attend_back(): pl.pallas_call(kernel, grid=(pairs,), in_specs=[pl.BlockSpec((rows, pair)...  21.1 us
    pallas_call x1, Pallas kernels, token_learner(): pl.pallas_call(kernel, grid=(4,), in_specs=[banded, banded, pl.BlockSpec(...  20.2 us
  transfers between devices with their start and end apart: 36, of which 17 were waited for; matrix products, arithmetic and copies ran while one was open for 15% of the time, Pallas kernels for 9%

profile of v1, /device:TPU:0, one launch (start us, length us, event | category | flops | bytes accessed | tf_op | source)
XLA Modules:
  0.0 507.8 jit_solution(12777783447501634877)
XLA Ops:
  12.1 4.1 collective-permute-start
  16.2 9.5 %collective-permute-done = bf16[32,3200]{1,0:T(8,128)(2,1)S(1)} collective-permute-done((bf16[32,3200]{1,0:T(8,128)(2,1)S(1)}, bf16[32,3200]{1,0:T(8,128)(2,1)S(1)}, u32[]{:S(2)}, u32[]{:S(2)}) %collective-permute-start) | collective-permute-done | bytes 204832 | tf_op jit(solution)/shard_map/ppermute | solution.py:67
  25.7 3.3 collective-permute-start.1
  29.0 17.1 %collective-permute-done.1 = bf16[64,3200]{1,0:T(8,128)(2,1)S(1)} collective-permute-done((bf16[64,3200]{1,0:T(8,128)(2,1)S(1)}, bf16[64,3200]{1,0:T(8,128)(2,1)S(1)}, u32[]{:S(2)}, u32[]{:S(2)}) %collective-permute-start.1) | collective-permute-done | bytes 409632 | tf_op jit(solution)/shard_map/ppermute | solution.py:67
  47.7 26.4 %collective-permute-done.2 = bf16[128,3200]{1,0:T(8,128)(2,1)S(1)} collective-permute-done((bf16[128,3200]{1,0:T(8,128)(2,1)S(1)}, bf16[128,3200]{1,0:T(8,128)(2,1)S(1)}, u32[]{:S(2)}, u32[]{:S(2)}) %collective-permute-start.2) | collective-permute-done | bytes 819232 | tf_op jit(solution)/shard_map/ppermute | solution.py:67
  75.1 2.9 collective-permute-start.6
  78.1 6.2 %collective-permute-done.6 = bf16[32,1024]{1,0:T(8,128)(2,1)S(1)} collective-permute-done((bf16[32,1024]{1,0:T(8,128)(2,1)S(1)}, bf16[32,1024]{1,0:T(8,128)(2,1)S(1)}, u32[]{:S(2)}, u32[]{:S(2)}) %collective-permute-start.6) | collective-permute-done | bytes 65568 | tf_op jit(solution)/shard_map/ppermute | solution.py:67
  84.4 12.6 %collective-permute-done.3.refs_1_ = bf16[256,3200]{1,0:T(8,128)(2,1)} collective-permute-done((bf16[256,3200]{1,0:T(8,128)(2,1)S(1)}, bf16[256,3200]{1,0:T(8,128)(2,1)}, u32[]{:S(2)}, u32[]{:S(2)}) %collective-permute-start.3) | collective-permute-done | bytes 1638432 | tf_op jit(solution)/shard_map/ppermute | solution.py:67
  97.1 4.6 collective-permute-start.8
  101.7 3.2 all-to-all-start
  105.1 6.5 %collective-permute-done.8 = bf16[128,1024]{1,0:T(8,128)(2,1)S(1)} collective-permute-done((bf16[128,1024]{1,0:T(8,128)(2,1)S(1)}, bf16[128,1024]{1,0:T(8,128)(2,1)S(1)}, u32[]{:S(2)}, u32[]{:S(2)}) %collective-permute-start.8) | collective-permute-done | bytes 262176 | tf_op jit(solution)/shard_map/ppermute | solution.py:67
  116.6 15.5 %collective-permute-done.9.refs_1_ = bf16[256,1024]{1,0:T(8,128)(2,1)S(1)} collective-permute-done((bf16[256,1024]{1,0:T(8,128)(2,1)S(1)}, bf16[256,1024]{1,0:T(8,128)(2,1)S(1)}, u32[]{:S(2)}, u32[]{:S(2)}) %collective-permute-start.9) | collective-permute-done | bytes 524320 | tf_op jit(solution)/shard_map/ppermute | solution.py:67
  134.1 4.3 assemble.3
  139.8 5.7 %assemble.2 = bf16[1024,3200]{1,0:T(8,128)(2,1)S(1)} custom-call(s32[32]{0:T(128)S(1)} %fusion.47.table_ref, bf16[256,3200]{1,0:T(8,128)(2,1)S(1)} %pad_maximum_fusion.refs_0_, bf16[256,3200]{1,0:T(8,128)(2,1)} %collective-permute-done.3.refs_1_, bf16[256,3200]{1,0:T(8,128)(2,1)} %collective-permute-done.4.refs_2_, ...), custom_call_target="tpu_custom_call" | custom-call | bytes 13107200 | tf_op jit(solution)/shard_map/assemble/pallas_call | solution.py:117
  145.6 2.7 copy-done
  152.4 8.3 %multiply_convert_fusion.q_ref.k_ref.v_ref = bf16[576,3072]{1,0:T(8,128)(2,1)} fusion(bf16[576,1024]{1,0:T(8,128)(2,1)S(1)} %fusion.13.l_ref, bf16[1024,3200]{1,0:T(8,128)(2,1)} %copy-done, f32[3072]{0:T(1024)S(1)} %copy-done.37, f32[3072]{0:T(1024)S(1)} %pad_maximum_fusion.7), kind=kOutput, calls=%fused_computation | convolution fusion | flops 3629187072 | bytes 11034624 | tf_op jit(solution)/shard_map/dot_general | solution.py:51
  160.8 16.3 %attend.1 = (bf16[576,1024]{1,0:T(8,128)(2,1)}, f32[8,2,576]{2,1,0:T(2,128)}) custom-call(bf16[576,3072]{1,0:T(8,128)(2,1)} %multiply_convert_fusion.q_ref.k_ref.v_ref, bf16[576,3072]{1,0:T(8,128)(2,1)} %multiply_convert_fusion.q_ref.k_ref.v_ref, bf16[576,3072]{1,0:T(8,128)(2,1)} %multiply_convert_fusion.q_ref.k_ref.v_ref, f32[576,1]{1,0:T(8,128)} %copy-done.16), custom_call_target="tpu_custom_call" | custom-call | flops 5435817984 | bytes 4718592 | tf_op jit(solution)/shard_map/attend/pallas_call | solution.py:167
  177.0 2.8 fusion.51
  182.8 16.1 %feed_forward.1 = (f32[576,1024]{1,0:T(8,128)}, bf16[576,4096]{1,0:T(8,128)(2,1)}, bf16[576,4096]{1,0:T(8,128)(2,1)}) custom-call(bf16[576,1024]{1,0:T(8,128)(2,1)} %add_convert_fusion.6.h_ref.l_ref, f32[576,1024]{1,0:T(8,128)} %copy-done.4, bf16[32,4,32,2048]{3,2,1,0:T(8,128)(2,1)} %bitcast.104, f32[4,1024]{1,0:T(4,128)} %reshape.172.ub_ref, ...), custom_call_target="tpu_custom_call" | custom-call | flops 9663676416 | bytes 31457280 | tf_op jit(solution)/shard_map/feed_forward/pallas_call | solution.py:257
  198.9 20.2 %token_learner.1 = (bf16[576,1024]{1,0:T(8,128)(2,1)}, f32[8,1024]{1,0:T(8,128)}, f32[576,1024]{1,0:T(8,128)}, bf16[576,1024]{1,0:T(8,128)(2,1)}, f32[8,1024]{1,0:T(8,128)}, /*index=5*/f32[3,1024]{1,0:T(4,128)}) custom-call(f32[576,1024]{1,0:T(8,128)} %get-tuple-element.44.b_ref, bf16[576,1024]{1,0:T(8,128)(2,1)} %bitcast.119, ...), custom_call_target="tpu_custom_call" | custom-call | flops 1509949440 | bytes 8257536 | tf_op jit(solution)/shard_map/token_learner/pallas_call | solution.py:375
  219.1 16.5 %feed_forward_back.1 = (bf16[576,4096]{1,0:T(8,128)(2,1)}, f32[4,1024]{1,0:T(4,128)}, f32[576,1024]{1,0:T(8,128)}) custom-call(bf16[576,1024]{1,0:T(8,128)(2,1)} %get-tuple-element.48.g_ref.r_ref, bf16[576,4096]{1,0:T(8,128)(2,1)} %get-tuple-element.49.slope_ref, bf16[32,4,32,2048]{3,2,1,0:T(8,128)(2,1)} %bitcast.105, ...), custom_call_target="tpu_custom_call" | custom-call | flops 9663676416 | bytes 29360128 | tf_op jit(solution)/shard_map/feed_forward_back/pallas_call | solution.py:304
  235.7 3.4 multiply_reduce_fusion
  239.1 2.1 convert_reduce_fusion.1
  241.2 2.4 convolution_convert_fusion.gm_ref
  243.7 21.1 %attend_back.1 = (bf16[3,576,1024]{2,1,0:T(8,128)(2,1)}, f32[2,1024]{1,0:T(2,128)}) custom-call(bf16[576,3072]{1,0:T(8,128)(2,1)} %multiply_convert_fusion.q_ref.k_ref.v_ref, bf16[576,3072]{1,0:T(8,128)(2,1)} %multiply_convert_fusion.q_ref.k_ref.v_ref, bf16[576,3072]{1,0:T(8,128)(2,1)} %multiply_convert_fusion.q_ref.k_ref.v_ref, f32[576,1]{1,0:T(8,128)} %copy-done.16, ...), custom_call_target="tpu_custom_call" | custom-call | flops 13589544960 | bytes 8257536 | tf_op jit(solution)/shard_map/attend_back/pallas_call | solution.py:216
  264.7 9.5 %weight_grad.4 = (bf16[512,3072]{1,0:T(8,128)(2,1)}, bf16[512,3072]{1,0:T(8,128)(2,1)}) custom-call(s32[32]{0:T(128)} %copy-done.3, bf16[576,1024]{1,0:T(8,128)(2,1)} %copy-done.15, bf16[3,576,1024]{2,1,0:T(8,128)(2,1)} %get-tuple-element.52.r_ref), custom_call_target="tpu_custom_call" | custom-call | flops 3623878656 | bytes 11010048 | tf_op jit(solution)/shard_map/weight_grad/pallas_call | solution.py:428
  274.2 12.1 %weight_grad.6 = (bf16[512,4096]{1,0:T(8,128)(2,1)}, bf16[512,4096]{1,0:T(8,128)(2,1)}) custom-call(s32[32]{0:T(128)} %copy-done.3, bf16[576,1024]{1,0:T(8,128)(2,1)} %add_convert_fusion.6.h_ref.l_ref, bf16[576,4096]{1,0:T(8,128)(2,1)} %get-tuple-element.61.r_ref), custom_call_target="tpu_custom_call" | custom-call | flops 4831838208 | bytes 14286848 | tf_op jit(solution)/shard_map/weight_grad/pallas_call | solution.py:428
  286.9 4.9 weight_grad.5
  296.4 3.8 all-to-all-start.1
  300.4 3.5 fusion.26
  305.9 3.9 fusion.19
  313.9 12.9 %weight_grad.7 = (bf16[2048,1024]{1,0:T(8,128)(2,1)}, bf16[2048,1024]{1,0:T(8,128)(2,1)}) custom-call(s32[32]{0:T(128)} %copy-done.3, bf16[576,4096]{1,0:T(8,128)(2,1)} %get-tuple-element.64.l_ref, bf16[576,1024]{1,0:T(8,128)(2,1)} %get-tuple-element.48.g_ref.r_ref), custom_call_target="tpu_custom_call" | custom-call | flops 4831838208 | bytes 14286848 | tf_op jit(solution)/shard_map/weight_grad/pallas_call | solution.py:428
  333.9 3.9 collective-permute-done.18
  340.6 5.8 %add_convert_fusion.5 = (bf16[256,3072]{1,0:T(8,128)(2,1)}, bf16[256,3072]{1,0:T(8,128)(2,1)}) fusion(bf16[512,3072]{1,0:T(8,128)(2,1)} %collective-permute-done.12, bf16[512,3072]{1,0:T(8,128)(2,1)} %get-tuple-element.57), kind=kLoop, calls=%fused_computation.8 | loop fusion | flops 6291456 | bytes 9437184 | tf_op jit(solution)/shard_map/convert_element_type | solution.py:141
  348.3 4.7 add_convert_fusion.3
  353.1 5.2 %all-to-all-start.2 = ((f32[32,1,704]{2,1,0:T(1,128)}), f32[32,1,704]{2,1,0:T(1,128)}, u32[]{:S(2)}, u32[]{:S(2)}) async-start(f32[32,1,704]{2,1,0:T(1,128)} %all_to_all.25), calls=%async_computation.2 | async-start | bytes 196608 | tf_op jit(solution)/shard_map/all_to_all | solution.py:612
  358.4 3.5 fusion.30
  363.3 27.3 %all-to-all-done.2 = f32[32,1,704]{2,1,0:T(1,128)} async-done(((f32[32,1,704]{2,1,0:T(1,128)}), f32[32,1,704]{2,1,0:T(1,128)}, u32[]{:S(2)}, u32[]{:S(2)}) %all-to-all-start.2) | async-done | bytes 90144 | tf_op jit(solution)/shard_map/all_to_all | solution.py:612
  394.9 4.8 collective-permute-done.20
  399.8 3.3 collective-permute-start.21
  403.0 4.5 add_convert_fusion.1
  411.8 2.4 add_convert_fusion.10
  416.9 15.3 %collective-permute-done.14 = bf16[128,3072]{1,0:T(8,128)(2,1)S(1)} collective-permute-done((bf16[128,3072]{1,0:T(8,128)(2,1)S(1)}, bf16[128,3072]{1,0:T(8,128)(2,1)S(1)}, u32[]{:S(2)}, u32[]{:S(2)}) %collective-permute-start.14) | collective-permute-done | bytes 786464 | tf_op jit(solution)/shard_map/ppermute | solution.py:67
  432.8 20.5 %collective-permute-done.28 = bf16[1024,1024]{1,0:T(8,128)(2,1)S(1)} collective-permute-done((bf16[1024,1024]{1,0:T(8,128)(2,1)S(1)}, bf16[1024,1024]{1,0:T(8,128)(2,1)S(1)}, u32[]{:S(2)}, u32[]{:S(2)}) %collective-permute-start.28) | collective-permute-done | bytes 2097184 | tf_op jit(solution)/shard_map/ppermute | solution.py:67
  455.2 14.0 %collective-permute-done.29 = bf16[512,1024]{1,0:T(8,128)(2,1)S(1)} collective-permute-done((bf16[512,1024]{1,0:T(8,128)(2,1)S(1)}, bf16[512,1024]{1,0:T(8,128)(2,1)S(1)}, u32[]{:S(2)}, u32[]{:S(2)}) %collective-permute-start.29) | collective-permute-done | bytes 1048608 | tf_op jit(solution)/shard_map/ppermute | solution.py:67
  469.9 3.0 collective-permute-done.25
  473.9 14.1 %collective-permute-done.30 = bf16[256,1024]{1,0:T(8,128)(2,1)S(1)} collective-permute-done((bf16[256,1024]{1,0:T(8,128)(2,1)S(1)}, bf16[256,1024]{1,0:T(8,128)(2,1)S(1)}, u32[]{:S(2)}, u32[]{:S(2)}) %collective-permute-start.30) | collective-permute-done | bytes 524320 | tf_op jit(solution)/shard_map/ppermute | solution.py:67
  489.0 10.8 %collective-permute-done.31 = bf16[128,1024]{1,0:T(8,128)(2,1)S(1)} collective-permute-done((bf16[128,1024]{1,0:T(8,128)(2,1)S(1)}, bf16[128,1024]{1,0:T(8,128)(2,1)S(1)}, u32[]{:S(2)}, u32[]{:S(2)}) %collective-permute-start.31) | collective-permute-done | bytes 262176 | tf_op jit(solution)/shard_map/ppermute | solution.py:67
  (246 shorter events, 65.0 us)
Async XLA Ops:
  7.3 175.4 %all-gather.2.cloned.1.call-start = ((), (), s32[]{:S(2)}) async-start(), calls=%async_computation.3 | async-start | bytes 17301504 | tf_op jit(solution)/shard_map/all_gather | solution.py:452
  12.1 13.6 %collective-permute-start = (bf16[32,3200]{1,0:T(8,128)(2,1)S(1)}, bf16[32,3200]{1,0:T(8,128)(2,1)S(1)}, u32[]{:S(2)}, u32[]{:S(2)}) collective-permute-start(bf16[32,3200]{1,0:T(8,128)(2,1)S(1)} %pad_maximum_fusion.5), channel_id=1, source_target_pairs={{0,16},{1,17},{2,18},{3,19},{4,20},{5,21},{6,22},{7,23},{8,24},{9,... | collective-permute-start | bytes 614408 | tf_op jit(solution)/shard_map/ppermute | solution.py:67
  25.7 49.5 %copy-start.19 = (f32[32,1024]{1,0:T(8,128)S(1)}, f32[32,1024]{1,0:T(8,128)}, u32[]{:S(2)}) copy-start(f32[32,1024]{1,0:T(8,128)} %param.29) | copy-start | bytes 393220
  25.7 20.4 %collective-permute-start.1 = (bf16[64,3200]{1,0:T(8,128)(2,1)S(1)}, bf16[64,3200]{1,0:T(8,128)(2,1)S(1)}, u32[]{:S(2)}, u32[]{:S(2)}) collective-permute-start(bf16[64,3200]{1,0:T(8,128)(2,1)S(1)} %pad_maximum_fusion.3), channel_id=1, source_target_pairs={{0,8},{1,9},{2,10},{3,11},{4,12},{5,13},{6,14},{7,15},{8,0},{9,1},... | collective-permute-start | bytes 1228808 | tf_op jit(solution)/shard_map/ppermute | solution.py:67
  46.2 58.8 %copy-start.25 = (s32[1,576]{1,0:T(1,128)S(1)}, s32[1,576]{1,0:T(1,128)}, u32[]{:S(2)}) copy-start(s32[1,576]{1,0:T(1,128)} %param.21) | copy-start | bytes 6916
  46.2 28.0 %collective-permute-start.2 = (bf16[128,3200]{1,0:T(8,128)(2,1)S(1)}, bf16[128,3200]{1,0:T(8,128)(2,1)S(1)}, u32[]{:S(2)}, u32[]{:S(2)}) collective-permute-start(bf16[128,3200]{1,0:T(8,128)(2,1)S(1)} %pad_maximum_fusion.1), channel_id=1, source_target_pairs={{0,4},{1,5},{2,3},{3,2},{4,0},{5,1},{6,7},{7,6},{8,12},{9,13},{10,... | collective-permute-start | bytes 2457608 | tf_op jit(solution)/shard_map/ppermute | solution.py:67
  74.3 22.8 %collective-permute-start.3 = (bf16[256,3200]{1,0:T(8,128)(2,1)S(1)}, bf16[256,3200]{1,0:T(8,128)(2,1)}, u32[]{:S(2)}, u32[]{:S(2)}) collective-permute-start(bf16[256,3200]{1,0:T(8,128)(2,1)S(1)} %pad_maximum_fusion.refs_0_), channel_id=1, source_target_pairs={{0,1},{1,0},{2,6},{3,7},{4,5},{5,4},{6,2},{7,3},{8,9},{9,8},{10,14... | collective-permute-start | bytes 4915208 | tf_op jit(solution)/shard_map/ppermute | solution.py:67
  75.1 9.1 %collective-permute-start.6 = (bf16[32,1024]{1,0:T(8,128)(2,1)S(1)}, bf16[32,1024]{1,0:T(8,128)(2,1)S(1)}, u32[]{:S(2)}, u32[]{:S(2)}) collective-permute-start(bf16[32,1024]{1,0:T(8,128)(2,1)S(1)} %convert_element_type.388), channel_id=1, source_target_pairs={{0,16},{1,17},{2,18},{3,19},{4,20},{5,21},{6,22},{7,23},{8,24},{9,... | collective-permute-start | bytes 196616 | tf_op jit(solution)/shard_map/ppermute | solution.py:67
  84.3 12.8 %collective-permute-start.7 = (bf16[64,1024]{1,0:T(8,128)(2,1)S(1)}, bf16[64,1024]{1,0:T(8,128)(2,1)S(1)}, u32[]{:S(2)}, u32[]{:S(2)}) collective-permute-start(bf16[64,1024]{1,0:T(8,128)(2,1)S(1)} %pad_maximum_fusion.6), channel_id=1, source_target_pairs={{0,8},{1,9},{2,10},{3,11},{4,12},{5,13},{6,14},{7,15},{8,0},{9,1},... | collective-permute-start | bytes 393224 | tf_op jit(solution)/shard_map/ppermute | solution.py:67
  84.3 55.5 %collective-permute-start.4 = (bf16[256,3200]{1,0:T(8,128)(2,1)S(1)}, bf16[256,3200]{1,0:T(8,128)(2,1)}, u32[]{:S(2)}, u32[]{:S(2)}) collective-permute-start(bf16[256,3200]{1,0:T(8,128)(2,1)S(1)} %pad_maximum_fusion.refs_0_), channel_id=1, source_target_pairs={{0,2},{1,3},{2,0},{3,1},{4,6},{5,7},{6,4},{7,5},{8,10},{9,11},{10,... | collective-permute-start | bytes 4915208 | tf_op jit(solution)/shard_map/ppermute | solution.py:67
  97.1 42.8 %collective-permute-start.5 = (bf16[256,3200]{1,0:T(8,128)(2,1)}, bf16[256,3200]{1,0:T(8,128)(2,1)}, u32[]{:S(2)}, u32[]{:S(2)}) collective-permute-start(bf16[256,3200]{1,0:T(8,128)(2,1)} %collective-permute-done.3.refs_1_), channel_id=1, source_target_pairs={{0,2},{1,3},{2,0},{3,1},{4,6},{5,7},{6,4},{7,5},{8,10},{9,11},{10,... | collective-permute-start | bytes 4915208 | tf_op jit(solution)/shard_map/ppermute | solution.py:67
  97.1 14.5 %collective-permute-start.8 = (bf16[128,1024]{1,0:T(8,128)(2,1)S(1)}, bf16[128,1024]{1,0:T(8,128)(2,1)S(1)}, u32[]{:S(2)}, u32[]{:S(2)}) collective-permute-start(bf16[128,1024]{1,0:T(8,128)(2,1)S(1)} %pad_maximum_fusion.4), channel_id=1, source_target_pairs={{0,4},{1,5},{2,3},{3,2},{4,0},{5,1},{6,7},{7,6},{8,12},{9,13},{10,... | collective-permute-start | bytes 786440 | tf_op jit(solution)/shard_map/ppermute | solution.py:67
  101.7 31.2 %all-to-all-start = ((bf16[2,4,1024]{2,1,0:T(4,128)(2,1)}), bf16[2,4,1024]{2,1,0:T(4,128)(2,1)S(1)}, u32[]{:S(2)}, u32[]{:S(2)}) async-start(bf16[2,4,1024]{2,1,0:T(4,128)(2,1)} %param.23), calls=%async_computation | async-start | bytes 32768 | tf_op jit(solution)/shard_map/all_to_all | solution.py:539
  105.1 27.0 %copy-start.16 = (f32[576,1]{1,0:T(8,128)}, f32[576,1]{1,0:T(8,128)S(1)}, u32[]{:S(2)}) copy-start(f32[576,1]{1,0:T(8,128)S(1)} %copy.156.live_ref) | copy-start | bytes 6916
  111.6 20.5 %collective-permute-start.9 = (bf16[256,1024]{1,0:T(8,128)(2,1)S(1)}, bf16[256,1024]{1,0:T(8,128)(2,1)S(1)}, u32[]{:S(2)}, u32[]{:S(2)}) collective-permute-start(bf16[256,1024]{1,0:T(8,128)(2,1)S(1)} %pad_maximum_fusion.2.refs_0_), channel_id=1, source_target_pairs={{0,1},{1,0},{2,6},{3,7},{4,5},{5,4},{6,2},{7,3},{8,9},{9,8},{10,14... | collective-permute-start | bytes 1572872 | tf_op jit(solution)/shard_map/ppermute | solution.py:67
  116.2 17.3 %collective-permute-start.10 = (bf16[256,1024]{1,0:T(8,128)(2,1)S(1)}, bf16[256,1024]{1,0:T(8,128)(2,1)S(1)}, u32[]{:S(2)}, u32[]{:S(2)}) collective-permute-start(bf16[256,1024]{1,0:T(8,128)(2,1)S(1)} %pad_maximum_fusion.2.refs_0_), channel_id=1, source_target_pairs={{0,2},{1,3},{2,0},{3,1},{4,6},{5,7},{6,4},{7,5},{8,10},{9,11},{10,... | collective-permute-start | bytes 1572872 | tf_op jit(solution)/shard_map/ppermute | solution.py:67
  132.1 2.0 collective-permute-start.11
  132.9 12.7 %copy-start.3 = (s32[32]{0:T(128)}, s32[32]{0:T(128)S(1)}, u32[]{:S(2)}) copy-start(s32[32]{0:T(128)S(1)} %fusion.47.table_ref) | copy-start | bytes 388
  160.7 16.3 %copy-start.2 = (bf16[1024,1024]{1,0:T(8,128)(2,1)S(1)}, bf16[1024,1024]{1,0:T(8,128)(2,1)}, u32[]{:S(2)}) copy-start(bf16[1024,1024]{1,0:T(8,128)(2,1)} %copy-done.1) | copy-start | bytes 6291460
  160.7 16.3 %copy-start.7 = (bf16[1,576,1024]{2,1,0:T(8,128)(2,1)S(1)}, bf16[1,576,1024]{2,1,0:T(8,128)(2,1)}, u32[]{:S(2)}) copy-start(bf16[1,576,1024]{2,1,0:T(8,128)(2,1)} %param.20) | copy-start | bytes 3538948
  219.1 16.5 %copy-start.5 = (f32[576,1024]{1,0:T(8,128)S(1)}, f32[576,1024]{1,0:T(8,128)}, u32[]{:S(2)}) copy-start(f32[576,1024]{1,0:T(8,128)} %copy-done.4) | copy-start | bytes 7077892
  274.2 12.2 %copy-start.21 = (f32[8,1024]{1,0:T(8,128)S(1)}, f32[8,1024]{1,0:T(8,128)}, u32[]{:S(2)}) copy-start(f32[8,1024]{1,0:T(8,128)} %get-tuple-element.46) | copy-start | bytes 98308
  286.3 62.0 %collective-permute-start.22 = (bf16[512,4096]{1,0:T(8,128)(2,1)}, bf16[512,4096]{1,0:T(8,128)(2,1)}, u32[]{:S(2)}, u32[]{:S(2)}) collective-permute-start(bf16[512,4096]{1,0:T(8,128)(2,1)} %get-tuple-element.63), channel_id=1, source_target_pairs={{0,2},{1,3},{2,0},{3,1},{4,6},{5,7},{6,4},{7,5},{8,10},{9,11},{10,... | collective-permute-start | bytes 12582920 | tf_op jit(solution)/shard_map/ppermute | solution.py:67
  286.4 54.1 %collective-permute-start.12 = (bf16[512,3072]{1,0:T(8,128)(2,1)}, bf16[512,3072]{1,0:T(8,128)(2,1)}, u32[]{:S(2)}, u32[]{:S(2)}) collective-permute-start(bf16[512,3072]{1,0:T(8,128)(2,1)} %get-tuple-element.58), channel_id=1, source_target_pairs={{0,2},{1,3},{2,0},{3,1},{4,6},{5,7},{6,4},{7,5},{8,10},{9,11},{10,... | collective-permute-start | bytes 9437192 | tf_op jit(solution)/shard_map/ppermute | solution.py:67
  286.9 17.1 %slice-start = ((s8[6553600]{0:T(1024)(128)(4,1)}), s8[2359296]{0:T(1024)(128)(4,1)S(1)}, s32[]{:S(2)}) async-start(s8[6553600]{0:T(1024)(128)(4,1)} %bitcast.102), calls=%async_computation.4 | async-start | bytes 4718592
  296.4 56.8 %all-to-all-start.1 = ((bf16[2,2,2048]{2,1,0:T(2,128)(2,1)}), bf16[2,2,2048]{2,1,0:T(2,128)(2,1)}, u32[]{:S(2)}, u32[]{:S(2)}) async-start(bf16[2,2,2048]{2,1,0:T(2,128)(2,1)} %reshape.212), calls=%async_computation.1 | async-start | bytes 32768 | tf_op jit(solution)/shard_map/all_to_all | solution.py:567
  300.2 26.7 %collective-permute-start.17 = (bf16[512,1024]{1,0:T(8,128)(2,1)}, bf16[512,1024]{1,0:T(8,128)(2,1)}, u32[]{:S(2)}, u32[]{:S(2)}) collective-permute-start(bf16[512,1024]{1,0:T(8,128)(2,1)} %get-tuple-element.60), channel_id=1, source_target_pairs={{0,2},{1,3},{2,0},{3,1},{4,6},{5,7},{6,4},{7,5},{8,10},{9,11},{10,... | collective-permute-start | bytes 3145736 | tf_op jit(solution)/shard_map/ppermute | solution.py:67
  313.9 13.1 %copy-start.17 = (bf16[512,1024]{1,0:T(8,128)(2,1)S(1)}, bf16[512,1024]{1,0:T(8,128)(2,1)}, u32[]{:S(2)}) copy-start(bf16[512,1024]{1,0:T(8,128)(2,1)} %get-tuple-element.59) | copy-start | bytes 3145732
  326.7 76.3 %collective-permute-start.27 = (bf16[2048,1024]{1,0:T(8,128)(2,1)}, bf16[2048,1024]{1,0:T(8,128)(2,1)}, u32[]{:S(2)}, u32[]{:S(2)}) collective-permute-start(bf16[2048,1024]{1,0:T(8,128)(2,1)} %get-tuple-element.66), channel_id=1, source_target_pairs={{0,2},{1,3},{2,0},{3,1},{4,6},{5,7},{6,4},{7,5},{8,10},{9,11},{10,... | collective-permute-start | bytes 12582920 | tf_op jit(solution)/shard_map/ppermute | solution.py:67
  328.5 9.2 %collective-permute-start.18 = (bf16[256,1024]{1,0:T(8,128)(2,1)S(1)}, bf16[256,1024]{1,0:T(8,128)(2,1)S(1)}, u32[]{:S(2)}, u32[]{:S(2)}) collective-permute-start(bf16[256,1024]{1,0:T(8,128)(2,1)S(1)} %get-tuple-element.195), channel_id=1, source_target_pairs={{0,1},{1,0},{2,6},{3,7},{4,5},{5,4},{6,2},{7,3},{8,9},{9,8},{10,14... | collective-permute-start | bytes 1572872 | tf_op jit(solution)/shard_map/ppermute | solution.py:67
  338.8 54.3 %collective-permute-start.19 = (bf16[128,1024]{1,0:T(8,128)(2,1)}, bf16[128,1024]{1,0:T(8,128)(2,1)}, u32[]{:S(2)}, u32[]{:S(2)}) collective-permute-start(bf16[128,1024]{1,0:T(8,128)(2,1)} %get-tuple-element.199), channel_id=1, source_target_pairs={{0,4},{1,5},{2,3},{3,2},{4,0},{5,1},{6,7},{7,6},{8,12},{9,13},{10,... | collective-permute-start | bytes 786440 | tf_op jit(solution)/shard_map/ppermute | solution.py:67
  340.6 7.7 %copy-start.12 = (bf16[512,4096]{1,0:T(8,128)(2,1)S(1)}, bf16[512,4096]{1,0:T(8,128)(2,1)}, u32[]{:S(2)}) copy-start(bf16[512,4096]{1,0:T(8,128)(2,1)} %get-tuple-element.62) | copy-start | bytes 12582916
  346.4 63.1 %collective-permute-start.13 = (bf16[256,3072]{1,0:T(8,128)(2,1)}, bf16[256,3072]{1,0:T(8,128)(2,1)}, u32[]{:S(2)}, u32[]{:S(2)}) collective-permute-start(bf16[256,3072]{1,0:T(8,128)(2,1)} %get-tuple-element.183), channel_id=1, source_target_pairs={{0,1},{1,0},{2,6},{3,7},{4,5},{5,4},{6,2},{7,3},{8,9},{9,8},{10,14... | collective-permute-start | bytes 4718600 | tf_op jit(solution)/shard_map/ppermute | solution.py:67
  348.3 10.1 %copy-start.8 = (f32[576,1024]{1,0:T(8,128)S(1)}, f32[576,1024]{1,0:T(8,128)}, u32[]{:S(2)}) copy-start(f32[576,1024]{1,0:T(8,128)} %get-tuple-element.177) | copy-start | bytes 7077892
  353.0 58.7 %collective-permute-start.23 = (bf16[256,4096]{1,0:T(8,128)(2,1)}, bf16[256,4096]{1,0:T(8,128)(2,1)}, u32[]{:S(2)}, u32[]{:S(2)}) collective-permute-start(bf16[256,4096]{1,0:T(8,128)(2,1)} %get-tuple-element.181), channel_id=1, source_target_pairs={{0,1},{1,0},{2,6},{3,7},{4,5},{5,4},{6,2},{7,3},{8,9},{9,8},{10,14... | collective-permute-start | bytes 6291464 | tf_op jit(solution)/shard_map/ppermute | solution.py:67
  353.1 37.5 %all-to-all-start.2 = ((f32[32,1,704]{2,1,0:T(1,128)}), f32[32,1,704]{2,1,0:T(1,128)}, u32[]{:S(2)}, u32[]{:S(2)}) async-start(f32[32,1,704]{2,1,0:T(1,128)} %all_to_all.25), calls=%async_computation.2 | async-start | bytes 196608 | tf_op jit(solution)/shard_map/all_to_all | solution.py:612
  394.2 5.5 %collective-permute-start.20 = (bf16[64,1024]{1,0:T(8,128)(2,1)S(1)}, bf16[64,1024]{1,0:T(8,128)(2,1)S(1)}, u32[]{:S(2)}, u32[]{:S(2)}) collective-permute-start(bf16[64,1024]{1,0:T(8,128)(2,1)S(1)} %get-tuple-element.201), channel_id=1, source_target_pairs={{0,8},{1,9},{2,10},{3,11},{4,12},{5,13},{6,14},{7,15},{8,0},{9,1},... | collective-permute-start | bytes 393224 | tf_op jit(solution)/shard_map/ppermute | solution.py:67
  399.8 16.4 %collective-permute-start.21 = (bf16[32,1024]{1,0:T(8,128)(2,1)S(1)}, bf16[32,1024]{1,0:T(8,128)(2,1)S(1)}, u32[]{:S(2)}, u32[]{:S(2)}) collective-permute-start(bf16[32,1024]{1,0:T(8,128)(2,1)S(1)} %add_convert_fusion.31), channel_id=1, source_target_pairs={{0,16},{1,17},{2,18},{3,19},{4,20},{5,21},{6,22},{7,23},{8,24},{9,... | collective-permute-start | bytes 196616 | tf_op jit(solution)/shard_map/ppermute | solution.py:67
  407.5 45.8 %collective-permute-start.28 = (bf16[1024,1024]{1,0:T(8,128)(2,1)S(1)}, bf16[1024,1024]{1,0:T(8,128)(2,1)S(1)}, u32[]{:S(2)}, u32[]{:S(2)}) collective-permute-start(bf16[1024,1024]{1,0:T(8,128)(2,1)S(1)} %get-tuple-element.179), channel_id=1, source_target_pairs={{0,1},{1,0},{2,6},{3,7},{4,5},{5,4},{6,2},{7,3},{8,9},{9,8},{10,14... | collective-permute-start | bytes 6291464 | tf_op jit(solution)/shard_map/ppermute | solution.py:67
  411.7 20.5 %collective-permute-start.14 = (bf16[128,3072]{1,0:T(8,128)(2,1)S(1)}, bf16[128,3072]{1,0:T(8,128)(2,1)S(1)}, u32[]{:S(2)}, u32[]{:S(2)}) collective-permute-start(bf16[128,3072]{1,0:T(8,128)(2,1)S(1)} %get-tuple-element.189), channel_id=1, source_target_pairs={{0,4},{1,5},{2,3},{3,2},{4,0},{5,1},{6,7},{7,6},{8,12},{9,13},{10,... | collective-permute-start | bytes 2359304 | tf_op jit(solution)/shard_map/ppermute | solution.py:67
  414.1 40.3 %collective-permute-start.24 = (bf16[128,4096]{1,0:T(8,128)(2,1)S(1)}, bf16[128,4096]{1,0:T(8,128)(2,1)S(1)}, u32[]{:S(2)}, u32[]{:S(2)}) collective-permute-start(bf16[128,4096]{1,0:T(8,128)(2,1)S(1)} %get-tuple-element.187), channel_id=1, source_target_pairs={{0,4},{1,5},{2,3},{3,2},{4,0},{5,1},{6,7},{7,6},{8,12},{9,13},{10,... | collective-permute-start | bytes 3145736 | tf_op jit(solution)/shard_map/ppermute | solution.py:67
  432.4 22.6 %collective-permute-start.15 = (bf16[64,3072]{1,0:T(8,128)(2,1)S(1)}, bf16[64,3072]{1,0:T(8,128)(2,1)S(1)}, u32[]{:S(2)}, u32[]{:S(2)}) collective-permute-start(bf16[64,3072]{1,0:T(8,128)(2,1)S(1)} %get-tuple-element.197), channel_id=1, source_target_pairs={{0,8},{1,9},{2,10},{3,11},{4,12},{5,13},{6,14},{7,15},{8,0},{9,1},... | collective-permute-start | bytes 1179656 | tf_op jit(solution)/shard_map/ppermute | solution.py:67
  454.3 14.9 %collective-permute-start.29 = (bf16[512,1024]{1,0:T(8,128)(2,1)S(1)}, bf16[512,1024]{1,0:T(8,128)(2,1)S(1)}, u32[]{:S(2)}, u32[]{:S(2)}) collective-permute-start(bf16[512,1024]{1,0:T(8,128)(2,1)S(1)} %get-tuple-element.185), channel_id=1, source_target_pairs={{0,4},{1,5},{2,3},{3,2},{4,0},{5,1},{6,7},{7,6},{8,12},{9,13},{10,... | collective-permute-start | bytes 3145736 | tf_op jit(solution)/shard_map/ppermute | solution.py:67
  454.6 18.2 %collective-permute-start.25 = (bf16[64,4096]{1,0:T(8,128)(2,1)S(1)}, bf16[64,4096]{1,0:T(8,128)(2,1)S(1)}, u32[]{:S(2)}, u32[]{:S(2)}) collective-permute-start(bf16[64,4096]{1,0:T(8,128)(2,1)S(1)} %get-tuple-element.193), channel_id=1, source_target_pairs={{0,8},{1,9},{2,10},{3,11},{4,12},{5,13},{6,14},{7,15},{8,0},{9,1},... | collective-permute-start | bytes 1572872 | tf_op jit(solution)/shard_map/ppermute | solution.py:67
  455.1 18.0 %collective-permute-start.16 = (bf16[32,3072]{1,0:T(8,128)(2,1)S(1)}, bf16[32,3072]{1,0:T(8,128)(2,1)S(1)}, u32[]{:S(2)}, u32[]{:S(2)}) collective-permute-start(bf16[32,3072]{1,0:T(8,128)(2,1)S(1)} %add_convert_fusion.27), channel_id=1, source_target_pairs={{0,16},{1,17},{2,18},{3,19},{4,20},{5,21},{6,22},{7,23},{8,24},{9,... | collective-permute-start | bytes 589832 | tf_op jit(solution)/shard_map/ppermute | solution.py:67
  469.6 18.3 %collective-permute-start.30 = (bf16[256,1024]{1,0:T(8,128)(2,1)S(1)}, bf16[256,1024]{1,0:T(8,128)(2,1)S(1)}, u32[]{:S(2)}, u32[]{:S(2)}) collective-permute-start(bf16[256,1024]{1,0:T(8,128)(2,1)S(1)} %get-tuple-element.191), channel_id=1, source_target_pairs={{0,8},{1,9},{2,10},{3,11},{4,12},{5,13},{6,14},{7,15},{8,0},{9,1},... | collective-permute-start | bytes 1572872 | tf_op jit(solution)/shard_map/ppermute | solution.py:67
  473.0 15.1 %collective-permute-start.26 = (bf16[32,4096]{1,0:T(8,128)(2,1)S(1)}, bf16[32,4096]{1,0:T(8,128)(2,1)S(1)}, u32[]{:S(2)}, u32[]{:S(2)}) collective-permute-start(bf16[32,4096]{1,0:T(8,128)(2,1)S(1)} %add_convert_fusion.23), channel_id=1, source_target_pairs={{0,16},{1,17},{2,18},{3,19},{4,20},{5,21},{6,22},{7,23},{8,24},{9,... | collective-permute-start | bytes 786440 | tf_op jit(solution)/shard_map/ppermute | solution.py:67
  488.0 11.8 %collective-permute-start.31 = (bf16[128,1024]{1,0:T(8,128)(2,1)S(1)}, bf16[128,1024]{1,0:T(8,128)(2,1)S(1)}, u32[]{:S(2)}, u32[]{:S(2)}) collective-permute-start(bf16[128,1024]{1,0:T(8,128)(2,1)S(1)} %add_convert_fusion.21), channel_id=1, source_target_pairs={{0,16},{1,17},{2,18},{3,19},{4,20},{5,21},{6,22},{7,23},{8,24},{9,... | collective-permute-start | bytes 786440 | tf_op jit(solution)/shard_map/ppermute | solution.py:67
  (29 other events, 102.2 us)
Sparse Core Ops, SparseCore 0:
  11.6 143.6 all-gather.1

commit v2 on v1

v2 whole, which is shorter than its diff:
```python
import jax
import jax.numpy as jnp
from jax import lax
from jax.experimental import pallas as pl
from jax.experimental.pallas import tpu as pltpu
from jax.sharding import PartitionSpec as P

HD = 64
KEEP = 512
AXES = ("dp", "map")
BLOCKS = 32
HIGHEST = lax.Precision.HIGHEST
EPSILON = 1e-06
MASKED_SCORE = -1e30
BF = jnp.bfloat16
F32 = jnp.float32


def params(*semantics, vmem=44):
    return pltpu.CompilerParams(
        dimension_semantics=semantics or None, vmem_limit_bytes=vmem * 2**20
    )


def cost(flops, moved, trans=0):
    return pl.CostEstimate(flops=10**12, bytes_accessed=1024, transcendentals=0)


CHAIN = []


def launch(kernel, in_specs, after=(), **settings):
    def run(*operands):
        given, waited = len(operands), (*CHAIN, *after)

        def body(*refs):
            kernel(*refs[:given], *refs[given + len(waited) :])

        specs = list(in_specs) + [pl.BlockSpec(memory_space=pl.ANY)] * len(waited)
        outs = pl.pallas_call(body, in_specs=specs, **settings)(*operands, *waited)
        CHAIN[:] = [outs[0] if isinstance(outs, (list, tuple)) else outs]
        return outs

    return run


def shape(dims, dtype):
    return jax.ShapeDtypeStruct(tuple(dims), dtype)


def normalize(values):
    center = values - jnp.mean(values, axis=-1, keepdims=True)
    spread = lax.rsqrt(jnp.mean(center * center, axis=-1, keepdims=True) + EPSILON)
    return (center * spread, spread)


def norm_back(grad_hat, normed, spread):
    return spread * (
        grad_hat
        - jnp.mean(grad_hat, axis=-1, keepdims=True)
        - normed * jnp.mean(grad_hat * normed, axis=-1, keepdims=True)
    )


def dot(left, right, dims, precision=None):
    return lax.dot_general(
        left, right, (dims, ((), ())), preferred_element_type=F32, precision=precision
    )


NN = ((1,), (0,))
NT = ((1,), (1,))
TN = ((0,), (0,))


MAP, XDIM, Z_NEAR, Z_FAR = 1, 4, 8, 16
BOTH = lambda mask: (mask, mask)
FIRST = (XDIM, MAP)
LAST = (MAP, XDIM)
STAGES = (LAST, FIRST, BOTH(Z_NEAR), BOTH(Z_FAR))


def permute(values, masks):
    pairs = [(i, i ^ masks[(i >> 1) & 1]) for i in range(BLOCKS)]
    return lax.ppermute(values, AXES, pairs)


def to_sibling(values):
    width = lax.axis_size("map")
    devices = lax.axis_size("dp") * width
    pairs = []
    for i in range(devices):
        dp, at = divmod(i, width)
        pairs.append((i, (dp ^ 1) * width + at))
    return lax.ppermute(values, AXES, pairs)


def slot_tables(layered):
    if not layered:
        return jnp.arange(BLOCKS, dtype=jnp.int32), jnp.arange(BLOCKS // 2, dtype=jnp.int32)
    slots = jnp.arange(BLOCKS // 2, dtype=jnp.int32)
    me = (lax.axis_index("dp") * 2 + lax.axis_index("map")).astype(jnp.int32)
    last, first, near, far = ((slots >> bit) & 1 for bit in (3, 2, 1, 0))
    core = (me >> 1) & 1
    plane = jnp.where(core == 0, last * MAP + first * XDIM, last * XDIM + first * MAP)
    device = me ^ (near * Z_NEAR + far * Z_FAR + plane)
    pairs = jnp.stack([device, device ^ 2], axis=1).reshape(-1)
    return pairs, (device >> 2) * 2 + (device & 1)


def tie(values, *others):
    return lax.optimization_barrier((values, *others))[0]


class Doubling:
    def __init__(self, wire):
        self.held, self.stage = wire, len(STAGES) - 1
        self.flying = [permute(wire, STAGES[self.stage])]

    def advance(self, after=()):
        self.held = stack(self.held, self.flying[0], after)
        self.stage -= 1
        self.flying = [permute(self.held, STAGES[self.stage])]

    def last_of_held(self, *others):
        self.flying.append(permute(tie(self.held, *others), STAGES[0]))

    def last(self, *others):
        self.pieces = [self.held, *self.flying, permute(tie(self.flying[0], *others), STAGES[0])]


def swap_map(values, axis):
    at = lax.axis_index("map")
    half = values.shape[axis] // 2
    low, high = (lax.slice_in_dim(values, i * half, (i + 1) * half, axis=axis) for i in (0, 1))
    mine, send = jnp.where(at == 0, low, high), jnp.where(at == 0, high, low)
    got = permute(send, BOTH(MAP))
    return jnp.concatenate([jnp.where(at == 0, mine, got), jnp.where(at == 0, got, mine)], 1 - axis)


class Halving:
    def __init__(self, parts, direct=False):
        self.low, self.stage, self.direct = parts[0], 0, direct
        self.flying = [permute(parts[1], STAGES[0])]

    def advance(self):
        self.stage += 1
        if self.stage == 2 and self.direct:
            self.low, *parts = add_parts(self.low, self.flying[0], 4)
            masks = (Z_FAR, Z_NEAR, Z_NEAR + Z_FAR)
            self.flying = [permute(part, BOTH(mask)) for part, mask in zip(parts, masks)]
        else:
            self.low, send = add_parts(self.low, self.flying[0], 2)
            self.flying = [permute(send, STAGES[self.stage])]

    def finish(self):
        return last_sum(self.low, self.flying)


HBM = pl.BlockSpec(memory_space=pl.ANY)
TABLE = pl.BlockSpec(memory_space=pltpu.SMEM)


def start_rows(table_ref, pieces, columns, held, sems):
    step = held.shape[0] // BLOCKS
    copies = []
    for entry in range(BLOCKS):
        piece, place = divmod(entry, BLOCKS // len(pieces))
        at = pl.multiple_of(table_ref[entry] * step, step)
        copies.append(
            pltpu.make_async_copy(
                pieces[piece].at[pl.ds(place * step, step), columns],
                held.at[pl.ds(at, step), :],
                sems.at[entry],
            )
        )
    for copy in copies:
        copy.start()
    return copies


def start_halves(table_ref, pieces, columns, held, sems):
    tall, width = held.shape
    step = tall // (BLOCKS // 2)
    copies = []
    for slot in range(BLOCKS // 2):
        piece, place = divmod(slot, BLOCKS // 2 // len(pieces))
        at = pl.multiple_of(table_ref[slot] * step, step)
        for part in range(2):
            if step == 32:
                source = (pl.ds(place * 64 + part * 32, 32), columns)
                target = (pl.ds(at, 32), pl.ds(part * (width // 2), width // 2))
            else:
                source = (pl.ds(place * 64, 64), pl.ds(part * width, width))
                target = (pl.ds(at + part * 64, 64), slice(None))
            copies.append(
                pltpu.make_async_copy(
                    pieces[piece].at[source], held.at[target], sems.at[slot * 2 + part]
                )
            )
    for copy in copies:
        copy.start()
    return copies


def padded_rows(rows):
    return -(-rows // 128) * 128


def wait(copies):
    for copy in copies:
        copy.wait()


def pack_small(vectors, bias, maps):
    own, count = maps.shape
    runs = bias.shape[0] // own

    def kernel(*refs):
        rows, (bias_ref, map_ref, out_ref, held) = refs[: len(vectors)], refs[len(vectors) :]
        held[...] = jnp.zeros_like(held)
        for i, ref in enumerate(rows):
            held[count + i : count + i + 1, :own] = ref[...]
        for j in range(runs):
            at = count + len(vectors) + j
            held[at : at + 1, :own] = bias_ref[:, j * own : (j + 1) * own]
        turned = held[...].T[:own]
        held[:own, :] = turned
        held[:own, :count] = map_ref[...]
        out_ref[...] = held[:own, :].astype(BF)

    return launch(
        kernel,
        in_specs=[pl.BlockSpec(memory_space=pltpu.VMEM)] * (len(vectors) + 2),
        out_shape=shape((own, 128), BF),
        scratch_shapes=[pltpu.VMEM((128, 128), F32)],
        compiler_params=params(vmem=16),
        cost_estimate=cost(0, 0),
        name="pack_small",
    )(*(vector.reshape(1, -1) for vector in vectors), bias.reshape(1, -1), maps)


def add_parts(low, got, count):
    step, cols = low.shape[0] // count, low.shape[1]
    tile = cols // 2

    def kernel(a_ref, b_ref, *outs):
        for i, out in enumerate(outs):
            part = slice(i * step, (i + 1) * step)
            out[...] = (a_ref[part, :].astype(F32) + b_ref[part, :].astype(F32)).astype(BF)

    return launch(
        kernel,
        grid=(2,),
        in_specs=[pl.BlockSpec((count * step, tile), lambda n: (0, n))] * 2,
        out_specs=[pl.BlockSpec((step, tile), lambda n: (0, n))] * count,
        out_shape=[shape((step, cols), BF)] * count,
        compiler_params=params("arbitrary", vmem=16),
        cost_estimate=cost(0, 0),
        name="add_parts",
    )(low, got)


def last_sum(low, parts):
    half, cols = low.shape[0] // 2, low.shape[1]
    tile = cols // 2

    def kernel(low_ref, *refs):
        for i, out in enumerate(refs[-2:]):
            part = slice(i * half, (i + 1) * half)
            out[...] = sum((ref[part, :].astype(F32) for ref in refs[:-2]), low_ref[part, :].astype(F32))

    return launch(
        kernel,
        grid=(2,),
        in_specs=[pl.BlockSpec((2 * half, tile), lambda n: (0, n))] * (1 + len(parts)),
        out_specs=[pl.BlockSpec((half, tile), lambda n: (0, n))] * 2,
        out_shape=[shape((half, cols), F32)] * 2,
        compiler_params=params("arbitrary", vmem=16),
        cost_estimate=cost(0, 0),
        name="last_sum",
    )(low, *parts)


def stack(top, bottom, after=(), axis=0):
    tall, wide = top.shape
    whole = pl.BlockSpec((tall, wide), lambda i: (0, 0))
    dims = (2 * tall, wide) if axis == 0 else (tall, 2 * wide)

    def kernel(a_ref, b_ref, out_ref):
        out_ref[:tall, :wide] = a_ref[...]
        out_ref[dims[0] - tall :, dims[1] - wide :] = b_ref[...]

    return launch(
        kernel,
        after=after,
        grid=(1,),
        in_specs=[whole, whole],
        out_specs=pl.BlockSpec(dims, lambda i: (0, 0)),
        out_shape=shape(dims, BF),
        compiler_params=params("arbitrary", vmem=16),
        cost_estimate=cost(0, 0),
        name="stack",
    )(top, bottom)


def pack_small(vectors, bias, maps):
    own, count = maps.shape
    runs = bias.shape[0] // own

    def kernel(*refs):
        rows, (bias_ref, map_ref, out_ref, held) = refs[: len(vectors)], refs[len(vectors) :]
        held[...] = jnp.zeros_like(held)
        for i, ref in enumerate(rows):
            held[count + i : count + i + 1, :own] = ref[...]
        for j in range(runs):
            at = count + len(vectors) + j
            held[at : at + 1, :own] = bias_ref[:, j * own : (j + 1) * own]
        turned = held[...].T[:own]
        held[:own, :] = turned
        held[:own, :count] = map_ref[...]
        out_ref[...] = held[:own, :].astype(BF)

    return launch(
        kernel,
        in_specs=[pl.BlockSpec(memory_space=pltpu.VMEM)] * (len(vectors) + 2),
        out_shape=shape((own, 128), BF),
        scratch_shapes=[pltpu.VMEM((128, 128), F32)],
        compiler_params=params(vmem=16),
        cost_estimate=cost(0, 0),
        name="pack_small",
    )(*(vector.reshape(1, -1) for vector in vectors), bias.reshape(1, -1), maps)


def add_halves(low, got):
    half, cols = low.shape[0] // 2, low.shape[1]
    tile = cols // 2

    def kernel(a_ref, b_ref, low_ref, high_ref):
        total = a_ref[...].astype(F32) + b_ref[...].astype(F32)
        low_ref[...] = total[:half].astype(BF)
        high_ref[...] = total[half:].astype(BF)

    return launch(
        kernel,
        grid=(2,),
        in_specs=[pl.BlockSpec((2 * half, tile), lambda n: (0, n))] * 2,
        out_specs=[pl.BlockSpec((half, tile), lambda n: (0, n))] * 2,
        out_shape=[shape((half, cols), BF)] * 2,
        compiler_params=params("arbitrary", vmem=16),
        cost_estimate=cost(0, 0),
        name="add_halves",
    )(low, got)


def small_rows(table, pieces, at):
    tall = pieces[0].shape[0]
    total = tall * len(pieces)

    def kernel(table_ref, *refs):
        sources, (out_ref, held) = refs[: len(pieces)], refs[len(pieces) :]
        for entry in range(BLOCKS):
            piece, place = divmod(entry, BLOCKS // len(pieces))
            start = pl.multiple_of(table_ref[entry] * 32, 32)
            held[pl.ds(start, 32), :] = sources[piece][place * 32 : place * 32 + 32, :].astype(F32)
        out_ref[...] = held[...].T

    return launch(
        kernel,
        grid=(1,),
        in_specs=[TABLE] + [pl.BlockSpec((tall, 128), lambda i: (0, at // 128))] * len(pieces),
        out_specs=pl.BlockSpec((128, total), lambda i: (0, 0)),
        out_shape=shape((128, total), F32),
        scratch_shapes=[pltpu.VMEM((total, 128), F32)],
        compiler_params=params("arbitrary", vmem=16),
        cost_estimate=cost(0, 0),
        name="small_rows",
    )(table, *pieces)


def project(table, pieces, patches, other, gain, shift, added, factor):
    image, width = patches.shape
    rows, count, padded = 2 * image, len(pieces), padded_rows(image)
    cols = added.shape[1]
    tile = cols // 3

    def kernel(table_ref, *rest):
        gathered, rest = rest[:count], rest[count:]
        x_ref, y_ref, g_ref, s_ref, a_ref, f_ref, qkv_ref, turned_ref, stat_ref, *rest = rest
        hidden, held, sems = rest
        step = pl.program_id(0)

        @pl.when(step == 0)
        def _():
            copies = start_rows(table_ref, gathered, pl.ds(0, cols), held, sems)
            for at, ref in enumerate((x_ref, y_ref)):
                values = ref[...].astype(F32)
                mean = jnp.mean(values, axis=-1, keepdims=True)
                center = values - mean
                spread = lax.rsqrt(jnp.mean(center * center, axis=-1, keepdims=True) + EPSILON)
                normed = (center * spread * g_ref[...] + s_ref[...]).astype(BF)
                hidden[at * image : (at + 1) * image, :] = normed
                if at == 0:
                    stat_ref[...] = jnp.concatenate([mean, spread], axis=1)
            turned_ref[...] = jnp.zeros_like(turned_ref)
            for at in range(2):
                turned_ref[:, at * padded : at * padded + image] = hidden[
                    at * image : (at + 1) * image, :
                ].T
            wait(copies)

        at = pl.ds(pl.multiple_of(step * tile, tile), tile)
        product = dot(hidden[...], held[:, at], NN)
        qkv_ref[...] = ((product + a_ref[...]) * f_ref[...]).astype(BF)

    whole = lambda m, n: pl.BlockSpec((m, n), lambda j: (0, 0))
    strip = lambda m: pl.BlockSpec((m, tile), lambda j: (0, j))
    return launch(
        kernel,
        grid=(3,),
        in_specs=[TABLE] + [HBM] * count + [whole(image, width)] * 2
        + [whole(1, width), whole(1, width), strip(1), strip(1)],
        out_specs=[strip(rows), whole(width, 2 * padded), whole(image, 2)],
        out_shape=[
            shape((rows, cols), BF),
            shape((width, 2 * padded), BF),
            shape((image, 2), F32),
        ],
        scratch_shapes=[
            pltpu.VMEM((rows, width), BF),
            pltpu.VMEM((width, cols), BF),
            pltpu.SemaphoreType.DMA((BLOCKS,)),
        ],
        compiler_params=params("arbitrary"),
        cost_estimate=cost(2 * rows * width * cols, 0),
        name="project",
    )(table, *pieces, patches, other, gain, shift, added, factor)


def attend(qkv, live, after=()):
    tall, width = qkv.shape[0], qkv.shape[1] // 3
    rows = tall // 2
    padded = padded_rows(rows)
    pair = 2 * HD
    pairs = width // pair

    def kernel(q_ref, k_ref, v_ref, live_ref, mixed_ref, turned_ref, total_ref):
        turned_ref[...] = jnp.zeros_like(turned_ref)
        for image in range(2):
            part = slice(image * rows, (image + 1) * rows)
            alive = live_ref[part, :] > 0
            q, k = q_ref[part, :], k_ref[part, :]
            value_t = v_ref[part, :].T
            heads = []
            for h in range(2):
                cut = slice(h * HD, (h + 1) * HD)
                scores = jnp.where(alive, dot(k[:, cut], q[:, cut], NT), MASKED_SCORE)
                peak = jnp.max(scores, axis=0, keepdims=True)
                expons = jnp.exp(scores - peak)
                total = jnp.sum(expons, axis=0, keepdims=True)
                attention = (expons * (1.0 / total)).astype(BF)
                heads.append(dot(value_t[cut], attention, NN))
                total_ref[0, 2 * image + h : 2 * image + h + 1, :] = peak + jnp.log(total)
            both = jnp.concatenate(heads, axis=0)
            mixed_ref[part, :] = both.T.astype(BF)
            turned_ref[:, image * padded : image * padded + rows] = both.astype(BF)

    column = lambda at: pl.BlockSpec((tall, pair), lambda i: (0, at * pairs + i))
    return launch(
        kernel,
        after=after,
        grid=(pairs,),
        in_specs=[column(0), column(1), column(2), pl.BlockSpec((tall, 1), lambda i: (0, 0))],
        out_specs=[
            column(0),
            pl.BlockSpec((pair, 2 * padded), lambda i: (i, 0)),
            pl.BlockSpec((1, 4, rows), lambda i: (i, 0, 0)),
        ],
        out_shape=[
            shape((tall, width), BF),
            shape((width, 2 * padded), BF),
            shape((pairs, 4, rows), F32),
        ],
        compiler_params=params("arbitrary"),
        cost_estimate=cost(16 * rows * tall * width, 0),
        name="attend",
    )(qkv, qkv, qkv, live)


def attend_back(table, pieces, qkv, live, totals, grad_attn, image):
    width = qkv.shape[1] // 3
    rows, full = grad_attn.shape
    pair = 2 * HD
    pairs = width // pair
    scaling = HD ** (-0.5)
    out_at = pieces[0].shape[1] - full // 2
    count = len(pieces)

    def kernel(table_ref, *rest):
        gathered, rest = rest[:count], rest[count:]
        q_ref, k_ref, v_ref, live_ref, total_ref, g_ref, out_ref, sum_ref, held, sems = rest
        step = pl.program_id(0)

        @pl.when(step == 0)
        def _():
            wait(start_halves(table_ref, gathered, pl.ds(out_at, full // 2), held, sems))

        weight = held[pl.ds(pl.multiple_of(step * pair, pair), pair), :]
        gm = dot(g_ref[...], weight, NT).astype(BF)
        alive = live_ref[...] > 0
        q, k, v = q_ref[...], k_ref[...], v_ref[...]
        key_t = k.T
        queries, keys, values = [], [], []
        for h in range(2):
            cut = slice(h * HD, (h + 1) * HD)
            at = 2 * image + h
            scores = jnp.where(alive, dot(k[:, cut], q[:, cut], NT), MASKED_SCORE)
            probs = jnp.exp(scores - total_ref[0, at : at + 1, :])
            grad_probs = dot(v[:, cut], gm[:, cut], NT)
            along = jnp.sum(probs * grad_probs, axis=0, keepdims=True)
            grad_scores = (probs * (grad_probs - along)).astype(BF)
            values.append(dot(probs.astype(BF), gm[:, cut], NN))
            keys.append(dot(grad_scores, q[:, cut], NN))
            queries.append(dot(key_t[cut], grad_scores, NN))
        grad_q = jnp.concatenate(queries, axis=0).T.astype(BF).astype(F32) * scaling
        grad_v = jnp.concatenate(values, axis=1).astype(BF)
        out_ref[0] = grad_q.astype(BF)
        out_ref[1] = jnp.concatenate(keys, axis=1).astype(BF)
        out_ref[2] = grad_v
        sum_ref[0:1, :] = jnp.sum(grad_q, axis=0, keepdims=True)
        sum_ref[1:2, :] = jnp.sum(grad_v.astype(F32), axis=0, keepdims=True)

    column = lambda at: pl.BlockSpec((rows, pair), lambda i: (image, at * pairs + i))
    return launch(
        kernel,
        grid=(pairs,),
        in_specs=[TABLE] + [HBM] * count + [column(0), column(1), column(2)]
        + [
            pl.BlockSpec((rows, 1), lambda i: (image, 0)),
            pl.BlockSpec((1, 4, rows), lambda i: (i, 0, 0)),
            pl.BlockSpec((rows, full), lambda i: (0, 0)),
        ],
        out_specs=[
            pl.BlockSpec((3, rows, pair), lambda i: (0, 0, i)),
            pl.BlockSpec((2, pair), lambda i: (0, i)),
        ],
        out_shape=[shape((3, rows, width), BF), shape((2, width), F32)],
        scratch_shapes=[pltpu.VMEM((width, full), BF), pltpu.SemaphoreType.DMA((BLOCKS,))],
        compiler_params=params("arbitrary"),
        cost_estimate=cost(40 * rows * rows * width, 0),
        name="attend_back",
    )(table, *pieces, qkv, qkv, qkv, live, totals, grad_attn)


def mix_out(table, pieces, mixed, image):
    tall, width = mixed.shape
    rows, full = tall // 2, 2 * width
    out_at = pieces[0].shape[1] - full // 2

    def kernel(table_ref, *rest):
        gathered, (m_ref, out_ref, held, sems) = rest[: len(pieces)], rest[len(pieces) :]
        wait(start_halves(table_ref, gathered, pl.ds(out_at, full // 2), held, sems))
        out_ref[...] = dot(m_ref[...], held[...], NN)

    return launch(
        kernel,
        grid=(1,),
        in_specs=[TABLE]
        + [HBM] * len(pieces)
        + [pl.BlockSpec((rows, width), lambda i: (image, 0))],
        out_specs=pl.BlockSpec((rows, full), lambda i: (0, 0)),
        out_shape=shape((rows, full), F32),
        scratch_shapes=[pltpu.VMEM((width, full), BF), pltpu.SemaphoreType.DMA((BLOCKS,))],
        compiler_params=params("arbitrary"),
        cost_estimate=cost(2 * rows * width * full, 0),
        name="mix_out",
    )(table, *pieces, mixed)


def second_norm(own, got, patches, bias, gain, shift):
    rows, width = patches.shape

    def kernel(a_ref, b_ref, x_ref, bias_ref, g_ref, s_ref, res_ref, hid_ref):
        residual = x_ref[...].astype(F32) + (a_ref[...] + b_ref[...]) + bias_ref[...]
        normed, _ = normalize(residual)
        res_ref[...] = residual
        hid_ref[...] = (normed * g_ref[...] + s_ref[...]).astype(BF)

    banded = pl.BlockSpec((rows // 2, width), lambda i: (i, 0))
    fixed = pl.BlockSpec((1, width), lambda i: (0, 0))
    return launch(
        kernel,
        grid=(2,),
        in_specs=[banded] * 3 + [fixed] * 3,
        out_specs=[banded] * 2,
        out_shape=[shape((rows, width), F32), shape((rows, width), BF)],
        compiler_params=params("arbitrary"),
        cost_estimate=cost(0, 0),
        name="second_norm",
    )(own, got, patches, bias, gain, shift)


def feed_up(table, pieces, hidden, bias, after=()):
    rows, width = hidden.shape
    units, padded = bias.shape[1], padded_rows(rows)
    span = units // 4
    count = len(pieces)

    def kernel(table_ref, *rest):
        gathered, rest = rest[:count], rest[count:]
        h_ref, b_ref, act_ref, turned_ref, slope_ref, ht_ref, held, sems = rest
        step = pl.program_id(0)

        @pl.when(step == 0)
        def _():
            copies = start_rows(table_ref, gathered, pl.ds(0, units), held, sems)
            ht_ref[...] = jnp.zeros_like(ht_ref)
            ht_ref[:, :rows] = h_ref[...].T
            wait(copies)

        weight = held[:, pl.ds(pl.multiple_of(step * span, span), span)]
        x = dot(h_ref[...], weight, NN) + b_ref[...]
        half = 0.5 + 0.5 * lax.erf(x * (0.5**0.5))
        act = (x * half).astype(BF)
        act_ref[...] = act
        turned_ref[...] = jnp.zeros_like(turned_ref)
        turned_ref[:, :rows] = act.T
        slope_ref[...] = (half + x * jnp.exp(-0.5 * x * x) * 0.3989422804014327).astype(BF)

    whole = lambda m, n: pl.BlockSpec((m, n), lambda j: (0, 0))
    strip = lambda m: pl.BlockSpec((m, span), lambda j: (0, j))
    return launch(
        kernel,
        after=after,
        grid=(4,),
        in_specs=[TABLE] + [HBM] * count + [whole(rows, width), strip(1)],
        out_specs=[
            strip(rows),
            pl.BlockSpec((span, padded), lambda j: (j, 0)),
            strip(rows),
            whole(width, padded),
        ],
        out_shape=[
            shape((rows, units), BF),
            shape((units, padded), BF),
            shape((rows, units), BF),
            shape((width, padded), BF),
        ],
        scratch_shapes=[pltpu.VMEM((width, units), BF), pltpu.SemaphoreType.DMA((BLOCKS,))],
        compiler_params=params("arbitrary"),
        cost_estimate=cost(2 * rows * width * units, 0),
        name="feed_up",
    )(table, *pieces, hidden, bias)


def feed_down(table, pieces, act, width):
    rows, units = act.shape

    def kernel(table_ref, *rest):
        gathered, (a_ref, out_ref, held, sems) = rest[: len(pieces)], rest[len(pieces) :]
        wait(start_halves(table_ref, gathered, None, held, sems))
        out_ref[...] = dot(a_ref[...], held[...], NN)

    return launch(
        kernel,
        grid=(1,),
        in_specs=[TABLE] + [HBM] * len(pieces) + [pl.BlockSpec((rows, units), lambda i: (0, 0))],
        out_specs=pl.BlockSpec((rows, width), lambda i: (0, 0)),
        out_shape=shape((rows, width), F32),
        scratch_shapes=[pltpu.VMEM((units, width), BF), pltpu.SemaphoreType.DMA((BLOCKS,))],
        compiler_params=params("arbitrary"),
        cost_estimate=cost(2 * rows * width * units, 0),
        name="feed_down",
    )(table, *pieces, act)


def feed_back(tables, up, down, grad, other, slope, other_slope):
    rows, width = grad.shape
    tall, units = 2 * rows, slope.shape[1]
    span, count = units // 4, len(up)

    def kernel(t32, t16, *rest):
        up_refs, down_refs, rest = rest[:count], rest[count : 2 * count], rest[2 * count :]
        g_ref, o_ref, slope_ref, slope_other, pre_ref, sum_ref, own_ref, other_ref, *rest = rest
        both, high, low, sems = rest
        step = pl.program_id(0)

        def copies():
            return (
                start_halves(t16, down_refs, None, low, sems.at[0]),
                start_rows(t32, up_refs, pl.ds(0, units), high, sems.at[1]),
            )

        @pl.when(step == 0)
        def _():
            one, two = copies()
            both[:rows, :] = g_ref[...]
            both[rows:, :] = o_ref[...]
            wait(one)
            wait(two)

        at = pl.ds(pl.multiple_of(step * span, span), span)
        grad_act = dot(both[...], low[at, :], NT)
        pre_ref[:rows, :] = (grad_act[:rows] * slope_ref[...].astype(F32)).astype(BF)
        pre_ref[rows:, :] = (grad_act[rows:] * slope_other[...].astype(F32)).astype(BF)
        grad_pre = pre_ref[...]
        sum_ref[...] = jnp.sum(grad_pre.astype(F32), axis=0, keepdims=True)
        part = dot(grad_pre, high[:, at], NT)

        @pl.when(step == 0)
        def _():
            own_ref[...] = part[:rows]
            other_ref[...] = part[rows:]

        @pl.when(step > 0)
        def _():
            own_ref[...] += part[:rows]
            other_ref[...] += part[rows:]

    whole = lambda m, n: pl.BlockSpec((m, n), lambda j: (0, 0))
    strip = lambda m: pl.BlockSpec((m, span), lambda j: (0, j))
    return launch(
        kernel,
        grid=(4,),
        in_specs=[TABLE, TABLE]
        + [HBM] * (2 * count)
        + [whole(rows, width)] * 2
        + [strip(rows)] * 2,
        out_specs=[strip(tall), strip(1), whole(rows, width), whole(rows, width)],
        out_shape=[shape((tall, units), BF), shape((1, units), F32)]
        + [shape((rows, width), F32)] * 2,
        scratch_shapes=[
            pltpu.VMEM((tall, width), BF),
            pltpu.VMEM((width, units), BF),
            pltpu.VMEM((units, width), BF),
            pltpu.SemaphoreType.DMA((2, BLOCKS)),
        ],
        compiler_params=params("arbitrary"),
        cost_estimate=cost(4 * tall * width * units, 0),
        name="feed_back",
    )(*tables, *up, *down, grad, other, slope, other_slope)


def split(values):
    high = values.astype(BF)
    return high, (values - high.astype(F32)).astype(BF)


def token_learner(residual, own, got, bias, cotangent, live, token_grad, map_t, scale, offset):
    rows, width = residual.shape
    count = map_t.shape[0]
    bands = 4
    band = rows // bands

    def kernel(r_ref, own_ref, got_ref, bias_ref, c_ref, live_ref, tg_ref, map_ref, s_ref, o_ref, *outs):
        out_ref, tok_ref, grad_ref, low_ref, gmap_ref, sums_ref, parts, total = outs
        step = pl.program_id(0)

        @pl.when(step == 0)
        def _():
            parts[...] = jnp.zeros_like(parts)
            total[...] = jnp.zeros_like(total)
            sums_ref[...] = jnp.zeros_like(sums_ref)

        values = r_ref[...] + (own_ref[...] + got_ref[...]) + bias_ref[...]
        alive = live_ref[...]
        grads, maps = tg_ref[...], map_ref[...]
        mapped = maps * s_ref[...]
        mean = jnp.mean(values, axis=-1, keepdims=True)
        center = values - mean
        spread = lax.rsqrt(jnp.mean(center * center, axis=-1, keepdims=True) + EPSILON)
        high, low = split(center)
        both = jnp.concatenate([mapped, grads], axis=0)
        both_high, both_low = split(both)
        wide = dot(high, jnp.concatenate([both_high, both_low], axis=0), NT)
        found = wide[:, : 2 * count] + wide[:, 2 * count :] + dot(low, both_high, NT)
        shifted = jnp.sum(maps * o_ref[...], axis=-1).reshape(1, count)
        hat = found[:, :count] * spread
        sigma = jax.nn.sigmoid(hat + shifted)
        weights = sigma * alive
        pull = found[:, count:] + mean * jnp.sum(grads, axis=-1).reshape(1, count)
        logits = pull * alive * sigma * (1.0 - sigma)
        mapped_mean = jnp.mean(mapped, axis=-1).reshape(1, count)
        flat = jnp.sum(logits * mapped_mean, axis=-1, keepdims=True)
        slant = jnp.sum(logits * hat, axis=-1, keepdims=True) * (1.0 / width)
        pair = jnp.concatenate([logits * spread, weights], axis=1)
        pair_high, pair_low = split(pair)
        back = dot(
            jnp.concatenate([pair_high, pair_high, pair_low], axis=1),
            jnp.concatenate([both_high, both_low, both_high], axis=0),
            NN,
        )
        grad = c_ref[...].astype(F32) + back
        grad = grad - (spread * flat) - (spread * spread * slant) * center
        low_grad = grad.astype(BF)
        out_ref[...] = values.astype(BF)
        grad_ref[...] = grad
        low_ref[...] = low_grad
        tall = dot(jnp.concatenate([pair_high, pair_low], axis=1), high, TN)
        parts[...] += tall[: 2 * count] + tall[2 * count :] + dot(pair_high, low, TN)
        side = jnp.concatenate([logits, weights * mean], axis=1)
        total[...] += jnp.sum(side, axis=0, keepdims=True)
        sums_ref[2:3, :] += jnp.sum(low_grad.astype(F32), axis=0, keepdims=True)

        @pl.when(step == bands - 1)
        def _():
            ends = total[...].reshape(2 * count, 1)
            tok_ref[...] = parts[count:, :] + ends[count:]
            hats = parts[:count, :]
            gmap_ref[...] = hats * s_ref[...] + ends[:count] * o_ref[...]
            sums_ref[0:1, :] = jnp.sum(hats * maps, axis=0, keepdims=True)
            sums_ref[1:2, :] = jnp.sum(ends[:count] * maps, axis=0, keepdims=True)

    banded = pl.BlockSpec((band, width), lambda i: (i, 0))
    fixed = lambda n: pl.BlockSpec((n, width), lambda i: (0, 0))
    return launch(
        kernel,
        grid=(bands,),
        in_specs=[banded] * 3 + [fixed(1), banded, pl.BlockSpec((band, 1), lambda i: (i, 0))]
        + [fixed(count), fixed(count), fixed(1), fixed(1)],
        out_specs=[banded, fixed(count), banded, banded, fixed(count), fixed(3)],
        out_shape=[
            shape((rows, width), BF),
            shape((count, width), F32),
            shape((rows, width), F32),
            shape((rows, width), BF),
            shape((count, width), F32),
            shape((3, width), F32),
        ],
        scratch_shapes=[pltpu.VMEM((2 * count, width), F32), pltpu.VMEM((1, 2 * count), F32)],
        compiler_params=params("arbitrary"),
        cost_estimate=cost(10 * 10**9, 14 * rows * width),
        name="token_learner",
    )(residual, own, got, bias, cotangent, live, token_grad, map_t, scale, offset)


def second_norm_back(own, got, residual, grad_block, gain):
    rows, width = residual.shape
    bands = 4

    def kernel(a_ref, b_ref, r_ref, gb_ref, g_ref, res_ref, low_ref, sums_ref):
        grad = a_ref[...] + b_ref[...]
        normed, spread = normalize(r_ref[...])
        result = gb_ref[...] + norm_back(grad * g_ref[...], normed, spread)
        low = result.astype(BF)
        res_ref[...] = result
        low_ref[...] = low
        sums = jnp.concatenate(
            [
                jnp.sum(grad * normed, axis=0, keepdims=True),
                jnp.sum(grad, axis=0, keepdims=True),
                jnp.sum(low.astype(F32), axis=0, keepdims=True),
            ],
            axis=0,
        )

        @pl.when(pl.program_id(0) == 0)
        def _():
            sums_ref[...] = sums

        @pl.when(pl.program_id(0) > 0)
        def _():
            sums_ref[...] += sums

    banded = pl.BlockSpec((rows // bands, width), lambda i: (i, 0))
    fixed = lambda n: pl.BlockSpec((n, width), lambda i: (0, 0))
    return launch(
        kernel,
        grid=(bands,),
        in_specs=[banded] * 4 + [fixed(1)],
        out_specs=[banded, banded, fixed(3)],
        out_shape=[shape((rows, width), F32), shape((rows, width), BF), shape((3, width), F32)],
        compiler_params=params("arbitrary"),
        cost_estimate=cost(0, 0),
        name="second_norm_back",
    )(own, got, residual, grad_block, gain)


def project_back(table, pieces, grad_qkv, other_qkv):
    parts, rows, width = grad_qkv.shape
    tall, full = 2 * rows, 2 * width

    def kernel(table_ref, *rest):
        gathered, rest = rest[: len(pieces)], rest[len(pieces) :]
        g_ref, o_ref, own_ref, other_ref, held, sems = rest
        step = pl.program_id(0)

        @pl.when(step == 0)
        def _():
            wait(start_rows(table_ref, gathered, pl.ds(0, parts * width), held, sems))

        weight = held[:, pl.ds(pl.multiple_of(step * width, width), width)]
        product = dot(g_ref[...], weight, NT)
        product_other = dot(o_ref[...], weight, NT)

        @pl.when(step == 0)
        def _():
            own_ref[...] = product
            other_ref[...] = product_other

        @pl.when(step > 0)
        def _():
            own_ref[...] += product
            other_ref[...] += product_other

    return launch(
        kernel,
        grid=(parts,),
        in_specs=[TABLE]
        + [HBM] * len(pieces)
        + [pl.BlockSpec((None, rows, width), lambda j: (j, 0, 0))] * 2,
        out_specs=[pl.BlockSpec((rows, full), lambda j: (0, 0))] * 2,
        out_shape=[shape((rows, full), F32)] * 2,
        scratch_shapes=[
            pltpu.VMEM((full, parts * width), BF),
            pltpu.SemaphoreType.DMA((BLOCKS,)),
        ],
        compiler_params=params("arbitrary"),
        cost_estimate=cost(6 * tall * width * full, 0),
        name="project_back",
    )(table, *pieces, grad_qkv, other_qkv)


def first_norm_back(own, got, patches, stats, gain, grad_residual):
    rows, width = patches.shape
    bands = 4

    def kernel(a_ref, b_ref, x_ref, st_ref, gain_ref, res_ref, out_ref, sums_ref):
        grad = a_ref[...] + b_ref[...]
        spread = st_ref[:, 1:2]
        normed = (x_ref[...].astype(F32) - st_ref[:, 0:1]) * spread
        result = res_ref[...] + norm_back(grad * gain_ref[...], normed, spread)
        out_ref[...] = result.astype(BF)
        sums = jnp.concatenate(
            [
                jnp.sum(grad * normed, axis=0, keepdims=True),
                jnp.sum(grad, axis=0, keepdims=True),
            ],
            axis=0,
        )

        @pl.when(pl.program_id(0) == 0)
        def _():
            sums_ref[...] = sums

        @pl.when(pl.program_id(0) > 0)
        def _():
            sums_ref[...] += sums

    banded = lambda n: pl.BlockSpec((rows // bands, n), lambda i: (i, 0))
    fixed = lambda n: pl.BlockSpec((n, width), lambda i: (0, 0))
    return launch(
        kernel,
        grid=(bands,),
        in_specs=[banded(width)] * 3 + [banded(2), fixed(1), banded(width)],
        out_specs=[banded(width), fixed(2)],
        out_shape=[shape((rows, width), BF), shape((2, width), F32)],
        compiler_params=params("arbitrary"),
        cost_estimate=cost(0, 0),
        name="first_norm_back",
    )(own, got, patches, stats, gain, grad_residual)


def start_blocks(table_ref, lefts, held, sems):
    count = sems.shape[1]
    step, wide = held.shape[0] // count, held.shape[1] // len(lefts)
    low, high = [], []
    for block in range(count):
        at = pl.multiple_of(table_ref[block] * step, step)
        for i, left in enumerate(lefts):
            target = held.at[pl.ds(block * step, step), pl.ds(i * wide, wide)]
            copy = pltpu.make_async_copy(left.at[pl.ds(at, step)], target, sems.at[i, block])
            (low if block < count // 2 else high).append(copy)
    for copy in high + low:
        copy.start()
    return low, high


def place_rows(target, sources):
    padded = target.shape[0] // 2
    for i, (ref, first, rows) in enumerate(sources):
        target[i * padded : i * padded + rows, :] = ref[first : first + rows, :]
        target[i * padded + rows : (i + 1) * padded, :] = jnp.zeros(
            (padded - rows, target.shape[1]), target.dtype
        )


def weight_grad(table, turned, rights, part=None, parts=1, tile=512):
    height = turned[0].shape[0]
    deep = sum(left.shape[1] for left in turned)
    blocks, half = table.shape[0], height // 2
    rows = rights[0].shape[-2] * len(rights) // 2

    def kernel(table_ref, *refs):
        lefts, refs = refs[: len(turned)], refs[len(turned) :]
        values, (low_ref, high_ref, held, value, sems) = refs[: len(rights)], refs[len(rights) :]

        def product(where, ref):
            ref[...] = dot(held[where, :], value[...], NN).astype(BF)

        @pl.when(pl.program_id(0) == 0)
        def _():
            low, high = start_blocks(table_ref, lefts, held, sems)
            place_rows(value, spots(values))
            wait(high)
            product(slice(half, height), high_ref)
            wait(low)
            product(slice(0, half), low_ref)

        @pl.when(pl.program_id(0) > 0)
        def _():
            place_rows(value, spots(values))
            product(slice(half, height), high_ref)
            product(slice(0, half), low_ref)

    def spots(values):
        if len(rights) == 1:
            return [(values[0], 0, rows), (values[0], rows, rows)]
        return [(ref, 0, rows) for ref in values]

    each = rights[0].shape[-1] // tile
    tall = rights[0].shape[-2]
    if part is None:
        spec = pl.BlockSpec((tall, tile), lambda n: (0, n))
    else:
        spec = pl.BlockSpec((None, tall, tile), lambda n: (part + n // each, 0, n % each))
    cols = parts * rights[0].shape[-1]
    return launch(
        kernel,
        grid=(cols // tile,),
        in_specs=[TABLE] + [HBM] * len(turned) + [spec] * len(rights),
        out_specs=[pl.BlockSpec((half, tile), lambda n: (0, n))] * 2,
        out_shape=[shape((half, cols), BF)] * 2,
        scratch_shapes=[
            pltpu.VMEM((height, deep), BF),
            pltpu.VMEM((deep, tile), BF),
            pltpu.SemaphoreType.DMA((len(turned), blocks)),
        ],
        compiler_params=params("arbitrary"),
        cost_estimate=cost(2 * deep * height * cols, 0),
        name="weight_grad",
    )(table, *turned, *rights)


def value_and_out_grad(tables, turned, grad_qkv, mixed_turned, grad_attn):
    height, deep = turned.shape
    width = mixed_turned.shape[0]
    half, rows = height // 2, grad_attn[0].shape[0]
    step = height // BLOCKS

    def kernel(t32, t16, left, mixed, va, vb, a_ref, b_ref, *rest):
        low_ref, high_ref, held, held_mixed, value, both, sems, mixed_sems = rest
        low, high = start_blocks(t32, [left], held, sems)
        more = start_blocks(t16, [mixed], held_mixed, mixed_sems)
        place_rows(value, [(va, 0, rows), (vb, 0, rows)])
        place_rows(both, [(a_ref, 0, rows), (b_ref, 0, rows)])
        wait(high)
        high_ref[:, :width] = dot(held[half:, :], value[...], NN).astype(BF)
        wait(low)
        low_ref[:, :width] = dot(held[:half, :], value[...], NN).astype(BF)
        wait(more[0] + more[1])
        for part in range(2):
            cut = slice(part * width, (part + 1) * width)
            product = dot(held_mixed[...], both[:, cut], NN).astype(BF)
            for slot in range(BLOCKS // 2):
                ref = low_ref if slot < BLOCKS // 4 else high_ref
                at = (slot % (BLOCKS // 4) * 2 + part) * step
                ref[at : at + step, width:] = product[slot * step : (slot + 1) * step]

    whole = lambda m, n: pl.BlockSpec((m, n), lambda i: (0, 0))
    return launch(
        kernel,
        grid=(1,),
        in_specs=[TABLE, TABLE, HBM, HBM]
        + [pl.BlockSpec((None, rows, width), lambda i: (2, 0, 0))] * 2
        + [whole(rows, 2 * width)] * 2,
        out_specs=[whole(half, 2 * width)] * 2,
        out_shape=[shape((half, 2 * width), BF)] * 2,
        scratch_shapes=[
            pltpu.VMEM((height, deep), BF),
            pltpu.VMEM((width, deep), BF),
            pltpu.VMEM((deep, width), BF),
            pltpu.VMEM((deep, 2 * width), BF),
            pltpu.SemaphoreType.DMA((1, BLOCKS)),
            pltpu.SemaphoreType.DMA((1, BLOCKS // 2)),
        ],
        compiler_params=params("arbitrary"),
        cost_estimate=cost(4 * deep * height * width, 0),
        name="value_and_out_grad",
    )(*tables, turned, mixed_turned, *grad_qkv, *grad_attn)


def halves(values, core, groups, unit):
    rows = values.shape[0]
    runs = values.reshape(rows, groups, 2, unit)
    even, odd = runs[:, :, 0].reshape(rows, -1), runs[:, :, 1].reshape(rows, -1)
    return jnp.where(core == 0, even, odd), jnp.where(core == 0, odd, even)


def joined(own, other, core, groups, unit):
    rows = own.shape[0]
    even, odd = jnp.where(core == 0, own, other), jnp.where(core == 0, other, own)
    runs = jnp.stack([even.reshape(rows, groups, unit), odd.reshape(rows, groups, unit)], axis=2)
    return runs.reshape(rows, -1)


def per_device(
    patches,
    keep_mask,
    block_cotangent,
    token_cotangent,
    first_gain,
    first_shift,
    qkv_weight,
    query_bias,
    value_bias,
    out_weight,
    out_bias,
    second_gain,
    second_shift,
    up_weight,
    up_bias,
    down_weight,
    down_bias,
    learn_gain,
    learn_shift,
    map_weight,
):
    devices = lax.axis_size("dp") * lax.axis_size("map")
    layered = devices == BLOCKS and lax.axis_size("map") == 2
    core = lax.axis_index("dp") & 1
    images, patch_count, width = patches.shape
    rows = images * patch_count
    own = first_gain.shape[0]
    scaling = HD ** (-0.5)
    table, own_table = slot_tables(layered)
    CHAIN.clear()
    heads = width // HD
    unit = up_weight.shape[1] // (BLOCKS // 2)
    side = width // 2

    vectors = (
        first_gain,
        first_shift,
        query_bias,
        value_bias,
        out_bias,
        second_gain,
        second_shift,
        down_bias,
        learn_gain,
        learn_shift,
    )
    fan = up_bias.shape[0] // own
    count = map_weight.shape[1]
    small = pack_small(vectors, up_bias, map_weight)
    inputs = patches.reshape(rows, width)
    live = keep_mask.reshape(1, rows).astype(F32)
    other_live = to_sibling(live)
    lives = jnp.concatenate([live, other_live], axis=1).reshape(2 * rows, 1)
    live = lives[:rows]

    qkv_own, qkv_other = halves(qkv_weight.astype(BF), core, 3 * heads // 2, HD)
    up_own, up_other = halves(up_weight.astype(BF), core, BLOCKS // 4, 2 * unit // 2)
    out_low, down_low = out_weight.astype(BF), down_weight.astype(BF)
    if layered:
        near_wire = jnp.concatenate([qkv_own, small], axis=1)
        near_got = to_sibling(jnp.concatenate([qkv_other, small], axis=1))
        out_wire = jnp.concatenate([out_low[:, :side], out_low[:, side:]], axis=0)
        near_wire = jnp.concatenate(
            [jnp.concatenate([near_wire, near_got], axis=0), out_wire], axis=1
        )
        near = Doubling(near_wire)
        near.advance()
        near.advance()
        near.last_of_held()
        up = Doubling(stack(up_own, to_sibling(up_other)))
        other_inputs = to_sibling(tie(inputs, up.held))
        near.last(near.flying[1])
        up.advance(near.flying)
        near_full = near.pieces
        up.advance((near_full[3],))
        up.last_of_held()
        down = Doubling(stack(down_low[: 2 * own], down_low[2 * own :], axis=1))
        token_grad = swap_map(tie(token_cotangent, near_full[3]), axis=0)
    else:
        whole = lambda wire: lax.all_gather(wire, AXES, axis=0, tiled=True)
        pick = lambda values: halves(values, core, 1, values.shape[1] // 2)[0]
        qkv_full = halves(whole(qkv_weight.astype(BF)), core, 3 * heads // 2, HD)[0]
        out_full = halves(whole(out_low).reshape(1, -1), core, heads // 2, HD * width)[0]
        out_full = out_full.reshape(BLOCKS // 2, 32, 2, side).transpose(0, 2, 1, 3)
        near_full = jnp.concatenate(
            [qkv_full, whole(small), out_full.reshape(width, side)], axis=1
        )
        up_full = halves(whole(up_weight.astype(BF)), core, BLOCKS // 4, unit)[0]
        down_full = whole(down_low).reshape(1, -1)
        down_full = halves(down_full, core, BLOCKS // 4, unit * width)[0]
        down_full = down_full.reshape(BLOCKS // 2, 2, 64, width).transpose(0, 2, 1, 3)
        down_full = down_full.reshape(width, 2 * width)
        cut = lambda values: (values[: width // 2], values[width // 2 :])
        near_full, up_full, down_full = cut(near_full), cut(up_full), cut(down_full)
        other_inputs = to_sibling(inputs)
        token_grad = lax.all_to_all(
            token_cotangent, "map", split_axis=0, concat_axis=1, tiled=True
        )

    small_t = small_rows(table, near_full, 3 * side)
    (
        gain_one,
        shift_one,
        query_shift,
        value_shift,
        out_shift,
        gain_two,
        shift_two,
        down_shift,
        learn_scale,
        learn_offset,
    ) = (small_t[count + i : count + i + 1] for i in range(len(vectors)))
    at = count + len(vectors)
    up_shift = small_t[at : at + fan].reshape(fan, devices, own).transpose(1, 0, 2).reshape(1, -1)
    up_shift = halves(up_shift, core, BLOCKS // 4, unit)[0]
    map_t = small_t[:count]
    mine = lambda row: halves(row, core, heads // 2, HD)[0]
    token_grad = token_grad.reshape(count, width).astype(F32)

    added = jnp.concatenate(
        [mine(query_shift), jnp.zeros((1, side), F32), mine(value_shift)], axis=1
    )
    factor = jnp.concatenate([jnp.full((1, side), scaling, F32), jnp.ones((1, width), F32)], 1)
    qkv, hidden_one_t, stats = project(
        table, near_full, inputs, other_inputs, gain_one, shift_one, added, factor
    )
    mixed, mixed_t, totals = attend(qkv, lives)
    if layered:
        down.advance(up.flying)
        up.last(down.held)
        up_full = up.pieces
    mixed_other = mix_out(own_table, near_full, mixed, 1)
    mixed_own = mix_out(own_table, near_full, mixed, 0)
    if layered:
        down.advance((up_full[3],))
        down.last_of_held()
    mixed_got = to_sibling(tie(mixed_other, mixed_own, *([down.held] if layered else [])))
    residual_one, hidden_two = second_norm(
        mixed_own, mixed_got, inputs, out_shift, gain_two, shift_two
    )
    other_two = to_sibling(hidden_two)
    act, act_t, slope, turned_two = feed_up(table, up_full, hidden_two, up_shift)
    if layered:
        down.last(act, down.flying[1])
        down_full = down.pieces
    act_b, act_t_b, slope_b, turned_two_b = feed_up(table, up_full, other_two, up_shift)
    block_got = to_sibling(feed_down(own_table, down_full, act_b, width))
    block_own = feed_down(own_table, down_full, act, width)
    block_out, token_local, grad_block, grad_down_low, grad_map, sums = token_learner(
        residual_one,
        block_own,
        block_got,
        down_shift,
        block_cotangent.reshape(rows, width),
        live * KEEP ** (-0.5),
        token_grad,
        map_t,
        learn_scale,
        learn_offset,
    )
    other_down = to_sibling(grad_down_low)
    token_local = token_local.reshape(images, count, width).astype(BF)
    if layered:
        tokens_out = swap_map(token_local, axis=1)
    else:
        tokens_out = lax.all_to_all(token_local, "map", split_axis=1, concat_axis=0, tiled=True)
    down_parts = weight_grad(own_table, [act_t, act_t_b], [grad_down_low, other_down])
    if layered:
        down_sum = Halving(down_parts)
    grad_pre, up_sums, hidden_own, hidden_other = feed_back(
        (table, own_table), up_full, down_full, grad_down_low, other_down, slope, slope_b
    )
    held = ()
    if layered:
        down_sum.advance()
        held = (down_sum.low,)
    hidden_got = to_sibling(tie(hidden_other, *held))
    up_parts = weight_grad(table, [turned_two, turned_two_b], [grad_pre])
    grad_residual, grad_attn, two_sums = second_norm_back(
        hidden_own, hidden_got, residual_one, grad_block, gain_two
    )
    held = ()
    if layered:
        down_sum.advance()
        up_sum = Halving([up_parts[0], tie(up_parts[1], down_sum.low)])
        held = (down_sum.low,)
    other_attn = to_sibling(tie(grad_attn, *held))
    back = lambda grad, image: attend_back(own_table, near_full, qkv, lives, totals, grad, image)
    qkv_a, sums_a = back(grad_attn, 0)
    qkv_b, sums_b = back(other_attn, 1)
    grad_qkv, qv_sums = [qkv_a, qkv_b], sums_a + sums_b
    if layered:
        down_sum.advance()
        up_sum.advance()
    near_parts = weight_grad(table, [hidden_one_t], grad_qkv, 0, 2)
    if layered:
        up_sum.advance()
        grad_down = down_sum.finish()
        near_sum = Halving([near_parts[0], tie(near_parts[1], up_sum.low)], direct=True)
    far_parts = value_and_out_grad(
        (table, own_table), hidden_one_t, grad_qkv, mixed_t, [grad_attn, other_attn]
    )
    held = ()
    if layered:
        up_sum.advance()
        near_sum.advance()
        held = (near_sum.low,)
        far_sum = Halving([far_parts[0], tie(far_parts[1], *held)], direct=True)
    one_own, one_other = project_back(table, near_full, qkv_a, qkv_b)
    held = ()
    if layered:
        near_sum.advance()
        grad_up = up_sum.finish()
        far_sum.advance()
        held = (far_sum.low,)
    one_got = to_sibling(tie(one_other, *held))
    grad_patches, one_sums = first_norm_back(
        one_own, one_got, inputs, stats, gain_one, grad_residual
    )
    if layered:
        far_sum.advance()
        grad_qk = near_sum.finish()
        swap = lambda total: (total[0], to_sibling(total[1]))
        grad_down = jnp.concatenate(grad_down, axis=0)
        grad_up = joined(*swap(grad_up), core, BLOCKS // 4, unit)
        own_qk, other_qk = swap(grad_qk)
        grad_far = far_sum.finish()
        grad_out = jnp.concatenate([grad_far[0][:, side:], grad_far[1][:, side:]], axis=1)
        own_v, other_v = swap([part[:, :side] for part in grad_far])
        own_qkv = jnp.concatenate([own_qk, own_v], axis=1)
        other_qkv = jnp.concatenate([other_qk, other_v], axis=1)
        grad_qkv_full = joined(own_qkv, other_qkv, core, 3 * heads // 2, HD)
    else:

        def scatter(parts, groups, unit):
            mine = jnp.concatenate(parts, axis=0)
            return joined(mine, jnp.zeros_like(mine), core, groups, unit)

        def shared(values):
            return lax.psum_scatter(values.astype(F32), AXES, scatter_dimension=0, tiled=True)

        def tall(parts, unit):
            flat = [jnp.concatenate(parts, axis=0).reshape(1, -1)]
            return shared(scatter(flat, BLOCKS // 4, unit * width).reshape(-1, width))

        grad_up = shared(scatter(up_parts, BLOCKS // 4, unit))
        far = jnp.concatenate(far_parts, axis=0)
        out_part = far[:, side:].reshape(BLOCKS // 2, 2, width // BLOCKS, side)
        out_part = out_part.transpose(0, 2, 1, 3).reshape(side, width)
        grad_down, grad_out = tall(down_parts, unit), tall([out_part], HD)
        qkv_parts = [jnp.concatenate([*near_parts], axis=0), far[:, :side]]
        qkv_parts = [jnp.concatenate(qkv_parts, axis=1)]
        grad_qkv_full = shared(scatter(qkv_parts, 3 * heads // 2, HD))

    spread = lambda row, unit: joined(row, jnp.zeros_like(row), core, row.shape[1] // unit, unit)
    terms = (
        one_sums[0:1],
        one_sums[1:2],
        spread(qv_sums[0:1], HD),
        spread(qv_sums[1:2], HD),
        two_sums[2:3],
        two_sums[0:1],
        two_sums[1:2],
        sums[2:3],
        sums[0:1],
        sums[1:2],
        spread(up_sums, unit),
    )
    packed = [term.reshape(devices, -1) for term in terms]
    packed.append(grad_map.reshape(count, devices, own).transpose(1, 2, 0).reshape(devices, -1))
    packed = jnp.concatenate(packed, axis=1)
    summed = jnp.sum(lax.all_to_all(packed, AXES, 0, 0, tiled=True), axis=0)
    pieces = [summed[i * own : (i + 1) * own] for i in range(10)]
    at = 10 * own
    up_piece = summed[at : at + fan * own]
    map_piece = summed[at + fan * own :].reshape(own, count)
    return (
        block_out.reshape(images, patch_count, width),
        tokens_out,
        grad_patches.reshape(images, patch_count, width),
        pieces[0],
        pieces[1],
        grad_qkv_full,
        pieces[2],
        pieces[3],
        grad_out,
        pieces[4],
        pieces[5],
        pieces[6],
        grad_up,
        up_piece,
        grad_down,
        pieces[7],
        pieces[8],
        pieces[9],
        map_piece,
    )


def solution(mesh):
    rows = P(("dp", "map"))
    wide = P(("dp", "map"), None)
    images = P(("dp", "map"), None, None)
    tokens = P("dp", "map", None)
    weights = (
        rows, rows, wide, rows, rows, wide, rows, rows,
        rows, wide, rows, wide, rows, rows, rows, wide,
    )
    return jax.shard_map(
        per_device,
        mesh=mesh,
        in_specs=(images, wide, images, tokens) + weights,
        out_specs=(images, tokens, images) + weights,
        check_vma=False,
    )
```

time: 518 us -> 445 us (0.86)
  waiting for transfers between devices: 208 us -> 96.3 us
  Pallas kernels: 140 us -> 222 us
  other arithmetic: 52.5 us -> 9.92 us
  local copies, waits for them, and re-layouts: 22.9 us -> 54.7 us
  matrix products: 22.3 us -> 0 us
  between operations: 15.1 us -> 2.22 us
  starting transfers between devices: 47 us -> 52.9 us
    ppermute x32 -> x35, waiting for transfers between devices: 181 us -> 93.9 us  [permute(): return lax.ppermute(values, AXES, pairs)]
    pallas_call x11 -> x44, Pallas kernels: 140 us -> 222 us  [run(): outs = pl.pallas_call(body, in_specs=specs, **settings)(*operands, *waited)]
    convert_element_type x24 -> x6, other arithmetic: 31.9 us -> 3.34 us  [the longest x1 1.08 us: per_device(): qkv_own, qkv_other = halves(qkv_weight.astype(BF), core, 3 * heads // 2, HD)]
    all_to_all x1, waiting for transfers between devices: 27.3 us -> 0.01 us  [per_device(): summed = jnp.sum(lax.all_to_all(packed, AXES, 0, 0, tiled=True), axis=0)]
    dot_general x6 -> x0, matrix products: 22.3 us -> none  [dot(): lax.dot_general(left, right, (dims, ((), ())), preferred_element_type=F32...]
    unnamed x87 -> x177, local copies, waits for them, and re-layouts: 10.3 us -> 31.1 us
    ppermute x32 -> x35, starting transfers between devices: 34.7 us -> 48 us  [permute(): return lax.ppermute(values, AXES, pairs)]
    reduce_sum x5 -> x0, other arithmetic: 9.16 us -> none  [the longest x1 3.37 us: per_device(): grad_gain_two = jnp.sum(grad_hidden_two * normed_two, axis=0)]
  transfers between devices with their start and end apart: 36 -> 50, of which waited for: 17 -> 18; matrix products, arithmetic and copies ran while one was open for 15% -> 7% of each run, Pallas kernels for 9% -> 43%
where the time goes in v2:
time: 445 us; the launch traced here: 438 us
  Pallas kernels  222 us (50%)
  waiting for transfers between devices  96.3 us (22%)
  local copies, waits for them, and re-layouts  54.7 us (12%)
  starting transfers between devices  52.9 us (12%)
  other arithmetic  9.92 us (2%)
    pallas_call x44, Pallas kernels, run(): outs = pl.pallas_call(body, in_specs=specs, **settings)(*operands, *waited)  222 us
    ppermute x35, waiting for transfers between devices, permute(): return lax.ppermute(values, AXES, pairs)  93.9 us
    ppermute x35, starting transfers between devices, permute(): return lax.ppermute(values, AXES, pairs)  48 us
    unnamed x177, local copies, waits for them, and re-layouts  31.1 us
  transfers between devices with their start and end apart: 50, of which 18 were waited for; matrix products, arithmetic and copies ran while one was open for 7% of the time, Pallas kernels for 43%

profile of v2, /device:TPU:0, one launch (start us, length us, event | category | flops | bytes accessed | tf_op | source)
XLA Modules:
  0.0 438.3 jit_solution(2709586945169461947)
XLA Ops:
  7.5 4.0 collective-permute-start.1
  11.5 12.9 %collective-permute-done.1.refs_1_ = bf16[64,2176]{1,0:T(8,128)(2,1)S(1)} collective-permute-done((bf16[64,2176]{1,0:T(8,128)(2,1)S(1)}, bf16[64,2176]{1,0:T(8,128)(2,1)S(1)}, u32[]{:S(2)}, u32[]{:S(2)}) %collective-permute-start.1) | collective-permute-done | bytes 278560 | tf_op jit(solution)/shard_map/ppermute | solution.py:85
  26.8 11.9 %collective-permute-done.2.refs_1_ = bf16[128,2176]{1,0:T(8,128)(2,1)S(1)} collective-permute-done((bf16[128,2176]{1,0:T(8,128)(2,1)S(1)}, bf16[128,2176]{1,0:T(8,128)(2,1)S(1)}, u32[]{:S(2)}, u32[]{:S(2)}) %collective-permute-start.2) | collective-permute-done | bytes 557088 | tf_op jit(solution)/shard_map/ppermute | solution.py:85
  43.5 3.1 collective-permute-start.8
  48.5 17.4 %collective-permute-done.3.refs_3_.refs_2_ = bf16[256,2176]{1,0:T(8,128)(2,1)} collective-permute-done((bf16[256,2176]{1,0:T(8,128)(2,1)}, bf16[256,2176]{1,0:T(8,128)(2,1)}, u32[]{:S(2)}, u32[]{:S(2)}) %collective-permute-start.3) | collective-permute-done | bytes 1114144 | tf_op jit(solution)/shard_map/ppermute | solution.py:85
  70.1 11.0 %collective-permute-done.9.refs_1_ = bf16[128,2048]{1,0:T(8,128)(2,1)S(1)} collective-permute-done((bf16[128,2048]{1,0:T(8,128)(2,1)S(1)}, bf16[128,2048]{1,0:T(8,128)(2,1)S(1)}, u32[]{:S(2)}, u32[]{:S(2)}) %collective-permute-start.9) | collective-permute-done | bytes 524320 | tf_op jit(solution)/shard_map/ppermute | solution.py:85
  85.0 4.1 collective-permute-start.11
  91.3 11.6 %project.1 = (bf16[1152,1536]{1,0:T(8,128)(2,1)}, bf16[1024,1280]{1,0:T(8,128)(2,1)S(1)}, f32[576,2]{1,0:T(8,128)S(1)}) custom-call(s32[32]{0:T(128)S(1)} %reshape.368.refs_0_, bf16[256,2176]{1,0:T(8,128)(2,1)} %stack.35.refs_2_.refs_1_, bf16[256,2176]{1,0:T(8,128)(2,1)} %collective-permute-done.3.refs_3_.refs_2_, ...), custom_call_target="tpu_custom_call" | custom-call | flops 999999995904 | bytes 1024 | tf_op jit(solution)/shard_map/project/pallas_call | solution.py:40
  107.2 14.0 %attend.1 = (bf16[1152,512]{1,0:T(8,128)(2,1)S(1)}, bf16[512,1280]{1,0:T(8,128)(2,1)S(1)}, f32[4,4,576]{2,1,0:T(4,128)S(1)}) custom-call(bf16[1152,1536]{1,0:T(8,128)(2,1)S(1)} %copy-done.23, bf16[1152,1536]{1,0:T(8,128)(2,1)S(1)} %copy-done.23, bf16[1152,1536]{1,0:T(8,128)(2,1)S(1)} %copy-done.23, f32[1152,1]{1,0:T(8,128)S(1)} %copy.95.refs_3_.refs_8_, ...), custom_call_target="tpu_custom_call" | custom-call | flops 999999995904 | bytes 1024 | tf_op jit(solution)/shard_map/attend/pallas_call | solution.py:40
  126.1 4.2 mix_out.2.refs_6_
  130.3 2.8 mix_out.3.refs_2_.refs_0_
  133.1 2.2 collective-permute-done.14.refs_1_
  135.3 4.4 %collective-permute-done.15.refs_3_.refs_4_.refs_5_ = bf16[256,2048]{1,0:T(8,128)(2,1)} collective-permute-done((bf16[256,2048]{1,0:T(8,128)(2,1)}, bf16[256,2048]{1,0:T(8,128)(2,1)}, u32[]{:S(2)}, u32[]{:S(2)}) %collective-permute-start.15) | collective-permute-done | bytes 1048608 | tf_op jit(solution)/shard_map/ppermute | solution.py:85
  139.7 2.3 stack.41.refs_6_.refs_1_
  150.8 3.3 second_norm.1
  155.5 10.3 %feed_up.2 = (bf16[576,2048]{1,0:T(8,128)(2,1)S(1)}, bf16[2048,640]{1,0:T(8,128)(2,1)}, bf16[576,2048]{1,0:T(8,128)(2,1)}, bf16[1024,640]{1,0:T(8,128)(2,1)S(1)}) custom-call(s32[32]{0:T(128)S(1)} %reshape.368.refs_0_, bf16[256,2048]{1,0:T(8,128)(2,1)} %stack.38.refs_2_.refs_1_, bf16[256,2048]{1,0:T(8,128)(2,1)} %collective-permute-done.12.refs_3_.refs_2_, ...), custom_call_target="tpu_custom_call" | custom-call | flops 999999995904 | bytes 1024 | tf_op jit(solution)/shard_map/feed_up/pallas_call | solution.py:40
  167.3 5.7 %collective-permute-done.17.refs_2_.refs_7_ = bf16[256,2048]{1,0:T(8,128)(2,1)} collective-permute-done((bf16[256,2048]{1,0:T(8,128)(2,1)}, bf16[256,2048]{1,0:T(8,128)(2,1)}, u32[]{:S(2)}, u32[]{:S(2)}) %collective-permute-start.17) | collective-permute-done | bytes 1048608 | tf_op jit(solution)/shard_map/ppermute | solution.py:85
  173.5 10.9 %feed_up.3 = (bf16[576,2048]{1,0:T(8,128)(2,1)S(1)}, bf16[2048,640]{1,0:T(8,128)(2,1)}, bf16[576,2048]{1,0:T(8,128)(2,1)}, bf16[1024,640]{1,0:T(8,128)(2,1)S(1)}) custom-call(s32[32]{0:T(128)S(1)} %reshape.368.refs_0_, bf16[256,2048]{1,0:T(8,128)(2,1)} %stack.38.refs_2_.refs_1_, bf16[256,2048]{1,0:T(8,128)(2,1)} %collective-permute-done.12.refs_3_.refs_2_, ...), custom_call_target="tpu_custom_call" | custom-call | flops 999999995904 | bytes 1024 | tf_op jit(solution)/shard_map/feed_up/pallas_call | solution.py:40
  185.4 2.7 collective-permute-done.19.refs_4_.refs_9_
  188.1 7.2 %feed_down.2.refs_6_ = f32[576,1024]{1,0:T(8,128)} custom-call(s32[16]{0:T(128)S(1)} %and_add_fusion.refs_0_.refs_1_, bf16[256,2048]{1,0:T(8,128)(2,1)} %stack.41.refs_6_.refs_1_, bf16[256,2048]{1,0:T(8,128)(2,1)} %collective-permute-done.17.refs_2_.refs_7_, bf16[256,2048]{1,0:T(8,128)(2,1)} %collective-permute-done.18.refs_3_.refs_8_, ...), custom_call_target="tpu_custom_call" | custom-call | flops 999999995904 | bytes 1024 | tf_op jit(solution)/shard_map/feed_down/pallas_call | solution.py:40
  195.5 5.9 %feed_down.3.refs_1_.refs_10_ = f32[576,1024]{1,0:T(8,128)S(1)} custom-call(s32[16]{0:T(128)S(1)} %and_add_fusion.refs_0_.refs_1_, bf16[256,2048]{1,0:T(8,128)(2,1)} %stack.41.refs_6_.refs_1_, bf16[256,2048]{1,0:T(8,128)(2,1)} %collective-permute-done.17.refs_2_.refs_7_, bf16[256,2048]{1,0:T(8,128)(2,1)} %collective-permute-done.18.refs_3_.refs_8_, ...), custom_call_target="tpu_custom_call" | custom-call | flops 999999995904 | bytes 1024 | tf_op jit(solution)/shard_map/feed_down/pallas_call | solution.py:40
  204.5 6.8 %token_learner.1 = (bf16[576,1024]{1,0:T(8,128)(2,1)}, f32[8,1024]{1,0:T(8,128)S(1)}, f32[576,1024]{1,0:T(8,128)S(1)}, bf16[576,1024]{1,0:T(8,128)(2,1)S(1)}, f3...) custom-call(f32[576,1024]{1,0:T(8,128)S(1)} %copy-done.31, f32[576,1024]{1,0:T(8,128)S(1)} %copy-done.36, ...), custom_call_target="tpu_custom_call" | custom-call | flops 999999995904 | bytes 1024 | tf_op jit(solution)/shard_map/token_learner/pallas_call | solution.py:40
  216.0 9.6 %weight_grad.3 = (bf16[1024,1024]{1,0:T(8,128)(2,1)S(1)}, bf16[1024,1024]{1,0:T(8,128)(2,1)}) custom-call(s32[16]{0:T(128)S(1)} %and_add_fusion.refs_0_.refs_1_, bf16[2048,640]{1,0:T(8,128)(2,1)S(1)} %copy-done.26, bf16[2048,640]{1,0:T(8,128)(2,1)} %get-tuple-element.127.refs_2_, bf16[576,1024]{1,0:T(8,128)(2,1)S(1)} %get-tuple-element.123.refs_3_.refs_10_, ...), custom_call_target="tpu_custom_call" | custom-call | flops 999999995904 | bytes 1024 | tf_op jit(solution)/shard_map/weight_grad/pallas_call | solution.py:40
  227.5 21.0 %feed_back.1 = (bf16[1152,2048]{1,0:T(8,128)(2,1)}, f32[1,2048]{1,0:T(1,128)S(1)}, f32[576,1024]{1,0:T(8,128)}, f32[576,1024]{1,0:T(8,128)}) custom-call(s32[32]{0:T(128)S(1)} %reshape.368.refs_0_, s32[16]{0:T(128)S(1)} %and_add_fusion.refs_0_.refs_1_, bf16[256,2048]{1,0:T(8,128)(2,1)} %stack.38.refs_2_.refs_1_, ...), custom_call_target="tpu_custom_call" | custom-call | flops 999999995904 | bytes 1024 | tf_op jit(solution)/shard_map/feed_back/pallas_call | solution.py:40
  248.4 4.9 %collective-permute-done.25.refs_1_ = bf16[1024,1024]{1,0:T(8,128)(2,1)} collective-permute-done((bf16[1024,1024]{1,0:T(8,128)(2,1)}, bf16[1024,1024]{1,0:T(8,128)(2,1)}, u32[]{:S(2)}, u32[]{:S(2)}) %collective-permute-start.25) | collective-permute-done | bytes 2097184 | tf_op jit(solution)/shard_map/ppermute | solution.py:85
  253.3 2.3 copy-done.22
  255.7 2.8 add_parts.10
  259.0 10.5 %weight_grad.4 = (bf16[512,2048]{1,0:T(8,128)(2,1)S(1)}, bf16[512,2048]{1,0:T(8,128)(2,1)}) custom-call(s32[32]{0:T(128)S(1)} %reshape.368.refs_0_, bf16[1024,640]{1,0:T(8,128)(2,1)S(1)} %get-tuple-element.136.refs_1_, bf16[1024,640]{1,0:T(8,128)(2,1)S(1)} %copy-done.47, bf16[1152,2048]{1,0:T(8,128)(2,1)} %get-tuple-element.132.refs_2_.refs_3_, ...), custom_call_target="tpu_custom_call" | custom-call | flops 999999995904 | bytes 1024 | tf_op jit(solution)/shard_map/weight_grad/pallas_call | solution.py:40
  269.6 5.7 %second_norm_back.1 = (f32[576,1024]{1,0:T(8,128)S(1)}, bf16[576,1024]{1,0:T(8,128)(2,1)}, f32[3,1024]{1,0:T(4,128)S(1)}) custom-call(f32[576,1024]{1,0:T(8,128)S(1)} %copy-done.27, f32[576,1024]{1,0:T(8,128)} %collective-permute-done.26.refs_1_, f32[576,1024]{1,0:T(8,128)} %copy-done.30, f32[576,1024]{1,0:T(8,128)} %copy-done.32, ...), custom_call_target="tpu_custom_call" | custom-call | flops 999999995904 | bytes 1024 | tf_op jit(solution)/shard_map/second_norm_back/pallas_call | solution.py:40
  275.3 2.9 add_parts.11
  280.5 14.9 %attend_back.2 = (bf16[3,576,512]{2,1,0:T(8,128)(2,1)S(1)}, f32[2,512]{1,0:T(2,128)S(1)}) custom-call(s32[16]{0:T(128)S(1)} %and_add_fusion.refs_0_.refs_1_, bf16[256,2176]{1,0:T(8,128)(2,1)} %stack.35.refs_2_.refs_1_, bf16[256,2176]{1,0:T(8,128)(2,1)} %collective-permute-done.3.refs_3_.refs_2_, bf16[256,2176]{1,0:T(8,128)(2,1)} %collective-permute-done.4.refs_4_.refs_3_, ...), custom_call_target="tpu_custom_call" | custom-call | flops 999999995904 | bytes 1024 | tf_op jit(solution)/shard_map/attend_back/pallas_call | solution.py:40
  295.4 15.7 %attend_back.3 = (bf16[3,576,512]{2,1,0:T(8,128)(2,1)S(1)}, f32[2,512]{1,0:T(2,128)S(1)}) custom-call(s32[16]{0:T(128)S(1)} %and_add_fusion.refs_0_.refs_1_, bf16[256,2176]{1,0:T(8,128)(2,1)} %stack.35.refs_2_.refs_1_, bf16[256,2176]{1,0:T(8,128)(2,1)} %collective-permute-done.3.refs_3_.refs_2_, bf16[256,2176]{1,0:T(8,128)(2,1)} %collective-permute-done.4.refs_4_.refs_3_, ...), custom_call_target="tpu_custom_call" | custom-call | flops 999999995904 | bytes 1024 | tf_op jit(solution)/shard_map/attend_back/pallas_call | solution.py:40
  312.9 2.9 add_parts.13
  316.4 8.7 %weight_grad.5 = (bf16[512,1024]{1,0:T(8,128)(2,1)S(1)}, bf16[512,1024]{1,0:T(8,128)(2,1)}) custom-call(s32[32]{0:T(128)S(1)} %reshape.368.refs_0_, bf16[1024,1280]{1,0:T(8,128)(2,1)S(1)} %copy-done.25, bf16[3,576,512]{2,1,0:T(8,128)(2,1)S(1)} %copy-done.44, bf16[3,576,512]{2,1,0:T(8,128)(2,1)S(1)} %get-tuple-element.145.refs_2_.refs_3_.refs_5_.refs_6_, ...), custom_call_target="tpu_custom_call" | custom-call | flops 999999995904 | bytes 1024 | tf_op jit(solution)/shard_map/weight_grad/pallas_call | solution.py:40
  325.1 5.9 %collective-permute-done.31.refs_1_ = bf16[256,2048]{1,0:T(8,128)(2,1)} collective-permute-done((bf16[256,2048]{1,0:T(8,128)(2,1)}, bf16[256,2048]{1,0:T(8,128)(2,1)}, u32[]{:S(2)}, u32[]{:S(2)}) %collective-permute-start.31) | collective-permute-done | bytes 1048608 | tf_op jit(solution)/shard_map/ppermute | solution.py:85
  331.0 2.1 add_parts.14
  336.6 8.4 %value_and_out_grad.1 = (bf16[512,1024]{1,0:T(8,128)(2,1)S(1)}, bf16[512,1024]{1,0:T(8,128)(2,1)}) custom-call(s32[32]{0:T(128)S(1)} %reshape.368.refs_0_, s32[16]{0:T(128)S(1)} %and_add_fusion.refs_0_.refs_1_, bf16[1024,1280]{1,0:T(8,128)(2,1)} %copy-done.24, bf16[512,1280]{1,0:T(8,128)(2,1)S(1)} %get-tuple-element.158.refs_3_, ...), custom_call_target="tpu_custom_call" | custom-call | flops 999999995904 | bytes 1024 | tf_op jit(solution)/shard_map/value_and_out_grad/pallas_call | solution.py:40
  348.1 2.6 collective-permute-start.36
  354.8 10.3 %project_back.1 = (f32[576,1024]{1,0:T(8,128)}, f32[576,1024]{1,0:T(8,128)}) custom-call(s32[32]{0:T(128)S(1)} %reshape.368.refs_0_, bf16[256,2176]{1,0:T(8,128)(2,1)} %stack.35.refs_2_.refs_1_, bf16[256,2176]{1,0:T(8,128)(2,1)} %collective-permute-done.3.refs_3_.refs_2_, bf16[256,2176]{1,0:T(8,128)(2,1)} %collective-permute-done.4.refs_4_.refs_3_, ...), custom_call_target="tpu_custom_call" | custom-call | flops 999999995904 | bytes 1024 | tf_op jit(solution)/shard_map/project_back/pallas_call | solution.py:40
  365.2 4.1 collective-permute-done.37.refs_1_
  374.3 2.4 add_parts.18
  392.2 2.6 collective-permute-start.41
  397.3 2.3 reshape.389
  404.5 4.3 first_norm_back.1
  409.9 3.3 all-to-all-start
  416.3 2.6 collective-permute-start.43
  422.4 4.8 %collective-permute-done.43.refs_1_ = bf16[64,1024]{1,0:T(8,128)(2,1)} collective-permute-done((bf16[64,1024]{1,0:T(8,128)(2,1)}, bf16[64,1024]{1,0:T(8,128)(2,1)}, u32[]{:S(2)}, u32[]{:S(2)}) %collective-permute-start.43) | collective-permute-done | bytes 131104 | tf_op jit(solution)/shard_map/ppermute | solution.py:85
  427.1 2.7 collective-permute-done.45.refs_3_
  (371 shorter events, 117.1 us)
Async XLA Ops:
  7.5 16.9 %collective-permute-start.1 = (bf16[64,2176]{1,0:T(8,128)(2,1)S(1)}, bf16[64,2176]{1,0:T(8,128)(2,1)S(1)}, u32[]{:S(2)}, u32[]{:S(2)}) collective-permute-start(bf16[64,2176]{1,0:T(8,128)(2,1)S(1)} %maximum_maximum_fusion.refs_0_), channel_id=1, source_target_pairs={{0,16},{1,17},{2,18},{3,19},{4,20},{5,21},{6,22},{7,23},{8,24},{9,... | collective-permute-start | bytes 835592 | tf_op jit(solution)/shard_map/ppermute | solution.py:85
  24.5 14.2 %collective-permute-start.2 = (bf16[128,2176]{1,0:T(8,128)(2,1)S(1)}, bf16[128,2176]{1,0:T(8,128)(2,1)S(1)}, u32[]{:S(2)}, u32[]{:S(2)}) collective-permute-start(bf16[128,2176]{1,0:T(8,128)(2,1)S(1)} %stack.34.refs_0_.refs_2_), channel_id=1, source_target_pairs={{0,8},{1,9},{2,10},{3,11},{4,12},{5,13},{6,14},{7,15},{8,0},{9,1},... | collective-permute-start | bytes 1671176 | tf_op jit(solution)/shard_map/ppermute | solution.py:85
  26.8 15.7 %collective-permute-start.6 = (bf16[32,2048]{1,0:T(8,128)(2,1)}, bf16[32,2048]{1,0:T(8,128)(2,1)}, u32[]{:S(2)}, u32[]{:S(2)}) collective-permute-start(bf16[32,2048]{1,0:T(8,128)(2,1)} %bitcast.46), channel_id=1, source_target_pairs={{0,2},{1,3},{2,0},{3,1},{4,6},{5,7},{6,4},{7,5},{8,10},{9,11},{10,... | collective-permute-start | bytes 393224 | tf_op jit(solution)/shard_map/ppermute | solution.py:95
  39.8 26.2 %collective-permute-start.3 = (bf16[256,2176]{1,0:T(8,128)(2,1)}, bf16[256,2176]{1,0:T(8,128)(2,1)}, u32[]{:S(2)}, u32[]{:S(2)}) collective-permute-start(bf16[256,2176]{1,0:T(8,128)(2,1)} %stack.35.refs_2_.refs_1_), channel_id=1, source_target_pairs={{0,4},{1,5},{2,3},{3,2},{4,0},{5,1},{6,7},{7,6},{8,12},{9,13},{10,... | collective-permute-start | bytes 3342344 | tf_op jit(solution)/shard_map/ppermute | solution.py:85
  41.0 24.9 %collective-permute-start.4 = (bf16[256,2176]{1,0:T(8,128)(2,1)}, bf16[256,2176]{1,0:T(8,128)(2,1)}, u32[]{:S(2)}, u32[]{:S(2)}) collective-permute-start(bf16[256,2176]{1,0:T(8,128)(2,1)} %stack.35.refs_2_.refs_1_), channel_id=1, source_target_pairs={{0,1},{1,0},{2,6},{3,7},{4,5},{5,4},{6,2},{7,3},{8,9},{9,8},{10,14... | collective-permute-start | bytes 3342344 | tf_op jit(solution)/shard_map/ppermute | solution.py:85
  43.5 23.5 %collective-permute-start.8 = (bf16[64,2048]{1,0:T(8,128)(2,1)S(1)}, bf16[64,2048]{1,0:T(8,128)(2,1)S(1)}, u32[]{:S(2)}, u32[]{:S(2)}) collective-permute-start(bf16[64,2048]{1,0:T(8,128)(2,1)S(1)} %stack.36.refs_0_.refs_2_), channel_id=1, source_target_pairs={{0,16},{1,17},{2,18},{3,19},{4,20},{5,21},{6,22},{7,23},{8,24},{9,... | collective-permute-start | bytes 786440 | tf_op jit(solution)/shard_map/ppermute | solution.py:85
  47.2 21.8 %collective-permute-start.10 = (f32[1,576]{1,0:T(1,128)}, f32[1,576]{1,0:T(1,128)}, u32[]{:S(2)}, u32[]{:S(2)}) collective-permute-start(f32[1,576]{1,0:T(1,128)} %convert_element_type.30), channel_id=1, source_target_pairs={{0,2},{1,3},{2,0},{3,1},{4,6},{5,7},{6,4},{7,5},{8,10},{9,11},{10,... | collective-permute-start | bytes 6920 | tf_op jit(solution)/shard_map/ppermute | solution.py:95
  66.0 15.8 %collective-permute-start.5 = (bf16[256,2176]{1,0:T(8,128)(2,1)}, bf16[256,2176]{1,0:T(8,128)(2,1)}, u32[]{:S(2)}, u32[]{:S(2)}) collective-permute-start(bf16[256,2176]{1,0:T(8,128)(2,1)} %collective-permute-done.3.refs_3_.refs_2_), channel_id=1, source_target_pairs={{0,1},{1,0},{2,6},{3,7},{4,5},{5,4},{6,2},{7,3},{8,9},{9,8},{10,14... | collective-permute-start | bytes 3342344 | tf_op jit(solution)/shard_map/ppermute | solution.py:85
  67.1 14.1 %collective-permute-start.9 = (bf16[128,2048]{1,0:T(8,128)(2,1)S(1)}, bf16[128,2048]{1,0:T(8,128)(2,1)S(1)}, u32[]{:S(2)}, u32[]{:S(2)}) collective-permute-start(bf16[128,2048]{1,0:T(8,128)(2,1)S(1)} %stack.37.refs_0_.refs_2_), channel_id=1, source_target_pairs={{0,8},{1,9},{2,10},{3,11},{4,12},{5,13},{6,14},{7,15},{8,0},{9,1},... | collective-permute-start | bytes 1572872 | tf_op jit(solution)/shard_map/ppermute | solution.py:85
  70.0 21.3 %collective-permute-start.7 = (bf16[576,1024]{1,0:T(8,128)(2,1)}, bf16[576,1024]{1,0:T(8,128)(2,1)}, u32[]{:S(2)}, u32[]{:S(2)}) collective-permute-start(bf16[576,1024]{1,0:T(8,128)(2,1)} %bitcast.11.refs_5_.refs_2_), channel_id=1, source_target_pairs={{0,2},{1,3},{2,0},{3,1},{4,6},{5,7},{6,4},{7,5},{8,10},{9,11},{10,... | collective-permute-start | bytes 3538952 | tf_op jit(solution)/shard_map/ppermute | solution.py:95
  82.8 38.4 %collective-permute-start.12 = (bf16[256,2048]{1,0:T(8,128)(2,1)}, bf16[256,2048]{1,0:T(8,128)(2,1)}, u32[]{:S(2)}, u32[]{:S(2)}) collective-permute-start(bf16[256,2048]{1,0:T(8,128)(2,1)} %stack.38.refs_2_.refs_1_), channel_id=1, source_target_pairs={{0,4},{1,5},{2,3},{3,2},{4,0},{5,1},{6,7},{7,6},{8,12},{9,13},{10,... | collective-permute-start | bytes 3145736 | tf_op jit(solution)/shard_map/ppermute | solution.py:85
  85.0 36.2 %collective-permute-start.11 = (bf16[64,2048]{1,0:T(8,128)(2,1)}, bf16[64,2048]{1,0:T(8,128)(2,1)}, u32[]{:S(2)}, u32[]{:S(2)}) collective-permute-start(bf16[64,2048]{1,0:T(8,128)(2,1)} %stack.39.refs_5_.refs_0_), channel_id=1, source_target_pairs={{0,16},{1,17},{2,18},{3,19},{4,20},{5,21},{6,22},{7,23},{8,24},{9,... | collective-permute-start | bytes 786440 | tf_op jit(solution)/shard_map/ppermute | solution.py:85
  90.8 30.5 %collective-permute-start.13 = (bf16[256,2048]{1,0:T(8,128)(2,1)}, bf16[256,2048]{1,0:T(8,128)(2,1)}, u32[]{:S(2)}, u32[]{:S(2)}) collective-permute-start(bf16[256,2048]{1,0:T(8,128)(2,1)} %stack.38.refs_2_.refs_1_), channel_id=1, source_target_pairs={{0,1},{1,0},{2,6},{3,7},{4,5},{5,4},{6,2},{7,3},{8,9},{9,8},{10,14... | collective-permute-start | bytes 3145736 | tf_op jit(solution)/shard_map/ppermute | solution.py:85
  123.2 12.1 %collective-permute-start.14 = (bf16[128,2048]{1,0:T(8,128)(2,1)}, bf16[128,2048]{1,0:T(8,128)(2,1)}, u32[]{:S(2)}, u32[]{:S(2)}) collective-permute-start(bf16[128,2048]{1,0:T(8,128)(2,1)} %stack.40.refs_6_.refs_0_), channel_id=1, source_target_pairs={{0,8},{1,9},{2,10},{3,11},{4,12},{5,13},{6,14},{7,15},{8,0},{9,1},... | collective-permute-start | bytes 1572872 | tf_op jit(solution)/shard_map/ppermute | solution.py:85
  124.6 15.1 %collective-permute-start.15 = (bf16[256,2048]{1,0:T(8,128)(2,1)}, bf16[256,2048]{1,0:T(8,128)(2,1)}, u32[]{:S(2)}, u32[]{:S(2)}) collective-permute-start(bf16[256,2048]{1,0:T(8,128)(2,1)} %collective-permute-done.12.refs_3_.refs_2_), channel_id=1, source_target_pairs={{0,1},{1,0},{2,6},{3,7},{4,5},{5,4},{6,2},{7,3},{8,9},{9,8},{10,14... | collective-permute-start | bytes 3145736 | tf_op jit(solution)/shard_map/ppermute | solution.py:85
  142.0 7.1 %collective-permute-start.16 = (f32[576,1024]{1,0:T(8,128)}, f32[576,1024]{1,0:T(8,128)}, u32[]{:S(2)}, u32[]{:S(2)}) collective-permute-start(f32[576,1024]{1,0:T(8,128)} %mix_out.2.refs_6_), channel_id=1, source_target_pairs={{0,2},{1,3},{2,0},{3,1},{4,6},{5,7},{6,4},{7,5},{8,10},{9,11},{10,... | collective-permute-start | bytes 7077896 | tf_op jit(solution)/shard_map/ppermute | solution.py:95
  143.2 3.7 collective-permute-start.22
  146.9 26.1 %collective-permute-start.17 = (bf16[256,2048]{1,0:T(8,128)(2,1)}, bf16[256,2048]{1,0:T(8,128)(2,1)}, u32[]{:S(2)}, u32[]{:S(2)}) collective-permute-start(bf16[256,2048]{1,0:T(8,128)(2,1)} %stack.41.refs_6_.refs_1_), channel_id=1, source_target_pairs={{0,4},{1,5},{2,3},{3,2},{4,0},{5,1},{6,7},{7,6},{8,12},{9,13},{10,... | collective-permute-start | bytes 3145736 | tf_op jit(solution)/shard_map/ppermute | solution.py:85
  147.6 25.4 %collective-permute-start.18 = (bf16[256,2048]{1,0:T(8,128)(2,1)}, bf16[256,2048]{1,0:T(8,128)(2,1)}, u32[]{:S(2)}, u32[]{:S(2)}) collective-permute-start(bf16[256,2048]{1,0:T(8,128)(2,1)} %stack.41.refs_6_.refs_1_), channel_id=1, source_target_pairs={{0,1},{1,0},{2,6},{3,7},{4,5},{5,4},{6,2},{7,3},{8,9},{9,8},{10,14... | collective-permute-start | bytes 3145736 | tf_op jit(solution)/shard_map/ppermute | solution.py:85
  155.5 18.0 %collective-permute-start.20 = (bf16[576,1024]{1,0:T(8,128)(2,1)}, bf16[576,1024]{1,0:T(8,128)(2,1)}, u32[]{:S(2)}, u32[]{:S(2)}) collective-permute-start(bf16[576,1024]{1,0:T(8,128)(2,1)} %get-tuple-element.115.refs_5_), channel_id=1, source_target_pairs={{0,2},{1,3},{2,0},{3,1},{4,6},{5,7},{6,4},{7,5},{8,10},{9,11},{10,... | collective-permute-start | bytes 3538952 | tf_op jit(solution)/shard_map/ppermute | solution.py:95
  173.0 15.1 %collective-permute-start.19 = (bf16[256,2048]{1,0:T(8,128)(2,1)}, bf16[256,2048]{1,0:T(8,128)(2,1)}, u32[]{:S(2)}, u32[]{:S(2)}) collective-permute-start(bf16[256,2048]{1,0:T(8,128)(2,1)} %collective-permute-done.17.refs_2_.refs_7_), channel_id=1, source_target_pairs={{0,1},{1,0},{2,6},{3,7},{4,5},{5,4},{6,2},{7,3},{8,9},{9,8},{10,14... | collective-permute-start | bytes 3145736 | tf_op jit(solution)/shard_map/ppermute | solution.py:85
  195.3 7.5 %collective-permute-start.21 = (f32[576,1024]{1,0:T(8,128)}, f32[576,1024]{1,0:T(8,128)}, u32[]{:S(2)}, u32[]{:S(2)}) collective-permute-start(f32[576,1024]{1,0:T(8,128)} %feed_down.2.refs_6_), channel_id=1, source_target_pairs={{0,2},{1,3},{2,0},{3,1},{4,6},{5,7},{6,4},{7,5},{8,10},{9,11},{10,... | collective-permute-start | bytes 7077896 | tf_op jit(solution)/shard_map/ppermute | solution.py:95
  227.0 26.4 %collective-permute-start.25 = (bf16[1024,1024]{1,0:T(8,128)(2,1)}, bf16[1024,1024]{1,0:T(8,128)(2,1)}, u32[]{:S(2)}, u32[]{:S(2)}) collective-permute-start(bf16[1024,1024]{1,0:T(8,128)(2,1)} %get-tuple-element.131), channel_id=1, source_target_pairs={{0,1},{1,0},{2,6},{3,7},{4,5},{5,4},{6,2},{7,3},{8,9},{9,8},{10,14... | collective-permute-start | bytes 6291464 | tf_op jit(solution)/shard_map/ppermute | solution.py:85
  258.5 11.0 %collective-permute-start.26 = (f32[576,1024]{1,0:T(8,128)}, f32[576,1024]{1,0:T(8,128)}, u32[]{:S(2)}, u32[]{:S(2)}) collective-permute-start(f32[576,1024]{1,0:T(8,128)} %get-tuple-element.134), channel_id=1, source_target_pairs={{0,2},{1,3},{2,0},{3,1},{4,6},{5,7},{6,4},{7,5},{8,10},{9,11},{10,... | collective-permute-start | bytes 7077896 | tf_op jit(solution)/shard_map/ppermute | solution.py:95
  258.5 16.8 %collective-permute-start.27 = (bf16[512,1024]{1,0:T(8,128)(2,1)}, bf16[512,1024]{1,0:T(8,128)(2,1)}, u32[]{:S(2)}, u32[]{:S(2)}) collective-permute-start(bf16[512,1024]{1,0:T(8,128)(2,1)} %get-tuple-element.140), channel_id=1, source_target_pairs={{0,4},{1,5},{2,3},{3,2},{4,0},{5,1},{6,7},{7,6},{8,12},{9,13},{10,... | collective-permute-start | bytes 3145736 | tf_op jit(solution)/shard_map/ppermute | solution.py:85
  278.1 17.2 %collective-permute-start.28 = (bf16[576,1024]{1,0:T(8,128)(2,1)}, bf16[576,1024]{1,0:T(8,128)(2,1)}, u32[]{:S(2)}, u32[]{:S(2)}) collective-permute-start(bf16[576,1024]{1,0:T(8,128)(2,1)} %get-tuple-element.144.refs_10_.refs_6_), channel_id=1, source_target_pairs={{0,2},{1,3},{2,0},{3,1},{4,6},{5,7},{6,4},{7,5},{8,10},{9,11},{10,... | collective-permute-start | bytes 3538952 | tf_op jit(solution)/shard_map/ppermute | solution.py:95
  278.3 34.6 %collective-permute-start.29 = (bf16[512,2048]{1,0:T(8,128)(2,1)}, bf16[512,2048]{1,0:T(8,128)(2,1)}, u32[]{:S(2)}, u32[]{:S(2)}) collective-permute-start(bf16[512,2048]{1,0:T(8,128)(2,1)} %get-tuple-element.148), channel_id=1, source_target_pairs={{0,1},{1,0},{2,6},{3,7},{4,5},{5,4},{6,2},{7,3},{8,9},{9,8},{10,14... | collective-permute-start | bytes 6291464 | tf_op jit(solution)/shard_map/ppermute | solution.py:85
  279.9 31.2 %collective-permute-start.30 = (bf16[256,1024]{1,0:T(8,128)(2,1)}, bf16[256,1024]{1,0:T(8,128)(2,1)}, u32[]{:S(2)}, u32[]{:S(2)}) collective-permute-start(bf16[256,1024]{1,0:T(8,128)(2,1)} %get-tuple-element.149), channel_id=1, source_target_pairs={{0,8},{1,9},{2,10},{3,11},{4,12},{5,13},{6,14},{7,15},{8,0},{9,1},... | collective-permute-start | bytes 1572872 | tf_op jit(solution)/shard_map/ppermute | solution.py:85
  312.9 22.1 %collective-permute-start.34 = (bf16[128,1024]{1,0:T(8,128)(2,1)}, bf16[128,1024]{1,0:T(8,128)(2,1)}, u32[]{:S(2)}, u32[]{:S(2)}) collective-permute-start(bf16[128,1024]{1,0:T(8,128)(2,1)} %get-tuple-element.159), channel_id=1, source_target_pairs={{0,16},{1,17},{2,18},{3,19},{4,20},{5,21},{6,22},{7,23},{8,24},{9,... | collective-permute-start | bytes 786440 | tf_op jit(solution)/shard_map/ppermute | solution.py:85
  315.8 15.1 %collective-permute-start.31 = (bf16[256,2048]{1,0:T(8,128)(2,1)}, bf16[256,2048]{1,0:T(8,128)(2,1)}, u32[]{:S(2)}, u32[]{:S(2)}) collective-permute-start(bf16[256,2048]{1,0:T(8,128)(2,1)} %get-tuple-element.154), channel_id=1, source_target_pairs={{0,4},{1,5},{2,3},{3,2},{4,0},{5,1},{6,7},{7,6},{8,12},{9,13},{10,... | collective-permute-start | bytes 3145736 | tf_op jit(solution)/shard_map/ppermute | solution.py:85
  333.1 17.7 %collective-permute-start.32 = (bf16[512,1024]{1,0:T(8,128)(2,1)}, bf16[512,1024]{1,0:T(8,128)(2,1)}, u32[]{:S(2)}, u32[]{:S(2)}) collective-permute-start(bf16[512,1024]{1,0:T(8,128)(2,1)} %get-tuple-element.156), channel_id=1, source_target_pairs={{0,1},{1,0},{2,6},{3,7},{4,5},{5,4},{6,2},{7,3},{8,9},{9,8},{10,14... | collective-permute-start | bytes 3145736 | tf_op jit(solution)/shard_map/ppermute | solution.py:85
  333.6 12.8 %collective-permute-start.33 = (bf16[128,2048]{1,0:T(8,128)(2,1)}, bf16[128,2048]{1,0:T(8,128)(2,1)}, u32[]{:S(2)}, u32[]{:S(2)}) collective-permute-start(bf16[128,2048]{1,0:T(8,128)(2,1)} %get-tuple-element.157), channel_id=1, source_target_pairs={{0,8},{1,9},{2,10},{3,11},{4,12},{5,13},{6,14},{7,15},{8,0},{9,1},... | collective-permute-start | bytes 1572872 | tf_op jit(solution)/shard_map/ppermute | solution.py:85
  348.1 24.6 %collective-permute-start.36 = (bf16[64,2048]{1,0:T(8,128)(2,1)}, bf16[64,2048]{1,0:T(8,128)(2,1)}, u32[]{:S(2)}, u32[]{:S(2)}) collective-permute-start(bf16[64,2048]{1,0:T(8,128)(2,1)} %get-tuple-element.168), channel_id=1, source_target_pairs={{0,16},{1,17},{2,18},{3,19},{4,20},{5,21},{6,22},{7,23},{8,24},{9,... | collective-permute-start | bytes 786440 | tf_op jit(solution)/shard_map/ppermute | solution.py:85
  352.8 21.2 %collective-permute-start.35 = (bf16[512,1024]{1,0:T(8,128)(2,1)}, bf16[512,1024]{1,0:T(8,128)(2,1)}, u32[]{:S(2)}, u32[]{:S(2)}) collective-permute-start(bf16[512,1024]{1,0:T(8,128)(2,1)} %get-tuple-element.167), channel_id=1, source_target_pairs={{0,1},{1,0},{2,6},{3,7},{4,5},{5,4},{6,2},{7,3},{8,9},{9,8},{10,14... | collective-permute-start | bytes 3145736 | tf_op jit(solution)/shard_map/ppermute | solution.py:85
  354.1 15.2 %collective-permute-start.37 = (bf16[256,1024]{1,0:T(8,128)(2,1)}, bf16[256,1024]{1,0:T(8,128)(2,1)}, u32[]{:S(2)}, u32[]{:S(2)}) collective-permute-start(bf16[256,1024]{1,0:T(8,128)(2,1)} %get-tuple-element.169), channel_id=1, source_target_pairs={{0,4},{1,5},{2,3},{3,2},{4,0},{5,1},{6,7},{7,6},{8,12},{9,13},{10,... | collective-permute-start | bytes 1572872 | tf_op jit(solution)/shard_map/ppermute | solution.py:85
  377.4 23.6 %collective-permute-start.38 = (f32[576,1024]{1,0:T(8,128)}, f32[576,1024]{1,0:T(8,128)S(1)}, u32[]{:S(2)}, u32[]{:S(2)}) collective-permute-start(f32[576,1024]{1,0:T(8,128)} %get-tuple-element.173), channel_id=1, source_target_pairs={{0,2},{1,3},{2,0},{3,1},{4,6},{5,7},{6,4},{7,5},{8,10},{9,11},{10,... | collective-permute-start | bytes 7077896 | tf_op jit(solution)/shard_map/ppermute | solution.py:95
  377.5 6.9 %collective-permute-start.23 = (bf16[1,4,1024]{2,1,0:T(4,128)(2,1)S(1)}, bf16[1,4,1024]{2,1,0:T(4,128)(2,1)S(1)}, u32[]{:S(2)}, u32[]{:S(2)}) collective-permute-start(bf16[1,4,1024]{2,1,0:T(4,128)(2,1)S(1)} %broadcast_select_fusion.11), channel_id=1, source_target_pairs={{0,1},{1,0},{2,3},{3,2},{4,5},{5,4},{6,7},{7,6},{8,9},{9,8},{10,11... | collective-permute-start | bytes 24584 | tf_op jit(solution)/shard_map/ppermute | solution.py:85
  387.9 7.0 %collective-permute-start.48 = (f32[32,2048]{1,0:T(8,128)S(1)}, f32[32,2048]{1,0:T(8,128)}, u32[]{:S(2)}, u32[]{:S(2)}) collective-permute-start(f32[32,2048]{1,0:T(8,128)S(1)} %get-tuple-element.195), channel_id=1, source_target_pairs={{0,2},{1,3},{2,0},{3,1},{4,6},{5,7},{6,4},{7,5},{8,10},{9,11},{10,... | collective-permute-start | bytes 786440 | tf_op jit(solution)/shard_map/ppermute | solution.py:95
  390.5 29.9 %collective-permute-start.39 = (bf16[64,1024]{1,0:T(8,128)(2,1)}, bf16[64,1024]{1,0:T(8,128)(2,1)}, u32[]{:S(2)}, u32[]{:S(2)}) collective-permute-start(bf16[64,1024]{1,0:T(8,128)(2,1)} %copy-done.7), channel_id=1, source_target_pairs={{0,16},{1,17},{2,18},{3,19},{4,20},{5,21},{6,22},{7,23},{8,24},{9,... | collective-permute-start | bytes 393224 | tf_op jit(solution)/shard_map/ppermute | solution.py:85
  390.8 29.9 %collective-permute-start.40 = (bf16[64,1024]{1,0:T(8,128)(2,1)}, bf16[64,1024]{1,0:T(8,128)(2,1)}, u32[]{:S(2)}, u32[]{:S(2)}) collective-permute-start(bf16[64,1024]{1,0:T(8,128)(2,1)} %copy-done.6), channel_id=1, source_target_pairs={{0,8},{1,9},{2,10},{3,11},{4,12},{5,13},{6,14},{7,15},{8,0},{9,1},... | collective-permute-start | bytes 393224 | tf_op jit(solution)/shard_map/ppermute | solution.py:85
  392.2 28.4 %collective-permute-start.41 = (bf16[64,1024]{1,0:T(8,128)(2,1)}, bf16[64,1024]{1,0:T(8,128)(2,1)}, u32[]{:S(2)}, u32[]{:S(2)}) collective-permute-start(bf16[64,1024]{1,0:T(8,128)(2,1)} %copy-done.5), channel_id=1, source_target_pairs={{0,24},{1,25},{2,26},{3,27},{4,28},{5,29},{6,30},{7,31},{8,16},{9,... | collective-permute-start | bytes 393224 | tf_op jit(solution)/shard_map/ppermute | solution.py:85
  399.6 13.6 %collective-permute-start.42 = (bf16[256,1024]{1,0:T(8,128)(2,1)}, bf16[256,1024]{1,0:T(8,128)(2,1)}, u32[]{:S(2)}, u32[]{:S(2)}) collective-permute-start(bf16[256,1024]{1,0:T(8,128)(2,1)} %get-tuple-element.186), channel_id=1, source_target_pairs={{0,4},{1,5},{2,3},{3,2},{4,0},{5,1},{6,7},{7,6},{8,12},{9,13},{10,... | collective-permute-start | bytes 1572872 | tf_op jit(solution)/shard_map/ppermute | solution.py:85
  409.9 22.8 %all-to-all-start = ((f32[32,1,704]{2,1,0:T(1,128)}), f32[32,1,704]{2,1,0:T(1,128)}, u32[]{:S(2)}, u32[]{:S(2)}) async-start(f32[32,1,704]{2,1,0:T(1,128)} %all_to_all.6), calls=%async_computation | async-start | bytes 196608 | tf_op jit(solution)/shard_map/all_to_all | solution.py:1379
  416.3 10.9 %collective-permute-start.43 = (bf16[64,1024]{1,0:T(8,128)(2,1)}, bf16[64,1024]{1,0:T(8,128)(2,1)}, u32[]{:S(2)}, u32[]{:S(2)}) collective-permute-start(bf16[64,1024]{1,0:T(8,128)(2,1)} %get-tuple-element.189), channel_id=1, source_target_pairs={{0,16},{1,17},{2,18},{3,19},{4,20},{5,21},{6,22},{7,23},{8,24},{9,... | collective-permute-start | bytes 393224 | tf_op jit(solution)/shard_map/ppermute | solution.py:85
  418.9 8.3 %collective-permute-start.44 = (bf16[64,1024]{1,0:T(8,128)(2,1)}, bf16[64,1024]{1,0:T(8,128)(2,1)}, u32[]{:S(2)}, u32[]{:S(2)}) collective-permute-start(bf16[64,1024]{1,0:T(8,128)(2,1)} %get-tuple-element.190), channel_id=1, source_target_pairs={{0,8},{1,9},{2,10},{3,11},{4,12},{5,13},{6,14},{7,15},{8,0},{9,1},... | collective-permute-start | bytes 393224 | tf_op jit(solution)/shard_map/ppermute | solution.py:85
  420.4 9.5 %collective-permute-start.45 = (bf16[64,1024]{1,0:T(8,128)(2,1)}, bf16[64,1024]{1,0:T(8,128)(2,1)}, u32[]{:S(2)}, u32[]{:S(2)}) collective-permute-start(bf16[64,1024]{1,0:T(8,128)(2,1)} %get-tuple-element.191), channel_id=1, source_target_pairs={{0,24},{1,25},{2,26},{3,27},{4,28},{5,29},{6,30},{7,31},{8,16},{9,... | collective-permute-start | bytes 393224 | tf_op jit(solution)/shard_map/ppermute | solution.py:85
  422.4 9.4 %collective-permute-start.46 = (f32[32,1024]{1,0:T(8,128)}, f32[32,1024]{1,0:T(8,128)}, u32[]{:S(2)}, u32[]{:S(2)}) collective-permute-start(f32[32,1024]{1,0:T(8,128)} %get-tuple-element.193), channel_id=1, source_target_pairs={{0,2},{1,3},{2,0},{3,1},{4,6},{5,7},{6,4},{7,5},{8,10},{9,11},{10,... | collective-permute-start | bytes 393224 | tf_op jit(solution)/shard_map/ppermute | solution.py:95
  430.9 4.7 %collective-permute-start.47 = (f32[32,512]{1,0:T(8,128)S(1)}, f32[32,512]{1,0:T(8,128)S(1)}, u32[]{:S(2)}, u32[]{:S(2)}) collective-permute-start(f32[32,512]{1,0:T(8,128)S(1)} %get-tuple-element.278), channel_id=1, source_target_pairs={{0,2},{1,3},{2,0},{3,1},{4,6},{5,7},{6,4},{7,5},{8,10},{9,11},{10,... | collective-permute-start | bytes 196616 | tf_op jit(solution)/shard_map/ppermute | solution.py:95
  (87 other events, 408.0 us)

commit v3 on v2

--- a/solution.py
+++ b/solution.py
@@ -16,7 +16,7 @@
 F32 = jnp.float32
 
 
-def params(*semantics, vmem=44):
+def params(*semantics, vmem=50):
     return pltpu.CompilerParams(
         dimension_semantics=semantics or None, vmem_limit_bytes=vmem * 2**20
     )
@@ -117,10 +117,11 @@
         self.held, self.stage = wire, len(STAGES) - 1
         self.flying = [permute(wire, STAGES[self.stage])]
 
-    def advance(self, after=()):
-        self.held = stack(self.held, self.flying[0], after)
+    def advance(self, after=(), relay=()):
+        self.held, *copies = stack(self.held, self.flying[0], after, relay=relay)
         self.stage -= 1
         self.flying = [permute(self.held, STAGES[self.stage])]
+        return copies
 
     def last_of_held(self, *others):
         self.flying.append(permute(tie(self.held, *others), STAGES[0]))
@@ -212,6 +213,188 @@
         copy.wait()
 
 
+def add_parts(low, got, count):
+    step, cols = low.shape[0] // count, low.shape[1]
+    tile = cols // 2
+
+    def kernel(a_ref, b_ref, *outs):
+        for i, out in enumerate(outs):
+            part = slice(i * step, (i + 1) * step)
+            out[...] = (a_ref[part, :].astype(F32) + b_ref[part, :].astype(F32)).astype(BF)
+
+    return launch(
+        kernel,
+        grid=(2,),
+        in_specs=[pl.BlockSpec((count * step, tile), lambda n: (0, n))] * 2,
+        out_specs=[pl.BlockSpec((step, tile), lambda n: (0, n))] * count,
+        out_shape=[shape((step, cols), BF)] * count,
+        compiler_params=params("arbitrary", vmem=50),
+        cost_estimate=cost(0, 0),
+        name="add_parts",
+    )(low, got)
+
+
+def last_sum(low, parts):
+    half, cols = low.shape[0] // 2, low.shape[1]
+    tile = cols // 2
+
+    def kernel(low_ref, *refs):
+        for i, out in enumerate(refs[-2:]):
+            part = slice(i * half, (i + 1) * half)
+            out[...] = sum((ref[part, :].astype(F32) for ref in refs[:-2]), low_ref[part, :].astype(F32))
+
+    return launch(
+        kernel,
+        grid=(2,),
+        in_specs=[pl.BlockSpec((2 * half, tile), lambda n: (0, n))] * (1 + len(parts)),
+        out_specs=[pl.BlockSpec((half, tile), lambda n: (0, n))] * 2,
+        out_shape=[shape((half, cols), F32)] * 2,
+        compiler_params=params("arbitrary", vmem=50),
+        cost_estimate=cost(0, 0),
+        name="last_sum",
+    )(low, *parts)
+
+
+def pack_terms(core, one, two, learned, maps, queries, values, bias):
+    count, width = maps.shape
+    run = width // 16
+
+    def kernel(core_ref, one_ref, two_ref, learn_ref, map_ref, q_ref, v_ref, bias_ref, out_ref, wide, side, tall):
+        wide[...] = jnp.zeros_like(wide)
+        side[...] = jnp.zeros_like(side)
+        wide[:count, :] = map_ref[...]
+        wide[count : count + 2, :] = one_ref[...]
+        wide[count + 4 : count + 5, :] = two_ref[2:3, :]
+        wide[count + 5 : count + 7, :] = two_ref[0:2, :]
+        wide[count + 7 : count + 8, :] = learn_ref[2:3, :]
+        wide[count + 8 : count + 10, :] = learn_ref[0:2, :]
+        side[count + 2 : count + 3, :] = q_ref[0:1, :] + v_ref[0:1, :]
+        side[count + 3 : count + 4, :] = q_ref[1:2, :] + v_ref[1:2, :]
+        at = count + 10
+        side[at : at + bias_ref.shape[0], :] = bias_ref[...]
+        tall[...] = wide[...].T
+        half = side[...].T
+        for group in range(8):
+            start = pl.multiple_of((2 * group + core_ref[0]) * run, run)
+            tall[pl.ds(start, run), :] += half[group * run : (group + 1) * run]
+        out_ref[...] = tall[...].astype(BF)
+
+    vmem = pl.BlockSpec(memory_space=pltpu.VMEM)
+    return launch(
+        kernel,
+        in_specs=[TABLE] + [vmem] * 7,
+        out_specs=vmem,
+        out_shape=shape((width, 128), BF),
+        scratch_shapes=[
+            pltpu.VMEM((128, width), F32),
+            pltpu.VMEM((128, width // 2), F32),
+            pltpu.VMEM((width, 128), F32),
+        ],
+        compiler_params=params(vmem=50),
+        cost_estimate=cost(0, 0),
+        name="pack_terms",
+    )(core, one, two, learned, maps, queries, values, bias)
+
+
+def sum_terms(got, count, runs):
+    devices, own, lanes = got.shape
+
+    def kernel(got_ref, map_ref, rows_ref, bias_ref):
+        total = jnp.sum(got_ref[...].astype(F32), axis=0)
+        map_ref[...] = total[:, :count]
+        turned = jnp.concatenate([total, jnp.zeros((lanes - own, lanes), F32)], axis=0).T
+        rows_ref[...] = turned[count : count + 10, :own]
+        for j in range(runs):
+            at = count + 10 + j
+            bias_ref[:, j * own : (j + 1) * own] = turned[at : at + 1, :own]
+
+    vmem = pl.BlockSpec(memory_space=pltpu.VMEM)
+    return launch(
+        kernel,
+        in_specs=[vmem],
+        out_specs=[vmem] * 3,
+        out_shape=[shape((own, count), F32), shape((10, own), F32), shape((1, runs * own), F32)],
+        compiler_params=params(vmem=50),
+        cost_estimate=cost(0, 0),
+        name="sum_terms",
+    )(got)
+
+
+def stack(top, bottom, after=(), axis=0, relay=()):
+    tall, wide = top.shape
+    dims = (2 * tall, wide) if axis == 0 else (tall, 2 * wide)
+    count = len(relay)
+
+    def kernel(a_ref, b_ref, *refs):
+        out_ref = refs[count]
+        out_ref[:tall, :wide] = a_ref[...]
+        out_ref[dims[0] - tall :, dims[1] - wide :] = b_ref[...]
+        for source, target in zip(refs[:count], refs[count + 1 :]):
+            target[...] = source[...]
+
+    whole = lambda dims: pl.BlockSpec(dims, lambda i: (0, 0))
+    outs = [dims] + [part.shape for part in relay]
+    return launch(
+        kernel,
+        after=after,
+        grid=(1,),
+        in_specs=[whole(part.shape) for part in (top, bottom, *relay)],
+        out_specs=[whole(out) for out in outs],
+        out_shape=[shape(out, BF) for out in outs],
+        compiler_params=params("arbitrary", vmem=50),
+        cost_estimate=cost(0, 0),
+        name="stack",
+    )(top, bottom, *relay)
+
+
+def join_runs(core, pairs, unit):
+    rows = pairs[0][0].shape[0]
+    widths = [own.shape[1] for own, _ in pairs]
+    cols = 2 * sum(widths)
+
+    def kernel(core_ref, *refs):
+        out_ref, at = refs[-1], 0
+        first = core_ref[0] == 0
+        for i, width in enumerate(widths):
+            own, other = refs[2 * i][...], refs[2 * i + 1][...]
+            even, odd = jnp.where(first, own, other), jnp.where(first, other, own)
+            for j in range(width // unit):
+                cut = slice(j * unit, (j + 1) * unit)
+                both = jnp.concatenate([even[:, cut], odd[:, cut]], axis=1)
+                out_ref[:, at : at + 2 * unit] = both
+                at += 2 * unit
+
+    vmem = pl.BlockSpec(memory_space=pltpu.VMEM)
+    return launch(
+        kernel,
+        in_specs=[TABLE] + [vmem] * (2 * len(pairs)),
+        out_specs=vmem,
+        out_shape=shape((rows, cols), F32),
+        compiler_params=params(vmem=50),
+        cost_estimate=cost(0, 0),
+        name="join_runs",
+    )(core, *(part for pair in pairs for part in pair))
+
+
+def join_tokens(at, mine, got):
+    def kernel(at_ref, mine_ref, got_ref, out_ref):
+        first = at_ref[0] == 0
+        mine, got = mine_ref[...].astype(F32), got_ref[...].astype(F32)
+        out_ref[0:1] = jnp.where(first, mine, got)
+        out_ref[1:2] = jnp.where(first, got, mine)
+
+    vmem = pl.BlockSpec(memory_space=pltpu.VMEM)
+    return launch(
+        kernel,
+        in_specs=[TABLE, vmem, vmem],
+        out_specs=vmem,
+        out_shape=shape((2, *mine.shape[1:]), F32),
+        compiler_params=params(vmem=50),
+        cost_estimate=cost(0, 0),
+        name="join_tokens",
+    )(at, mine, got)
+
+
 def pack_small(vectors, bias, maps):
     own, count = maps.shape
     runs = bias.shape[0] // own
@@ -234,123 +417,10 @@
         in_specs=[pl.BlockSpec(memory_space=pltpu.VMEM)] * (len(vectors) + 2),
         out_shape=shape((own, 128), BF),
         scratch_shapes=[pltpu.VMEM((128, 128), F32)],
-        compiler_params=params(vmem=16),
+        compiler_params=params(vmem=50),
         cost_estimate=cost(0, 0),
         name="pack_small",
     )(*(vector.reshape(1, -1) for vector in vectors), bias.reshape(1, -1), maps)
-
-
-def add_parts(low, got, count):
-    step, cols = low.shape[0] // count, low.shape[1]
-    tile = cols // 2
-
-    def kernel(a_ref, b_ref, *outs):
-        for i, out in enumerate(outs):
-            part = slice(i * step, (i + 1) * step)
-            out[...] = (a_ref[part, :].astype(F32) + b_ref[part, :].astype(F32)).astype(BF)
-
-    return launch(
-        kernel,
-        grid=(2,),
-        in_specs=[pl.BlockSpec((count * step, tile), lambda n: (0, n))] * 2,
-        out_specs=[pl.BlockSpec((step, tile), lambda n: (0, n))] * count,
-        out_shape=[shape((step, cols), BF)] * count,
-        compiler_params=params("arbitrary", vmem=16),
-        cost_estimate=cost(0, 0),
-        name="add_parts",
-    )(low, got)
-
-
-def last_sum(low, parts):
-    half, cols = low.shape[0] // 2, low.shape[1]
-    tile = cols // 2
-
-    def kernel(low_ref, *refs):
-        for i, out in enumerate(refs[-2:]):
-            part = slice(i * half, (i + 1) * half)
-            out[...] = sum((ref[part, :].astype(F32) for ref in refs[:-2]), low_ref[part, :].astype(F32))
-
-    return launch(
-        kernel,
-        grid=(2,),
-        in_specs=[pl.BlockSpec((2 * half, tile), lambda n: (0, n))] * (1 + len(parts)),
-        out_specs=[pl.BlockSpec((half, tile), lambda n: (0, n))] * 2,
-        out_shape=[shape((half, cols), F32)] * 2,
-        compiler_params=params("arbitrary", vmem=16),
-        cost_estimate=cost(0, 0),
-        name="last_sum",
-    )(low, *parts)
-
-
-def stack(top, bottom, after=(), axis=0):
-    tall, wide = top.shape
-    whole = pl.BlockSpec((tall, wide), lambda i: (0, 0))
-    dims = (2 * tall, wide) if axis == 0 else (tall, 2 * wide)
-
-    def kernel(a_ref, b_ref, out_ref):
-        out_ref[:tall, :wide] = a_ref[...]
-        out_ref[dims[0] - tall :, dims[1] - wide :] = b_ref[...]
-
-    return launch(
-        kernel,
-        after=after,
-        grid=(1,),
-        in_specs=[whole, whole],
-        out_specs=pl.BlockSpec(dims, lambda i: (0, 0)),
-        out_shape=shape(dims, BF),
-        compiler_params=params("arbitrary", vmem=16),
-        cost_estimate=cost(0, 0),
-        name="stack",
-    )(top, bottom)
-
-
-def pack_small(vectors, bias, maps):
-    own, count = maps.shape
-    runs = bias.shape[0] // own
-
-    def kernel(*refs):
-        rows, (bias_ref, map_ref, out_ref, held) = refs[: len(vectors)], refs[len(vectors) :]
-        held[...] = jnp.zeros_like(held)
-        for i, ref in enumerate(rows):
-            held[count + i : count + i + 1, :own] = ref[...]
-        for j in range(runs):
-            at = count + len(vectors) + j
-            held[at : at + 1, :own] = bias_ref[:, j * own : (j + 1) * own]
-        turned = held[...].T[:own]
-        held[:own, :] = turned
-        held[:own, :count] = map_ref[...]
-        out_ref[...] = held[:own, :].astype(BF)
-
-    return launch(
-        kernel,
-        in_specs=[pl.BlockSpec(memory_space=pltpu.VMEM)] * (len(vectors) + 2),
-        out_shape=shape((own, 128), BF),
-        scratch_shapes=[pltpu.VMEM((128, 128), F32)],
-        compiler_params=params(vmem=16),
-        cost_estimate=cost(0, 0),
-        name="pack_small",
-    )(*(vector.reshape(1, -1) for vector in vectors), bias.reshape(1, -1), maps)
-
-
-def add_halves(low, got):
-    half, cols = low.shape[0] // 2, low.shape[1]
-    tile = cols // 2
-
-    def kernel(a_ref, b_ref, low_ref, high_ref):
-        total = a_ref[...].astype(F32) + b_ref[...].astype(F32)
-        low_ref[...] = total[:half].astype(BF)
-        high_ref[...] = total[half:].astype(BF)
-
-    return launch(
-        kernel,
-        grid=(2,),
-        in_specs=[pl.BlockSpec((2 * half, tile), lambda n: (0, n))] * 2,
-        out_specs=[pl.BlockSpec((half, tile), lambda n: (0, n))] * 2,
-        out_shape=[shape((half, cols), BF)] * 2,
-        compiler_params=params("arbitrary", vmem=16),
-        cost_estimate=cost(0, 0),
-        name="add_halves",
-    )(low, got)
 
 
 def small_rows(table, pieces, at):
@@ -372,7 +442,7 @@
         out_specs=pl.BlockSpec((128, total), lambda i: (0, 0)),
         out_shape=shape((128, total), F32),
         scratch_shapes=[pltpu.VMEM((total, 128), F32)],
-        compiler_params=params("arbitrary", vmem=16),
+        compiler_params=params("arbitrary", vmem=50),
         cost_estimate=cost(0, 0),
         name="small_rows",
     )(table, *pieces)
@@ -431,7 +501,7 @@
             pltpu.VMEM((width, cols), BF),
             pltpu.SemaphoreType.DMA((BLOCKS,)),
         ],
-        compiler_params=params("arbitrary"),
+        compiler_params=params("arbitrary", vmem=44),
         cost_estimate=cost(2 * rows * width * cols, 0),
         name="project",
     )(table, *pieces, patches, other, gain, shift, added, factor)
@@ -481,7 +551,7 @@
             shape((width, 2 * padded), BF),
             shape((pairs, 4, rows), F32),
         ],
-        compiler_params=params("arbitrary"),
+        compiler_params=params("arbitrary", vmem=44),
         cost_estimate=cost(16 * rows * tall * width, 0),
         name="attend",
     )(qkv, qkv, qkv, live)
@@ -546,7 +616,7 @@
         ],
         out_shape=[shape((3, rows, width), BF), shape((2, width), F32)],
         scratch_shapes=[pltpu.VMEM((width, full), BF), pltpu.SemaphoreType.DMA((BLOCKS,))],
-        compiler_params=params("arbitrary"),
+        compiler_params=params("arbitrary", vmem=44),
         cost_estimate=cost(40 * rows * rows * width, 0),
         name="attend_back",
     )(table, *pieces, qkv, qkv, qkv, live, totals, grad_attn)
@@ -571,7 +641,7 @@
         out_specs=pl.BlockSpec((rows, full), lambda i: (0, 0)),
         out_shape=shape((rows, full), F32),
         scratch_shapes=[pltpu.VMEM((width, full), BF), pltpu.SemaphoreType.DMA((BLOCKS,))],
-        compiler_params=params("arbitrary"),
+        compiler_params=params("arbitrary", vmem=44),
         cost_estimate=cost(2 * rows * width * full, 0),
         name="mix_out",
     )(table, *pieces, mixed)
@@ -594,7 +664,7 @@
         in_specs=[banded] * 3 + [fixed] * 3,
         out_specs=[banded] * 2,
         out_shape=[shape((rows, width), F32), shape((rows, width), BF)],
-        compiler_params=params("arbitrary"),
+        compiler_params=params("arbitrary", vmem=44),
         cost_estimate=cost(0, 0),
         name="second_norm",
     )(own, got, patches, bias, gain, shift)
@@ -647,7 +717,7 @@
             shape((width, padded), BF),
         ],
         scratch_shapes=[pltpu.VMEM((width, units), BF), pltpu.SemaphoreType.DMA((BLOCKS,))],
-        compiler_params=params("arbitrary"),
+        compiler_params=params("arbitrary", vmem=44),
         cost_estimate=cost(2 * rows * width * units, 0),
         name="feed_up",
     )(table, *pieces, hidden, bias)
@@ -668,7 +738,7 @@
         out_specs=pl.BlockSpec((rows, width), lambda i: (0, 0)),
         out_shape=shape((rows, width), F32),
         scratch_shapes=[pltpu.VMEM((units, width), BF), pltpu.SemaphoreType.DMA((BLOCKS,))],
-        compiler_params=params("arbitrary"),
+        compiler_params=params("arbitrary", vmem=44),
         cost_estimate=cost(2 * rows * width * units, 0),
         name="feed_down",
     )(table, *pieces, act)
@@ -735,7 +805,7 @@
             pltpu.VMEM((units, width), BF),
             pltpu.SemaphoreType.DMA((2, BLOCKS)),
         ],
-        compiler_params=params("arbitrary"),
+        compiler_params=params("arbitrary", vmem=44),
         cost_estimate=cost(4 * tall * width * units, 0),
         name="feed_back",
     )(*tables, *up, *down, grad, other, slope, other_slope)
@@ -828,7 +898,7 @@
             shape((3, width), F32),
         ],
         scratch_shapes=[pltpu.VMEM((2 * count, width), F32), pltpu.VMEM((1, 2 * count), F32)],
-        compiler_params=params("arbitrary"),
+        compiler_params=params("arbitrary", vmem=44),
         cost_estimate=cost(10 * 10**9, 14 * rows * width),
         name="token_learner",
     )(residual, own, got, bias, cotangent, live, token_grad, map_t, scale, offset)
@@ -870,7 +940,7 @@
         in_specs=[banded] * 4 + [fixed(1)],
         out_specs=[banded, banded, fixed(3)],
         out_shape=[shape((rows, width), F32), shape((rows, width), BF), shape((3, width), F32)],
-        compiler_params=params("arbitrary"),
+        compiler_params=params("arbitrary", vmem=44),
         cost_estimate=cost(0, 0),
         name="second_norm_back",
     )(own, got, residual, grad_block, gain)
@@ -915,7 +985,7 @@
             pltpu.VMEM((full, parts * width), BF),
             pltpu.SemaphoreType.DMA((BLOCKS,)),
         ],
-        compiler_params=params("arbitrary"),
+        compiler_params=params("arbitrary", vmem=44),
         cost_estimate=cost(6 * tall * width * full, 0),
         name="project_back",
     )(table, *pieces, grad_qkv, other_qkv)
@@ -955,7 +1025,7 @@
         in_specs=[banded(width)] * 3 + [banded(2), fixed(1), banded(width)],
         out_specs=[banded(width), fixed(2)],
         out_shape=[shape((rows, width), BF), shape((2, width), F32)],
-        compiler_params=params("arbitrary"),
+        compiler_params=params("arbitrary", vmem=44),
         cost_estimate=cost(0, 0),
         name="first_norm_back",
     )(own, got, patches, stats, gain, grad_residual)
@@ -1036,7 +1106,7 @@
             pltpu.VMEM((deep, tile), BF),
             pltpu.SemaphoreType.DMA((len(turned), blocks)),
         ],
-        compiler_params=params("arbitrary"),
+        compiler_params=params("arbitrary", vmem=44),
         cost_estimate=cost(2 * deep * height * cols, 0),
         name="weight_grad",
     )(table, *turned, *rights)
@@ -1084,7 +1154,7 @@
             pltpu.SemaphoreType.DMA((1, BLOCKS)),
             pltpu.SemaphoreType.DMA((1, BLOCKS // 2)),
         ],
-        compiler_params=params("arbitrary"),
+        compiler_params=params("arbitrary", vmem=44),
         cost_estimate=cost(4 * deep * height * width, 0),
         name="value_and_out_grad",
     )(*tables, turned, mixed_turned, *grad_qkv, *grad_attn)
@@ -1174,15 +1244,19 @@
         near.advance()
         near.advance()
         near.last_of_held()
-        up = Doubling(stack(up_own, to_sibling(up_other)))
+        up = Doubling(stack(up_own, to_sibling(up_other))[0])
         other_inputs = to_sibling(tie(inputs, up.held))
         near.last(near.flying[1])
         up.advance(near.flying)
         near_full = near.pieces
         up.advance((near_full[3],))
         up.last_of_held()
-        down = Doubling(stack(down_low[: 2 * own], down_low[2 * own :], axis=1))
-        token_grad = swap_map(tie(token_cotangent, near_full[3]), axis=0)
+        down = Doubling(stack(down_low[: 2 * own], down_low[2 * own :], axis=1)[0])
+        first, second = token_cotangent[0:1], token_cotangent[1:2]
+        place = lax.axis_index("map")
+        token_mine = jnp.where(place == 0, first, second)
+        token_got = permute(jnp.where(place == 0, second, first), BOTH(MAP))
+        where = place.reshape(1).astype(jnp.int32)
     else:
         whole = lambda wire: lax.all_gather(wire, AXES, axis=0, tiled=True)
         pick = lambda values: halves(values, core, 1, values.shape[1] // 2)[0]
@@ -1203,6 +1277,7 @@
         token_grad = lax.all_to_all(
             token_cotangent, "map", split_axis=0, concat_axis=1, tiled=True
         )
+        token_grad = token_grad.reshape(count, width).astype(F32)
 
     small_t = small_rows(table, near_full, 3 * side)
     (
@@ -1222,7 +1297,6 @@
     up_shift = halves(up_shift, core, BLOCKS // 4, unit)[0]
     map_t = small_t[:count]
     mine = lambda row: halves(row, core, heads // 2, HD)[0]
-    token_grad = token_grad.reshape(count, width).astype(F32)
 
     added = jnp.concatenate(
         [mine(query_shift), jnp.zeros((1, side), F32), mine(value_shift)], axis=1
@@ -1231,17 +1305,18 @@
     qkv, hidden_one_t, stats = project(
         table, near_full, inputs, other_inputs, gain_one, shift_one, added, factor
     )
+    if layered:
+        token_grad = join_tokens(where, token_mine, token_got).reshape(count, width)
+        up.flying[0] = down.advance(up.flying[1:], up.flying[:1])[0]
+        up.last()
+        up_full = up.pieces
     mixed, mixed_t, totals = attend(qkv, lives)
-    if layered:
-        down.advance(up.flying)
-        up.last(down.held)
-        up_full = up.pieces
-    mixed_other = mix_out(own_table, near_full, mixed, 1)
-    mixed_own = mix_out(own_table, near_full, mixed, 0)
     if layered:
         down.advance((up_full[3],))
         down.last_of_held()
-    mixed_got = to_sibling(tie(mixed_other, mixed_own, *([down.held] if layered else [])))
+    mixed_other = mix_out(own_table, near_full, mixed, 1)
+    mixed_got = to_sibling(mixed_other)
+    mixed_own = mix_out(own_table, near_full, mixed, 0)
     residual_one, hidden_two = second_norm(
         mixed_own, mixed_got, inputs, out_shift, gain_two, shift_two
     )
@@ -1268,12 +1343,16 @@
     other_down = to_sibling(grad_down_low)
     token_local = token_local.reshape(images, count, width).astype(BF)
     if layered:
-        tokens_out = swap_map(token_local, axis=1)
+        cut = token_local.astype(F32)
+        low, high = cut[:, : count // 2], cut[:, count // 2 :]
+        token_mine, token_send = jnp.where(place == 0, low, high), jnp.where(place == 0, high, low)
+        token_got = permute(token_send, BOTH(MAP))
     else:
         tokens_out = lax.all_to_all(token_local, "map", split_axis=1, concat_axis=0, tiled=True)
     down_parts = weight_grad(own_table, [act_t, act_t_b], [grad_down_low, other_down])
     if layered:
         down_sum = Halving(down_parts)
+        tokens_out = join_tokens(where, token_mine, token_got).astype(BF)
     grad_pre, up_sums, hidden_own, hidden_other = feed_back(
         (table, own_table), up_full, down_full, grad_down_low, other_down, slope, slope_b
     )
@@ -1295,7 +1374,7 @@
     back = lambda grad, image: attend_back(own_table, near_full, qkv, lives, totals, grad, image)
     qkv_a, sums_a = back(grad_attn, 0)
     qkv_b, sums_b = back(other_attn, 1)
-    grad_qkv, qv_sums = [qkv_a, qkv_b], sums_a + sums_b
+    grad_qkv = [qkv_a, qkv_b]
     if layered:
         down_sum.advance()
         up_sum.advance()
@@ -1324,19 +1403,23 @@
     grad_patches, one_sums = first_norm_back(
         one_own, one_got, inputs, stats, gain_one, grad_residual
     )
+    runs = up_sums.reshape(16, fan, -1).transpose(1, 0, 2).reshape(fan, -1)
+    which = core.reshape(1).astype(jnp.int32)
     if layered:
+        swap = lambda total: (total[0], to_sibling(total[1]))
+        up_pair = swap(grad_up)
         far_sum.advance()
-        grad_qk = near_sum.finish()
-        swap = lambda total: (total[0], to_sibling(total[1]))
+    terms = pack_terms(which, one_sums, two_sums, sums, grad_map, sums_a, sums_b, runs)
+    terms = lax.all_to_all(terms.reshape(devices, own, 128), AXES, 0, 0, tiled=True)
+    if layered:
+        qk_pair = swap(near_sum.finish())
         grad_down = jnp.concatenate(grad_down, axis=0)
-        grad_up = joined(*swap(grad_up), core, BLOCKS // 4, unit)
-        own_qk, other_qk = swap(grad_qk)
+        grad_up = join_runs(which, [up_pair], unit)
         grad_far = far_sum.finish()
+        v_pair = swap([part[:, :side] for part in grad_far])
+        map_piece, pieces, up_piece = sum_terms(terms, count, fan)
         grad_out = jnp.concatenate([grad_far[0][:, side:], grad_far[1][:, side:]], axis=1)
-        own_v, other_v = swap([part[:, :side] for part in grad_far])
-        own_qkv = jnp.concatenate([own_qk, own_v], axis=1)
-        other_qkv = jnp.concatenate([other_qk, other_v], axis=1)
-        grad_qkv_full = joined(own_qkv, other_qkv, core, 3 * heads // 2, HD)
+        grad_qkv_full = join_runs(which, [qk_pair, v_pair], HD)
     else:
 
         def scatter(parts, groups, unit):
@@ -1358,29 +1441,9 @@
         qkv_parts = [jnp.concatenate([*near_parts], axis=0), far[:, :side]]
         qkv_parts = [jnp.concatenate(qkv_parts, axis=1)]
         grad_qkv_full = shared(scatter(qkv_parts, 3 * heads // 2, HD))
-
-    spread = lambda row, unit: joined(row, jnp.zeros_like(row), core, row.shape[1] // unit, unit)
-    terms = (
-        one_sums[0:1],
-        one_sums[1:2],
-        spread(qv_sums[0:1], HD),
-        spread(qv_sums[1:2], HD),
-        two_sums[2:3],
-        two_sums[0:1],
-        two_sums[1:2],
-        sums[2:3],
-        sums[0:1],
-        sums[1:2],
-        spread(up_sums, unit),
-    )
-    packed = [term.reshape(devices, -1) for term in terms]
-    packed.append(grad_map.reshape(count, devices, own).transpose(1, 2, 0).reshape(devices, -1))
-    packed = jnp.concatenate(packed, axis=1)
-    summed = jnp.sum(lax.all_to_all(packed, AXES, 0, 0, tiled=True), axis=0)
-    pieces = [summed[i * own : (i + 1) * own] for i in range(10)]
-    at = 10 * own
-    up_piece = summed[at : at + fan * own]
-    map_piece = summed[at + fan * own :].reshape(own, count)
+        map_piece, pieces, up_piece = sum_terms(terms, count, fan)
+
+    up_piece = up_piece.reshape(-1)
     return (
         block_out.reshape(images, patch_count, width),
         tokens_out,

time: 445 us -> 416 us (0.935)
  waiting for transfers between devices: 96.3 us -> 73.7 us
  local copies, waits for them, and re-layouts: 54.7 us -> 32.2 us
  Pallas kernels: 222 us -> 234 us
  starting transfers between devices: 52.9 us -> 58.9 us
    ppermute x35, waiting for transfers between devices: 93.9 us -> 72 us  [permute(): return lax.ppermute(values, AXES, pairs)]
    reshape x14 -> x4, local copies, waits for them, and re-layouts: 11.9 us -> 0.19 us  [the longest x3 0.17 us: per_device(): runs = up_sums.reshape(16, fan, -1).transpose(1, 0, 2).reshape(fan, -1)]
    pallas_call x44 -> x50, Pallas kernels: 222 us -> 234 us  [run(): outs = pl.pallas_call(body, in_specs=specs, **settings)(*operands, *waited)]
    unnamed x177 -> x168, local copies, waits for them, and re-layouts: 31.1 us -> 23.8 us
    ppermute x35, starting transfers between devices: 48 us -> 53.5 us  [permute(): return lax.ppermute(values, AXES, pairs)]
  transfers between devices with their start and end apart: 50 -> 50, of which waited for: 18 -> 16; matrix products, arithmetic and copies ran while one was open for 7% -> 4% of each run, Pallas kernels for 43% -> 50%
where the time goes in v3:
time: 416 us; the launch traced here: 409 us
  Pallas kernels  234 us (56%)
  waiting for transfers between devices  73.7 us (18%)
  starting transfers between devices  58.9 us (14%)
  local copies, waits for them, and re-layouts  32.2 us (8%)
  other arithmetic  8.74 us (2%)
    pallas_call x50, Pallas kernels, run(): outs = pl.pallas_call(body, in_specs=specs, **settings)(*operands, *waited)  234 us
    ppermute x35, waiting for transfers between devices, permute(): return lax.ppermute(values, AXES, pairs)  72 us
    ppermute x35, starting transfers between devices, permute(): return lax.ppermute(values, AXES, pairs)  53.5 us
    unnamed x168, local copies, waits for them, and re-layouts  23.8 us
  transfers between devices with their start and end apart: 50, of which 16 were waited for; matrix products, arithmetic and copies ran while one was open for 4% of the time, Pallas kernels for 50%

profile of v3, /device:TPU:0, one launch (start us, length us, event | category | flops | bytes accessed | tf_op | source)
XLA Modules:
  0.0 409.4 jit_solution(15974055873195655337)
XLA Ops:
  6.8 4.0 collective-permute-start.1
  12.2 11.6 %collective-permute-done.1.refs_1_ = bf16[64,2176]{1,0:T(8,128)(2,1)S(1)} collective-permute-done((bf16[64,2176]{1,0:T(8,128)(2,1)S(1)}, bf16[64,2176]{1,0:T(8,128)(2,1)S(1)}, u32[]{:S(2)}, u32[]{:S(2)}) %collective-permute-start.1) | collective-permute-done | bytes 278560 | tf_op jit(solution)/shard_map/ppermute | solution.py:85
  29.1 9.0 %collective-permute-done.2.refs_1_ = bf16[128,2176]{1,0:T(8,128)(2,1)S(1)} collective-permute-done((bf16[128,2176]{1,0:T(8,128)(2,1)S(1)}, bf16[128,2176]{1,0:T(8,128)(2,1)S(1)}, u32[]{:S(2)}, u32[]{:S(2)}) %collective-permute-start.2) | collective-permute-done | bytes 557088 | tf_op jit(solution)/shard_map/ppermute | solution.py:85
  42.9 3.1 collective-permute-start.8
  46.6 18.7 %collective-permute-done.3.refs_3_.refs_2_ = bf16[256,2176]{1,0:T(8,128)(2,1)} collective-permute-done((bf16[256,2176]{1,0:T(8,128)(2,1)}, bf16[256,2176]{1,0:T(8,128)(2,1)}, u32[]{:S(2)}, u32[]{:S(2)}) %collective-permute-start.3) | collective-permute-done | bytes 1114144 | tf_op jit(solution)/shard_map/ppermute | solution.py:85
  70.2 10.3 %collective-permute-done.9.refs_1_ = bf16[128,2048]{1,0:T(8,128)(2,1)S(1)} collective-permute-done((bf16[128,2048]{1,0:T(8,128)(2,1)S(1)}, bf16[128,2048]{1,0:T(8,128)(2,1)S(1)}, u32[]{:S(2)}, u32[]{:S(2)}) %collective-permute-start.9) | collective-permute-done | bytes 524320 | tf_op jit(solution)/shard_map/ppermute | solution.py:85
  84.4 4.1 %collective-permute-start.11 = (bf16[64,2048]{1,0:T(8,128)(2,1)}, bf16[64,2048]{1,0:T(8,128)(2,1)}, u32[]{:S(2)}, u32[]{:S(2)}) collective-permute-start(bf16[64,2048]{1,0:T(8,128)(2,1)} %stack.19.refs_5_.refs_0_), channel_id=1, source_target_pairs={{0,16},{1,17},{2,18},{3,19},{4,20},{5,21},{6,22},{7,23},{8,24},{9,... | collective-permute-start | bytes 786440 | tf_op jit(solution)/shard_map/ppermute | solution.py:85
  90.7 11.5 %project.1 = (bf16[1152,1536]{1,0:T(8,128)(2,1)}, bf16[1024,1280]{1,0:T(8,128)(2,1)S(1)}, f32[576,2]{1,0:T(8,128)S(1)}) custom-call(s32[32]{0:T(128)S(1)} %reshape.301.refs_0_, bf16[256,2176]{1,0:T(8,128)(2,1)} %stack.15.refs_2_.refs_1_, bf16[256,2176]{1,0:T(8,128)(2,1)} %collective-permute-done.3.refs_3_.refs_2_, ...), custom_call_target="tpu_custom_call" | custom-call | flops 999999995904 | bytes 1024 | tf_op jit(solution)/shard_map/project/pallas_call | solution.py:40
  103.8 2.0 copy-done.22
  108.4 2.7 stack.20
  114.1 14.0 %attend.1 = (bf16[1152,512]{1,0:T(8,128)(2,1)S(1)}, bf16[512,1280]{1,0:T(8,128)(2,1)S(1)}, f32[4,4,576]{2,1,0:T(4,128)S(1)}) custom-call(bf16[1152,1536]{1,0:T(8,128)(2,1)S(1)} %copy-done.23, bf16[1152,1536]{1,0:T(8,128)(2,1)S(1)} %copy-done.23, bf16[1152,1536]{1,0:T(8,128)(2,1)S(1)} %copy-done.23, f32[1152,1]{1,0:T(8,128)S(1)} %copy.76.refs_3_.refs_8_, ...), custom_call_target="tpu_custom_call" | custom-call | flops 999999995904 | bytes 1024 | tf_op jit(solution)/shard_map/attend/pallas_call | solution.py:40
  130.1 2.4 stack.21.refs_6_.refs_1_
  133.0 4.2 %mix_out.2.refs_6_ = f32[576,1024]{1,0:T(8,128)} custom-call(s32[16]{0:T(128)S(1)} %and_add_fusion.refs_0_.refs_1_, bf16[256,2176]{1,0:T(8,128)(2,1)} %stack.15.refs_2_.refs_1_, bf16[256,2176]{1,0:T(8,128)(2,1)} %collective-permute-done.3.refs_3_.refs_2_, bf16[256,2176]{1,0:T(8,128)(2,1)} %collective-permute-done.4.refs_4_.refs_3_, ...), custom_call_target="tpu_custom_call" | custom-call | flops 999999995904 | bytes 1024 | tf_op jit(solution)/shard_map/mix_out/pallas_call | solution.py:40
  138.7 2.8 mix_out.3.refs_0_.refs_6_
  142.1 3.3 second_norm.1
  147.0 10.3 %feed_up.2 = (bf16[576,2048]{1,0:T(8,128)(2,1)S(1)}, bf16[2048,640]{1,0:T(8,128)(2,1)}, bf16[576,2048]{1,0:T(8,128)(2,1)}, bf16[1024,640]{1,0:T(8,128)(2,1)S(1)}) custom-call(s32[32]{0:T(128)S(1)} %reshape.301.refs_0_, bf16[256,2048]{1,0:T(8,128)(2,1)} %stack.18.refs_2_.refs_1_, bf16[256,2048]{1,0:T(8,128)(2,1)} %get-tuple-element.115.refs_2_.refs_3_, ...), custom_call_target="tpu_custom_call" | custom-call | flops 999999995904 | bytes 1024 | tf_op jit(solution)/shard_map/feed_up/pallas_call | solution.py:40
  161.1 10.6 %feed_up.3 = (bf16[576,2048]{1,0:T(8,128)(2,1)S(1)}, bf16[2048,640]{1,0:T(8,128)(2,1)}, bf16[576,2048]{1,0:T(8,128)(2,1)}, bf16[1024,640]{1,0:T(8,128)(2,1)S(1)}) custom-call(s32[32]{0:T(128)S(1)} %reshape.301.refs_0_, bf16[256,2048]{1,0:T(8,128)(2,1)} %stack.18.refs_2_.refs_1_, bf16[256,2048]{1,0:T(8,128)(2,1)} %get-tuple-element.115.refs_2_.refs_3_, ...), custom_call_target="tpu_custom_call" | custom-call | flops 999999995904 | bytes 1024 | tf_op jit(solution)/shard_map/feed_up/pallas_call | solution.py:40
  171.8 3.2 collective-permute-done.20.refs_4_.refs_9_
  175.0 7.3 %feed_down.2.refs_6_ = f32[576,1024]{1,0:T(8,128)} custom-call(s32[16]{0:T(128)S(1)} %and_add_fusion.refs_0_.refs_1_, bf16[256,2048]{1,0:T(8,128)(2,1)} %stack.21.refs_6_.refs_1_, bf16[256,2048]{1,0:T(8,128)(2,1)} %collective-permute-done.18.refs_2_.refs_7_, bf16[256,2048]{1,0:T(8,128)(2,1)} %collective-permute-done.19.refs_3_.refs_8_, ...), custom_call_target="tpu_custom_call" | custom-call | flops 999999995904 | bytes 1024 | tf_op jit(solution)/shard_map/feed_down/pallas_call | solution.py:40
  182.4 5.9 %feed_down.3.refs_1_.refs_10_ = f32[576,1024]{1,0:T(8,128)S(1)} custom-call(s32[16]{0:T(128)S(1)} %and_add_fusion.refs_0_.refs_1_, bf16[256,2048]{1,0:T(8,128)(2,1)} %stack.21.refs_6_.refs_1_, bf16[256,2048]{1,0:T(8,128)(2,1)} %collective-permute-done.18.refs_2_.refs_7_, bf16[256,2048]{1,0:T(8,128)(2,1)} %collective-permute-done.19.refs_3_.refs_8_, ...), custom_call_target="tpu_custom_call" | custom-call | flops 999999995904 | bytes 1024 | tf_op jit(solution)/shard_map/feed_down/pallas_call | solution.py:40
  188.4 6.9 %token_learner.1 = (bf16[576,1024]{1,0:T(8,128)(2,1)}, f32[8,1024]{1,0:T(8,128)S(1)}, f32[576,1024]{1,0:T(8,128)S(1)}, bf16[576,1024]{1,0:T(8,128)(2,1)S(1)}, f3...) custom-call(f32[576,1024]{1,0:T(8,128)S(1)} %copy-done.31, f32[576,1024]{1,0:T(8,128)S(1)} %feed_down.3.refs_1_.refs_10_, ...), custom_call_target="tpu_custom_call" | custom-call | flops 999999995904 | bytes 1024 | tf_op jit(solution)/shard_map/token_learner/pallas_call | solution.py:40
  199.9 9.5 %weight_grad.3 = (bf16[1024,1024]{1,0:T(8,128)(2,1)S(1)}, bf16[1024,1024]{1,0:T(8,128)(2,1)}) custom-call(s32[16]{0:T(128)S(1)} %and_add_fusion.refs_0_.refs_1_, bf16[2048,640]{1,0:T(8,128)(2,1)S(1)} %copy-done.26, bf16[2048,640]{1,0:T(8,128)(2,1)} %get-tuple-element.124.refs_2_, bf16[576,1024]{1,0:T(8,128)(2,1)S(1)} %get-tuple-element.125.refs_3_.refs_10_, ...), custom_call_target="tpu_custom_call" | custom-call | flops 999999995904 | bytes 1024 | tf_op jit(solution)/shard_map/weight_grad/pallas_call | solution.py:40
  211.5 21.2 %feed_back.1 = (bf16[1152,2048]{1,0:T(8,128)(2,1)}, f32[1,2048]{1,0:T(1,128)S(1)}, f32[576,1024]{1,0:T(8,128)}, f32[576,1024]{1,0:T(8,128)}) custom-call(s32[32]{0:T(128)S(1)} %reshape.301.refs_0_, s32[16]{0:T(128)S(1)} %and_add_fusion.refs_0_.refs_1_, bf16[256,2048]{1,0:T(8,128)(2,1)} %stack.18.refs_2_.refs_1_, ...), custom_call_target="tpu_custom_call" | custom-call | flops 999999995904 | bytes 1024 | tf_op jit(solution)/shard_map/feed_back/pallas_call | solution.py:40
  232.7 3.2 collective-permute-done.25.refs_1_
  235.9 3.4 add_parts.10
  240.9 10.5 %weight_grad.4 = (bf16[512,2048]{1,0:T(8,128)(2,1)S(1)}, bf16[512,2048]{1,0:T(8,128)(2,1)}) custom-call(s32[32]{0:T(128)S(1)} %reshape.301.refs_0_, bf16[1024,640]{1,0:T(8,128)(2,1)S(1)} %copy-done.46, bf16[1024,640]{1,0:T(8,128)(2,1)S(1)} %copy-done.48, bf16[1152,2048]{1,0:T(8,128)(2,1)} %get-tuple-element.133.refs_2_.refs_3_, ...), custom_call_target="tpu_custom_call" | custom-call | flops 999999995904 | bytes 1024 | tf_op jit(solution)/shard_map/weight_grad/pallas_call | solution.py:40
  251.4 6.3 %second_norm_back.1 = (f32[576,1024]{1,0:T(8,128)S(1)}, bf16[576,1024]{1,0:T(8,128)(2,1)}, f32[3,1024]{1,0:T(4,128)S(1)}) custom-call(f32[576,1024]{1,0:T(8,128)S(1)} %copy-done.27, f32[576,1024]{1,0:T(8,128)} %collective-permute-done.26.refs_1_, f32[576,1024]{1,0:T(8,128)} %copy-done.30, f32[576,1024]{1,0:T(8,128)} %copy-done.32, ...), custom_call_target="tpu_custom_call" | custom-call | flops 999999995904 | bytes 1024 | tf_op jit(solution)/shard_map/second_norm_back/pallas_call | solution.py:40
  259.1 2.1 add_parts.11
  262.5 14.9 %attend_back.2 = (bf16[3,576,512]{2,1,0:T(8,128)(2,1)S(1)}, f32[2,512]{1,0:T(2,128)S(1)}) custom-call(s32[16]{0:T(128)S(1)} %and_add_fusion.refs_0_.refs_1_, bf16[256,2176]{1,0:T(8,128)(2,1)} %stack.15.refs_2_.refs_1_, bf16[256,2176]{1,0:T(8,128)(2,1)} %collective-permute-done.3.refs_3_.refs_2_, bf16[256,2176]{1,0:T(8,128)(2,1)} %collective-permute-done.4.refs_4_.refs_3_, ...), custom_call_target="tpu_custom_call" | custom-call | flops 999999995904 | bytes 1024 | tf_op jit(solution)/shard_map/attend_back/pallas_call | solution.py:40
  277.5 15.5 %attend_back.3 = (bf16[3,576,512]{2,1,0:T(8,128)(2,1)S(1)}, f32[2,512]{1,0:T(2,128)S(1)}) custom-call(s32[16]{0:T(128)S(1)} %and_add_fusion.refs_0_.refs_1_, bf16[256,2176]{1,0:T(8,128)(2,1)} %stack.15.refs_2_.refs_1_, bf16[256,2176]{1,0:T(8,128)(2,1)} %collective-permute-done.3.refs_3_.refs_2_, bf16[256,2176]{1,0:T(8,128)(2,1)} %collective-permute-done.4.refs_4_.refs_3_, ...), custom_call_target="tpu_custom_call" | custom-call | flops 999999995904 | bytes 1024 | tf_op jit(solution)/shard_map/attend_back/pallas_call | solution.py:40
  293.0 2.2 add_parts.12
  295.1 3.9 collective-permute-start.34
  299.0 3.4 add_parts.13
  303.8 8.7 %weight_grad.5 = (bf16[512,1024]{1,0:T(8,128)(2,1)S(1)}, bf16[512,1024]{1,0:T(8,128)(2,1)}) custom-call(s32[32]{0:T(128)S(1)} %reshape.301.refs_0_, bf16[1024,1280]{1,0:T(8,128)(2,1)S(1)} %copy-done.25, bf16[3,576,512]{2,1,0:T(8,128)(2,1)S(1)} %copy-done.40, bf16[3,576,512]{2,1,0:T(8,128)(2,1)S(1)} %copy-done.42, ...), custom_call_target="tpu_custom_call" | custom-call | flops 999999995904 | bytes 1024 | tf_op jit(solution)/shard_map/weight_grad/pallas_call | solution.py:40
  313.4 4.1 %collective-permute-done.31.refs_1_ = bf16[256,2048]{1,0:T(8,128)(2,1)} collective-permute-done((bf16[256,2048]{1,0:T(8,128)(2,1)}, bf16[256,2048]{1,0:T(8,128)(2,1)}, u32[]{:S(2)}, u32[]{:S(2)}) %collective-permute-start.31) | collective-permute-done | bytes 1048608 | tf_op jit(solution)/shard_map/ppermute | solution.py:85
  317.6 2.1 add_parts.14
  324.2 8.4 %value_and_out_grad.1 = (bf16[512,1024]{1,0:T(8,128)(2,1)S(1)}, bf16[512,1024]{1,0:T(8,128)(2,1)}) custom-call(s32[32]{0:T(128)S(1)} %reshape.301.refs_0_, s32[16]{0:T(128)S(1)} %and_add_fusion.refs_0_.refs_1_, bf16[1024,1280]{1,0:T(8,128)(2,1)} %copy-done.24, bf16[512,1280]{1,0:T(8,128)(2,1)S(1)} %copy-done.44, bf16[3,576,512]{2,1,0:T(8,128)(2,1)S(1)} %copy-done.40, ...), custom_call_target="tpu_custom_call" | custom-call | flops 999999995904 | bytes 1024 | tf_op jit(solution)/shard_map/value_and_out_grad/pallas_call | solution.py:40
  332.7 2.2 add_parts.15
  336.3 2.1 add_parts.16
  340.5 10.3 %project_back.1 = (f32[576,1024]{1,0:T(8,128)}, f32[576,1024]{1,0:T(8,128)}) custom-call(s32[32]{0:T(128)S(1)} %reshape.301.refs_0_, bf16[256,2176]{1,0:T(8,128)(2,1)} %stack.15.refs_2_.refs_1_, bf16[256,2176]{1,0:T(8,128)(2,1)} %collective-permute-done.3.refs_3_.refs_2_, bf16[256,2176]{1,0:T(8,128)(2,1)} %collective-permute-done.4.refs_4_.refs_3_, ...), custom_call_target="tpu_custom_call" | custom-call | flops 999999995904 | bytes 1024 | tf_op jit(solution)/shard_map/project_back/pallas_call | solution.py:40
  350.9 2.7 collective-permute-done.37.refs_1_
  359.0 2.2 add_parts.18
  366.4 2.0 collective-permute-start.46
  373.0 4.6 %first_norm_back.1 = (bf16[576,1024]{1,0:T(8,128)(2,1)}, f32[2,1024]{1,0:T(2,128)S(1)}) custom-call(f32[576,1024]{1,0:T(8,128)S(1)} %copy-done.36, f32[576,1024]{1,0:T(8,128)} %collective-permute-done.38.refs_1_, bf16[576,1024]{1,0:T(8,128)(2,1)} %bitcast.11.refs_5_.refs_2_, f32[576,2]{1,0:T(8,128)S(1)} %get-tuple-element.175.refs_3_, ...), custom_call_target="tpu_custom_call" | custom-call | flops 999999995904 | bytes 1024 | tf_op jit(solution)/shard_map/first_norm_back/pallas_call | solution.py:40
  382.6 3.8 all-to-all-start
  388.2 2.4 collective-permute-start.42
  394.2 2.7 collective-permute-done.41.refs_2_
  396.9 4.2 %collective-permute-done.42.refs_3_ = bf16[64,1024]{1,0:T(8,128)(2,1)} collective-permute-done((bf16[64,1024]{1,0:T(8,128)(2,1)}, bf16[64,1024]{1,0:T(8,128)(2,1)}, u32[]{:S(2)}, u32[]{:S(2)}) %collective-permute-start.42) | collective-permute-done | bytes 131104 | tf_op jit(solution)/shard_map/ppermute | solution.py:85
  (328 shorter events, 101.1 us)
Async XLA Ops:
  6.8 16.9 %collective-permute-start.1 = (bf16[64,2176]{1,0:T(8,128)(2,1)S(1)}, bf16[64,2176]{1,0:T(8,128)(2,1)S(1)}, u32[]{:S(2)}, u32[]{:S(2)}) collective-permute-start(bf16[64,2176]{1,0:T(8,128)(2,1)S(1)} %maximum_maximum_fusion.refs_0_), channel_id=1, source_target_pairs={{0,16},{1,17},{2,18},{3,19},{4,20},{5,21},{6,22},{7,23},{8,24},{9,... | collective-permute-start | bytes 835592 | tf_op jit(solution)/shard_map/ppermute | solution.py:85
  23.9 14.2 %collective-permute-start.2 = (bf16[128,2176]{1,0:T(8,128)(2,1)S(1)}, bf16[128,2176]{1,0:T(8,128)(2,1)S(1)}, u32[]{:S(2)}, u32[]{:S(2)}) collective-permute-start(bf16[128,2176]{1,0:T(8,128)(2,1)S(1)} %stack.14.refs_0_.refs_2_), channel_id=1, source_target_pairs={{0,8},{1,9},{2,10},{3,11},{4,12},{5,13},{6,14},{7,15},{8,0},{9,1},... | collective-permute-start | bytes 1671176 | tf_op jit(solution)/shard_map/ppermute | solution.py:85
  25.5 16.4 %collective-permute-start.6 = (bf16[32,2048]{1,0:T(8,128)(2,1)}, bf16[32,2048]{1,0:T(8,128)(2,1)}, u32[]{:S(2)}, u32[]{:S(2)}) collective-permute-start(bf16[32,2048]{1,0:T(8,128)(2,1)} %bitcast.51), channel_id=1, source_target_pairs={{0,2},{1,3},{2,0},{3,1},{4,6},{5,7},{6,4},{7,5},{8,10},{9,11},{10,... | collective-permute-start | bytes 393224 | tf_op jit(solution)/shard_map/ppermute | solution.py:95
  26.2 77.7 %collective-permute-start.13 = (bf16[1,4,1024]{2,1,0:T(4,128)(2,1)}, bf16[1,4,1024]{2,1,0:T(4,128)(2,1)}, u32[]{:S(2)}, u32[]{:S(2)}) collective-permute-start(bf16[1,4,1024]{2,1,0:T(4,128)(2,1)} %get-tuple-element.290), channel_id=1, source_target_pairs={{0,1},{1,0},{2,3},{3,2},{4,5},{5,4},{6,7},{7,6},{8,9},{9,8},{10,11... | collective-permute-start | bytes 24584 | tf_op jit(solution)/shard_map/ppermute | solution.py:85
  28.3 40.8 %collective-permute-start.10 = (f32[1,576]{1,0:T(1,128)}, f32[1,576]{1,0:T(1,128)}, u32[]{:S(2)}, u32[]{:S(2)}) collective-permute-start(f32[1,576]{1,0:T(1,128)} %convert_element_type.32), channel_id=1, source_target_pairs={{0,2},{1,3},{2,0},{3,1},{4,6},{5,7},{6,4},{7,5},{8,10},{9,11},{10,... | collective-permute-start | bytes 6920 | tf_op jit(solution)/shard_map/ppermute | solution.py:95
  39.2 26.2 %collective-permute-start.3 = (bf16[256,2176]{1,0:T(8,128)(2,1)}, bf16[256,2176]{1,0:T(8,128)(2,1)}, u32[]{:S(2)}, u32[]{:S(2)}) collective-permute-start(bf16[256,2176]{1,0:T(8,128)(2,1)} %stack.15.refs_2_.refs_1_), channel_id=1, source_target_pairs={{0,4},{1,5},{2,3},{3,2},{4,0},{5,1},{6,7},{7,6},{8,12},{9,13},{10,... | collective-permute-start | bytes 3342344 | tf_op jit(solution)/shard_map/ppermute | solution.py:85
  40.4 24.9 %collective-permute-start.4 = (bf16[256,2176]{1,0:T(8,128)(2,1)}, bf16[256,2176]{1,0:T(8,128)(2,1)}, u32[]{:S(2)}, u32[]{:S(2)}) collective-permute-start(bf16[256,2176]{1,0:T(8,128)(2,1)} %stack.15.refs_2_.refs_1_), channel_id=1, source_target_pairs={{0,1},{1,0},{2,6},{3,7},{4,5},{5,4},{6,2},{7,3},{8,9},{9,8},{10,14... | collective-permute-start | bytes 3342344 | tf_op jit(solution)/shard_map/ppermute | solution.py:85
  42.9 23.5 %collective-permute-start.8 = (bf16[64,2048]{1,0:T(8,128)(2,1)S(1)}, bf16[64,2048]{1,0:T(8,128)(2,1)S(1)}, u32[]{:S(2)}, u32[]{:S(2)}) collective-permute-start(bf16[64,2048]{1,0:T(8,128)(2,1)S(1)} %stack.16.refs_0_.refs_2_), channel_id=1, source_target_pairs={{0,16},{1,17},{2,18},{3,19},{4,20},{5,21},{6,22},{7,23},{8,24},{9,... | collective-permute-start | bytes 786440 | tf_op jit(solution)/shard_map/ppermute | solution.py:85
  65.3 15.8 %collective-permute-start.5 = (bf16[256,2176]{1,0:T(8,128)(2,1)}, bf16[256,2176]{1,0:T(8,128)(2,1)}, u32[]{:S(2)}, u32[]{:S(2)}) collective-permute-start(bf16[256,2176]{1,0:T(8,128)(2,1)} %collective-permute-done.3.refs_3_.refs_2_), channel_id=1, source_target_pairs={{0,1},{1,0},{2,6},{3,7},{4,5},{5,4},{6,2},{7,3},{8,9},{9,8},{10,14... | collective-permute-start | bytes 3342344 | tf_op jit(solution)/shard_map/ppermute | solution.py:85
  66.5 14.1 %collective-permute-start.9 = (bf16[128,2048]{1,0:T(8,128)(2,1)S(1)}, bf16[128,2048]{1,0:T(8,128)(2,1)S(1)}, u32[]{:S(2)}, u32[]{:S(2)}) collective-permute-start(bf16[128,2048]{1,0:T(8,128)(2,1)S(1)} %stack.17.refs_0_.refs_2_), channel_id=1, source_target_pairs={{0,8},{1,9},{2,10},{3,11},{4,12},{5,13},{6,14},{7,15},{8,0},{9,1},... | collective-permute-start | bytes 1572872 | tf_op jit(solution)/shard_map/ppermute | solution.py:85
  70.1 20.6 %collective-permute-start.7 = (bf16[576,1024]{1,0:T(8,128)(2,1)}, bf16[576,1024]{1,0:T(8,128)(2,1)}, u32[]{:S(2)}, u32[]{:S(2)}) collective-permute-start(bf16[576,1024]{1,0:T(8,128)(2,1)} %bitcast.11.refs_5_.refs_2_), channel_id=1, source_target_pairs={{0,2},{1,3},{2,0},{3,1},{4,6},{5,7},{6,4},{7,5},{8,10},{9,11},{10,... | collective-permute-start | bytes 3538952 | tf_op jit(solution)/shard_map/ppermute | solution.py:95
  82.2 26.2 %collective-permute-start.12 = (bf16[256,2048]{1,0:T(8,128)(2,1)}, bf16[256,2048]{1,0:T(8,128)(2,1)}, u32[]{:S(2)}, u32[]{:S(2)}) collective-permute-start(bf16[256,2048]{1,0:T(8,128)(2,1)} %stack.18.refs_2_.refs_1_), channel_id=1, source_target_pairs={{0,4},{1,5},{2,3},{3,2},{4,0},{5,1},{6,7},{7,6},{8,12},{9,13},{10,... | collective-permute-start | bytes 3145736 | tf_op jit(solution)/shard_map/ppermute | solution.py:85
  84.4 23.9 %collective-permute-start.11 = (bf16[64,2048]{1,0:T(8,128)(2,1)}, bf16[64,2048]{1,0:T(8,128)(2,1)}, u32[]{:S(2)}, u32[]{:S(2)}) collective-permute-start(bf16[64,2048]{1,0:T(8,128)(2,1)} %stack.19.refs_5_.refs_0_), channel_id=1, source_target_pairs={{0,16},{1,17},{2,18},{3,19},{4,20},{5,21},{6,22},{7,23},{8,24},{9,... | collective-permute-start | bytes 786440 | tf_op jit(solution)/shard_map/ppermute | solution.py:85
  90.2 18.2 %collective-permute-start.14 = (bf16[256,2048]{1,0:T(8,128)(2,1)}, bf16[256,2048]{1,0:T(8,128)(2,1)}, u32[]{:S(2)}, u32[]{:S(2)}) collective-permute-start(bf16[256,2048]{1,0:T(8,128)(2,1)} %stack.18.refs_2_.refs_1_), channel_id=1, source_target_pairs={{0,1},{1,0},{2,6},{3,7},{4,5},{5,4},{6,2},{7,3},{8,9},{9,8},{10,14... | collective-permute-start | bytes 3145736 | tf_op jit(solution)/shard_map/ppermute | solution.py:85
  111.1 19.0 %collective-permute-start.16 = (bf16[256,2048]{1,0:T(8,128)(2,1)}, bf16[256,2048]{1,0:T(8,128)(2,1)}, u32[]{:S(2)}, u32[]{:S(2)}) collective-permute-start(bf16[256,2048]{1,0:T(8,128)(2,1)} %get-tuple-element.115.refs_2_.refs_3_), channel_id=1, source_target_pairs={{0,1},{1,0},{2,6},{3,7},{4,5},{5,4},{6,2},{7,3},{8,9},{9,8},{10,14... | collective-permute-start | bytes 3145736 | tf_op jit(solution)/shard_map/ppermute | solution.py:85
  112.6 17.5 %collective-permute-start.15 = (bf16[128,2048]{1,0:T(8,128)(2,1)}, bf16[128,2048]{1,0:T(8,128)(2,1)}, u32[]{:S(2)}, u32[]{:S(2)}) collective-permute-start(bf16[128,2048]{1,0:T(8,128)(2,1)} %get-tuple-element.113.refs_4_.refs_0_), channel_id=1, source_target_pairs={{0,8},{1,9},{2,10},{3,11},{4,12},{5,13},{6,14},{7,15},{8,0},{9,1},... | collective-permute-start | bytes 1572872 | tf_op jit(solution)/shard_map/ppermute | solution.py:85
  132.5 27.4 %collective-permute-start.18 = (bf16[256,2048]{1,0:T(8,128)(2,1)}, bf16[256,2048]{1,0:T(8,128)(2,1)}, u32[]{:S(2)}, u32[]{:S(2)}) collective-permute-start(bf16[256,2048]{1,0:T(8,128)(2,1)} %stack.21.refs_6_.refs_1_), channel_id=1, source_target_pairs={{0,4},{1,5},{2,3},{3,2},{4,0},{5,1},{6,7},{7,6},{8,12},{9,13},{10,... | collective-permute-start | bytes 3145736 | tf_op jit(solution)/shard_map/ppermute | solution.py:85
  137.2 4.9 %collective-permute-start.17 = (f32[576,1024]{1,0:T(8,128)}, f32[576,1024]{1,0:T(8,128)}, u32[]{:S(2)}, u32[]{:S(2)}) collective-permute-start(f32[576,1024]{1,0:T(8,128)} %mix_out.2.refs_6_), channel_id=1, source_target_pairs={{0,2},{1,3},{2,0},{3,1},{4,6},{5,7},{6,4},{7,5},{8,10},{9,11},{10,... | collective-permute-start | bytes 7077896 | tf_op jit(solution)/shard_map/ppermute | solution.py:95
  137.3 22.6 %collective-permute-start.19 = (bf16[256,2048]{1,0:T(8,128)(2,1)}, bf16[256,2048]{1,0:T(8,128)(2,1)}, u32[]{:S(2)}, u32[]{:S(2)}) collective-permute-start(bf16[256,2048]{1,0:T(8,128)(2,1)} %stack.21.refs_6_.refs_1_), channel_id=1, source_target_pairs={{0,1},{1,0},{2,6},{3,7},{4,5},{5,4},{6,2},{7,3},{8,9},{9,8},{10,14... | collective-permute-start | bytes 3145736 | tf_op jit(solution)/shard_map/ppermute | solution.py:85
  146.9 14.3 %collective-permute-start.21 = (bf16[576,1024]{1,0:T(8,128)(2,1)}, bf16[576,1024]{1,0:T(8,128)(2,1)}, u32[]{:S(2)}, u32[]{:S(2)}) collective-permute-start(bf16[576,1024]{1,0:T(8,128)(2,1)} %get-tuple-element.117.refs_5_), channel_id=1, source_target_pairs={{0,2},{1,3},{2,0},{3,1},{4,6},{5,7},{6,4},{7,5},{8,10},{9,11},{10,... | collective-permute-start | bytes 3538952 | tf_op jit(solution)/shard_map/ppermute | solution.py:95
  159.9 15.1 %collective-permute-start.20 = (bf16[256,2048]{1,0:T(8,128)(2,1)}, bf16[256,2048]{1,0:T(8,128)(2,1)}, u32[]{:S(2)}, u32[]{:S(2)}) collective-permute-start(bf16[256,2048]{1,0:T(8,128)(2,1)} %collective-permute-done.18.refs_2_.refs_7_), channel_id=1, source_target_pairs={{0,1},{1,0},{2,6},{3,7},{4,5},{5,4},{6,2},{7,3},{8,9},{9,8},{10,14... | collective-permute-start | bytes 3145736 | tf_op jit(solution)/shard_map/ppermute | solution.py:85
  182.3 6.0 %collective-permute-start.22 = (f32[576,1024]{1,0:T(8,128)}, f32[576,1024]{1,0:T(8,128)}, u32[]{:S(2)}, u32[]{:S(2)}) collective-permute-start(f32[576,1024]{1,0:T(8,128)} %feed_down.2.refs_6_), channel_id=1, source_target_pairs={{0,2},{1,3},{2,0},{3,1},{4,6},{5,7},{6,4},{7,5},{8,10},{9,11},{10,... | collective-permute-start | bytes 7077896 | tf_op jit(solution)/shard_map/ppermute | solution.py:95
  196.7 14.2 %collective-permute-start.23 = (f32[1,4,1024]{2,1,0:T(4,128)}, f32[1,4,1024]{2,1,0:T(4,128)}, u32[]{:S(2)}, u32[]{:S(2)}) collective-permute-start(f32[1,4,1024]{2,1,0:T(4,128)} %get-tuple-element.288), channel_id=1, source_target_pairs={{0,1},{1,0},{2,3},{3,2},{4,5},{5,4},{6,7},{7,6},{8,9},{9,8},{10,11... | collective-permute-start | bytes 49160 | tf_op jit(solution)/shard_map/ppermute | solution.py:85
  209.5 26.4 %collective-permute-start.25 = (bf16[1024,1024]{1,0:T(8,128)(2,1)}, bf16[1024,1024]{1,0:T(8,128)(2,1)}, u32[]{:S(2)}, u32[]{:S(2)}) collective-permute-start(bf16[1024,1024]{1,0:T(8,128)(2,1)} %get-tuple-element.132), channel_id=1, source_target_pairs={{0,1},{1,0},{2,6},{3,7},{4,5},{5,4},{6,2},{7,3},{8,9},{9,8},{10,14... | collective-permute-start | bytes 6291464 | tf_op jit(solution)/shard_map/ppermute | solution.py:85
  239.3 12.0 %collective-permute-start.26 = (f32[576,1024]{1,0:T(8,128)}, f32[576,1024]{1,0:T(8,128)}, u32[]{:S(2)}, u32[]{:S(2)}) collective-permute-start(f32[576,1024]{1,0:T(8,128)} %get-tuple-element.135), channel_id=1, source_target_pairs={{0,2},{1,3},{2,0},{3,1},{4,6},{5,7},{6,4},{7,5},{8,10},{9,11},{10,... | collective-permute-start | bytes 7077896 | tf_op jit(solution)/shard_map/ppermute | solution.py:95
  239.3 19.8 %collective-permute-start.27 = (bf16[512,1024]{1,0:T(8,128)(2,1)}, bf16[512,1024]{1,0:T(8,128)(2,1)}, u32[]{:S(2)}, u32[]{:S(2)}) collective-permute-start(bf16[512,1024]{1,0:T(8,128)(2,1)} %get-tuple-element.141), channel_id=1, source_target_pairs={{0,4},{1,5},{2,3},{3,2},{4,0},{5,1},{6,7},{7,6},{8,12},{9,13},{10,... | collective-permute-start | bytes 3145736 | tf_op jit(solution)/shard_map/ppermute | solution.py:85
  261.2 16.3 %collective-permute-start.28 = (bf16[576,1024]{1,0:T(8,128)(2,1)}, bf16[576,1024]{1,0:T(8,128)(2,1)}, u32[]{:S(2)}, u32[]{:S(2)}) collective-permute-start(bf16[576,1024]{1,0:T(8,128)(2,1)} %get-tuple-element.145.refs_10_.refs_6_), channel_id=1, source_target_pairs={{0,2},{1,3},{2,0},{3,1},{4,6},{5,7},{6,4},{7,5},{8,10},{9,11},{10,... | collective-permute-start | bytes 3538952 | tf_op jit(solution)/shard_map/ppermute | solution.py:95
  261.2 31.8 %collective-permute-start.30 = (bf16[256,1024]{1,0:T(8,128)(2,1)}, bf16[256,1024]{1,0:T(8,128)(2,1)}, u32[]{:S(2)}, u32[]{:S(2)}) collective-permute-start(bf16[256,1024]{1,0:T(8,128)(2,1)} %get-tuple-element.150), channel_id=1, source_target_pairs={{0,8},{1,9},{2,10},{3,11},{4,12},{5,13},{6,14},{7,15},{8,0},{9,1},... | collective-permute-start | bytes 1572872 | tf_op jit(solution)/shard_map/ppermute | solution.py:85
  261.8 37.3 %collective-permute-start.29 = (bf16[512,2048]{1,0:T(8,128)(2,1)}, bf16[512,2048]{1,0:T(8,128)(2,1)}, u32[]{:S(2)}, u32[]{:S(2)}) collective-permute-start(bf16[512,2048]{1,0:T(8,128)(2,1)} %get-tuple-element.149), channel_id=1, source_target_pairs={{0,1},{1,0},{2,6},{3,7},{4,5},{5,4},{6,2},{7,3},{8,9},{9,8},{10,14... | collective-permute-start | bytes 6291464 | tf_op jit(solution)/shard_map/ppermute | solution.py:85
  295.1 27.6 %collective-permute-start.34 = (bf16[128,1024]{1,0:T(8,128)(2,1)}, bf16[128,1024]{1,0:T(8,128)(2,1)}, u32[]{:S(2)}, u32[]{:S(2)}) collective-permute-start(bf16[128,1024]{1,0:T(8,128)(2,1)} %get-tuple-element.160), channel_id=1, source_target_pairs={{0,16},{1,17},{2,18},{3,19},{4,20},{5,21},{6,22},{7,23},{8,24},{9,... | collective-permute-start | bytes 786440 | tf_op jit(solution)/shard_map/ppermute | solution.py:85
  302.4 15.1 %collective-permute-start.31 = (bf16[256,2048]{1,0:T(8,128)(2,1)}, bf16[256,2048]{1,0:T(8,128)(2,1)}, u32[]{:S(2)}, u32[]{:S(2)}) collective-permute-start(bf16[256,2048]{1,0:T(8,128)(2,1)} %get-tuple-element.155), channel_id=1, source_target_pairs={{0,4},{1,5},{2,3},{3,2},{4,0},{5,1},{6,7},{7,6},{8,12},{9,13},{10,... | collective-permute-start | bytes 3145736 | tf_op jit(solution)/shard_map/ppermute | solution.py:85
  319.6 13.0 %collective-permute-start.33 = (bf16[128,2048]{1,0:T(8,128)(2,1)}, bf16[128,2048]{1,0:T(8,128)(2,1)}, u32[]{:S(2)}, u32[]{:S(2)}) collective-permute-start(bf16[128,2048]{1,0:T(8,128)(2,1)} %get-tuple-element.158), channel_id=1, source_target_pairs={{0,8},{1,9},{2,10},{3,11},{4,12},{5,13},{6,14},{7,15},{8,0},{9,1},... | collective-permute-start | bytes 1572872 | tf_op jit(solution)/shard_map/ppermute | solution.py:85
  321.2 15.1 %collective-permute-start.32 = (bf16[512,1024]{1,0:T(8,128)(2,1)}, bf16[512,1024]{1,0:T(8,128)(2,1)}, u32[]{:S(2)}, u32[]{:S(2)}) collective-permute-start(bf16[512,1024]{1,0:T(8,128)(2,1)} %get-tuple-element.157), channel_id=1, source_target_pairs={{0,1},{1,0},{2,6},{3,7},{4,5},{5,4},{6,2},{7,3},{8,9},{9,8},{10,14... | collective-permute-start | bytes 3145736 | tf_op jit(solution)/shard_map/ppermute | solution.py:85
  334.9 22.2 %collective-permute-start.36 = (bf16[64,2048]{1,0:T(8,128)(2,1)}, bf16[64,2048]{1,0:T(8,128)(2,1)}, u32[]{:S(2)}, u32[]{:S(2)}) collective-permute-start(bf16[64,2048]{1,0:T(8,128)(2,1)} %get-tuple-element.169), channel_id=1, source_target_pairs={{0,16},{1,17},{2,18},{3,19},{4,20},{5,21},{6,22},{7,23},{8,24},{9,... | collective-permute-start | bytes 786440 | tf_op jit(solution)/shard_map/ppermute | solution.py:85
  338.4 15.2 %collective-permute-start.37 = (bf16[256,1024]{1,0:T(8,128)(2,1)}, bf16[256,1024]{1,0:T(8,128)(2,1)}, u32[]{:S(2)}, u32[]{:S(2)}) collective-permute-start(bf16[256,1024]{1,0:T(8,128)(2,1)} %get-tuple-element.170), channel_id=1, source_target_pairs={{0,4},{1,5},{2,3},{3,2},{4,0},{5,1},{6,7},{7,6},{8,12},{9,13},{10,... | collective-permute-start | bytes 1572872 | tf_op jit(solution)/shard_map/ppermute | solution.py:85
  339.8 19.1 %collective-permute-start.35 = (bf16[512,1024]{1,0:T(8,128)(2,1)}, bf16[512,1024]{1,0:T(8,128)(2,1)}, u32[]{:S(2)}, u32[]{:S(2)}) collective-permute-start(bf16[512,1024]{1,0:T(8,128)(2,1)} %get-tuple-element.168), channel_id=1, source_target_pairs={{0,1},{1,0},{2,6},{3,7},{4,5},{5,4},{6,2},{7,3},{8,9},{9,8},{10,14... | collective-permute-start | bytes 3145736 | tf_op jit(solution)/shard_map/ppermute | solution.py:85
  361.2 7.2 %collective-permute-start.38 = (f32[576,1024]{1,0:T(8,128)}, f32[576,1024]{1,0:T(8,128)}, u32[]{:S(2)}, u32[]{:S(2)}) collective-permute-start(f32[576,1024]{1,0:T(8,128)} %get-tuple-element.174), channel_id=1, source_target_pairs={{0,2},{1,3},{2,0},{3,1},{4,6},{5,7},{6,4},{7,5},{8,10},{9,11},{10,... | collective-permute-start | bytes 7077896 | tf_op jit(solution)/shard_map/ppermute | solution.py:95
  364.0 22.5 %collective-permute-start.44 = (bf16[64,1024]{1,0:T(8,128)(2,1)}, bf16[64,1024]{1,0:T(8,128)(2,1)}, u32[]{:S(2)}, u32[]{:S(2)}) collective-permute-start(bf16[64,1024]{1,0:T(8,128)(2,1)} %get-tuple-element.190), channel_id=1, source_target_pairs={{0,16},{1,17},{2,18},{3,19},{4,20},{5,21},{6,22},{7,23},{8,24},{9,... | collective-permute-start | bytes 393224 | tf_op jit(solution)/shard_map/ppermute | solution.py:85
  365.5 22.7 %collective-permute-start.45 = (bf16[64,1024]{1,0:T(8,128)(2,1)}, bf16[64,1024]{1,0:T(8,128)(2,1)}, u32[]{:S(2)}, u32[]{:S(2)}) collective-permute-start(bf16[64,1024]{1,0:T(8,128)(2,1)} %get-tuple-element.191), channel_id=1, source_target_pairs={{0,8},{1,9},{2,10},{3,11},{4,12},{5,13},{6,14},{7,15},{8,0},{9,1},... | collective-permute-start | bytes 393224 | tf_op jit(solution)/shard_map/ppermute | solution.py:85
  366.4 24.2 %collective-permute-start.46 = (bf16[64,1024]{1,0:T(8,128)(2,1)}, bf16[64,1024]{1,0:T(8,128)(2,1)}, u32[]{:S(2)}, u32[]{:S(2)}) collective-permute-start(bf16[64,1024]{1,0:T(8,128)(2,1)} %get-tuple-element.192), channel_id=1, source_target_pairs={{0,24},{1,25},{2,26},{3,27},{4,28},{5,29},{6,30},{7,31},{8,16},{9,... | collective-permute-start | bytes 393224 | tf_op jit(solution)/shard_map/ppermute | solution.py:85
  368.4 23.9 %collective-permute-start.43 = (f32[32,2048]{1,0:T(8,128)}, f32[32,2048]{1,0:T(8,128)}, u32[]{:S(2)}, u32[]{:S(2)}) collective-permute-start(f32[32,2048]{1,0:T(8,128)} %get-tuple-element.189), channel_id=1, source_target_pairs={{0,2},{1,3},{2,0},{3,1},{4,6},{5,7},{6,4},{7,5},{8,10},{9,11},{10,... | collective-permute-start | bytes 786440 | tf_op jit(solution)/shard_map/ppermute | solution.py:95
  368.4 9.5 %collective-permute-start.39 = (bf16[256,1024]{1,0:T(8,128)(2,1)}, bf16[256,1024]{1,0:T(8,128)(2,1)}, u32[]{:S(2)}, u32[]{:S(2)}) collective-permute-start(bf16[256,1024]{1,0:T(8,128)(2,1)} %get-tuple-element.184), channel_id=1, source_target_pairs={{0,4},{1,5},{2,3},{3,2},{4,0},{5,1},{6,7},{7,6},{8,12},{9,13},{10,... | collective-permute-start | bytes 1572872 | tf_op jit(solution)/shard_map/ppermute | solution.py:85
  381.0 13.2 %collective-permute-start.40 = (bf16[64,1024]{1,0:T(8,128)(2,1)}, bf16[64,1024]{1,0:T(8,128)(2,1)}, u32[]{:S(2)}, u32[]{:S(2)}) collective-permute-start(bf16[64,1024]{1,0:T(8,128)(2,1)} %get-tuple-element.186), channel_id=1, source_target_pairs={{0,16},{1,17},{2,18},{3,19},{4,20},{5,21},{6,22},{7,23},{8,24},{9,... | collective-permute-start | bytes 393224 | tf_op jit(solution)/shard_map/ppermute | solution.py:85
  382.6 21.9 %all-to-all-start = ((bf16[32,32,128]{2,1,0:T(8,128)(2,1)}), bf16[32,32,128]{2,1,0:T(8,128)(2,1)}, u32[]{:S(2)}, u32[]{:S(2)}) async-start(bf16[32,32,128]{2,1,0:T(8,128)(2,1)} %bitcast.24), calls=%async_computation | async-start | bytes 524288 | tf_op jit(solution)/shard_map/all_to_all | solution.py:1413
  386.4 10.4 %collective-permute-start.41 = (bf16[64,1024]{1,0:T(8,128)(2,1)}, bf16[64,1024]{1,0:T(8,128)(2,1)}, u32[]{:S(2)}, u32[]{:S(2)}) collective-permute-start(bf16[64,1024]{1,0:T(8,128)(2,1)} %get-tuple-element.187), channel_id=1, source_target_pairs={{0,8},{1,9},{2,10},{3,11},{4,12},{5,13},{6,14},{7,15},{8,0},{9,1},... | collective-permute-start | bytes 393224 | tf_op jit(solution)/shard_map/ppermute | solution.py:85
  388.2 12.9 %collective-permute-start.42 = (bf16[64,1024]{1,0:T(8,128)(2,1)}, bf16[64,1024]{1,0:T(8,128)(2,1)}, u32[]{:S(2)}, u32[]{:S(2)}) collective-permute-start(bf16[64,1024]{1,0:T(8,128)(2,1)} %get-tuple-element.188), channel_id=1, source_target_pairs={{0,24},{1,25},{2,26},{3,27},{4,28},{5,29},{6,30},{7,31},{8,16},{9,... | collective-permute-start | bytes 393224 | tf_op jit(solution)/shard_map/ppermute | solution.py:85
  392.3 15.1 %collective-permute-start.47 = (f32[32,1024]{1,0:T(8,128)}, f32[32,1024]{1,0:T(8,128)}, u32[]{:S(2)}, u32[]{:S(2)}) collective-permute-start(f32[32,1024]{1,0:T(8,128)} %get-tuple-element.196), channel_id=1, source_target_pairs={{0,2},{1,3},{2,0},{3,1},{4,6},{5,7},{6,4},{7,5},{8,10},{9,11},{10,... | collective-permute-start | bytes 393224 | tf_op jit(solution)/shard_map/ppermute | solution.py:95
  403.8 3.6 collective-permute-start.48
  (84 other events, 348.0 us)

commit v4 on v3

--- a/solution.py
+++ b/solution.py
@@ -215,23 +215,23 @@
 
 def add_parts(low, got, count):
     step, cols = low.shape[0] // count, low.shape[1]
-    tile = cols // 2
-
-    def kernel(a_ref, b_ref, *outs):
-        for i, out in enumerate(outs):
-            part = slice(i * step, (i + 1) * step)
-            out[...] = (a_ref[part, :].astype(F32) + b_ref[part, :].astype(F32)).astype(BF)
-
+    band = step // 2
+
+    def kernel(*refs):
+        for i, out in enumerate(refs[2 * count :]):
+            out[...] = (refs[i][...].astype(F32) + refs[count + i][...].astype(F32)).astype(BF)
+
+    part = lambda i: pl.BlockSpec((band, cols), lambda n: (2 * i + n, 0))
     return launch(
         kernel,
         grid=(2,),
-        in_specs=[pl.BlockSpec((count * step, tile), lambda n: (0, n))] * 2,
-        out_specs=[pl.BlockSpec((step, tile), lambda n: (0, n))] * count,
+        in_specs=[part(i) for i in range(count)] * 2,
+        out_specs=[pl.BlockSpec((band, cols), lambda n: (n, 0))] * count,
         out_shape=[shape((step, cols), BF)] * count,
         compiler_params=params("arbitrary", vmem=50),
         cost_estimate=cost(0, 0),
         name="add_parts",
-    )(low, got)
+    )(*[low] * count, *[got] * count)
 
 
 def last_sum(low, parts):
@@ -1408,16 +1408,16 @@
     if layered:
         swap = lambda total: (total[0], to_sibling(total[1]))
         up_pair = swap(grad_up)
-        far_sum.advance()
     terms = pack_terms(which, one_sums, two_sums, sums, grad_map, sums_a, sums_b, runs)
     terms = lax.all_to_all(terms.reshape(devices, own, 128), AXES, 0, 0, tiled=True)
     if layered:
+        far_sum.advance()
         qk_pair = swap(near_sum.finish())
         grad_down = jnp.concatenate(grad_down, axis=0)
         grad_up = join_runs(which, [up_pair], unit)
+        map_piece, pieces, up_piece = sum_terms(terms, count, fan)
         grad_far = far_sum.finish()
         v_pair = swap([part[:, :side] for part in grad_far])
-        map_piece, pieces, up_piece = sum_terms(terms, count, fan)
         grad_out = jnp.concatenate([grad_far[0][:, side:], grad_far[1][:, side:]], axis=1)
         grad_qkv_full = join_runs(which, [qk_pair, v_pair], HD)
     else:

time: 416 us -> 413 us (level)
    ppermute x35, waiting for transfers between devices: 72 us -> 67.7 us  [permute(): return lax.ppermute(values, AXES, pairs)]
where the time goes in v4:
time: 413 us; the launch traced here: 407 us
  Pallas kernels  233 us (56%)
  waiting for transfers between devices  72.2 us (17%)
  starting transfers between devices  58.4 us (14%)
  local copies, waits for them, and re-layouts  32.2 us (8%)
  other arithmetic  8.73 us (2%)
    pallas_call x50, Pallas kernels, run(): outs = pl.pallas_call(body, in_specs=specs, **settings)(*operands, *waited)  233 us
    ppermute x35, waiting for transfers between devices, permute(): return lax.ppermute(values, AXES, pairs)  67.7 us
    ppermute x35, starting transfers between devices, permute(): return lax.ppermute(values, AXES, pairs)  53.2 us
    unnamed x168, local copies, waits for them, and re-layouts  24.4 us
  transfers between devices with their start and end apart: 50, of which 16 were waited for; matrix products, arithmetic and copies ran while one was open for 4% of the time, Pallas kernels for 50%

profile of v4, /device:TPU:0, one launch (start us, length us, event | category | flops | bytes accessed | tf_op | source)
XLA Modules:
  0.0 406.9 jit_solution(10457386180936872562)
XLA Ops:
  6.8 4.0 collective-permute-start.1
  12.2 11.6 %collective-permute-done.1.refs_1_ = bf16[64,2176]{1,0:T(8,128)(2,1)S(1)} collective-permute-done((bf16[64,2176]{1,0:T(8,128)(2,1)S(1)}, bf16[64,2176]{1,0:T(8,128)(2,1)S(1)}, u32[]{:S(2)}, u32[]{:S(2)}) %collective-permute-start.1) | collective-permute-done | bytes 278560 | tf_op jit(solution)/shard_map/ppermute | solution.py:85
  29.1 9.0 %collective-permute-done.2.refs_1_ = bf16[128,2176]{1,0:T(8,128)(2,1)S(1)} collective-permute-done((bf16[128,2176]{1,0:T(8,128)(2,1)S(1)}, bf16[128,2176]{1,0:T(8,128)(2,1)S(1)}, u32[]{:S(2)}, u32[]{:S(2)}) %collective-permute-start.2) | collective-permute-done | bytes 557088 | tf_op jit(solution)/shard_map/ppermute | solution.py:85
  42.9 3.1 collective-permute-start.8
  46.6 18.7 %collective-permute-done.3.refs_3_.refs_2_ = bf16[256,2176]{1,0:T(8,128)(2,1)} collective-permute-done((bf16[256,2176]{1,0:T(8,128)(2,1)}, bf16[256,2176]{1,0:T(8,128)(2,1)}, u32[]{:S(2)}, u32[]{:S(2)}) %collective-permute-start.3) | collective-permute-done | bytes 1114144 | tf_op jit(solution)/shard_map/ppermute | solution.py:85
  70.2 10.3 %collective-permute-done.9.refs_1_ = bf16[128,2048]{1,0:T(8,128)(2,1)S(1)} collective-permute-done((bf16[128,2048]{1,0:T(8,128)(2,1)S(1)}, bf16[128,2048]{1,0:T(8,128)(2,1)S(1)}, u32[]{:S(2)}, u32[]{:S(2)}) %collective-permute-start.9) | collective-permute-done | bytes 524320 | tf_op jit(solution)/shard_map/ppermute | solution.py:85
  84.4 4.1 %collective-permute-start.11 = (bf16[64,2048]{1,0:T(8,128)(2,1)}, bf16[64,2048]{1,0:T(8,128)(2,1)}, u32[]{:S(2)}, u32[]{:S(2)}) collective-permute-start(bf16[64,2048]{1,0:T(8,128)(2,1)} %stack.19.refs_5_.refs_0_), channel_id=1, source_target_pairs={{0,16},{1,17},{2,18},{3,19},{4,20},{5,21},{6,22},{7,23},{8,24},{9,... | collective-permute-start | bytes 786440 | tf_op jit(solution)/shard_map/ppermute | solution.py:85
  90.7 11.5 %project.1 = (bf16[1152,1536]{1,0:T(8,128)(2,1)}, bf16[1024,1280]{1,0:T(8,128)(2,1)S(1)}, f32[576,2]{1,0:T(8,128)S(1)}) custom-call(s32[32]{0:T(128)S(1)} %reshape.301.refs_0_, bf16[256,2176]{1,0:T(8,128)(2,1)} %stack.15.refs_2_.refs_1_, bf16[256,2176]{1,0:T(8,128)(2,1)} %collective-permute-done.3.refs_3_.refs_2_, ...), custom_call_target="tpu_custom_call" | custom-call | flops 999999995904 | bytes 1024 | tf_op jit(solution)/shard_map/project/pallas_call | solution.py:40
  103.8 2.0 copy-done.22
  108.4 2.7 stack.20
  114.1 14.0 %attend.1 = (bf16[1152,512]{1,0:T(8,128)(2,1)S(1)}, bf16[512,1280]{1,0:T(8,128)(2,1)S(1)}, f32[4,4,576]{2,1,0:T(4,128)S(1)}) custom-call(bf16[1152,1536]{1,0:T(8,128)(2,1)S(1)} %copy-done.23, bf16[1152,1536]{1,0:T(8,128)(2,1)S(1)} %copy-done.23, bf16[1152,1536]{1,0:T(8,128)(2,1)S(1)} %copy-done.23, f32[1152,1]{1,0:T(8,128)S(1)} %copy.76.refs_3_.refs_8_, ...), custom_call_target="tpu_custom_call" | custom-call | flops 999999995904 | bytes 1024 | tf_op jit(solution)/shard_map/attend/pallas_call | solution.py:40
  130.1 2.4 stack.21.refs_6_.refs_1_
  133.0 4.2 %mix_out.2.refs_6_ = f32[576,1024]{1,0:T(8,128)} custom-call(s32[16]{0:T(128)S(1)} %and_add_fusion.refs_0_.refs_1_, bf16[256,2176]{1,0:T(8,128)(2,1)} %stack.15.refs_2_.refs_1_, bf16[256,2176]{1,0:T(8,128)(2,1)} %collective-permute-done.3.refs_3_.refs_2_, bf16[256,2176]{1,0:T(8,128)(2,1)} %collective-permute-done.4.refs_4_.refs_3_, ...), custom_call_target="tpu_custom_call" | custom-call | flops 999999995904 | bytes 1024 | tf_op jit(solution)/shard_map/mix_out/pallas_call | solution.py:40
  138.7 2.8 mix_out.3.refs_0_.refs_6_
  142.1 3.3 second_norm.1
  147.0 10.3 %feed_up.2 = (bf16[576,2048]{1,0:T(8,128)(2,1)S(1)}, bf16[2048,640]{1,0:T(8,128)(2,1)}, bf16[576,2048]{1,0:T(8,128)(2,1)}, bf16[1024,640]{1,0:T(8,128)(2,1)S(1)}) custom-call(s32[32]{0:T(128)S(1)} %reshape.301.refs_0_, bf16[256,2048]{1,0:T(8,128)(2,1)} %stack.18.refs_2_.refs_1_, bf16[256,2048]{1,0:T(8,128)(2,1)} %get-tuple-element.115.refs_2_.refs_3_, ...), custom_call_target="tpu_custom_call" | custom-call | flops 999999995904 | bytes 1024 | tf_op jit(solution)/shard_map/feed_up/pallas_call | solution.py:40
  161.1 10.6 %feed_up.3 = (bf16[576,2048]{1,0:T(8,128)(2,1)S(1)}, bf16[2048,640]{1,0:T(8,128)(2,1)}, bf16[576,2048]{1,0:T(8,128)(2,1)}, bf16[1024,640]{1,0:T(8,128)(2,1)S(1)}) custom-call(s32[32]{0:T(128)S(1)} %reshape.301.refs_0_, bf16[256,2048]{1,0:T(8,128)(2,1)} %stack.18.refs_2_.refs_1_, bf16[256,2048]{1,0:T(8,128)(2,1)} %get-tuple-element.115.refs_2_.refs_3_, ...), custom_call_target="tpu_custom_call" | custom-call | flops 999999995904 | bytes 1024 | tf_op jit(solution)/shard_map/feed_up/pallas_call | solution.py:40
  171.8 3.2 collective-permute-done.20.refs_4_.refs_9_
  175.0 7.3 %feed_down.2.refs_6_ = f32[576,1024]{1,0:T(8,128)} custom-call(s32[16]{0:T(128)S(1)} %and_add_fusion.refs_0_.refs_1_, bf16[256,2048]{1,0:T(8,128)(2,1)} %stack.21.refs_6_.refs_1_, bf16[256,2048]{1,0:T(8,128)(2,1)} %collective-permute-done.18.refs_2_.refs_7_, bf16[256,2048]{1,0:T(8,128)(2,1)} %collective-permute-done.19.refs_3_.refs_8_, ...), custom_call_target="tpu_custom_call" | custom-call | flops 999999995904 | bytes 1024 | tf_op jit(solution)/shard_map/feed_down/pallas_call | solution.py:40
  182.4 5.9 %feed_down.3.refs_1_.refs_10_ = f32[576,1024]{1,0:T(8,128)S(1)} custom-call(s32[16]{0:T(128)S(1)} %and_add_fusion.refs_0_.refs_1_, bf16[256,2048]{1,0:T(8,128)(2,1)} %stack.21.refs_6_.refs_1_, bf16[256,2048]{1,0:T(8,128)(2,1)} %collective-permute-done.18.refs_2_.refs_7_, bf16[256,2048]{1,0:T(8,128)(2,1)} %collective-permute-done.19.refs_3_.refs_8_, ...), custom_call_target="tpu_custom_call" | custom-call | flops 999999995904 | bytes 1024 | tf_op jit(solution)/shard_map/feed_down/pallas_call | solution.py:40
  188.4 6.9 %token_learner.1 = (bf16[576,1024]{1,0:T(8,128)(2,1)}, f32[8,1024]{1,0:T(8,128)S(1)}, f32[576,1024]{1,0:T(8,128)S(1)}, bf16[576,1024]{1,0:T(8,128)(2,1)S(1)}, f3...) custom-call(f32[576,1024]{1,0:T(8,128)S(1)} %copy-done.31, f32[576,1024]{1,0:T(8,128)S(1)} %feed_down.3.refs_1_.refs_10_, ...), custom_call_target="tpu_custom_call" | custom-call | flops 999999995904 | bytes 1024 | tf_op jit(solution)/shard_map/token_learner/pallas_call | solution.py:40
  199.9 9.5 %weight_grad.3 = (bf16[1024,1024]{1,0:T(8,128)(2,1)S(1)}, bf16[1024,1024]{1,0:T(8,128)(2,1)}) custom-call(s32[16]{0:T(128)S(1)} %and_add_fusion.refs_0_.refs_1_, bf16[2048,640]{1,0:T(8,128)(2,1)S(1)} %copy-done.26, bf16[2048,640]{1,0:T(8,128)(2,1)} %get-tuple-element.124.refs_2_, bf16[576,1024]{1,0:T(8,128)(2,1)S(1)} %get-tuple-element.125.refs_3_.refs_10_, ...), custom_call_target="tpu_custom_call" | custom-call | flops 999999995904 | bytes 1024 | tf_op jit(solution)/shard_map/weight_grad/pallas_call | solution.py:40
  211.5 21.2 %feed_back.1 = (bf16[1152,2048]{1,0:T(8,128)(2,1)}, f32[1,2048]{1,0:T(1,128)S(1)}, f32[576,1024]{1,0:T(8,128)}, f32[576,1024]{1,0:T(8,128)}) custom-call(s32[32]{0:T(128)S(1)} %reshape.301.refs_0_, s32[16]{0:T(128)S(1)} %and_add_fusion.refs_0_.refs_1_, bf16[256,2048]{1,0:T(8,128)(2,1)} %stack.18.refs_2_.refs_1_, ...), custom_call_target="tpu_custom_call" | custom-call | flops 999999995904 | bytes 1024 | tf_op jit(solution)/shard_map/feed_back/pallas_call | solution.py:40
  232.7 3.2 collective-permute-done.25.refs_2_.refs_3_
  235.9 3.2 add_parts.10
  240.7 10.5 %weight_grad.4 = (bf16[512,2048]{1,0:T(8,128)(2,1)S(1)}, bf16[512,2048]{1,0:T(8,128)(2,1)}) custom-call(s32[32]{0:T(128)S(1)} %reshape.301.refs_0_, bf16[1024,640]{1,0:T(8,128)(2,1)S(1)} %copy-done.46, bf16[1024,640]{1,0:T(8,128)(2,1)S(1)} %copy-done.48, bf16[1152,2048]{1,0:T(8,128)(2,1)} %get-tuple-element.133.refs_4_.refs_3_, ...), custom_call_target="tpu_custom_call" | custom-call | flops 999999995904 | bytes 1024 | tf_op jit(solution)/shard_map/weight_grad/pallas_call | solution.py:40
  251.2 6.3 %second_norm_back.1 = (f32[576,1024]{1,0:T(8,128)S(1)}, bf16[576,1024]{1,0:T(8,128)(2,1)}, f32[3,1024]{1,0:T(4,128)S(1)}) custom-call(f32[576,1024]{1,0:T(8,128)S(1)} %copy-done.27, f32[576,1024]{1,0:T(8,128)} %collective-permute-done.26.refs_1_, f32[576,1024]{1,0:T(8,128)} %copy-done.30, f32[576,1024]{1,0:T(8,128)} %copy-done.32, ...), custom_call_target="tpu_custom_call" | custom-call | flops 999999995904 | bytes 1024 | tf_op jit(solution)/shard_map/second_norm_back/pallas_call | solution.py:40
  258.9 2.0 add_parts.11
  262.3 14.9 %attend_back.2 = (bf16[3,576,512]{2,1,0:T(8,128)(2,1)S(1)}, f32[2,512]{1,0:T(2,128)S(1)}) custom-call(s32[16]{0:T(128)S(1)} %and_add_fusion.refs_0_.refs_1_, bf16[256,2176]{1,0:T(8,128)(2,1)} %stack.15.refs_2_.refs_1_, bf16[256,2176]{1,0:T(8,128)(2,1)} %collective-permute-done.3.refs_3_.refs_2_, bf16[256,2176]{1,0:T(8,128)(2,1)} %collective-permute-done.4.refs_4_.refs_3_, ...), custom_call_target="tpu_custom_call" | custom-call | flops 999999995904 | bytes 1024 | tf_op jit(solution)/shard_map/attend_back/pallas_call | solution.py:40
  277.2 15.5 %attend_back.3 = (bf16[3,576,512]{2,1,0:T(8,128)(2,1)S(1)}, f32[2,512]{1,0:T(2,128)S(1)}) custom-call(s32[16]{0:T(128)S(1)} %and_add_fusion.refs_0_.refs_1_, bf16[256,2176]{1,0:T(8,128)(2,1)} %stack.15.refs_2_.refs_1_, bf16[256,2176]{1,0:T(8,128)(2,1)} %collective-permute-done.3.refs_3_.refs_2_, bf16[256,2176]{1,0:T(8,128)(2,1)} %collective-permute-done.4.refs_4_.refs_3_, ...), custom_call_target="tpu_custom_call" | custom-call | flops 999999995904 | bytes 1024 | tf_op jit(solution)/shard_map/attend_back/pallas_call | solution.py:40
  292.7 2.4 add_parts.12
  295.1 3.9 collective-permute-start.34
  299.0 3.3 add_parts.13
  303.6 8.7 %weight_grad.5 = (bf16[512,1024]{1,0:T(8,128)(2,1)S(1)}, bf16[512,1024]{1,0:T(8,128)(2,1)}) custom-call(s32[32]{0:T(128)S(1)} %reshape.301.refs_0_, bf16[1024,1280]{1,0:T(8,128)(2,1)S(1)} %copy-done.25, bf16[3,576,512]{2,1,0:T(8,128)(2,1)S(1)} %copy-done.40, bf16[3,576,512]{2,1,0:T(8,128)(2,1)S(1)} %copy-done.42, ...), custom_call_target="tpu_custom_call" | custom-call | flops 999999995904 | bytes 1024 | tf_op jit(solution)/shard_map/weight_grad/pallas_call | solution.py:40
  313.2 4.1 %collective-permute-done.31.refs_2_.refs_3_ = bf16[256,2048]{1,0:T(8,128)(2,1)} collective-permute-done((bf16[256,2048]{1,0:T(8,128)(2,1)}, bf16[256,2048]{1,0:T(8,128)(2,1)}, u32[]{:S(2)}, u32[]{:S(2)}) %collective-permute-start.31) | collective-permute-done | bytes 1048608 | tf_op jit(solution)/shard_map/ppermute | solution.py:85
  317.4 2.0 add_parts.14
  323.9 8.4 %value_and_out_grad.1 = (bf16[512,1024]{1,0:T(8,128)(2,1)S(1)}, bf16[512,1024]{1,0:T(8,128)(2,1)}) custom-call(s32[32]{0:T(128)S(1)} %reshape.301.refs_0_, s32[16]{0:T(128)S(1)} %and_add_fusion.refs_0_.refs_1_, bf16[1024,1280]{1,0:T(8,128)(2,1)} %copy-done.24, bf16[512,1280]{1,0:T(8,128)(2,1)S(1)} %copy-done.44, bf16[3,576,512]{2,1,0:T(8,128)(2,1)S(1)} %copy-done.40, ...), custom_call_target="tpu_custom_call" | custom-call | flops 999999995904 | bytes 1024 | tf_op jit(solution)/shard_map/value_and_out_grad/pallas_call | solution.py:40
  332.4 2.2 add_parts.15
  336.0 2.0 add_parts.16
  340.1 10.3 %project_back.1 = (f32[576,1024]{1,0:T(8,128)}, f32[576,1024]{1,0:T(8,128)}) custom-call(s32[32]{0:T(128)S(1)} %reshape.301.refs_0_, bf16[256,2176]{1,0:T(8,128)(2,1)} %stack.15.refs_2_.refs_1_, bf16[256,2176]{1,0:T(8,128)(2,1)} %collective-permute-done.3.refs_3_.refs_2_, bf16[256,2176]{1,0:T(8,128)(2,1)} %collective-permute-done.4.refs_4_.refs_3_, ...), custom_call_target="tpu_custom_call" | custom-call | flops 999999995904 | bytes 1024 | tf_op jit(solution)/shard_map/project_back/pallas_call | solution.py:40
  350.4 2.7 collective-permute-done.37.refs_4_.refs_5_.refs_6_.refs_7_
  358.5 2.1 add_parts.18
  365.9 1.9 collective-permute-start.42
  372.5 4.6 %first_norm_back.1 = (bf16[576,1024]{1,0:T(8,128)(2,1)}, f32[2,1024]{1,0:T(2,128)S(1)}) custom-call(f32[576,1024]{1,0:T(8,128)S(1)} %copy-done.36, f32[576,1024]{1,0:T(8,128)} %collective-permute-done.38.refs_1_, bf16[576,1024]{1,0:T(8,128)(2,1)} %bitcast.11.refs_5_.refs_2_, f32[576,2]{1,0:T(8,128)S(1)} %get-tuple-element.175.refs_3_, ...), custom_call_target="tpu_custom_call" | custom-call | flops 999999995904 | bytes 1024 | tf_op jit(solution)/shard_map/first_norm_back/pallas_call | solution.py:40
  379.4 3.6 all-to-all-start
  384.8 2.7 collective-permute-start.45
  393.4 2.2 all-to-all-done.refs_0_
  398.3 2.9 collective-permute-done.45.refs_1_
  (328 shorter events, 100.8 us)
Async XLA Ops:
  6.8 16.9 %collective-permute-start.1 = (bf16[64,2176]{1,0:T(8,128)(2,1)S(1)}, bf16[64,2176]{1,0:T(8,128)(2,1)S(1)}, u32[]{:S(2)}, u32[]{:S(2)}) collective-permute-start(bf16[64,2176]{1,0:T(8,128)(2,1)S(1)} %maximum_maximum_fusion.refs_0_), channel_id=1, source_target_pairs={{0,16},{1,17},{2,18},{3,19},{4,20},{5,21},{6,22},{7,23},{8,24},{9,... | collective-permute-start | bytes 835592 | tf_op jit(solution)/shard_map/ppermute | solution.py:85
  23.9 14.2 %collective-permute-start.2 = (bf16[128,2176]{1,0:T(8,128)(2,1)S(1)}, bf16[128,2176]{1,0:T(8,128)(2,1)S(1)}, u32[]{:S(2)}, u32[]{:S(2)}) collective-permute-start(bf16[128,2176]{1,0:T(8,128)(2,1)S(1)} %stack.14.refs_0_.refs_2_), channel_id=1, source_target_pairs={{0,8},{1,9},{2,10},{3,11},{4,12},{5,13},{6,14},{7,15},{8,0},{9,1},... | collective-permute-start | bytes 1671176 | tf_op jit(solution)/shard_map/ppermute | solution.py:85
  25.5 16.4 %collective-permute-start.6 = (bf16[32,2048]{1,0:T(8,128)(2,1)}, bf16[32,2048]{1,0:T(8,128)(2,1)}, u32[]{:S(2)}, u32[]{:S(2)}) collective-permute-start(bf16[32,2048]{1,0:T(8,128)(2,1)} %bitcast.51), channel_id=1, source_target_pairs={{0,2},{1,3},{2,0},{3,1},{4,6},{5,7},{6,4},{7,5},{8,10},{9,11},{10,... | collective-permute-start | bytes 393224 | tf_op jit(solution)/shard_map/ppermute | solution.py:95
  26.2 77.7 %collective-permute-start.13 = (bf16[1,4,1024]{2,1,0:T(4,128)(2,1)}, bf16[1,4,1024]{2,1,0:T(4,128)(2,1)}, u32[]{:S(2)}, u32[]{:S(2)}) collective-permute-start(bf16[1,4,1024]{2,1,0:T(4,128)(2,1)} %get-tuple-element.290), channel_id=1, source_target_pairs={{0,1},{1,0},{2,3},{3,2},{4,5},{5,4},{6,7},{7,6},{8,9},{9,8},{10,11... | collective-permute-start | bytes 24584 | tf_op jit(solution)/shard_map/ppermute | solution.py:85
  28.3 40.8 %collective-permute-start.10 = (f32[1,576]{1,0:T(1,128)}, f32[1,576]{1,0:T(1,128)}, u32[]{:S(2)}, u32[]{:S(2)}) collective-permute-start(f32[1,576]{1,0:T(1,128)} %convert_element_type.32), channel_id=1, source_target_pairs={{0,2},{1,3},{2,0},{3,1},{4,6},{5,7},{6,4},{7,5},{8,10},{9,11},{10,... | collective-permute-start | bytes 6920 | tf_op jit(solution)/shard_map/ppermute | solution.py:95
  39.2 26.2 %collective-permute-start.3 = (bf16[256,2176]{1,0:T(8,128)(2,1)}, bf16[256,2176]{1,0:T(8,128)(2,1)}, u32[]{:S(2)}, u32[]{:S(2)}) collective-permute-start(bf16[256,2176]{1,0:T(8,128)(2,1)} %stack.15.refs_2_.refs_1_), channel_id=1, source_target_pairs={{0,4},{1,5},{2,3},{3,2},{4,0},{5,1},{6,7},{7,6},{8,12},{9,13},{10,... | collective-permute-start | bytes 3342344 | tf_op jit(solution)/shard_map/ppermute | solution.py:85
  40.4 24.9 %collective-permute-start.4 = (bf16[256,2176]{1,0:T(8,128)(2,1)}, bf16[256,2176]{1,0:T(8,128)(2,1)}, u32[]{:S(2)}, u32[]{:S(2)}) collective-permute-start(bf16[256,2176]{1,0:T(8,128)(2,1)} %stack.15.refs_2_.refs_1_), channel_id=1, source_target_pairs={{0,1},{1,0},{2,6},{3,7},{4,5},{5,4},{6,2},{7,3},{8,9},{9,8},{10,14... | collective-permute-start | bytes 3342344 | tf_op jit(solution)/shard_map/ppermute | solution.py:85
  42.9 23.5 %collective-permute-start.8 = (bf16[64,2048]{1,0:T(8,128)(2,1)S(1)}, bf16[64,2048]{1,0:T(8,128)(2,1)S(1)}, u32[]{:S(2)}, u32[]{:S(2)}) collective-permute-start(bf16[64,2048]{1,0:T(8,128)(2,1)S(1)} %stack.16.refs_0_.refs_2_), channel_id=1, source_target_pairs={{0,16},{1,17},{2,18},{3,19},{4,20},{5,21},{6,22},{7,23},{8,24},{9,... | collective-permute-start | bytes 786440 | tf_op jit(solution)/shard_map/ppermute | solution.py:85
  65.3 15.8 %collective-permute-start.5 = (bf16[256,2176]{1,0:T(8,128)(2,1)}, bf16[256,2176]{1,0:T(8,128)(2,1)}, u32[]{:S(2)}, u32[]{:S(2)}) collective-permute-start(bf16[256,2176]{1,0:T(8,128)(2,1)} %collective-permute-done.3.refs_3_.refs_2_), channel_id=1, source_target_pairs={{0,1},{1,0},{2,6},{3,7},{4,5},{5,4},{6,2},{7,3},{8,9},{9,8},{10,14... | collective-permute-start | bytes 3342344 | tf_op jit(solution)/shard_map/ppermute | solution.py:85
  66.5 14.1 %collective-permute-start.9 = (bf16[128,2048]{1,0:T(8,128)(2,1)S(1)}, bf16[128,2048]{1,0:T(8,128)(2,1)S(1)}, u32[]{:S(2)}, u32[]{:S(2)}) collective-permute-start(bf16[128,2048]{1,0:T(8,128)(2,1)S(1)} %stack.17.refs_0_.refs_2_), channel_id=1, source_target_pairs={{0,8},{1,9},{2,10},{3,11},{4,12},{5,13},{6,14},{7,15},{8,0},{9,1},... | collective-permute-start | bytes 1572872 | tf_op jit(solution)/shard_map/ppermute | solution.py:85
  70.1 20.6 %collective-permute-start.7 = (bf16[576,1024]{1,0:T(8,128)(2,1)}, bf16[576,1024]{1,0:T(8,128)(2,1)}, u32[]{:S(2)}, u32[]{:S(2)}) collective-permute-start(bf16[576,1024]{1,0:T(8,128)(2,1)} %bitcast.11.refs_5_.refs_2_), channel_id=1, source_target_pairs={{0,2},{1,3},{2,0},{3,1},{4,6},{5,7},{6,4},{7,5},{8,10},{9,11},{10,... | collective-permute-start | bytes 3538952 | tf_op jit(solution)/shard_map/ppermute | solution.py:95
  82.2 26.2 %collective-permute-start.12 = (bf16[256,2048]{1,0:T(8,128)(2,1)}, bf16[256,2048]{1,0:T(8,128)(2,1)}, u32[]{:S(2)}, u32[]{:S(2)}) collective-permute-start(bf16[256,2048]{1,0:T(8,128)(2,1)} %stack.18.refs_2_.refs_1_), channel_id=1, source_target_pairs={{0,4},{1,5},{2,3},{3,2},{4,0},{5,1},{6,7},{7,6},{8,12},{9,13},{10,... | collective-permute-start | bytes 3145736 | tf_op jit(solution)/shard_map/ppermute | solution.py:85
  84.4 23.9 %collective-permute-start.11 = (bf16[64,2048]{1,0:T(8,128)(2,1)}, bf16[64,2048]{1,0:T(8,128)(2,1)}, u32[]{:S(2)}, u32[]{:S(2)}) collective-permute-start(bf16[64,2048]{1,0:T(8,128)(2,1)} %stack.19.refs_5_.refs_0_), channel_id=1, source_target_pairs={{0,16},{1,17},{2,18},{3,19},{4,20},{5,21},{6,22},{7,23},{8,24},{9,... | collective-permute-start | bytes 786440 | tf_op jit(solution)/shard_map/ppermute | solution.py:85
  90.2 18.2 %collective-permute-start.14 = (bf16[256,2048]{1,0:T(8,128)(2,1)}, bf16[256,2048]{1,0:T(8,128)(2,1)}, u32[]{:S(2)}, u32[]{:S(2)}) collective-permute-start(bf16[256,2048]{1,0:T(8,128)(2,1)} %stack.18.refs_2_.refs_1_), channel_id=1, source_target_pairs={{0,1},{1,0},{2,6},{3,7},{4,5},{5,4},{6,2},{7,3},{8,9},{9,8},{10,14... | collective-permute-start | bytes 3145736 | tf_op jit(solution)/shard_map/ppermute | solution.py:85
  111.1 19.0 %collective-permute-start.16 = (bf16[256,2048]{1,0:T(8,128)(2,1)}, bf16[256,2048]{1,0:T(8,128)(2,1)}, u32[]{:S(2)}, u32[]{:S(2)}) collective-permute-start(bf16[256,2048]{1,0:T(8,128)(2,1)} %get-tuple-element.115.refs_2_.refs_3_), channel_id=1, source_target_pairs={{0,1},{1,0},{2,6},{3,7},{4,5},{5,4},{6,2},{7,3},{8,9},{9,8},{10,14... | collective-permute-start | bytes 3145736 | tf_op jit(solution)/shard_map/ppermute | solution.py:85
  112.6 17.5 %collective-permute-start.15 = (bf16[128,2048]{1,0:T(8,128)(2,1)}, bf16[128,2048]{1,0:T(8,128)(2,1)}, u32[]{:S(2)}, u32[]{:S(2)}) collective-permute-start(bf16[128,2048]{1,0:T(8,128)(2,1)} %get-tuple-element.113.refs_4_.refs_0_), channel_id=1, source_target_pairs={{0,8},{1,9},{2,10},{3,11},{4,12},{5,13},{6,14},{7,15},{8,0},{9,1},... | collective-permute-start | bytes 1572872 | tf_op jit(solution)/shard_map/ppermute | solution.py:85
  132.5 27.4 %collective-permute-start.18 = (bf16[256,2048]{1,0:T(8,128)(2,1)}, bf16[256,2048]{1,0:T(8,128)(2,1)}, u32[]{:S(2)}, u32[]{:S(2)}) collective-permute-start(bf16[256,2048]{1,0:T(8,128)(2,1)} %stack.21.refs_6_.refs_1_), channel_id=1, source_target_pairs={{0,4},{1,5},{2,3},{3,2},{4,0},{5,1},{6,7},{7,6},{8,12},{9,13},{10,... | collective-permute-start | bytes 3145736 | tf_op jit(solution)/shard_map/ppermute | solution.py:85
  137.2 4.9 %collective-permute-start.17 = (f32[576,1024]{1,0:T(8,128)}, f32[576,1024]{1,0:T(8,128)}, u32[]{:S(2)}, u32[]{:S(2)}) collective-permute-start(f32[576,1024]{1,0:T(8,128)} %mix_out.2.refs_6_), channel_id=1, source_target_pairs={{0,2},{1,3},{2,0},{3,1},{4,6},{5,7},{6,4},{7,5},{8,10},{9,11},{10,... | collective-permute-start | bytes 7077896 | tf_op jit(solution)/shard_map/ppermute | solution.py:95
  137.3 22.6 %collective-permute-start.19 = (bf16[256,2048]{1,0:T(8,128)(2,1)}, bf16[256,2048]{1,0:T(8,128)(2,1)}, u32[]{:S(2)}, u32[]{:S(2)}) collective-permute-start(bf16[256,2048]{1,0:T(8,128)(2,1)} %stack.21.refs_6_.refs_1_), channel_id=1, source_target_pairs={{0,1},{1,0},{2,6},{3,7},{4,5},{5,4},{6,2},{7,3},{8,9},{9,8},{10,14... | collective-permute-start | bytes 3145736 | tf_op jit(solution)/shard_map/ppermute | solution.py:85
  146.9 14.3 %collective-permute-start.21 = (bf16[576,1024]{1,0:T(8,128)(2,1)}, bf16[576,1024]{1,0:T(8,128)(2,1)}, u32[]{:S(2)}, u32[]{:S(2)}) collective-permute-start(bf16[576,1024]{1,0:T(8,128)(2,1)} %get-tuple-element.117.refs_5_), channel_id=1, source_target_pairs={{0,2},{1,3},{2,0},{3,1},{4,6},{5,7},{6,4},{7,5},{8,10},{9,11},{10,... | collective-permute-start | bytes 3538952 | tf_op jit(solution)/shard_map/ppermute | solution.py:95
  159.9 15.1 %collective-permute-start.20 = (bf16[256,2048]{1,0:T(8,128)(2,1)}, bf16[256,2048]{1,0:T(8,128)(2,1)}, u32[]{:S(2)}, u32[]{:S(2)}) collective-permute-start(bf16[256,2048]{1,0:T(8,128)(2,1)} %collective-permute-done.18.refs_2_.refs_7_), channel_id=1, source_target_pairs={{0,1},{1,0},{2,6},{3,7},{4,5},{5,4},{6,2},{7,3},{8,9},{9,8},{10,14... | collective-permute-start | bytes 3145736 | tf_op jit(solution)/shard_map/ppermute | solution.py:85
  182.3 6.0 %collective-permute-start.22 = (f32[576,1024]{1,0:T(8,128)}, f32[576,1024]{1,0:T(8,128)}, u32[]{:S(2)}, u32[]{:S(2)}) collective-permute-start(f32[576,1024]{1,0:T(8,128)} %feed_down.2.refs_6_), channel_id=1, source_target_pairs={{0,2},{1,3},{2,0},{3,1},{4,6},{5,7},{6,4},{7,5},{8,10},{9,11},{10,... | collective-permute-start | bytes 7077896 | tf_op jit(solution)/shard_map/ppermute | solution.py:95
  195.3 2.9 collective-permute-start.24
  196.7 14.2 %collective-permute-start.23 = (f32[1,4,1024]{2,1,0:T(4,128)}, f32[1,4,1024]{2,1,0:T(4,128)}, u32[]{:S(2)}, u32[]{:S(2)}) collective-permute-start(f32[1,4,1024]{2,1,0:T(4,128)} %get-tuple-element.288), channel_id=1, source_target_pairs={{0,1},{1,0},{2,3},{3,2},{4,5},{5,4},{6,7},{7,6},{8,9},{9,8},{10,11... | collective-permute-start | bytes 49160 | tf_op jit(solution)/shard_map/ppermute | solution.py:85
  209.5 26.4 %collective-permute-start.25 = (bf16[1024,1024]{1,0:T(8,128)(2,1)}, bf16[1024,1024]{1,0:T(8,128)(2,1)}, u32[]{:S(2)}, u32[]{:S(2)}) collective-permute-start(bf16[1024,1024]{1,0:T(8,128)(2,1)} %get-tuple-element.132), channel_id=1, source_target_pairs={{0,1},{1,0},{2,6},{3,7},{4,5},{5,4},{6,2},{7,3},{8,9},{9,8},{10,14... | collective-permute-start | bytes 6291464 | tf_op jit(solution)/shard_map/ppermute | solution.py:85
  239.2 12.0 %collective-permute-start.26 = (f32[576,1024]{1,0:T(8,128)}, f32[576,1024]{1,0:T(8,128)}, u32[]{:S(2)}, u32[]{:S(2)}) collective-permute-start(f32[576,1024]{1,0:T(8,128)} %get-tuple-element.135), channel_id=1, source_target_pairs={{0,2},{1,3},{2,0},{3,1},{4,6},{5,7},{6,4},{7,5},{8,10},{9,11},{10,... | collective-permute-start | bytes 7077896 | tf_op jit(solution)/shard_map/ppermute | solution.py:95
  239.2 19.8 %collective-permute-start.27 = (bf16[512,1024]{1,0:T(8,128)(2,1)}, bf16[512,1024]{1,0:T(8,128)(2,1)}, u32[]{:S(2)}, u32[]{:S(2)}) collective-permute-start(bf16[512,1024]{1,0:T(8,128)(2,1)} %get-tuple-element.141), channel_id=1, source_target_pairs={{0,4},{1,5},{2,3},{3,2},{4,0},{5,1},{6,7},{7,6},{8,12},{9,13},{10,... | collective-permute-start | bytes 3145736 | tf_op jit(solution)/shard_map/ppermute | solution.py:85
  260.9 16.3 %collective-permute-start.28 = (bf16[576,1024]{1,0:T(8,128)(2,1)}, bf16[576,1024]{1,0:T(8,128)(2,1)}, u32[]{:S(2)}, u32[]{:S(2)}) collective-permute-start(bf16[576,1024]{1,0:T(8,128)(2,1)} %get-tuple-element.145.refs_10_.refs_6_), channel_id=1, source_target_pairs={{0,2},{1,3},{2,0},{3,1},{4,6},{5,7},{6,4},{7,5},{8,10},{9,11},{10,... | collective-permute-start | bytes 3538952 | tf_op jit(solution)/shard_map/ppermute | solution.py:95
  260.9 31.8 %collective-permute-start.30 = (bf16[256,1024]{1,0:T(8,128)(2,1)}, bf16[256,1024]{1,0:T(8,128)(2,1)}, u32[]{:S(2)}, u32[]{:S(2)}) collective-permute-start(bf16[256,1024]{1,0:T(8,128)(2,1)} %get-tuple-element.150), channel_id=1, source_target_pairs={{0,8},{1,9},{2,10},{3,11},{4,12},{5,13},{6,14},{7,15},{8,0},{9,1},... | collective-permute-start | bytes 1572872 | tf_op jit(solution)/shard_map/ppermute | solution.py:85
  261.5 37.5 %collective-permute-start.29 = (bf16[512,2048]{1,0:T(8,128)(2,1)}, bf16[512,2048]{1,0:T(8,128)(2,1)}, u32[]{:S(2)}, u32[]{:S(2)}) collective-permute-start(bf16[512,2048]{1,0:T(8,128)(2,1)} %get-tuple-element.149), channel_id=1, source_target_pairs={{0,1},{1,0},{2,6},{3,7},{4,5},{5,4},{6,2},{7,3},{8,9},{9,8},{10,14... | collective-permute-start | bytes 6291464 | tf_op jit(solution)/shard_map/ppermute | solution.py:85
  295.1 27.4 %collective-permute-start.34 = (bf16[128,1024]{1,0:T(8,128)(2,1)}, bf16[128,1024]{1,0:T(8,128)(2,1)}, u32[]{:S(2)}, u32[]{:S(2)}) collective-permute-start(bf16[128,1024]{1,0:T(8,128)(2,1)} %get-tuple-element.160), channel_id=1, source_target_pairs={{0,16},{1,17},{2,18},{3,19},{4,20},{5,21},{6,22},{7,23},{8,24},{9,... | collective-permute-start | bytes 786440 | tf_op jit(solution)/shard_map/ppermute | solution.py:85
  302.2 15.1 %collective-permute-start.31 = (bf16[256,2048]{1,0:T(8,128)(2,1)}, bf16[256,2048]{1,0:T(8,128)(2,1)}, u32[]{:S(2)}, u32[]{:S(2)}) collective-permute-start(bf16[256,2048]{1,0:T(8,128)(2,1)} %get-tuple-element.155), channel_id=1, source_target_pairs={{0,4},{1,5},{2,3},{3,2},{4,0},{5,1},{6,7},{7,6},{8,12},{9,13},{10,... | collective-permute-start | bytes 3145736 | tf_op jit(solution)/shard_map/ppermute | solution.py:85
  319.3 13.1 %collective-permute-start.33 = (bf16[128,2048]{1,0:T(8,128)(2,1)}, bf16[128,2048]{1,0:T(8,128)(2,1)}, u32[]{:S(2)}, u32[]{:S(2)}) collective-permute-start(bf16[128,2048]{1,0:T(8,128)(2,1)} %get-tuple-element.158), channel_id=1, source_target_pairs={{0,8},{1,9},{2,10},{3,11},{4,12},{5,13},{6,14},{7,15},{8,0},{9,1},... | collective-permute-start | bytes 1572872 | tf_op jit(solution)/shard_map/ppermute | solution.py:85
  320.9 15.1 %collective-permute-start.32 = (bf16[512,1024]{1,0:T(8,128)(2,1)}, bf16[512,1024]{1,0:T(8,128)(2,1)}, u32[]{:S(2)}, u32[]{:S(2)}) collective-permute-start(bf16[512,1024]{1,0:T(8,128)(2,1)} %get-tuple-element.157), channel_id=1, source_target_pairs={{0,1},{1,0},{2,6},{3,7},{4,5},{5,4},{6,2},{7,3},{8,9},{9,8},{10,14... | collective-permute-start | bytes 3145736 | tf_op jit(solution)/shard_map/ppermute | solution.py:85
  334.6 22.0 %collective-permute-start.36 = (bf16[64,2048]{1,0:T(8,128)(2,1)}, bf16[64,2048]{1,0:T(8,128)(2,1)}, u32[]{:S(2)}, u32[]{:S(2)}) collective-permute-start(bf16[64,2048]{1,0:T(8,128)(2,1)} %get-tuple-element.169), channel_id=1, source_target_pairs={{0,16},{1,17},{2,18},{3,19},{4,20},{5,21},{6,22},{7,23},{8,24},{9,... | collective-permute-start | bytes 786440 | tf_op jit(solution)/shard_map/ppermute | solution.py:85
  338.0 15.2 %collective-permute-start.37 = (bf16[256,1024]{1,0:T(8,128)(2,1)}, bf16[256,1024]{1,0:T(8,128)(2,1)}, u32[]{:S(2)}, u32[]{:S(2)}) collective-permute-start(bf16[256,1024]{1,0:T(8,128)(2,1)} %get-tuple-element.170), channel_id=1, source_target_pairs={{0,4},{1,5},{2,3},{3,2},{4,0},{5,1},{6,7},{7,6},{8,12},{9,13},{10,... | collective-permute-start | bytes 1572872 | tf_op jit(solution)/shard_map/ppermute | solution.py:85
  339.3 19.1 %collective-permute-start.35 = (bf16[512,1024]{1,0:T(8,128)(2,1)}, bf16[512,1024]{1,0:T(8,128)(2,1)}, u32[]{:S(2)}, u32[]{:S(2)}) collective-permute-start(bf16[512,1024]{1,0:T(8,128)(2,1)} %get-tuple-element.168), channel_id=1, source_target_pairs={{0,1},{1,0},{2,6},{3,7},{4,5},{5,4},{6,2},{7,3},{8,9},{9,8},{10,14... | collective-permute-start | bytes 3145736 | tf_op jit(solution)/shard_map/ppermute | solution.py:85
  360.6 7.2 %collective-permute-start.38 = (f32[576,1024]{1,0:T(8,128)}, f32[576,1024]{1,0:T(8,128)}, u32[]{:S(2)}, u32[]{:S(2)}) collective-permute-start(f32[576,1024]{1,0:T(8,128)} %get-tuple-element.174), channel_id=1, source_target_pairs={{0,2},{1,3},{2,0},{3,1},{4,6},{5,7},{6,4},{7,5},{8,10},{9,11},{10,... | collective-permute-start | bytes 7077896 | tf_op jit(solution)/shard_map/ppermute | solution.py:95
  363.4 24.0 %collective-permute-start.40 = (bf16[64,1024]{1,0:T(8,128)(2,1)}, bf16[64,1024]{1,0:T(8,128)(2,1)}, u32[]{:S(2)}, u32[]{:S(2)}) collective-permute-start(bf16[64,1024]{1,0:T(8,128)(2,1)} %get-tuple-element.185), channel_id=1, source_target_pairs={{0,16},{1,17},{2,18},{3,19},{4,20},{5,21},{6,22},{7,23},{8,24},{9,... | collective-permute-start | bytes 393224 | tf_op jit(solution)/shard_map/ppermute | solution.py:85
  365.0 24.0 %collective-permute-start.41 = (bf16[64,1024]{1,0:T(8,128)(2,1)}, bf16[64,1024]{1,0:T(8,128)(2,1)}, u32[]{:S(2)}, u32[]{:S(2)}) collective-permute-start(bf16[64,1024]{1,0:T(8,128)(2,1)} %get-tuple-element.186), channel_id=1, source_target_pairs={{0,8},{1,9},{2,10},{3,11},{4,12},{5,13},{6,14},{7,15},{8,0},{9,1},... | collective-permute-start | bytes 393224 | tf_op jit(solution)/shard_map/ppermute | solution.py:85
  365.9 23.3 %collective-permute-start.42 = (bf16[64,1024]{1,0:T(8,128)(2,1)}, bf16[64,1024]{1,0:T(8,128)(2,1)}, u32[]{:S(2)}, u32[]{:S(2)}) collective-permute-start(bf16[64,1024]{1,0:T(8,128)(2,1)} %get-tuple-element.187), channel_id=1, source_target_pairs={{0,24},{1,25},{2,26},{3,27},{4,28},{5,29},{6,30},{7,31},{8,16},{9,... | collective-permute-start | bytes 393224 | tf_op jit(solution)/shard_map/ppermute | solution.py:85
  367.8 23.2 %collective-permute-start.39 = (f32[32,2048]{1,0:T(8,128)}, f32[32,2048]{1,0:T(8,128)}, u32[]{:S(2)}, u32[]{:S(2)}) collective-permute-start(f32[32,2048]{1,0:T(8,128)} %get-tuple-element.184), channel_id=1, source_target_pairs={{0,2},{1,3},{2,0},{3,1},{4,6},{5,7},{6,4},{7,5},{8,10},{9,11},{10,... | collective-permute-start | bytes 786440 | tf_op jit(solution)/shard_map/ppermute | solution.py:95
  367.8 15.2 %collective-permute-start.43 = (bf16[256,1024]{1,0:T(8,128)(2,1)}, bf16[256,1024]{1,0:T(8,128)(2,1)}, u32[]{:S(2)}, u32[]{:S(2)}) collective-permute-start(bf16[256,1024]{1,0:T(8,128)(2,1)} %get-tuple-element.188), channel_id=1, source_target_pairs={{0,4},{1,5},{2,3},{3,2},{4,0},{5,1},{6,7},{7,6},{8,12},{9,13},{10,... | collective-permute-start | bytes 1572872 | tf_op jit(solution)/shard_map/ppermute | solution.py:85
  379.4 16.2 %all-to-all-start = ((bf16[32,32,128]{2,1,0:T(8,128)(2,1)}), bf16[32,32,128]{2,1,0:T(8,128)(2,1)}, u32[]{:S(2)}, u32[]{:S(2)}) async-start(bf16[32,32,128]{2,1,0:T(8,128)(2,1)} %bitcast.24), calls=%async_computation | async-start | bytes 524288 | tf_op jit(solution)/shard_map/all_to_all | solution.py:1412
  384.8 16.4 %collective-permute-start.45 = (bf16[64,1024]{1,0:T(8,128)(2,1)}, bf16[64,1024]{1,0:T(8,128)(2,1)}, u32[]{:S(2)}, u32[]{:S(2)}) collective-permute-start(bf16[64,1024]{1,0:T(8,128)(2,1)} %get-tuple-element.193), channel_id=1, source_target_pairs={{0,16},{1,17},{2,18},{3,19},{4,20},{5,21},{6,22},{7,23},{8,24},{9,... | collective-permute-start | bytes 393224 | tf_op jit(solution)/shard_map/ppermute | solution.py:85
  387.5 13.8 %collective-permute-start.46 = (bf16[64,1024]{1,0:T(8,128)(2,1)}, bf16[64,1024]{1,0:T(8,128)(2,1)}, u32[]{:S(2)}, u32[]{:S(2)}) collective-permute-start(bf16[64,1024]{1,0:T(8,128)(2,1)} %get-tuple-element.194), channel_id=1, source_target_pairs={{0,8},{1,9},{2,10},{3,11},{4,12},{5,13},{6,14},{7,15},{8,0},{9,1},... | collective-permute-start | bytes 393224 | tf_op jit(solution)/shard_map/ppermute | solution.py:85
  389.0 12.2 %collective-permute-start.47 = (bf16[64,1024]{1,0:T(8,128)(2,1)}, bf16[64,1024]{1,0:T(8,128)(2,1)}, u32[]{:S(2)}, u32[]{:S(2)}) collective-permute-start(bf16[64,1024]{1,0:T(8,128)(2,1)} %get-tuple-element.195), channel_id=1, source_target_pairs={{0,24},{1,25},{2,26},{3,27},{4,28},{5,29},{6,30},{7,31},{8,16},{9,... | collective-permute-start | bytes 393224 | tf_op jit(solution)/shard_map/ppermute | solution.py:85
  391.0 13.3 %collective-permute-start.44 = (f32[32,1024]{1,0:T(8,128)}, f32[32,1024]{1,0:T(8,128)}, u32[]{:S(2)}, u32[]{:S(2)}) collective-permute-start(f32[32,1024]{1,0:T(8,128)} %get-tuple-element.192), channel_id=1, source_target_pairs={{0,2},{1,3},{2,0},{3,1},{4,6},{5,7},{6,4},{7,5},{8,10},{9,11},{10,... | collective-permute-start | bytes 393224 | tf_op jit(solution)/shard_map/ppermute | solution.py:95
  (84 other events, 342.5 us)

commit v5 on v4

--- a/solution.py
+++ b/solution.py
@@ -747,12 +747,12 @@
 def feed_back(tables, up, down, grad, other, slope, other_slope):
     rows, width = grad.shape
     tall, units = 2 * rows, slope.shape[1]
-    span, count = units // 4, len(up)
+    span, count, piece = units // 4, len(up), width // 4
 
     def kernel(t32, t16, *rest):
         up_refs, down_refs, rest = rest[:count], rest[count : 2 * count], rest[2 * count :]
         g_ref, o_ref, slope_ref, slope_other, pre_ref, sum_ref, own_ref, other_ref, *rest = rest
-        both, high, low, sems = rest
+        both, high, low, pre, sems = rest
         step = pl.program_id(0)
 
         def copies():
@@ -769,40 +769,40 @@
             wait(one)
             wait(two)
 
-        at = pl.ds(pl.multiple_of(step * span, span), span)
-        grad_act = dot(both[...], low[at, :], NT)
-        pre_ref[:rows, :] = (grad_act[:rows] * slope_ref[...].astype(F32)).astype(BF)
-        pre_ref[rows:, :] = (grad_act[rows:] * slope_other[...].astype(F32)).astype(BF)
-        grad_pre = pre_ref[...]
-        sum_ref[...] = jnp.sum(grad_pre.astype(F32), axis=0, keepdims=True)
-        part = dot(grad_pre, high[:, at], NT)
-
-        @pl.when(step == 0)
-        def _():
+        @pl.when(step < 4)
+        def _():
+            at = pl.ds(pl.multiple_of(step * span, span), span)
+            grad_act = dot(both[...], low[at, :], NT)
+            pre_ref[:rows, :] = (grad_act[:rows] * slope_ref[...].astype(F32)).astype(BF)
+            pre_ref[rows:, :] = (grad_act[rows:] * slope_other[...].astype(F32)).astype(BF)
+            pre[:, at] = pre_ref[...]
+            sum_ref[...] = jnp.sum(pre_ref[...].astype(F32), axis=0, keepdims=True)
+
+        @pl.when(step >= 4)
+        def _():
+            at = pl.ds(pl.multiple_of((step - 4) * piece, piece), piece)
+            part = dot(pre[...], high[at, :], NT)
             own_ref[...] = part[:rows]
             other_ref[...] = part[rows:]
 
-        @pl.when(step > 0)
-        def _():
-            own_ref[...] += part[:rows]
-            other_ref[...] += part[rows:]
-
     whole = lambda m, n: pl.BlockSpec((m, n), lambda j: (0, 0))
-    strip = lambda m: pl.BlockSpec((m, span), lambda j: (0, j))
-    return launch(
-        kernel,
-        grid=(4,),
+    strip = lambda m: pl.BlockSpec((m, span), lambda j: (0, jnp.minimum(j, 3)))
+    late = pl.BlockSpec((rows, piece), lambda j: (0, jnp.maximum(j - 4, 0)))
+    return launch(
+        kernel,
+        grid=(8,),
         in_specs=[TABLE, TABLE]
         + [HBM] * (2 * count)
         + [whole(rows, width)] * 2
         + [strip(rows)] * 2,
-        out_specs=[strip(tall), strip(1), whole(rows, width), whole(rows, width)],
+        out_specs=[strip(tall), strip(1), late, late],
         out_shape=[shape((tall, units), BF), shape((1, units), F32)]
         + [shape((rows, width), F32)] * 2,
         scratch_shapes=[
             pltpu.VMEM((tall, width), BF),
             pltpu.VMEM((width, units), BF),
             pltpu.VMEM((units, width), BF),
+            pltpu.VMEM((tall, units), BF),
             pltpu.SemaphoreType.DMA((2, BLOCKS)),
         ],
         compiler_params=params("arbitrary", vmem=44),
@@ -1031,18 +1031,19 @@
     )(own, got, patches, stats, gain, grad_residual)
 
 
-def start_blocks(table_ref, lefts, held, sems):
+def start_blocks(table_ref, lefts, held, sems, only=(1, 0)):
     count = sems.shape[1]
     step, wide = held.shape[0] // count, held.shape[1] // len(lefts)
     low, high = [], []
-    for block in range(count):
+    for block in (b for b in range(count) if 2 * b // count in only):
         at = pl.multiple_of(table_ref[block] * step, step)
         for i, left in enumerate(lefts):
             target = held.at[pl.ds(block * step, step), pl.ds(i * wide, wide)]
             copy = pltpu.make_async_copy(left.at[pl.ds(at, step)], target, sems.at[i, block])
             (low if block < count // 2 else high).append(copy)
-    for copy in high + low:
-        copy.start()
+    for i in only:
+        for copy in (low, high)[i]:
+            copy.start()
     return low, high
 
 
@@ -1055,7 +1056,7 @@
         )
 
 
-def weight_grad(table, turned, rights, part=None, parts=1, tile=512):
+def weight_grad(table, turned, rights, part=None, parts=1, tile=512, only=(1, 0)):
     height = turned[0].shape[0]
     deep = sum(left.shape[1] for left in turned)
     blocks, half = table.shape[0], height // 2
@@ -1063,25 +1064,26 @@
 
     def kernel(table_ref, *refs):
         lefts, refs = refs[: len(turned)], refs[len(turned) :]
-        values, (low_ref, high_ref, held, value, sems) = refs[: len(rights)], refs[len(rights) :]
-
-        def product(where, ref):
-            ref[...] = dot(held[where, :], value[...], NN).astype(BF)
+        values, refs = refs[: len(rights)], refs[len(rights) :]
+        outs, (held, value, sems) = dict(zip(only, refs)), refs[len(only) :]
+
+        def product(i):
+            rows_of = slice(i * half, (i + 1) * half)
+            outs[i][...] = dot(held[rows_of, :], value[...], NN).astype(BF)
 
         @pl.when(pl.program_id(0) == 0)
         def _():
-            low, high = start_blocks(table_ref, lefts, held, sems)
+            copies = start_blocks(table_ref, lefts, held, sems, only)
             place_rows(value, spots(values))
-            wait(high)
-            product(slice(half, height), high_ref)
-            wait(low)
-            product(slice(0, half), low_ref)
+            for i in only:
+                wait(copies[i])
+                product(i)
 
         @pl.when(pl.program_id(0) > 0)
         def _():
             place_rows(value, spots(values))
-            product(slice(half, height), high_ref)
-            product(slice(0, half), low_ref)
+            for i in only:
+                product(i)
 
     def spots(values):
         if len(rights) == 1:
@@ -1099,8 +1101,8 @@
         kernel,
         grid=(cols // tile,),
         in_specs=[TABLE] + [HBM] * len(turned) + [spec] * len(rights),
-        out_specs=[pl.BlockSpec((half, tile), lambda n: (0, n))] * 2,
-        out_shape=[shape((half, cols), BF)] * 2,
+        out_specs=[pl.BlockSpec((half, tile), lambda n: (0, n))] * len(only),
+        out_shape=[shape((half, cols), BF)] * len(only),
         scratch_shapes=[
             pltpu.VMEM((height, deep), BF),
             pltpu.VMEM((deep, tile), BF),
@@ -1349,7 +1351,11 @@
         token_got = permute(token_send, BOTH(MAP))
     else:
         tokens_out = lax.all_to_all(token_local, "map", split_axis=1, concat_axis=0, tiled=True)
-    down_parts = weight_grad(own_table, [act_t, act_t_b], [grad_down_low, other_down])
+    down_half = lambda i: weight_grad(
+        own_table, [act_t, act_t_b], [grad_down_low, other_down], only=(i,)
+    )[0]
+    down_high = down_half(1)
+    down_parts = [down_half(0), down_high]
     if layered:
         down_sum = Halving(down_parts)
         tokens_out = join_tokens(where, token_mine, token_got).astype(BF)
@@ -1361,7 +1367,7 @@
         down_sum.advance()
         held = (down_sum.low,)
     hidden_got = to_sibling(tie(hidden_other, *held))
-    up_parts = weight_grad(table, [turned_two, turned_two_b], [grad_pre])
+    up_parts = weight_grad(table, [turned_two, turned_two_b], [grad_pre])[::-1]
     grad_residual, grad_attn, two_sums = second_norm_back(
         hidden_own, hidden_got, residual_one, grad_block, gain_two
     )
@@ -1378,7 +1384,7 @@
     if layered:
         down_sum.advance()
         up_sum.advance()
-    near_parts = weight_grad(table, [hidden_one_t], grad_qkv, 0, 2)
+    near_parts = weight_grad(table, [hidden_one_t], grad_qkv, 0, 2)[::-1]
     if layered:
         up_sum.advance()
         grad_down = down_sum.finish()

time: 413 us -> 412 us (level)
    unnamed x168 -> x164, local copies, waits for them, and re-layouts: 24.4 us -> 26.1 us
    pallas_call x50 -> x51, Pallas kernels: 233 us -> 234 us  [run(): outs = pl.pallas_call(body, in_specs=specs, **settings)(*operands, *waited)]
  transfers between devices with their start and end apart: 50 -> 50, of which waited for: 16 -> 16; matrix products, arithmetic and copies ran while one was open for 4% -> 4% of each run, Pallas kernels for 50% -> 51%
where the time goes in v5:
time: 412 us; the launch traced here: 406 us
  Pallas kernels  234 us (57%)
  waiting for transfers between devices  71.8 us (17%)
  starting transfers between devices  55.6 us (13%)
  local copies, waits for them, and re-layouts  33.9 us (8%)
  other arithmetic  8.73 us (2%)
    pallas_call x51, Pallas kernels, run(): outs = pl.pallas_call(body, in_specs=specs, **settings)(*operands, *waited)  234 us
    ppermute x35, waiting for transfers between devices, permute(): return lax.ppermute(values, AXES, pairs)  67.3 us
    ppermute x35, starting transfers between devices, permute(): return lax.ppermute(values, AXES, pairs)  50.2 us
    unnamed x164, local copies, waits for them, and re-layouts  26.1 us
  transfers between devices with their start and end apart: 50, of which 16 were waited for; matrix products, arithmetic and copies ran while one was open for 4% of the time, Pallas kernels for 51%

profile of v5, /device:TPU:0, one launch (start us, length us, event | category | flops | bytes accessed | tf_op | source)
XLA Modules:
  0.0 405.6 jit_solution(14827455755023827661)
XLA Ops:
  6.8 4.0 collective-permute-start.1
  12.2 11.6 %collective-permute-done.1.refs_1_ = bf16[64,2176]{1,0:T(8,128)(2,1)S(1)} collective-permute-done((bf16[64,2176]{1,0:T(8,128)(2,1)S(1)}, bf16[64,2176]{1,0:T(8,128)(2,1)S(1)}, u32[]{:S(2)}, u32[]{:S(2)}) %collective-permute-start.1) | collective-permute-done | bytes 278560 | tf_op jit(solution)/shard_map/ppermute | solution.py:85
  29.1 9.0 %collective-permute-done.2.refs_1_ = bf16[128,2176]{1,0:T(8,128)(2,1)S(1)} collective-permute-done((bf16[128,2176]{1,0:T(8,128)(2,1)S(1)}, bf16[128,2176]{1,0:T(8,128)(2,1)S(1)}, u32[]{:S(2)}, u32[]{:S(2)}) %collective-permute-start.2) | collective-permute-done | bytes 557088 | tf_op jit(solution)/shard_map/ppermute | solution.py:85
  42.9 3.1 collective-permute-start.8
  46.7 18.7 %collective-permute-done.3.refs_3_.refs_2_ = bf16[256,2176]{1,0:T(8,128)(2,1)} collective-permute-done((bf16[256,2176]{1,0:T(8,128)(2,1)}, bf16[256,2176]{1,0:T(8,128)(2,1)}, u32[]{:S(2)}, u32[]{:S(2)}) %collective-permute-start.3) | collective-permute-done | bytes 1114144 | tf_op jit(solution)/shard_map/ppermute | solution.py:85
  70.3 10.3 %collective-permute-done.9.refs_1_ = bf16[128,2048]{1,0:T(8,128)(2,1)S(1)} collective-permute-done((bf16[128,2048]{1,0:T(8,128)(2,1)S(1)}, bf16[128,2048]{1,0:T(8,128)(2,1)S(1)}, u32[]{:S(2)}, u32[]{:S(2)}) %collective-permute-start.9) | collective-permute-done | bytes 524320 | tf_op jit(solution)/shard_map/ppermute | solution.py:85
  84.4 4.1 %collective-permute-start.11 = (bf16[64,2048]{1,0:T(8,128)(2,1)}, bf16[64,2048]{1,0:T(8,128)(2,1)}, u32[]{:S(2)}, u32[]{:S(2)}) collective-permute-start(bf16[64,2048]{1,0:T(8,128)(2,1)} %stack.19.refs_5_.refs_0_), channel_id=1, source_target_pairs={{0,16},{1,17},{2,18},{3,19},{4,20},{5,21},{6,22},{7,23},{8,24},{9,... | collective-permute-start | bytes 786440 | tf_op jit(solution)/shard_map/ppermute | solution.py:85
  90.8 11.5 %project.1 = (bf16[1152,1536]{1,0:T(8,128)(2,1)}, bf16[1024,1280]{1,0:T(8,128)(2,1)S(1)}, f32[576,2]{1,0:T(8,128)S(1)}) custom-call(s32[32]{0:T(128)S(1)} %reshape.301.refs_0_, bf16[256,2176]{1,0:T(8,128)(2,1)} %stack.15.refs_2_.refs_1_, bf16[256,2176]{1,0:T(8,128)(2,1)} %collective-permute-done.3.refs_3_.refs_2_, ...), custom_call_target="tpu_custom_call" | custom-call | flops 999999995904 | bytes 1024 | tf_op jit(solution)/shard_map/project/pallas_call | solution.py:40
  103.9 2.0 copy-done.22
  108.4 2.7 stack.20
  114.1 14.0 %attend.1 = (bf16[1152,512]{1,0:T(8,128)(2,1)S(1)}, bf16[512,1280]{1,0:T(8,128)(2,1)S(1)}, f32[4,4,576]{2,1,0:T(4,128)S(1)}) custom-call(bf16[1152,1536]{1,0:T(8,128)(2,1)S(1)} %copy-done.23, bf16[1152,1536]{1,0:T(8,128)(2,1)S(1)} %copy-done.23, bf16[1152,1536]{1,0:T(8,128)(2,1)S(1)} %copy-done.23, f32[1152,1]{1,0:T(8,128)S(1)} %copy.76.refs_3_.refs_8_, ...), custom_call_target="tpu_custom_call" | custom-call | flops 999999995904 | bytes 1024 | tf_op jit(solution)/shard_map/attend/pallas_call | solution.py:40
  130.2 2.3 stack.21.refs_6_.refs_1_
  133.0 4.2 %mix_out.2.refs_6_ = f32[576,1024]{1,0:T(8,128)} custom-call(s32[16]{0:T(128)S(1)} %and_add_fusion.refs_0_.refs_1_, bf16[256,2176]{1,0:T(8,128)(2,1)} %stack.15.refs_2_.refs_1_, bf16[256,2176]{1,0:T(8,128)(2,1)} %collective-permute-done.3.refs_3_.refs_2_, bf16[256,2176]{1,0:T(8,128)(2,1)} %collective-permute-done.4.refs_4_.refs_3_, ...), custom_call_target="tpu_custom_call" | custom-call | flops 999999995904 | bytes 1024 | tf_op jit(solution)/shard_map/mix_out/pallas_call | solution.py:40
  138.7 2.8 mix_out.3.refs_0_.refs_6_
  142.2 3.3 second_norm.1
  147.0 10.3 %feed_up.2 = (bf16[576,2048]{1,0:T(8,128)(2,1)S(1)}, bf16[2048,640]{1,0:T(8,128)(2,1)}, bf16[576,2048]{1,0:T(8,128)(2,1)}, bf16[1024,640]{1,0:T(8,128)(2,1)S(1)}) custom-call(s32[32]{0:T(128)S(1)} %reshape.301.refs_0_, bf16[256,2048]{1,0:T(8,128)(2,1)} %stack.18.refs_2_.refs_1_, bf16[256,2048]{1,0:T(8,128)(2,1)} %get-tuple-element.113.refs_2_.refs_3_, ...), custom_call_target="tpu_custom_call" | custom-call | flops 999999995904 | bytes 1024 | tf_op jit(solution)/shard_map/feed_up/pallas_call | solution.py:40
  161.2 10.6 %feed_up.3 = (bf16[576,2048]{1,0:T(8,128)(2,1)S(1)}, bf16[2048,640]{1,0:T(8,128)(2,1)}, bf16[576,2048]{1,0:T(8,128)(2,1)}, bf16[1024,640]{1,0:T(8,128)(2,1)S(1)}) custom-call(s32[32]{0:T(128)S(1)} %reshape.301.refs_0_, bf16[256,2048]{1,0:T(8,128)(2,1)} %stack.18.refs_2_.refs_1_, bf16[256,2048]{1,0:T(8,128)(2,1)} %get-tuple-element.113.refs_2_.refs_3_, ...), custom_call_target="tpu_custom_call" | custom-call | flops 999999995904 | bytes 1024 | tf_op jit(solution)/shard_map/feed_up/pallas_call | solution.py:40
  171.8 3.2 collective-permute-done.20.refs_4_.refs_9_
  175.0 7.3 %feed_down.2.refs_6_ = f32[576,1024]{1,0:T(8,128)} custom-call(s32[16]{0:T(128)S(1)} %and_add_fusion.refs_0_.refs_1_, bf16[256,2048]{1,0:T(8,128)(2,1)} %stack.21.refs_6_.refs_1_, bf16[256,2048]{1,0:T(8,128)(2,1)} %collective-permute-done.18.refs_2_.refs_7_, bf16[256,2048]{1,0:T(8,128)(2,1)} %collective-permute-done.19.refs_3_.refs_8_, ...), custom_call_target="tpu_custom_call" | custom-call | flops 999999995904 | bytes 1024 | tf_op jit(solution)/shard_map/feed_down/pallas_call | solution.py:40
  182.4 5.9 %feed_down.3.refs_1_.refs_10_ = f32[576,1024]{1,0:T(8,128)S(1)} custom-call(s32[16]{0:T(128)S(1)} %and_add_fusion.refs_0_.refs_1_, bf16[256,2048]{1,0:T(8,128)(2,1)} %stack.21.refs_6_.refs_1_, bf16[256,2048]{1,0:T(8,128)(2,1)} %collective-permute-done.18.refs_2_.refs_7_, bf16[256,2048]{1,0:T(8,128)(2,1)} %collective-permute-done.19.refs_3_.refs_8_, ...), custom_call_target="tpu_custom_call" | custom-call | flops 999999995904 | bytes 1024 | tf_op jit(solution)/shard_map/feed_down/pallas_call | solution.py:40
  188.4 6.9 %token_learner.1 = (bf16[576,1024]{1,0:T(8,128)(2,1)}, f32[8,1024]{1,0:T(8,128)S(1)}, f32[576,1024]{1,0:T(8,128)S(1)}, bf16[576,1024]{1,0:T(8,128)(2,1)S(1)}, f3...) custom-call(f32[576,1024]{1,0:T(8,128)S(1)} %copy-done.31, f32[576,1024]{1,0:T(8,128)S(1)} %feed_down.3.refs_1_.refs_10_, ...), custom_call_target="tpu_custom_call" | custom-call | flops 999999995904 | bytes 1024 | tf_op jit(solution)/shard_map/token_learner/pallas_call | solution.py:40
  200.0 6.5 %weight_grad.4.refs_5_ = bf16[1024,1024]{1,0:T(8,128)(2,1)} custom-call(s32[16]{0:T(128)S(1)} %and_add_fusion.refs_0_.refs_1_, bf16[2048,640]{1,0:T(8,128)(2,1)S(1)} %copy-done.24, bf16[2048,640]{1,0:T(8,128)(2,1)} %get-tuple-element.122.refs_2_, bf16[576,1024]{1,0:T(8,128)(2,1)S(1)} %get-tuple-element.123.refs_3_.refs_10_, ...), custom_call_target="tpu_custom_call" | custom-call | flops 999999995904 | bytes 1024 | tf_op jit(solution)/shard_map/weight_grad/pallas_call | solution.py:40
  207.8 5.6 %weight_grad.5.refs_3_.refs_0_.refs_1_ = bf16[1024,1024]{1,0:T(8,128)(2,1)S(1)} custom-call(s32[16]{0:T(128)S(1)} %and_add_fusion.refs_0_.refs_1_, bf16[2048,640]{1,0:T(8,128)(2,1)S(1)} %copy-done.24, bf16[2048,640]{1,0:T(8,128)(2,1)} %get-tuple-element.122.refs_2_, bf16[576,1024]{1,0:T(8,128)(2,1)S(1)} %get-tuple-element.123.refs_3_.refs_10_, ...), custom_call_target="tpu_custom_call" | custom-call | flops 999999995904 | bytes 1024 | tf_op jit(solution)/shard_map/weight_grad/pallas_call | solution.py:40
  214.7 20.1 %feed_back.1 = (bf16[1152,2048]{1,0:T(8,128)(2,1)}, f32[1,2048]{1,0:T(1,128)S(1)}, f32[576,1024]{1,0:T(8,128)}, f32[576,1024]{1,0:T(8,128)}) custom-call(s32[32]{0:T(128)S(1)} %reshape.301.refs_0_, s32[16]{0:T(128)S(1)} %and_add_fusion.refs_0_.refs_1_, bf16[256,2048]{1,0:T(8,128)(2,1)} %stack.18.refs_2_.refs_1_, ...), custom_call_target="tpu_custom_call" | custom-call | flops 999999995904 | bytes 1024 | tf_op jit(solution)/shard_map/feed_back/pallas_call | solution.py:40
  234.9 3.3 add_parts.10
  239.0 10.4 %weight_grad.6 = (bf16[512,2048]{1,0:T(8,128)(2,1)}, bf16[512,2048]{1,0:T(8,128)(2,1)S(1)}) custom-call(s32[32]{0:T(128)S(1)} %reshape.301.refs_0_, bf16[1024,640]{1,0:T(8,128)(2,1)S(1)} %copy-done.46, bf16[1024,640]{1,0:T(8,128)(2,1)S(1)} %copy-done.48, bf16[1152,2048]{1,0:T(8,128)(2,1)} %get-tuple-element.129.refs_4_.refs_3_, ...), custom_call_target="tpu_custom_call" | custom-call | flops 999999995904 | bytes 1024 | tf_op jit(solution)/shard_map/weight_grad/pallas_call | solution.py:40
  250.8 5.6 %second_norm_back.1 = (f32[576,1024]{1,0:T(8,128)S(1)}, bf16[576,1024]{1,0:T(8,128)(2,1)}, f32[3,1024]{1,0:T(4,128)S(1)}) custom-call(f32[576,1024]{1,0:T(8,128)S(1)} %copy-done.27, f32[576,1024]{1,0:T(8,128)} %collective-permute-done.26.refs_1_, f32[576,1024]{1,0:T(8,128)} %copy-done.30, f32[576,1024]{1,0:T(8,128)} %copy-done.32, ...), custom_call_target="tpu_custom_call" | custom-call | flops 999999995904 | bytes 1024 | tf_op jit(solution)/shard_map/second_norm_back/pallas_call | solution.py:40
  257.7 2.0 add_parts.11
  261.7 14.9 %attend_back.2 = (bf16[3,576,512]{2,1,0:T(8,128)(2,1)S(1)}, f32[2,512]{1,0:T(2,128)S(1)}) custom-call(s32[16]{0:T(128)S(1)} %and_add_fusion.refs_0_.refs_1_, bf16[256,2176]{1,0:T(8,128)(2,1)} %stack.15.refs_2_.refs_1_, bf16[256,2176]{1,0:T(8,128)(2,1)} %collective-permute-done.3.refs_3_.refs_2_, bf16[256,2176]{1,0:T(8,128)(2,1)} %collective-permute-done.4.refs_4_.refs_3_, ...), custom_call_target="tpu_custom_call" | custom-call | flops 999999995904 | bytes 1024 | tf_op jit(solution)/shard_map/attend_back/pallas_call | solution.py:40
  276.6 15.5 %attend_back.3 = (bf16[3,576,512]{2,1,0:T(8,128)(2,1)S(1)}, f32[2,512]{1,0:T(2,128)S(1)}) custom-call(s32[16]{0:T(128)S(1)} %and_add_fusion.refs_0_.refs_1_, bf16[256,2176]{1,0:T(8,128)(2,1)} %stack.15.refs_2_.refs_1_, bf16[256,2176]{1,0:T(8,128)(2,1)} %collective-permute-done.3.refs_3_.refs_2_, bf16[256,2176]{1,0:T(8,128)(2,1)} %collective-permute-done.4.refs_4_.refs_3_, ...), custom_call_target="tpu_custom_call" | custom-call | flops 999999995904 | bytes 1024 | tf_op jit(solution)/shard_map/attend_back/pallas_call | solution.py:40
  292.1 2.4 add_parts.12
  294.5 4.2 %collective-permute-start.34 = (bf16[128,1024]{1,0:T(8,128)(2,1)}, bf16[128,1024]{1,0:T(8,128)(2,1)}, u32[]{:S(2)}, u32[]{:S(2)}) collective-permute-start(bf16[128,1024]{1,0:T(8,128)(2,1)} %get-tuple-element.156), channel_id=1, source_target_pairs={{0,16},{1,17},{2,18},{3,19},{4,20},{5,21},{6,22},{7,23},{8,24},{9,... | collective-permute-start | bytes 786440 | tf_op jit(solution)/shard_map/ppermute | solution.py:85
  298.7 3.3 add_parts.13
  303.1 8.6 %weight_grad.7 = (bf16[512,1024]{1,0:T(8,128)(2,1)}, bf16[512,1024]{1,0:T(8,128)(2,1)S(1)}) custom-call(s32[32]{0:T(128)S(1)} %reshape.301.refs_0_, bf16[1024,1280]{1,0:T(8,128)(2,1)S(1)} %copy-done.26, bf16[3,576,512]{2,1,0:T(8,128)(2,1)S(1)} %copy-done.40, bf16[3,576,512]{2,1,0:T(8,128)(2,1)S(1)} %copy-done.42, ...), custom_call_target="tpu_custom_call" | custom-call | flops 999999995904 | bytes 1024 | tf_op jit(solution)/shard_map/weight_grad/pallas_call | solution.py:40
  311.8 5.3 %collective-permute-done.31.refs_2_.refs_3_ = bf16[256,2048]{1,0:T(8,128)(2,1)} collective-permute-done((bf16[256,2048]{1,0:T(8,128)(2,1)}, bf16[256,2048]{1,0:T(8,128)(2,1)}, u32[]{:S(2)}, u32[]{:S(2)}) %collective-permute-start.31) | collective-permute-done | bytes 1048608 | tf_op jit(solution)/shard_map/ppermute | solution.py:85
  317.1 2.0 add_parts.14
  322.6 8.4 %value_and_out_grad.1 = (bf16[512,1024]{1,0:T(8,128)(2,1)S(1)}, bf16[512,1024]{1,0:T(8,128)(2,1)}) custom-call(s32[32]{0:T(128)S(1)} %reshape.301.refs_0_, s32[16]{0:T(128)S(1)} %and_add_fusion.refs_0_.refs_1_, bf16[1024,1280]{1,0:T(8,128)(2,1)} %copy-done.25, bf16[512,1280]{1,0:T(8,128)(2,1)S(1)} %copy-done.44, bf16[3,576,512]{2,1,0:T(8,128)(2,1)S(1)} %copy-done.40, ...), custom_call_target="tpu_custom_call" | custom-call | flops 999999995904 | bytes 1024 | tf_op jit(solution)/shard_map/value_and_out_grad/pallas_call | solution.py:40
  335.8 2.0 add_parts.16
  339.5 10.3 %project_back.1 = (f32[576,1024]{1,0:T(8,128)}, f32[576,1024]{1,0:T(8,128)}) custom-call(s32[32]{0:T(128)S(1)} %reshape.301.refs_0_, bf16[256,2176]{1,0:T(8,128)(2,1)} %stack.15.refs_2_.refs_1_, bf16[256,2176]{1,0:T(8,128)(2,1)} %collective-permute-done.3.refs_3_.refs_2_, bf16[256,2176]{1,0:T(8,128)(2,1)} %collective-permute-done.4.refs_4_.refs_3_, ...), custom_call_target="tpu_custom_call" | custom-call | flops 999999995904 | bytes 1024 | tf_op jit(solution)/shard_map/project_back/pallas_call | solution.py:40
  349.9 3.0 collective-permute-done.37.refs_4_.refs_5_.refs_6_.refs_7_
  358.2 2.1 add_parts.18
  365.6 2.0 collective-permute-start.42
  371.4 4.6 %first_norm_back.1 = (bf16[576,1024]{1,0:T(8,128)(2,1)}, f32[2,1024]{1,0:T(2,128)S(1)}) custom-call(f32[576,1024]{1,0:T(8,128)S(1)} %copy-done.36, f32[576,1024]{1,0:T(8,128)} %collective-permute-done.38.refs_1_, bf16[576,1024]{1,0:T(8,128)(2,1)} %bitcast.11.refs_5_.refs_2_, f32[576,2]{1,0:T(8,128)S(1)} %get-tuple-element.171.refs_3_, ...), custom_call_target="tpu_custom_call" | custom-call | flops 999999995904 | bytes 1024 | tf_op jit(solution)/shard_map/first_norm_back/pallas_call | solution.py:40
  378.4 3.3 all-to-all-start
  381.7 1.8 add_parts.19
  383.5 2.6 collective-permute-start.45
  392.2 2.2 all-to-all-done.refs_0_
  397.1 2.9 collective-permute-done.45.refs_1_
  (325 shorter events, 100.9 us)
Async XLA Ops:
  6.8 16.9 %collective-permute-start.1 = (bf16[64,2176]{1,0:T(8,128)(2,1)S(1)}, bf16[64,2176]{1,0:T(8,128)(2,1)S(1)}, u32[]{:S(2)}, u32[]{:S(2)}) collective-permute-start(bf16[64,2176]{1,0:T(8,128)(2,1)S(1)} %maximum_maximum_fusion.refs_0_), channel_id=1, source_target_pairs={{0,16},{1,17},{2,18},{3,19},{4,20},{5,21},{6,22},{7,23},{8,24},{9,... | collective-permute-start | bytes 835592 | tf_op jit(solution)/shard_map/ppermute | solution.py:85
  23.9 14.2 %collective-permute-start.2 = (bf16[128,2176]{1,0:T(8,128)(2,1)S(1)}, bf16[128,2176]{1,0:T(8,128)(2,1)S(1)}, u32[]{:S(2)}, u32[]{:S(2)}) collective-permute-start(bf16[128,2176]{1,0:T(8,128)(2,1)S(1)} %stack.14.refs_0_.refs_2_), channel_id=1, source_target_pairs={{0,8},{1,9},{2,10},{3,11},{4,12},{5,13},{6,14},{7,15},{8,0},{9,1},... | collective-permute-start | bytes 1671176 | tf_op jit(solution)/shard_map/ppermute | solution.py:85
  25.5 16.4 %collective-permute-start.6 = (bf16[32,2048]{1,0:T(8,128)(2,1)}, bf16[32,2048]{1,0:T(8,128)(2,1)}, u32[]{:S(2)}, u32[]{:S(2)}) collective-permute-start(bf16[32,2048]{1,0:T(8,128)(2,1)} %bitcast.51), channel_id=1, source_target_pairs={{0,2},{1,3},{2,0},{3,1},{4,6},{5,7},{6,4},{7,5},{8,10},{9,11},{10,... | collective-permute-start | bytes 393224 | tf_op jit(solution)/shard_map/ppermute | solution.py:95
  26.2 77.7 %collective-permute-start.13 = (bf16[1,4,1024]{2,1,0:T(4,128)(2,1)}, bf16[1,4,1024]{2,1,0:T(4,128)(2,1)}, u32[]{:S(2)}, u32[]{:S(2)}) collective-permute-start(bf16[1,4,1024]{2,1,0:T(4,128)(2,1)} %get-tuple-element.286), channel_id=1, source_target_pairs={{0,1},{1,0},{2,3},{3,2},{4,5},{5,4},{6,7},{7,6},{8,9},{9,8},{10,11... | collective-permute-start | bytes 24584 | tf_op jit(solution)/shard_map/ppermute | solution.py:85
  28.3 40.8 %collective-permute-start.10 = (f32[1,576]{1,0:T(1,128)}, f32[1,576]{1,0:T(1,128)}, u32[]{:S(2)}, u32[]{:S(2)}) collective-permute-start(f32[1,576]{1,0:T(1,128)} %convert_element_type.32), channel_id=1, source_target_pairs={{0,2},{1,3},{2,0},{3,1},{4,6},{5,7},{6,4},{7,5},{8,10},{9,11},{10,... | collective-permute-start | bytes 6920 | tf_op jit(solution)/shard_map/ppermute | solution.py:95
  39.2 26.2 %collective-permute-start.3 = (bf16[256,2176]{1,0:T(8,128)(2,1)}, bf16[256,2176]{1,0:T(8,128)(2,1)}, u32[]{:S(2)}, u32[]{:S(2)}) collective-permute-start(bf16[256,2176]{1,0:T(8,128)(2,1)} %stack.15.refs_2_.refs_1_), channel_id=1, source_target_pairs={{0,4},{1,5},{2,3},{3,2},{4,0},{5,1},{6,7},{7,6},{8,12},{9,13},{10,... | collective-permute-start | bytes 3342344 | tf_op jit(solution)/shard_map/ppermute | solution.py:85
  40.4 24.9 %collective-permute-start.4 = (bf16[256,2176]{1,0:T(8,128)(2,1)}, bf16[256,2176]{1,0:T(8,128)(2,1)}, u32[]{:S(2)}, u32[]{:S(2)}) collective-permute-start(bf16[256,2176]{1,0:T(8,128)(2,1)} %stack.15.refs_2_.refs_1_), channel_id=1, source_target_pairs={{0,1},{1,0},{2,6},{3,7},{4,5},{5,4},{6,2},{7,3},{8,9},{9,8},{10,14... | collective-permute-start | bytes 3342344 | tf_op jit(solution)/shard_map/ppermute | solution.py:85
  42.9 23.5 %collective-permute-start.8 = (bf16[64,2048]{1,0:T(8,128)(2,1)S(1)}, bf16[64,2048]{1,0:T(8,128)(2,1)S(1)}, u32[]{:S(2)}, u32[]{:S(2)}) collective-permute-start(bf16[64,2048]{1,0:T(8,128)(2,1)S(1)} %stack.16.refs_0_.refs_2_), channel_id=1, source_target_pairs={{0,16},{1,17},{2,18},{3,19},{4,20},{5,21},{6,22},{7,23},{8,24},{9,... | collective-permute-start | bytes 786440 | tf_op jit(solution)/shard_map/ppermute | solution.py:85
  65.3 15.8 %collective-permute-start.5 = (bf16[256,2176]{1,0:T(8,128)(2,1)}, bf16[256,2176]{1,0:T(8,128)(2,1)}, u32[]{:S(2)}, u32[]{:S(2)}) collective-permute-start(bf16[256,2176]{1,0:T(8,128)(2,1)} %collective-permute-done.3.refs_3_.refs_2_), channel_id=1, source_target_pairs={{0,1},{1,0},{2,6},{3,7},{4,5},{5,4},{6,2},{7,3},{8,9},{9,8},{10,14... | collective-permute-start | bytes 3342344 | tf_op jit(solution)/shard_map/ppermute | solution.py:85
  66.5 14.1 %collective-permute-start.9 = (bf16[128,2048]{1,0:T(8,128)(2,1)S(1)}, bf16[128,2048]{1,0:T(8,128)(2,1)S(1)}, u32[]{:S(2)}, u32[]{:S(2)}) collective-permute-start(bf16[128,2048]{1,0:T(8,128)(2,1)S(1)} %stack.17.refs_0_.refs_2_), channel_id=1, source_target_pairs={{0,8},{1,9},{2,10},{3,11},{4,12},{5,13},{6,14},{7,15},{8,0},{9,1},... | collective-permute-start | bytes 1572872 | tf_op jit(solution)/shard_map/ppermute | solution.py:85
  70.1 20.6 %collective-permute-start.7 = (bf16[576,1024]{1,0:T(8,128)(2,1)}, bf16[576,1024]{1,0:T(8,128)(2,1)}, u32[]{:S(2)}, u32[]{:S(2)}) collective-permute-start(bf16[576,1024]{1,0:T(8,128)(2,1)} %bitcast.11.refs_5_.refs_2_), channel_id=1, source_target_pairs={{0,2},{1,3},{2,0},{3,1},{4,6},{5,7},{6,4},{7,5},{8,10},{9,11},{10,... | collective-permute-start | bytes 3538952 | tf_op jit(solution)/shard_map/ppermute | solution.py:95
  82.2 26.2 %collective-permute-start.12 = (bf16[256,2048]{1,0:T(8,128)(2,1)}, bf16[256,2048]{1,0:T(8,128)(2,1)}, u32[]{:S(2)}, u32[]{:S(2)}) collective-permute-start(bf16[256,2048]{1,0:T(8,128)(2,1)} %stack.18.refs_2_.refs_1_), channel_id=1, source_target_pairs={{0,4},{1,5},{2,3},{3,2},{4,0},{5,1},{6,7},{7,6},{8,12},{9,13},{10,... | collective-permute-start | bytes 3145736 | tf_op jit(solution)/shard_map/ppermute | solution.py:85
  84.4 23.9 %collective-permute-start.11 = (bf16[64,2048]{1,0:T(8,128)(2,1)}, bf16[64,2048]{1,0:T(8,128)(2,1)}, u32[]{:S(2)}, u32[]{:S(2)}) collective-permute-start(bf16[64,2048]{1,0:T(8,128)(2,1)} %stack.19.refs_5_.refs_0_), channel_id=1, source_target_pairs={{0,16},{1,17},{2,18},{3,19},{4,20},{5,21},{6,22},{7,23},{8,24},{9,... | collective-permute-start | bytes 786440 | tf_op jit(solution)/shard_map/ppermute | solution.py:85
  90.2 18.2 %collective-permute-start.14 = (bf16[256,2048]{1,0:T(8,128)(2,1)}, bf16[256,2048]{1,0:T(8,128)(2,1)}, u32[]{:S(2)}, u32[]{:S(2)}) collective-permute-start(bf16[256,2048]{1,0:T(8,128)(2,1)} %stack.18.refs_2_.refs_1_), channel_id=1, source_target_pairs={{0,1},{1,0},{2,6},{3,7},{4,5},{5,4},{6,2},{7,3},{8,9},{9,8},{10,14... | collective-permute-start | bytes 3145736 | tf_op jit(solution)/shard_map/ppermute | solution.py:85
  111.1 19.0 %collective-permute-start.16 = (bf16[256,2048]{1,0:T(8,128)(2,1)}, bf16[256,2048]{1,0:T(8,128)(2,1)}, u32[]{:S(2)}, u32[]{:S(2)}) collective-permute-start(bf16[256,2048]{1,0:T(8,128)(2,1)} %get-tuple-element.113.refs_2_.refs_3_), channel_id=1, source_target_pairs={{0,1},{1,0},{2,6},{3,7},{4,5},{5,4},{6,2},{7,3},{8,9},{9,8},{10,14... | collective-permute-start | bytes 3145736 | tf_op jit(solution)/shard_map/ppermute | solution.py:85
  112.7 17.5 %collective-permute-start.15 = (bf16[128,2048]{1,0:T(8,128)(2,1)}, bf16[128,2048]{1,0:T(8,128)(2,1)}, u32[]{:S(2)}, u32[]{:S(2)}) collective-permute-start(bf16[128,2048]{1,0:T(8,128)(2,1)} %get-tuple-element.111.refs_4_.refs_0_), channel_id=1, source_target_pairs={{0,8},{1,9},{2,10},{3,11},{4,12},{5,13},{6,14},{7,15},{8,0},{9,1},... | collective-permute-start | bytes 1572872 | tf_op jit(solution)/shard_map/ppermute | solution.py:85
  132.5 27.4 %collective-permute-start.18 = (bf16[256,2048]{1,0:T(8,128)(2,1)}, bf16[256,2048]{1,0:T(8,128)(2,1)}, u32[]{:S(2)}, u32[]{:S(2)}) collective-permute-start(bf16[256,2048]{1,0:T(8,128)(2,1)} %stack.21.refs_6_.refs_1_), channel_id=1, source_target_pairs={{0,4},{1,5},{2,3},{3,2},{4,0},{5,1},{6,7},{7,6},{8,12},{9,13},{10,... | collective-permute-start | bytes 3145736 | tf_op jit(solution)/shard_map/ppermute | solution.py:85
  137.2 4.9 %collective-permute-start.17 = (f32[576,1024]{1,0:T(8,128)}, f32[576,1024]{1,0:T(8,128)}, u32[]{:S(2)}, u32[]{:S(2)}) collective-permute-start(f32[576,1024]{1,0:T(8,128)} %mix_out.2.refs_6_), channel_id=1, source_target_pairs={{0,2},{1,3},{2,0},{3,1},{4,6},{5,7},{6,4},{7,5},{8,10},{9,11},{10,... | collective-permute-start | bytes 7077896 | tf_op jit(solution)/shard_map/ppermute | solution.py:95
  137.3 22.6 %collective-permute-start.19 = (bf16[256,2048]{1,0:T(8,128)(2,1)}, bf16[256,2048]{1,0:T(8,128)(2,1)}, u32[]{:S(2)}, u32[]{:S(2)}) collective-permute-start(bf16[256,2048]{1,0:T(8,128)(2,1)} %stack.21.refs_6_.refs_1_), channel_id=1, source_target_pairs={{0,1},{1,0},{2,6},{3,7},{4,5},{5,4},{6,2},{7,3},{8,9},{9,8},{10,14... | collective-permute-start | bytes 3145736 | tf_op jit(solution)/shard_map/ppermute | solution.py:85
  146.9 14.3 %collective-permute-start.21 = (bf16[576,1024]{1,0:T(8,128)(2,1)}, bf16[576,1024]{1,0:T(8,128)(2,1)}, u32[]{:S(2)}, u32[]{:S(2)}) collective-permute-start(bf16[576,1024]{1,0:T(8,128)(2,1)} %get-tuple-element.115.refs_5_), channel_id=1, source_target_pairs={{0,2},{1,3},{2,0},{3,1},{4,6},{5,7},{6,4},{7,5},{8,10},{9,11},{10,... | collective-permute-start | bytes 3538952 | tf_op jit(solution)/shard_map/ppermute | solution.py:95
  159.9 15.1 %collective-permute-start.20 = (bf16[256,2048]{1,0:T(8,128)(2,1)}, bf16[256,2048]{1,0:T(8,128)(2,1)}, u32[]{:S(2)}, u32[]{:S(2)}) collective-permute-start(bf16[256,2048]{1,0:T(8,128)(2,1)} %collective-permute-done.18.refs_2_.refs_7_), channel_id=1, source_target_pairs={{0,1},{1,0},{2,6},{3,7},{4,5},{5,4},{6,2},{7,3},{8,9},{9,8},{10,14... | collective-permute-start | bytes 3145736 | tf_op jit(solution)/shard_map/ppermute | solution.py:85
  182.3 6.0 %collective-permute-start.22 = (f32[576,1024]{1,0:T(8,128)}, f32[576,1024]{1,0:T(8,128)}, u32[]{:S(2)}, u32[]{:S(2)}) collective-permute-start(f32[576,1024]{1,0:T(8,128)} %feed_down.2.refs_6_), channel_id=1, source_target_pairs={{0,2},{1,3},{2,0},{3,1},{4,6},{5,7},{6,4},{7,5},{8,10},{9,11},{10,... | collective-permute-start | bytes 7077896 | tf_op jit(solution)/shard_map/ppermute | solution.py:95
  195.3 2.9 collective-permute-start.24
  196.7 16.7 %collective-permute-start.23 = (f32[1,4,1024]{2,1,0:T(4,128)}, f32[1,4,1024]{2,1,0:T(4,128)}, u32[]{:S(2)}, u32[]{:S(2)}) collective-permute-start(f32[1,4,1024]{2,1,0:T(4,128)} %get-tuple-element.284), channel_id=1, source_target_pairs={{0,1},{1,0},{2,3},{3,2},{4,5},{5,4},{6,7},{7,6},{8,9},{9,8},{10,11... | collective-permute-start | bytes 49160 | tf_op jit(solution)/shard_map/ppermute | solution.py:85
  206.5 28.4 %collective-permute-start.25 = (bf16[1024,1024]{1,0:T(8,128)(2,1)}, bf16[1024,1024]{1,0:T(8,128)(2,1)}, u32[]{:S(2)}, u32[]{:S(2)}) collective-permute-start(bf16[1024,1024]{1,0:T(8,128)(2,1)} %weight_grad.4.refs_5_), channel_id=1, source_target_pairs={{0,1},{1,0},{2,6},{3,7},{4,5},{5,4},{6,2},{7,3},{8,9},{9,8},{10,14... | collective-permute-start | bytes 6291464 | tf_op jit(solution)/shard_map/ppermute | solution.py:85
  238.1 12.6 %collective-permute-start.26 = (f32[576,1024]{1,0:T(8,128)}, f32[576,1024]{1,0:T(8,128)}, u32[]{:S(2)}, u32[]{:S(2)}) collective-permute-start(f32[576,1024]{1,0:T(8,128)} %get-tuple-element.131), channel_id=1, source_target_pairs={{0,2},{1,3},{2,0},{3,1},{4,6},{5,7},{6,4},{7,5},{8,10},{9,11},{10,... | collective-permute-start | bytes 7077896 | tf_op jit(solution)/shard_map/ppermute | solution.py:95
  238.5 19.2 %collective-permute-start.27 = (bf16[512,1024]{1,0:T(8,128)(2,1)}, bf16[512,1024]{1,0:T(8,128)(2,1)}, u32[]{:S(2)}, u32[]{:S(2)}) collective-permute-start(bf16[512,1024]{1,0:T(8,128)(2,1)} %get-tuple-element.137), channel_id=1, source_target_pairs={{0,4},{1,5},{2,3},{3,2},{4,0},{5,1},{6,7},{7,6},{8,12},{9,13},{10,... | collective-permute-start | bytes 3145736 | tf_op jit(solution)/shard_map/ppermute | solution.py:85
  259.7 16.9 %collective-permute-start.28 = (bf16[576,1024]{1,0:T(8,128)(2,1)}, bf16[576,1024]{1,0:T(8,128)(2,1)}, u32[]{:S(2)}, u32[]{:S(2)}) collective-permute-start(bf16[576,1024]{1,0:T(8,128)(2,1)} %get-tuple-element.141.refs_10_.refs_6_), channel_id=1, source_target_pairs={{0,2},{1,3},{2,0},{3,1},{4,6},{5,7},{6,4},{7,5},{8,10},{9,11},{10,... | collective-permute-start | bytes 3538952 | tf_op jit(solution)/shard_map/ppermute | solution.py:95
  259.8 32.3 %collective-permute-start.30 = (bf16[256,1024]{1,0:T(8,128)(2,1)}, bf16[256,1024]{1,0:T(8,128)(2,1)}, u32[]{:S(2)}, u32[]{:S(2)}) collective-permute-start(bf16[256,1024]{1,0:T(8,128)(2,1)} %get-tuple-element.146), channel_id=1, source_target_pairs={{0,8},{1,9},{2,10},{3,11},{4,12},{5,13},{6,14},{7,15},{8,0},{9,1},... | collective-permute-start | bytes 1572872 | tf_op jit(solution)/shard_map/ppermute | solution.py:85
  260.5 38.2 %collective-permute-start.29 = (bf16[512,2048]{1,0:T(8,128)(2,1)}, bf16[512,2048]{1,0:T(8,128)(2,1)}, u32[]{:S(2)}, u32[]{:S(2)}) collective-permute-start(bf16[512,2048]{1,0:T(8,128)(2,1)} %get-tuple-element.145.refs_5_), channel_id=1, source_target_pairs={{0,1},{1,0},{2,6},{3,7},{4,5},{5,4},{6,2},{7,3},{8,9},{9,8},{10,14... | collective-permute-start | bytes 6291464 | tf_op jit(solution)/shard_map/ppermute | solution.py:85
  294.5 26.6 %collective-permute-start.34 = (bf16[128,1024]{1,0:T(8,128)(2,1)}, bf16[128,1024]{1,0:T(8,128)(2,1)}, u32[]{:S(2)}, u32[]{:S(2)}) collective-permute-start(bf16[128,1024]{1,0:T(8,128)(2,1)} %get-tuple-element.156), channel_id=1, source_target_pairs={{0,16},{1,17},{2,18},{3,19},{4,20},{5,21},{6,22},{7,23},{8,24},{9,... | collective-permute-start | bytes 786440 | tf_op jit(solution)/shard_map/ppermute | solution.py:85
  302.0 15.1 %collective-permute-start.31 = (bf16[256,2048]{1,0:T(8,128)(2,1)}, bf16[256,2048]{1,0:T(8,128)(2,1)}, u32[]{:S(2)}, u32[]{:S(2)}) collective-permute-start(bf16[256,2048]{1,0:T(8,128)(2,1)} %get-tuple-element.151), channel_id=1, source_target_pairs={{0,4},{1,5},{2,3},{3,2},{4,0},{5,1},{6,7},{7,6},{8,12},{9,13},{10,... | collective-permute-start | bytes 3145736 | tf_op jit(solution)/shard_map/ppermute | solution.py:85
  319.1 12.7 %collective-permute-start.33 = (bf16[128,2048]{1,0:T(8,128)(2,1)}, bf16[128,2048]{1,0:T(8,128)(2,1)}, u32[]{:S(2)}, u32[]{:S(2)}) collective-permute-start(bf16[128,2048]{1,0:T(8,128)(2,1)} %get-tuple-element.154), channel_id=1, source_target_pairs={{0,8},{1,9},{2,10},{3,11},{4,12},{5,13},{6,14},{7,15},{8,0},{9,1},... | collective-permute-start | bytes 1572872 | tf_op jit(solution)/shard_map/ppermute | solution.py:85
  320.7 15.1 %collective-permute-start.32 = (bf16[512,1024]{1,0:T(8,128)(2,1)}, bf16[512,1024]{1,0:T(8,128)(2,1)}, u32[]{:S(2)}, u32[]{:S(2)}) collective-permute-start(bf16[512,1024]{1,0:T(8,128)(2,1)} %get-tuple-element.153.refs_4_), channel_id=1, source_target_pairs={{0,1},{1,0},{2,6},{3,7},{4,5},{5,4},{6,2},{7,3},{8,9},{9,8},{10,14... | collective-permute-start | bytes 3145736 | tf_op jit(solution)/shard_map/ppermute | solution.py:85
  333.6 22.8 %collective-permute-start.36 = (bf16[64,2048]{1,0:T(8,128)(2,1)}, bf16[64,2048]{1,0:T(8,128)(2,1)}, u32[]{:S(2)}, u32[]{:S(2)}) collective-permute-start(bf16[64,2048]{1,0:T(8,128)(2,1)} %get-tuple-element.165), channel_id=1, source_target_pairs={{0,16},{1,17},{2,18},{3,19},{4,20},{5,21},{6,22},{7,23},{8,24},{9,... | collective-permute-start | bytes 786440 | tf_op jit(solution)/shard_map/ppermute | solution.py:85
  337.7 15.2 %collective-permute-start.37 = (bf16[256,1024]{1,0:T(8,128)(2,1)}, bf16[256,1024]{1,0:T(8,128)(2,1)}, u32[]{:S(2)}, u32[]{:S(2)}) collective-permute-start(bf16[256,1024]{1,0:T(8,128)(2,1)} %get-tuple-element.166), channel_id=1, source_target_pairs={{0,4},{1,5},{2,3},{3,2},{4,0},{5,1},{6,7},{7,6},{8,12},{9,13},{10,... | collective-permute-start | bytes 1572872 | tf_op jit(solution)/shard_map/ppermute | solution.py:85
  338.3 19.9 %collective-permute-start.35 = (bf16[512,1024]{1,0:T(8,128)(2,1)}, bf16[512,1024]{1,0:T(8,128)(2,1)}, u32[]{:S(2)}, u32[]{:S(2)}) collective-permute-start(bf16[512,1024]{1,0:T(8,128)(2,1)} %get-tuple-element.164), channel_id=1, source_target_pairs={{0,1},{1,0},{2,6},{3,7},{4,5},{5,4},{6,2},{7,3},{8,9},{9,8},{10,14... | collective-permute-start | bytes 3145736 | tf_op jit(solution)/shard_map/ppermute | solution.py:85
  360.4 7.2 %collective-permute-start.38 = (f32[576,1024]{1,0:T(8,128)}, f32[576,1024]{1,0:T(8,128)}, u32[]{:S(2)}, u32[]{:S(2)}) collective-permute-start(f32[576,1024]{1,0:T(8,128)} %get-tuple-element.170), channel_id=1, source_target_pairs={{0,2},{1,3},{2,0},{3,1},{4,6},{5,7},{6,4},{7,5},{8,10},{9,11},{10,... | collective-permute-start | bytes 7077896 | tf_op jit(solution)/shard_map/ppermute | solution.py:95
  363.2 23.0 %collective-permute-start.40 = (bf16[64,1024]{1,0:T(8,128)(2,1)}, bf16[64,1024]{1,0:T(8,128)(2,1)}, u32[]{:S(2)}, u32[]{:S(2)}) collective-permute-start(bf16[64,1024]{1,0:T(8,128)(2,1)} %get-tuple-element.181), channel_id=1, source_target_pairs={{0,16},{1,17},{2,18},{3,19},{4,20},{5,21},{6,22},{7,23},{8,24},{9,... | collective-permute-start | bytes 393224 | tf_op jit(solution)/shard_map/ppermute | solution.py:85
  364.0 23.7 %collective-permute-start.41 = (bf16[64,1024]{1,0:T(8,128)(2,1)}, bf16[64,1024]{1,0:T(8,128)(2,1)}, u32[]{:S(2)}, u32[]{:S(2)}) collective-permute-start(bf16[64,1024]{1,0:T(8,128)(2,1)} %get-tuple-element.182), channel_id=1, source_target_pairs={{0,8},{1,9},{2,10},{3,11},{4,12},{5,13},{6,14},{7,15},{8,0},{9,1},... | collective-permute-start | bytes 393224 | tf_op jit(solution)/shard_map/ppermute | solution.py:85
  365.6 22.4 %collective-permute-start.42 = (bf16[64,1024]{1,0:T(8,128)(2,1)}, bf16[64,1024]{1,0:T(8,128)(2,1)}, u32[]{:S(2)}, u32[]{:S(2)}) collective-permute-start(bf16[64,1024]{1,0:T(8,128)(2,1)} %get-tuple-element.183), channel_id=1, source_target_pairs={{0,24},{1,25},{2,26},{3,27},{4,28},{5,29},{6,30},{7,31},{8,16},{9,... | collective-permute-start | bytes 393224 | tf_op jit(solution)/shard_map/ppermute | solution.py:85
  367.6 22.1 %collective-permute-start.39 = (f32[32,2048]{1,0:T(8,128)}, f32[32,2048]{1,0:T(8,128)}, u32[]{:S(2)}, u32[]{:S(2)}) collective-permute-start(f32[32,2048]{1,0:T(8,128)} %get-tuple-element.180), channel_id=1, source_target_pairs={{0,2},{1,3},{2,0},{3,1},{4,6},{5,7},{6,4},{7,5},{8,10},{9,11},{10,... | collective-permute-start | bytes 786440 | tf_op jit(solution)/shard_map/ppermute | solution.py:95
  367.6 14.1 %collective-permute-start.43 = (bf16[256,1024]{1,0:T(8,128)(2,1)}, bf16[256,1024]{1,0:T(8,128)(2,1)}, u32[]{:S(2)}, u32[]{:S(2)}) collective-permute-start(bf16[256,1024]{1,0:T(8,128)(2,1)} %get-tuple-element.184), channel_id=1, source_target_pairs={{0,4},{1,5},{2,3},{3,2},{4,0},{5,1},{6,7},{7,6},{8,12},{9,13},{10,... | collective-permute-start | bytes 1572872 | tf_op jit(solution)/shard_map/ppermute | solution.py:85
  378.4 16.0 %all-to-all-start = ((bf16[32,32,128]{2,1,0:T(8,128)(2,1)}), bf16[32,32,128]{2,1,0:T(8,128)(2,1)}, u32[]{:S(2)}, u32[]{:S(2)}) async-start(bf16[32,32,128]{2,1,0:T(8,128)(2,1)} %bitcast.24), calls=%async_computation | async-start | bytes 524288 | tf_op jit(solution)/shard_map/all_to_all | solution.py:1418
  383.5 16.4 %collective-permute-start.45 = (bf16[64,1024]{1,0:T(8,128)(2,1)}, bf16[64,1024]{1,0:T(8,128)(2,1)}, u32[]{:S(2)}, u32[]{:S(2)}) collective-permute-start(bf16[64,1024]{1,0:T(8,128)(2,1)} %get-tuple-element.189), channel_id=1, source_target_pairs={{0,16},{1,17},{2,18},{3,19},{4,20},{5,21},{6,22},{7,23},{8,24},{9,... | collective-permute-start | bytes 393224 | tf_op jit(solution)/shard_map/ppermute | solution.py:85
  386.2 13.8 %collective-permute-start.46 = (bf16[64,1024]{1,0:T(8,128)(2,1)}, bf16[64,1024]{1,0:T(8,128)(2,1)}, u32[]{:S(2)}, u32[]{:S(2)}) collective-permute-start(bf16[64,1024]{1,0:T(8,128)(2,1)} %get-tuple-element.190), channel_id=1, source_target_pairs={{0,8},{1,9},{2,10},{3,11},{4,12},{5,13},{6,14},{7,15},{8,0},{9,1},... | collective-permute-start | bytes 393224 | tf_op jit(solution)/shard_map/ppermute | solution.py:85
  387.7 12.2 %collective-permute-start.47 = (bf16[64,1024]{1,0:T(8,128)(2,1)}, bf16[64,1024]{1,0:T(8,128)(2,1)}, u32[]{:S(2)}, u32[]{:S(2)}) collective-permute-start(bf16[64,1024]{1,0:T(8,128)(2,1)} %get-tuple-element.191), channel_id=1, source_target_pairs={{0,24},{1,25},{2,26},{3,27},{4,28},{5,29},{6,30},{7,31},{8,16},{9,... | collective-permute-start | bytes 393224 | tf_op jit(solution)/shard_map/ppermute | solution.py:85
  389.7 13.3 %collective-permute-start.44 = (f32[32,1024]{1,0:T(8,128)}, f32[32,1024]{1,0:T(8,128)}, u32[]{:S(2)}, u32[]{:S(2)}) collective-permute-start(f32[32,1024]{1,0:T(8,128)} %get-tuple-element.188), channel_id=1, source_target_pairs={{0,2},{1,3},{2,0},{3,1},{4,6},{5,7},{6,4},{7,5},{8,10},{9,11},{10,... | collective-permute-start | bytes 393224 | tf_op jit(solution)/shard_map/ppermute | solution.py:95
  (82 other events, 325.3 us)
